TPU v7x, 32 devices: a whole 2x2x4 slice. The times are simulated.
32 devices in a mesh: px: 4 (over y, core), py: 8 (over z, x).
Axes of the slice: x: 2, y: 2, z: 4, core: 2. Of those that a mesh axis runs over, the one named last changes fastest.
Arguments:
- control_start: float32 [2, 8, 64, 2048], P(None, 'py', None, 'px'), may hold values from -12 to 12
- coef_x: float32 [8, 64, 2048], P('py', None, 'px'), may hold values from 0.1 to 0.45
- coef_y: float32 [8, 64, 2048], P('py', 'px'), may hold values from 0.1 to 0.45
- innovation: float32 [32768, 128], P(('px', 'py')), may hold values from -6 to 6
- obs_weight: float32 [32768, 128], P(('px', 'py')), may hold values from 0.25 to 4
- interp: float32 [32768], P(('px', 'py')), may hold values from 0 to 1
- obs_owner: int32 [32768, 1], P(('px', 'py')), may hold values from 0 to 7; in each aligned block of 1024 rows (0 to 1023, 1024 to 2047, ...) at most 384 rows name the same one
- cell_key: int32 [32768], P(('px', 'py')), may hold values from 0 to 31
- stencil: int32 [32768], P(('px', 'py')), may hold values from 0 to 14
Outputs:
- control: float32 [2, 8, 64, 2048], P(None, 'py', None, 'px')
- residual: float32 [2, 8, 64, 2048], P(None, 'py', None, 'px')
Inputs may be any that keep to these rules, and one draw needn't show every extreme that they name: `obs_owner`: at most 384 of the observation rows of one device name the same owner, and exactly 384 do for some owner on some device.
All inputs are finite; a program needn't handle non-finite values.
Results may differ from a plain program's by a relative error of at most 0.00023.
Values sent between devices are 32-bit elements; how exact they have to be, the bound alone decides.
No kernel may reach another device: no remote copies, remote signals or barrier semaphores. Data moves between devices by JAX's collectives and lax.ppermute only.
A program may use at most 64 MiB of HBM per device.

v0:
```python
import jax
import jax.numpy as jnp
from jax import lax
from jax.sharding import PartitionSpec as P

F = 2
SEG = 128
M = 4
ITERS = 2
LZ = 1
LX = 16
NB = 16


def diffuse(values, coeffs, axis_dim):
    length = values.shape[axis_dim]
    face_coef = lax.slice_in_dim(coeffs[None], 0, length - 1, axis=axis_dim)
    pad_after = [(0, 0)] * values.ndim
    pad_before = [(0, 0)] * values.ndim
    pad_after[axis_dim] = (0, 1)
    pad_before[axis_dim] = (1, 0)
    for repeat in range(M):
        next_cell = lax.slice_in_dim(values, 1, length, axis=axis_dim)
        this_cell = lax.slice_in_dim(values, 0, length - 1, axis=axis_dim)
        flux_face = face_coef * (next_cell - this_cell)
        values = values + jnp.pad(flux_face, pad_after) - jnp.pad(flux_face, pad_before)
    return values


def build_interp(shares_in, rows_in, row_count):
    row_ids = jnp.arange(row_count, dtype=jnp.int32)[None, :]
    lower_hit = (rows_in[:, None] == row_ids).astype(jnp.float32)
    upper_hit = (rows_in[:, None] + NB == row_ids).astype(jnp.float32)
    shares = shares_in[:, None]
    return (1.0 - shares) * lower_hit + shares * upper_hit


def misfit(state_in, observed, weights, interp_matrix):
    flat_field = state_in.reshape(-1, SEG)
    modelled = jnp.dot(
        interp_matrix,
        flat_field,
        precision=lax.Precision.HIGHEST,
        preferred_element_type=jnp.float32,
    )
    weighted = weights * (observed - modelled)
    result = lax.dot_general(
        interp_matrix,
        weighted,
        (((0,), (0,)), ((), ())),
        precision=lax.Precision.HIGHEST,
        preferred_element_type=jnp.float32,
    )
    return result.reshape(state_in.shape)


def dot_total(left_side, right_side):
    return lax.psum(jnp.sum(left_side * right_side), ("px", "py"))


def shards(
    control_start, coef_x, coef_y, innovation, obs_weight, interp, obs_owner, cell_key, stencil
):
    groups = lax.axis_size("py")
    capacity = 3 * innovation.shape[0] // groups
    coef_x = coef_x.at[:, -1, :].set(0.0)
    coef_y = coef_y.at[:, :, -1].set(0.0)
    field_id = cell_key // (LZ * NB)
    level_local = cell_key // NB % LZ
    row_index = ((field_id * LZ + level_local) * LX + stencil) * NB + cell_key % NB
    targets = obs_owner[:, 0]
    onehot = (targets[:, None] == jnp.arange(groups, dtype=jnp.int32)[None, :]).astype(jnp.int32)
    earlier = jnp.cumsum(onehot, axis=0) - onehot
    slot_index = jnp.sum(earlier * onehot, axis=1)
    slot_target = targets * capacity + slot_index
    total_slots = groups * capacity

    def bucket(values_in):
        buf_shape = (total_slots,) + values_in.shape[1:]
        return jnp.zeros(buf_shape, values_in.dtype).at[slot_target].set(values_in)

    arrived = (
        lax.all_to_all(bucket(innovation), "py", split_axis=0, concat_axis=0, tiled=True),
        lax.all_to_all(bucket(obs_weight), "py", split_axis=0, concat_axis=0, tiled=True),
        lax.all_to_all(bucket(interp), "py", split_axis=0, concat_axis=0, tiled=True),
        lax.all_to_all(bucket(row_index), "py", split_axis=0, concat_axis=0, tiled=True),
    )
    observed, weights, shares_in, rows_in = arrived
    interp_matrix = build_interp(shares_in, rows_in, F * LZ * LX * NB)

    def forward(values_in):
        turned = lax.all_to_all(
            diffuse(values_in, coef_x, 2), "px", split_axis=2, concat_axis=3, tiled=True
        )
        return diffuse(turned, coef_y, 3)

    def adjoint(values_in):
        turned = lax.all_to_all(
            diffuse(values_in, coef_y, 3), "px", split_axis=3, concat_axis=2, tiled=True
        )
        return diffuse(turned, coef_x, 2)

    no_data = jnp.zeros_like(observed)
    residual = (
        adjoint(misfit(forward(control_start), observed, weights, interp_matrix)) - control_start
    )
    control = control_start
    direction = residual
    norm_now = dot_total(residual, residual)
    for repeat in range(ITERS):
        applied = direction - adjoint(misfit(forward(direction), no_data, weights, interp_matrix))
        step_size = norm_now / dot_total(direction, applied)
        control = control + step_size * direction
        residual = residual - step_size * applied
        norm_next = dot_total(residual, residual)
        direction = residual + norm_next / norm_now * direction
        norm_now = norm_next
    return (control, residual)


def solution(mesh):
    return jax.shard_map(
        shards,
        mesh=mesh,
        in_specs=(
            P(None, "py", None, "px"),
            P("py", None, "px"),
            P("py", "px", None),
            P(("px", "py"), None),
            P(("px", "py"), None),
            P(("px", "py")),
            P(("px", "py"), None),
            P(("px", "py")),
            P(("px", "py")),
        ),
        out_specs=(P(None, "py", None, "px"), P(None, "py", None, "px")),
        check_vma=False,
    )
```

profile of v0, /device:TPU:0, one launch (start us, length us, event | category | flops | bytes accessed | tf_op | source)
XLA Modules:
  0.0 408.2 jit_solution(5414545878473693141)
XLA Ops:
  5.5 5.0 %scatter_custom_fusion.1 = f32[3072]{0:T(1024)} fusion(s32[1024]{0:T(1024)S(1)} %bitcast.145, f32[1024]{0:T(1024)} %param.18, f32[]{:T(128)} %constant.119.clone.1), kind=kCustom, calls=%fused_computation.218 | custom fusion | bytes 12800 | tf_op jit(solution)/shard_map/scatter | solution.py:80
  10.6 7.3 %all-to-all-start.1 = ((f32[8,384,1]{1,2,0:T(1,128)}), f32[8,384,1]{1,2,0:T(1,128)S(1)}, u32[]{:S(2)}, u32[]{:S(2)}) async-start(f32[8,384,1]{1,2,0:T(1,128)} %bitcast.8), calls=%async_computation.1 | async-start | bytes 24576 | tf_op jit(solution)/shard_map/all_to_all | solution.py:85
  21.5 4.9 %scatter_custom_fusion = s32[3072]{0:T(1024)} fusion(s32[1024]{0:T(1024)S(1)} %bitcast.146, s32[1024]{0:T(1024)S(1)} %fusion.105, s32[]{:T(128)} %constant.110.clone.1), kind=kCustom, calls=%fused_computation.226 | custom fusion | bytes 12292 | tf_op jit(solution)/shard_map/scatter | solution.py:80
  26.4 6.0 %all-to-all-start = ((s32[8,384,1]{1,2,0:T(1,128)}), s32[8,384,1]{1,2,0:T(1,128)S(1)}, u32[]{:S(2)}, u32[]{:S(2)}) async-start(s32[8,384,1]{1,2,0:T(1,128)} %bitcast.6), calls=%async_computation | async-start | bytes 24576 | tf_op jit(solution)/shard_map/all_to_all | solution.py:86
  33.4 5.6 %all-to-all-done = s32[8,384,1]{1,2,0:T(1,128)S(1)} async-done(((s32[8,384,1]{1,2,0:T(1,128)}), s32[8,384,1]{1,2,0:T(1,128)S(1)}, u32[]{:S(2)}, u32[]{:S(2)}) %all-to-all-start) | async-done | bytes 12320 | tf_op jit(solution)/shard_map/all_to_all | solution.py:86
  42.4 4.7 %scatter_custom_fusion.2 = f32[3072,128]{1,0:T(8,128)} fusion(s32[1024]{0:T(1024)S(1)} %bitcast.147, f32[1024,128]{1,0:T(8,128)} %param.17, f32[]{:T(128)} %constant.119.clone.1), kind=kCustom, calls=%fused_computation.51 | custom fusion | bytes 1573376 | tf_op jit(solution)/shard_map/scatter | solution.py:80
  52.1 4.7 %scatter_custom_fusion.3 = f32[3072,128]{1,0:T(8,128)} fusion(s32[1024]{0:T(1024)S(1)} %bitcast.148, f32[1024,128]{1,0:T(8,128)} %param.16, f32[]{:T(128)} %constant.119.clone.1), kind=kCustom, calls=%fused_computation.49 | custom fusion | bytes 1573376 | tf_op jit(solution)/shard_map/scatter | solution.py:80
  57.2 31.9 %all-to-all-done.2 = f32[8,384,128]{2,1,0:T(8,128)S(1)} async-done(((f32[8,384,128]{2,1,0:T(8,128)}), f32[8,384,128]{2,1,0:T(8,128)S(1)}, u32[]{:S(2)}, u32[]{:S(2)}) %all-to-all-start.2) | async-done | bytes 1572896 | tf_op jit(solution)/shard_map/all_to_all | solution.py:84
  89.1 4.3 %all-to-all-start.3 = ((f32[8,384,128]{2,1,0:T(8,128)}), f32[8,384,128]{2,1,0:T(8,128)}, u32[]{:S(2)}, u32[]{:S(2)}) async-start(f32[8,384,128]{2,1,0:T(8,128)} %bitcast.12), calls=%async_computation.3 | async-start | bytes 3145728 | tf_op jit(solution)/shard_map/all_to_all | solution.py:83
  94.3 35.7 %all-to-all-done.3 = f32[8,384,128]{2,1,0:T(8,128)} async-done(((f32[8,384,128]{2,1,0:T(8,128)}), f32[8,384,128]{2,1,0:T(8,128)}, u32[]{:S(2)}, u32[]{:S(2)}) %all-to-all-start.3) | async-done | bytes 1572896 | tf_op jit(solution)/shard_map/all_to_all | solution.py:83
  130.0 9.3 %fusion.11 = f32[3072,128]{1,0:T(8,128)S(1)} fusion(f32[3072,128]{1,0:T(8,128)S(1)} %bitcast.116, f32[3072,128]{1,0:T(8,128)} %bitcast.13, f32[512,128]{1,0:T(8,128)S(1)} %reshape.123, f32[3072]{0:T(1024)S(1)} %bitcast.128, s32[3072]{0:T(1024)S(1)} %broadcast_add_fusion, f32[3072]{0:T(1024)S(1)} %broadcast_subtract_fusion, s32[3072]{0:T(1024)S(1)} %bitcast.135), kind=kOutput, calls=%fused_computation.18 | convolution fusion | flops 2424569856 | bytes 5029888 | tf_op jit(solution)/shard_map/dot_general | solution.py:40
  139.3 11.8 %fusion.4 = f32[512,128]{1,0:T(8,128)S(1)} fusion(f32[3072,128]{1,0:T(8,128)S(1)} %fusion.11, f32[3072]{0:T(1024)S(1)} %bitcast.129, s32[3072]{0:T(1024)S(1)} %broadcast_add_fusion, f32[3072]{0:T(1024)S(1)} %broadcast_subtract_fusion, s32[3072]{0:T(1024)S(1)} %bitcast.136), kind=kOutput, calls=%fused_computation.10 | convolution fusion | flops 2423783424 | bytes 1884160 | tf_op jit(solution)/shard_map/dot_general | solution.py:47
  156.4 8.4 %all_to_all.153 = f32[4,1,16384]{2,1,0:T(1,128)S(1)} all-to-all(f32[4,1,16384]{2,1,0:T(1,128)S(1)} %reshape.170), channel_id=1, replica_groups=mesh['px'=4,'py'=8] {'px'}, dimensions={0} | all-to-all | bytes 524288 | tf_op jit(solution)/shard_map/all_to_all | solution.py:98
  172.3 8.4 %all_to_all.154 = f32[2,1,64,512]{3,0,1,2:T(2,128)S(1)} all-to-all(f32[2,1,64,512]{3,0,1,2:T(2,128)S(1)} %copy.115), channel_id=1, replica_groups=mesh['px'=4,'py'=8] {'px'}, dimensions={2} | all-to-all | bytes 524288 | tf_op jit(solution)/shard_map/all_to_all | solution.py:92
  182.8 9.3 %fusion.10 = f32[3072,128]{1,0:T(8,128)S(1)} fusion(f32[3072,128]{1,0:T(8,128)S(1)} %bitcast.117, f32[512,128]{1,0:T(8,128)S(1)} %reshape.125, f32[3072]{0:T(1024)S(1)} %bitcast.130, s32[3072]{0:T(1024)S(1)} %broadcast_add_fusion, f32[3072]{0:T(1024)S(1)} %broadcast_subtract_fusion, s32[3072]{0:T(1024)S(1)} %bitcast.137), kind=kOutput, calls=%fused_computation.17 | convolution fusion | flops 2424569856 | bytes 3457024 | tf_op jit(solution)/shard_map/dot_general | solution.py:40
  192.1 11.8 %fusion.2 = f32[512,128]{1,0:T(8,128)S(1)} fusion(f32[3072,128]{1,0:T(8,128)S(1)} %fusion.10, f32[3072]{0:T(1024)S(1)} %bitcast.131, s32[3072]{0:T(1024)S(1)} %broadcast_add_fusion, f32[3072]{0:T(1024)S(1)} %broadcast_subtract_fusion, s32[3072]{0:T(1024)S(1)} %bitcast.138), kind=kOutput, calls=%fused_computation.8 | convolution fusion | flops 2423783424 | bytes 1884160 | tf_op jit(solution)/shard_map/dot_general | solution.py:47
  209.1 8.4 %all_to_all.155 = f32[4,1,16384]{2,1,0:T(1,128)S(1)} all-to-all(f32[4,1,16384]{2,1,0:T(1,128)S(1)} %reshape.172), channel_id=1, replica_groups=mesh['px'=4,'py'=8] {'px'}, dimensions={0} | all-to-all | bytes 524288 | tf_op jit(solution)/shard_map/all_to_all | solution.py:98
  223.9 37.3 %all-reduce.96 = (f32[]{:T(128)}, f32[]{:T(128)}) all-reduce(f32[]{:T(128)} %get-tuple-element.35, f32[]{:T(128)} %get-tuple-element.34), channel_id=1, replica_groups=mesh['px'=4,'py'=8] {'px','py'}, use_global_device_ids=true, to_apply=%region_8.9 | all-reduce | flops 2 | bytes 16 | tf_op jit(solution)/shard_map/psum | solution.py:58
  263.2 42.5 %psum.30 = f32[]{:T(128)} all-reduce(f32[]{:T(128)} %get-tuple-element.38), channel_id=1, replica_groups=mesh['px'=4,'py'=8] {'px','py'}, use_global_device_ids=true, to_apply=%region_12.13 | all-reduce | flops 1 | bytes 8 | tf_op jit(solution)/shard_map/psum | solution.py:58
  307.6 9.6 %all_to_all.156 = f32[2,1,64,512]{3,0,1,2:T(2,128)S(1)} all-to-all(f32[2,1,64,512]{3,0,1,2:T(2,128)S(1)} %copy.122), channel_id=1, replica_groups=mesh['px'=4,'py'=8] {'px'}, dimensions={2} | all-to-all | bytes 524288 | tf_op jit(solution)/shard_map/all_to_all | solution.py:92
  319.3 9.1 %fusion.9 = f32[3072,128]{1,0:T(8,128)S(1)} fusion(f32[3072,128]{1,0:T(8,128)S(1)} %bitcast.118, f32[512,128]{1,0:T(8,128)S(1)} %reshape.127, f32[3072]{0:T(1024)S(1)} %bitcast.132, s32[3072]{0:T(1024)S(1)} %broadcast_add_fusion, f32[3072]{0:T(1024)S(1)} %broadcast_subtract_fusion, s32[3072]{0:T(1024)S(1)} %bitcast.139), kind=kOutput, calls=%fused_computation.16 | convolution fusion | flops 2424569856 | bytes 3457024 | tf_op jit(solution)/shard_map/dot_general | solution.py:40
  328.5 11.8 %fusion = f32[512,128]{1,0:T(8,128)S(1)} fusion(f32[3072,128]{1,0:T(8,128)S(1)} %fusion.9, f32[3072]{0:T(1024)S(1)} %bitcast.133, s32[3072]{0:T(1024)S(1)} %broadcast_add_fusion, f32[3072]{0:T(1024)S(1)} %broadcast_subtract_fusion, s32[3072]{0:T(1024)S(1)} %bitcast.140), kind=kOutput, calls=%fused_computation.6 | convolution fusion | flops 2423783424 | bytes 1884160 | tf_op jit(solution)/shard_map/dot_general | solution.py:47
  348.4 9.4 %all_to_all.157 = f32[4,1,16384]{2,1,0:T(1,128)S(1)} all-to-all(f32[4,1,16384]{2,1,0:T(1,128)} %reshape.174), channel_id=1, replica_groups=mesh['px'=4,'py'=8] {'px'}, dimensions={0} | all-to-all | bytes 524288 | tf_op jit(solution)/shard_map/all_to_all | solution.py:98
  367.6 37.8 %psum.31 = f32[]{:T(128)} all-reduce(f32[]{:T(128)} %multiply_reduce_fusion), channel_id=1, replica_groups=mesh['px'=4,'py'=8] {'px','py'}, use_global_device_ids=true, to_apply=%region_14.15 | all-reduce | flops 1 | bytes 8 | tf_op jit(solution)/shard_map/psum | solution.py:58
  (163 shorter events, 67.2 us)
Async XLA Ops:
  10.6 15.9 %all-to-all-start.1 = ((f32[8,384,1]{1,2,0:T(1,128)}), f32[8,384,1]{1,2,0:T(1,128)S(1)}, u32[]{:S(2)}, u32[]{:S(2)}) async-start(f32[8,384,1]{1,2,0:T(1,128)} %bitcast.8), calls=%async_computation.1 | async-start | bytes 24576 | tf_op jit(solution)/shard_map/all_to_all | solution.py:85
  20.8 0.7 copy-start.5
  20.8 0.7 copy-start.6
  26.4 12.5 %all-to-all-start = ((s32[8,384,1]{1,2,0:T(1,128)}), s32[8,384,1]{1,2,0:T(1,128)S(1)}, u32[]{:S(2)}, u32[]{:S(2)}) async-start(s32[8,384,1]{1,2,0:T(1,128)} %bitcast.6), calls=%async_computation | async-start | bytes 24576 | tf_op jit(solution)/shard_map/all_to_all | solution.py:86
  39.0 9.4 %all-to-all-start.4 = ((f32[2,1,64,512]{3,0,1,2:T(2,128)}), f32[2,1,64,512]{3,0,1,2:T(2,128)S(1)}, u32[]{:S(2)}, u32[]{:S(2)}) async-start(f32[2,1,64,512]{3,0,1,2:T(2,128)} %copy.108), calls=%async_computation.4 | async-start | bytes 524288 | tf_op jit(solution)/shard_map/all_to_all | solution.py:92
  48.4 8.4 %copy-start.4 = (f32[1,16,2048]{2,1,0:T(8,128)S(1)}, f32[1,16,2048]{2,1,0:T(8,128)}, u32[]{:S(2)}) copy-start(f32[1,16,2048]{2,1,0:T(8,128)} %param.15) | copy-start | bytes 393220
  48.4 40.7 %all-to-all-start.2 = ((f32[8,384,128]{2,1,0:T(8,128)}), f32[8,384,128]{2,1,0:T(8,128)S(1)}, u32[]{:S(2)}, u32[]{:S(2)}) async-start(f32[8,384,128]{2,1,0:T(8,128)} %bitcast.10), calls=%async_computation.2 | async-start | bytes 3145728 | tf_op jit(solution)/shard_map/all_to_all | solution.py:84
  89.1 40.9 %copy-start.1 = (f32[8,384,128]{2,1,0:T(8,128)}, f32[8,384,128]{2,1,0:T(8,128)S(1)}, u32[]{:S(2)}) copy-start(f32[8,384,128]{2,1,0:T(8,128)S(1)} %all-to-all-done.2) | copy-start | bytes 4718596
  89.1 40.9 %all-to-all-start.3 = ((f32[8,384,128]{2,1,0:T(8,128)}), f32[8,384,128]{2,1,0:T(8,128)}, u32[]{:S(2)}, u32[]{:S(2)}) async-start(f32[8,384,128]{2,1,0:T(8,128)} %bitcast.12), calls=%async_computation.3 | async-start | bytes 3145728 | tf_op jit(solution)/shard_map/all_to_all | solution.py:83
  170.6 1.0 copy-start
  181.4 1.4 copy-start.2
  317.9 1.4 copy-start.3
where the time goes:
time: 416 us; the launch traced here: 408 us
  blocking collectives  162 us (39%)
  waiting for transfers between devices  74.5 us (18%)
  matrix products  63.1 us (15%)
  local copies, waits for them, and re-layouts  53.6 us (13%)
  starting transfers between devices  24.7 us (6%)
  other arithmetic  24.5 us (6%)
  between operations  5.91 us (1%)
    psum x3, blocking collectives, dot_total(): return lax.psum(jnp.sum(left_side * right_side), ('px', 'py'))  118 us
    all_to_all x1, waiting for transfers between devices, shards(): lax.all_to_all(bucket(innovation), 'py', split_axis=0, concat_axis=0, til...  35.7 us
    dot_general x3, matrix products, misfit(): lax.dot_general(interp_matrix, weighted, (((0,), (0,)), ((), ())), precis...  35.4 us
    all_to_all x1, waiting for transfers between devices, shards(): lax.all_to_all(bucket(obs_weight), 'py', split_axis=0, concat_axis=0, til...  31.9 us
    dot_general x3, matrix products, misfit(): jnp.dot(interp_matrix, flat_field, precision=lax.Precision.HIGHEST, prefe...  27.7 us
    all_to_all x3, blocking collectives, adjoint(): lax.all_to_all(diffuse(values_in, coef_y, 3), 'px', split_axis=3, concat_...  26.3 us
    unnamed x20, local copies, waits for them, and re-layouts  21.4 us
    scatter x4, local copies, waits for them, and re-layouts, bucket(): return jnp.zeros(buf_shape, values_in.dtype).at[slot_target].set(values_in)  19.3 us
  transfers between devices with their start and end apart: 5, of which 4 were waited for; matrix products, arithmetic and copies ran while one was open for 5% of the time, Pallas kernels for 0%

commit v1 on v0

v1 whole, which is shorter than its diff:
```python
import functools

import jax
import jax.numpy as jnp
from jax import lax
from jax.experimental import pallas as pl
from jax.experimental.pallas import tpu as pltpu
from jax.sharding import PartitionSpec as P

F = 2
SEG = 128
M = 4
NB = 16
LX = 16
ROWS = F * NB * LX
HALF = SEG // 2
VMEM_BYTES = 32 * 1024 * 1024


def iota(shape, axis):
    return lax.broadcasted_iota(jnp.int32, shape, axis)


def flag(condition, kind=jnp.bfloat16):
    return jnp.where(condition, 1.0, 0.0).astype(kind)


def mxu(left, right):
    return jnp.dot(left, right, preferred_element_type=jnp.float32)


def split_parts(values, count):
    parts = []
    for _ in range(count):
        part = values.astype(jnp.bfloat16)
        parts.append(part)
        values = values - part.astype(jnp.float32)
    return parts


def ends_tile(before, after):
    return jnp.where(iota(after.shape, after.ndim - 1) < HALF, after, before)


def sweep(values, coeffs, axis):
    size = values.shape[axis]
    for _ in range(M):
        flux = coeffs * (pltpu.roll(values, size - 1, axis) - values)
        values = values + flux - pltpu.roll(flux, 1, axis)
    return values


def pack_kernel(groups, cap, blk, block_rows, own_ref, key_ref, sten_ref, itp_ref, w_ref, d_ref,
                cy_ref, out_ref, cy_out, slot_v, slot_s, sem):
    chunks = own_ref.shape[0]
    nb = cap // blk
    own = own_ref[...]
    high = groups * chunks
    shift = chunks.bit_length() - 1
    masks = [flag(own == o, jnp.float32) for o in range(groups)]
    hits = jnp.concatenate(masks, axis=0).astype(jnp.bfloat16)
    square = (SEG, SEG)
    within = mxu(hits, flag(iota(square, 0) < iota(square, 1)))
    tallies = mxu(hits, jnp.ones(square, jnp.bfloat16)).astype(jnp.bfloat16)
    line, column = iota((high, high), 0), iota((high, high), 1)
    same = (line >> shift) == (column >> shift)
    ranks = within + mxu(flag(same & (column < line)), tallies)
    totals = mxu(flag(same), tallies)
    rank = sum(masks[o] * ranks[o * chunks:(o + 1) * chunks] for o in range(groups))
    rank = rank.astype(jnp.int32)
    slot_v[...] = own * block_rows + rank
    copy = pltpu.make_async_copy(slot_v, slot_s, sem)
    copy.start()

    def clear(o, carry):
        start = pl.multiple_of(o * block_rows, 8)
        out_ref[pl.ds(start, block_rows), :] = jnp.zeros((block_rows, SEG), jnp.float32)
        return carry

    lax.fori_loop(0, groups, clear, 0)

    width = cy_out.shape[2] - SEG
    columns = cy_ref.shape[1]
    cy = cy_ref[...]
    cy = jnp.where(iota(cy.shape, 1) == columns - 1, 0.0, cy)
    empty = jnp.zeros((cy.shape[0], SEG), jnp.float32)
    for q in range(columns // width):
        low, top = q * width, (q + 1) * width
        cy_out[q, :, :width] = cy[:, low:top]
        before = cy[:, low - SEG:low] if low > 0 else empty
        after = cy[:, top:top + SEG] if top < columns else empty
        cy_out[q, :, width:] = ends_tile(before, after)

    log = blk.bit_length() - 1
    place = own * nb + (rank >> log)
    lane = rank & (blk - 1)
    key, sten, itp = key_ref[...], sten_ref[...], itp_ref[...]
    tall = groups * nb
    meta = jnp.zeros((5 * tall, SEG), jnp.float32)
    for i in range(chunks):
        chosen = iota((tall, SEG), 0) == place[i:i + 1]
        parts = split_parts(itp[i:i + 1], 3)
        parts += [key[i:i + 1].astype(jnp.bfloat16), sten[i:i + 1].astype(jnp.bfloat16)]
        left = [jnp.where(chosen, part.astype(jnp.float32), 0.0) for part in parts]
        right = flag(iota(square, 0) == lane[i:i + 1])
        meta = meta + lax.dot_general(
            jnp.concatenate(left, axis=0).astype(jnp.bfloat16), right,
            (((1,), (1,)), ((), ())), preferred_element_type=jnp.float32)
    shares = meta[:tall] + meta[tall:2 * tall] + meta[2 * tall:3 * tall]
    targets = meta[3 * tall:4 * tall] * LX + meta[4 * tall:]
    for o in range(groups):
        base = o * block_rows + 2 * cap
        out_ref[base:base + nb, :] = shares[o * nb:(o + 1) * nb]
        out_ref[base + nb:base + 2 * nb, :] = targets[o * nb:(o + 1) * nb]
        out_ref[base + 2 * nb:base + 2 * nb + 1, :] = totals[o * chunks:o * chunks + 1]

    copy.wait()

    def place_rows(g, carry):
        start = pl.multiple_of(g * 8, 8)
        weights = w_ref[pl.ds(start, 8), :]
        products = weights * d_ref[pl.ds(start, 8), :]
        for i in range(8):
            slot = slot_s[g // 16, (g % 16) * 8 + i]
            out_ref[pl.ds(slot, 1), :] = weights[i:i + 1]
            out_ref[pl.ds(slot + cap, 1), :] = products[i:i + 1]
        return carry

    lax.fori_loop(0, w_ref.shape[0] // 8, place_rows, 0)


def gather_kernel(groups, cap, blk, block_rows, in_ref, out_ref, acc_ref):
    nb = cap // blk
    acc_ref[...] = jnp.zeros_like(acc_ref)

    def block(index, carry):
        source, part = index // nb, index % nb
        base = pl.multiple_of(source * block_rows, 8)
        count = in_ref[pl.ds(base + 2 * cap + 2 * nb, 1), :][0, 0]

        @pl.when(count > (part * blk).astype(jnp.float32))
        def _():
            share = in_ref[pl.ds(base + 2 * cap + part, 1), :]
            target = in_ref[pl.ds(base + 2 * cap + nb + part, 1), :][:, :blk]
            upper = jnp.broadcast_to(share, (SEG, SEG)).T[:blk]
            lower = 1.0 - upper
            start = pl.multiple_of(base + part * blk, 8)
            weights = in_ref[pl.ds(start, blk), :]
            start = pl.multiple_of(base + cap + part * blk, 8)
            products = in_ref[pl.ds(start, blk), :]
            lower_w, upper_w = lower * weights, upper * weights
            values = jnp.concatenate(
                [lower * lower_w, upper * lower_w, upper * upper_w,
                 lower * products, upper * products], axis=1)
            hit = flag(iota((ROWS, blk), 0).astype(jnp.float32) == target)
            acc_ref[...] += mxu(
                jnp.concatenate([hit, hit], axis=1),
                jnp.concatenate(split_parts(values, 2), axis=0))

        return carry

    lax.fori_loop(0, groups * nb, block, 0)

    width = out_ref.shape[3] - SEG
    per = width // SEG
    empty = jnp.zeros((LX, SEG), jnp.float32)
    fields = (
        acc_ref[:, :SEG] + pltpu.roll(acc_ref[:, 2 * SEG:3 * SEG], 1, 0),
        acc_ref[:, SEG:2 * SEG],
        acc_ref[:, 3 * SEG:4 * SEG] + pltpu.roll(acc_ref[:, 4 * SEG:], 1, 0),
    )
    for channel, values in enumerate(fields):
        for f in range(F):
            tiles = [values[(f * NB + b) * LX:(f * NB + b + 1) * LX] for b in range(NB)]
            for q in range(NB // per):
                for j in range(per):
                    out_ref[q, channel * F + f, :, j * SEG:(j + 1) * SEG] = tiles[q * per + j]
                before = tiles[q * per - 1] if q > 0 else empty
                after = tiles[(q + 1) * per] if (q + 1) * per < NB else empty
                out_ref[q, channel * F + f, :, width:] = ends_tile(before, after)


def sweep_x_into(to_ref, from_ref, cx_ref, plus_ref=None, sign=1.0):
    for low in range(0, cx_ref.shape[1], SEG):
        tile = slice(low, low + SEG)
        values = sweep(from_ref[:, tile], cx_ref[:, tile], 0)
        if plus_ref is not None:
            values = values + sign * plus_ref[:, tile]
        to_ref[:, tile] = values


def sweep_y_into(to_ref, from_ref, cy_ref):
    for low in range(0, cy_ref.shape[0], 8):
        lines = slice(low, low + 8)
        to_ref[lines, :] = sweep(from_ref[lines, :], cy_ref[lines, :], 1)


def start_kernel(c0_ref, cx_ref, prev_ref, next_ref, cy_ref, c0_out, cx_out, cy_out, u_out):
    width = c0_ref.shape[2]
    for p in range(cy_ref.shape[0]):
        cy_out[p * LX:(p + 1) * LX, :] = cy_ref[p]
    last = cx_ref.shape[0] - 1
    cx_out[:, :width] = cx_ref[...]
    cx_out[:, width:] = ends_tile(prev_ref[F], next_ref[F])
    cx_out[last:, :] = jnp.zeros((1, width + SEG), jnp.float32)
    for f in range(F):
        c0_out[f, :, :width] = c0_ref[f]
        c0_out[f, :, width:] = ends_tile(prev_ref[f], next_ref[f])
        sweep_x_into(u_out.at[f], c0_out.at[f], cx_out)
        sweep_y_into(u_out.at[f], u_out.at[f], cy_out)


def solve_kernel(obs_ref, c0_ref, cx_ref, cy_ref, u_ref, r_out, q_out, qq_out, dots_out,
                 vec, coef, work):
    width = r_out.shape[2]
    parts = obs_ref.shape[0]
    for p in range(parts):
        for channel in range(3 * F):
            coef[channel, p * LX:(p + 1) * LX, :] = obs_ref[p, channel]

    def normal(f, values, tile):
        size = values.shape[0]
        side = coef[F + f, :, tile]
        return (coef[f, :, tile] * values + side * pltpu.roll(values, size - 1, 0)
                + pltpu.roll(side * values, 1, 0))

    tiles = [slice(low, low + SEG) for low in range(0, width + SEG, SEG)]

    def first(f, carry):
        for tile in tiles:
            work[:, tile] = coef[2 * F + f, :, tile] - normal(f, u_ref[f, :, tile], tile)
        sweep_y_into(work, work, cy_ref)
        sweep_x_into(vec.at[0, f], work, cx_ref, c0_ref.at[f], -1.0)
        return carry

    lax.fori_loop(0, F, first, 0)

    def apply(index, carry):
        step, f = index // F, index % F
        sweep_x_into(work, vec.at[step, f], cx_ref)
        sweep_y_into(work, work, cy_ref)
        for tile in tiles:
            work[:, tile] = normal(f, work[:, tile], tile)
        sweep_y_into(work, work, cy_ref)
        sweep_x_into(vec.at[step + 1, f], work, cx_ref, vec.at[step, f])
        return carry

    lax.fori_loop(0, 2 * F, apply, 0)

    sums = [jnp.zeros((8, SEG), jnp.float32) for _ in range(5)]
    for f in range(F):
        r_out[f] = vec[0, f, :, :width]
        q_out[f] = vec[1, f, :, :width]
        qq_out[f] = vec[2, f, :, :width]
        for low in range(0, vec.shape[2], 8):
            for tile in tiles[:-1]:
                r = vec[0, f, low:low + 8, tile]
                q = vec[1, f, low:low + 8, tile]
                qq = vec[2, f, low:low + 8, tile]
                for i, product in enumerate((r * r, r * q, q * q, r * qq, q * qq)):
                    sums[i] = sums[i] + product
    lines = [jnp.sum(s, axis=0, keepdims=True) for s in sums]
    dots = jnp.concatenate(lines + [jnp.zeros((3, SEG), jnp.float32)], axis=0)
    for device in range(dots_out.shape[0]):
        dots_out[device] = dots


def finish_kernel(dots_ref, c0_ref, r_ref, q_ref, qq_ref, control_out, residual_out):
    dots = jnp.sum(dots_ref[...], axis=0)
    rr, rq, qq2, rqq, qqq = (dots[i:i + 1] for i in range(5))

    def total(line):
        return jnp.sum(line, axis=1, keepdims=True)

    rr_sum = total(rr)
    alpha = rr_sum / total(rq)
    new_sum = total(rr - 2.0 * alpha * rq + alpha * alpha * qq2)
    more = 1.0 + new_sum / rr_sum
    curve = total(more * more * rq - more * alpha * (rqq + qq2) + alpha * alpha * qqq)
    second = new_sum / curve
    first_weight = alpha + second * more
    both = alpha * second
    for f in range(F):
        r, q = r_ref[f], q_ref[f]
        control_out[f] = c0_ref[f] + first_weight * r - both * q
        residual_out[f] = r - first_weight * q + both * qq_ref[f]


def call(kernel, out_shape, scratch=(), in_specs=None):
    params = {} if in_specs is None else {"in_specs": in_specs}
    return pl.pallas_call(
        kernel,
        out_shape=out_shape,
        scratch_shapes=list(scratch),
        compiler_params=pltpu.CompilerParams(vmem_limit_bytes=VMEM_BYTES),
        **params,
    )


def f32(*shape):
    return jax.ShapeDtypeStruct(shape, jnp.float32)


def shards(
    control_start, coef_x, coef_y, innovation, obs_weight, interp, obs_owner, cell_key, stencil
):
    groups, spans = lax.axis_size("py"), lax.axis_size("px")
    rows = innovation.shape[0]
    cap = 3 * rows // groups
    blk = SEG if cap % SEG == 0 else HALF
    nb = cap // blk
    block_rows = 2 * cap + -(-(2 * nb + 1) // 8) * 8
    chunks = rows // SEG
    nx, width = control_start.shape[2], control_start.shape[3]
    ext = width + SEG
    c0, cx = control_start[:, 0], coef_x[0]

    packed, cy_parts = call(
        functools.partial(pack_kernel, groups, cap, blk, block_rows),
        (f32(groups * block_rows, SEG), f32(spans, LX, ext)),
        [pltpu.VMEM((chunks, SEG), jnp.int32), pltpu.SMEM((chunks, SEG), jnp.int32),
         pltpu.SemaphoreType.DMA],
    )(
        obs_owner.reshape(chunks, SEG), cell_key.reshape(chunks, SEG),
        stencil.reshape(chunks, SEG), interp.reshape(chunks, SEG),
        obs_weight, innovation, coef_y[0],
    )
    arrived = lax.all_to_all(packed, "py", split_axis=0, concat_axis=0, tiled=True)

    cy_lines = lax.all_to_all(cy_parts, "px", split_axis=0, concat_axis=0, tiled=True)
    fields = jnp.concatenate([c0, cx[None]], axis=0)
    steps = [(i, i + 1) for i in range(spans - 1)]
    from_prev = lax.ppermute(fields[:, :, -SEG:], "px", steps)
    from_next = lax.ppermute(fields[:, :, :SEG], "px", [(j, i) for i, j in steps])
    c0_ext, cx_ext, cy_ext, u_ext = call(
        start_kernel,
        (f32(F, nx, ext), f32(nx, ext), f32(nx, ext), f32(F, nx, ext)),
    )(c0, cx, from_prev, from_next, cy_lines)

    obs_parts = call(
        functools.partial(gather_kernel, groups, cap, blk, block_rows),
        f32(spans, 3 * F, LX, ext),
        [pltpu.VMEM((ROWS, 5 * SEG), jnp.float32)],
    )(arrived)
    obs_fields = lax.all_to_all(obs_parts, "px", split_axis=0, concat_axis=0, tiled=True)

    r, q, qq, dots = call(
        solve_kernel,
        (f32(F, nx, width),) * 3 + (f32(groups * spans, 8, SEG),),
        [pltpu.VMEM((3, F, nx, ext), jnp.float32), pltpu.VMEM((3 * F, nx, ext), jnp.float32),
         pltpu.VMEM((nx, ext), jnp.float32)],
    )(obs_fields, c0_ext, cx_ext, cy_ext, u_ext)
    dots = lax.all_to_all(dots, ("px", "py"), split_axis=0, concat_axis=0, tiled=True)
    control, residual = call(finish_kernel, (f32(F, nx, width),) * 2)(dots, c0, r, q, qq)
    return control[:, None], residual[:, None]


def solution(mesh):
    return jax.shard_map(
        shards,
        mesh=mesh,
        in_specs=(
            P(None, "py", None, "px"),
            P("py", None, "px"),
            P("py", "px", None),
            P(("px", "py"), None),
            P(("px", "py"), None),
            P(("px", "py")),
            P(("px", "py"), None),
            P(("px", "py")),
            P(("px", "py")),
        ),
        out_specs=(P(None, "py", None, "px"), P(None, "py", None, "px")),
        check_vma=False,
    )
```

time: 416 us -> 148 us (0.36); the launches traced: 408 us -> 147 us
  waiting for transfers between devices: 74.5 us -> 5.74 us
  blocking collectives: 162 us -> 95.8 us
  matrix products: 63.1 us -> 0 us
  local copies, waits for them, and re-layouts: 53.6 us -> 7.6 us
  Pallas kernels: 0 us -> 24.2 us
  other arithmetic: 24.5 us -> 0.79 us
  starting transfers between devices: 24.7 us -> 11.7 us
  between operations: 5.91 us -> 0.75 us
    psum x3 -> x0, blocking collectives: 118 us -> none  [dot_total(): return lax.psum(jnp.sum(left_side * right_side), ('px', 'py'))]
    all_to_all x5 -> x2, waiting for transfers between devices: 74.5 us -> 3.16 us  [the longest x1 3.16 us: shards(): lax.all_to_all(obs_parts, 'px', split_axis=0, concat_axis=0, tiled=True)]
    dot_general x6 -> x0, matrix products: 63.1 us -> none  [the longest x3 35.4 us: misfit(): lax.dot_general(interp_matrix, weighted, (((0,), (0,)), ((), ())), precis...]
    all_to_all x5 -> x2, blocking collectives: 44.3 us -> 95.8 us  [the longest x1 79.2 us: shards(): lax.all_to_all(packed, 'py', split_axis=0, concat_axis=0, tiled=True)]
    pallas_call x0 -> x5, Pallas kernels: none -> 24.2 us  [the longest x1 8.32 us: shards(): call(functools.partial(gather_kernel, groups, cap, blk, block_rows), f32(...]
    scatter x4 -> x0, local copies, waits for them, and re-layouts: 19.3 us -> none  [bucket(): return jnp.zeros(buf_shape, values_in.dtype).at[slot_target].set(values_in)]
    all_to_all x5 -> x2, starting transfers between devices: 24.7 us -> 7.61 us  [the longest x1 4.1 us: shards(): lax.all_to_all(cy_parts, 'px', split_axis=0, concat_axis=0, tiled=True)]
    unnamed x20 -> x22, local copies, waits for them, and re-layouts: 21.4 us -> 7.6 us
  transfers between devices with their start and end apart: 5 -> 4, of which waited for: 4 -> 2; matrix products, arithmetic and copies ran while one was open for 5% -> 1% of each run, Pallas kernels for 0% -> 7%
where the time goes in v1:
time: 148 us; the launch traced here: 147 us
  blocking collectives  95.8 us (65%)
  Pallas kernels  24.2 us (16%)
  starting transfers between devices  11.7 us (8%)
  local copies, waits for them, and re-layouts  7.6 us (5%)
  waiting for transfers between devices  5.74 us (4%)
    all_to_all x1, blocking collectives, shards(): lax.all_to_all(packed, 'py', split_axis=0, concat_axis=0, tiled=True)  79.2 us
    all_to_all x1, blocking collectives, shards(): lax.all_to_all(dots, ('px', 'py'), split_axis=0, concat_axis=0, tiled=True)  16.6 us
    pallas_call x1, Pallas kernels, shards(): call(functools.partial(gather_kernel, groups, cap, blk, block_rows), f32(...  8.32 us
    pallas_call x1, Pallas kernels, shards(): call(solve_kernel, (f32(F, nx, width),) * 3 + (f32(groups * spans, 8, SEG...  8.09 us
    unnamed x22, local copies, waits for them, and re-layouts  7.6 us
    pallas_call x1, Pallas kernels, shards(): call(functools.partial(pack_kernel, groups, cap, blk, block_rows), (f32(g...  4.34 us
    all_to_all x1, starting transfers between devices, shards(): lax.all_to_all(cy_parts, 'px', split_axis=0, concat_axis=0, tiled=True)  4.1 us
    all_to_all x1, starting transfers between devices, shards(): lax.all_to_all(obs_parts, 'px', split_axis=0, concat_axis=0, tiled=True)  3.51 us
  transfers between devices with their start and end apart: 4, of which 2 were waited for; matrix products, arithmetic and copies ran while one was open for 1% of the time, Pallas kernels for 7%

profile of v1, /device:TPU:0, one launch (start us, length us, event | category | flops | bytes accessed | tf_op | source)
XLA Modules:
  0.0 146.7 jit_solution(8338476386748850282)
XLA Ops:
  0.6 1.0 copy-done.2
  1.7 1.0 copy-done.3
  2.7 0.9 copy-done.6
  3.6 0.7 copy-done.7
  4.3 0.7 copy-done.8
  5.0 0.7 copy-done.9
  5.7 0.7 copy-done.10
  6.4 4.3 %shard_map.104 = (f32[6208,128]{1,0:T(8,128)S(1)}, f32[4,16,640]{2,1,0:T(8,128)S(1)}) custom-call(s32[8,128]{1,0:T(8,128)S(1)} %bitcast.22, s32[8,128]{1,0:T(8,128)S(1)} %bitcast.23, s32[8,128]{1,0:T(8,128)S(1)} %bitcast.24, f32[8,128]{1,0:T(8,128)S(1)} %bitcast.25, f32[1024,128]{1,0:T(8,128)S(1)} %copy-done.2, f32[1024,128]{1,0:T(8,128)S(1)} %copy-done.3, ...), custom_call_target="tpu_custom_call" | custom-call | tf_op jit(solution)/shard_map/pallas_call | solution.py:318
  10.7 0.0 copy-start.5
  10.7 79.2 %all_to_all.26 = f32[8,776,128]{2,1,0:T(8,128)S(1)} all-to-all(f32[8,776,128]{2,1,0:T(8,128)S(1)} %bitcast.16), channel_id=1, replica_groups=mesh['px'=4,'py'=8] {'py'}, dimensions={0} | all-to-all | bytes 6356992 | tf_op jit(solution)/shard_map/all_to_all | solution.py:328
  90.0 4.1 %all-to-all-start.2 = ((f32[4,16,640]{2,1,0:T(8,128)}), f32[4,16,640]{2,1,0:T(8,128)}, u32[]{:S(2)}, u32[]{:S(2)}) async-start(f32[4,16,640]{2,1,0:T(8,128)} %copy-done.5), calls=%async_computation.2 | async-start | bytes 327680 | tf_op jit(solution)/shard_map/all_to_all | solution.py:330
  94.1 8.3 %shard_map.105 = f32[4,6,16,640]{3,2,1,0:T(8,128)S(1)} custom-call(f32[6208,128]{1,0:T(8,128)S(1)} %bitcast.15), custom_call_target="tpu_custom_call" | custom-call | tf_op jit(solution)/shard_map/pallas_call | solution.py:340
  102.4 1.0 copy-done
  103.4 3.5 %all-to-all-start.1 = ((f32[4,6,16,640]{3,2,1,0:T(8,128)}), f32[4,6,16,640]{3,2,1,0:T(8,128)S(1)}, u32[]{:S(2)}, u32[]{:S(2)}) async-start(f32[4,6,16,640]{3,2,1,0:T(8,128)} %copy-done), calls=%async_computation.1 | async-start | bytes 1966080 | tf_op jit(solution)/shard_map/all_to_all | solution.py:345
  106.9 0.8 pad_maximum_fusion
  107.7 2.8 %collective-permute-start = (f32[3,64,128]{2,1,0:T(8,128)S(1)}, f32[3,64,128]{2,1,0:T(8,128)S(1)}, u32[]{:S(2)}, u32[]{:S(2)}) collective-permute-start(f32[3,64,128]{2,1,0:T(8,128)S(1)} %get-tuple-element.29), channel_id=1, source_target_pairs={{0,8},{8,16},{16,24},{1,9},{9,17},{17,25},{2,10},{10,18},{18,26},{... | collective-permute-start | bytes 294920 | tf_op jit(solution)/shard_map/ppermute | solution.py:333
  110.5 1.3 collective-permute-start.1
  111.8 2.6 %collective-permute-done.1.next_ref = f32[3,64,128]{2,1,0:T(8,128)S(1)} collective-permute-done((f32[3,64,128]{2,1,0:T(8,128)S(1)}, f32[3,64,128]{2,1,0:T(8,128)S(1)}, u32[]{:S(2)}, u32[]{:S(2)}) %collective-permute-start.1) | collective-permute-done | bytes 98336 | tf_op jit(solution)/shard_map/ppermute | solution.py:334
  114.4 0.9 copy-done.4
  115.3 2.1 %shard_map.106 = (f32[2,64,640]{2,1,0:T(8,128)S(1)}, f32[64,640]{1,0:T(8,128)S(1)}, f32[64,640]{1,0:T(8,128)S(1)}, f32[2,64,640]{2,1,0:T(8,128)S(1)}) custom-call(f32[2,64,512]{2,1,0:T(8,128)S(1)} %bitcast.18, f32[64,512]{1,0:T(8,128)S(1)} %bitcast.20, f32[3,64,128]{2,1,0:T(8,128)S(1)} %collective-permute-done.prev_ref, ...), custom_call_target="tpu_custom_call" | custom-call | tf_op jit(solution)/shard_map/pallas_call | solution.py:335
  117.5 3.2 %all-to-all-done.1.obs_ref = f32[4,6,16,640]{3,2,1,0:T(8,128)S(1)} async-done(((f32[4,6,16,640]{3,2,1,0:T(8,128)}), f32[4,6,16,640]{3,2,1,0:T(8,128)S(1)}, u32[]{:S(2)}, u32[]{:S(2)}) %all-to-all-start.1) | async-done | bytes 983072 | tf_op jit(solution)/shard_map/all_to_all | solution.py:345
  120.6 8.1 %shard_map.107 = (f32[2,64,512]{2,1,0:T(8,128)S(1)}, f32[2,64,512]{2,1,0:T(8,128)S(1)}, f32[2,64,512]{2,1,0:T(8,128)S(1)}, f32[32,8,128]{2,1,0:T(8,128)S(1)}) custom-call(f32[4,6,16,640]{3,2,1,0:T(8,128)S(1)} %all-to-all-done.1.obs_ref, f32[2,64,640]{2,1,0:T(8,128)S(1)} %get-tuple-element.16.c0_ref, f32[64,640]{1,0:T(8,128)S(1)} %get-tuple-element.17.cx_ref, ...), custom_call_target="tpu_custom_call" | custom-call | tf_op jit(solution)/shard_map/pallas_call | solution.py:347
  128.7 16.6 %all_to_all.27.dots_ref = f32[32,8,128]{2,1,0:T(8,128)S(1)} all-to-all(f32[32,8,128]{2,1,0:T(8,128)S(1)} %get-tuple-element.20), channel_id=1, replica_groups=mesh['px'=4,'py'=8] {'px','py'}, dimensions={0} | all-to-all | bytes 262144 | tf_op jit(solution)/shard_map/all_to_all | solution.py:353
  145.3 1.3 shard_map.108
  (14 shorter events, 0.0 us)
Async XLA Ops:
  0.6 1.0 copy-start.2
  1.7 1.0 copy-start.3
  2.7 0.9 copy-start.6
  3.6 0.7 copy-start.7
  4.3 0.7 copy-start.8
  5.0 0.7 copy-start.9
  5.7 0.7 copy-start.10
  10.7 79.2 %copy-start.5 = (f32[4,16,640]{2,1,0:T(8,128)}, f32[4,16,640]{2,1,0:T(8,128)S(1)}, u32[]{:S(2)}) copy-start(f32[4,16,640]{2,1,0:T(8,128)S(1)} %get-tuple-element.15) | copy-start | bytes 491524
  90.0 16.9 %copy-start.1 = (f32[2,1,64,512]{3,2,1,0:T(8,128)S(1)}, f32[2,1,64,512]{3,2,1,0:T(8,128)}, u32[]{:S(2)}) copy-start(f32[2,1,64,512]{3,2,1,0:T(8,128)} %param.9) | copy-start | bytes 786436
  90.0 13.4 %all-to-all-start.2 = ((f32[4,16,640]{2,1,0:T(8,128)}), f32[4,16,640]{2,1,0:T(8,128)}, u32[]{:S(2)}, u32[]{:S(2)}) async-start(f32[4,16,640]{2,1,0:T(8,128)} %copy-done.5), calls=%async_computation.2 | async-start | bytes 327680 | tf_op jit(solution)/shard_map/all_to_all | solution.py:330
  102.4 1.0 copy-start
  103.4 17.2 %all-to-all-start.1 = ((f32[4,6,16,640]{3,2,1,0:T(8,128)}), f32[4,6,16,640]{3,2,1,0:T(8,128)S(1)}, u32[]{:S(2)}, u32[]{:S(2)}) async-start(f32[4,6,16,640]{3,2,1,0:T(8,128)} %copy-done), calls=%async_computation.1 | async-start | bytes 1966080 | tf_op jit(solution)/shard_map/all_to_all | solution.py:345
  107.7 4.1 %collective-permute-start = (f32[3,64,128]{2,1,0:T(8,128)S(1)}, f32[3,64,128]{2,1,0:T(8,128)S(1)}, u32[]{:S(2)}, u32[]{:S(2)}) collective-permute-start(f32[3,64,128]{2,1,0:T(8,128)S(1)} %get-tuple-element.29), channel_id=1, source_target_pairs={{0,8},{8,16},{16,24},{1,9},{9,17},{17,25},{2,10},{10,18},{18,26},{... | collective-permute-start | bytes 294920 | tf_op jit(solution)/shard_map/ppermute | solution.py:333
  110.5 3.9 %collective-permute-start.1 = (f32[3,64,128]{2,1,0:T(8,128)S(1)}, f32[3,64,128]{2,1,0:T(8,128)S(1)}, u32[]{:S(2)}, u32[]{:S(2)}) collective-permute-start(f32[3,64,128]{2,1,0:T(8,128)S(1)} %get-tuple-element.28), channel_id=1, source_target_pairs={{8,0},{16,8},{24,16},{9,1},{17,9},{25,17},{10,2},{18,10},{26,18},{... | collective-permute-start | bytes 294920 | tf_op jit(solution)/shard_map/ppermute | solution.py:334
  114.4 0.9 copy-start.4

commit v2 on v1

--- a/solution.py
+++ b/solution.py
@@ -15,6 +15,7 @@
 ROWS = F * NB * LX
 HALF = SEG // 2
 VMEM_BYTES = 32 * 1024 * 1024
+PACK_BYTES = 60 * 1024 * 1024
 
 
 def iota(shape, axis):
@@ -50,8 +51,34 @@
     return values
 
 
-def pack_kernel(groups, cap, blk, block_rows, own_ref, key_ref, sten_ref, itp_ref, w_ref, d_ref,
-                cy_ref, out_ref, cy_out, slot_v, slot_s, sem):
+def pack_kernel(groups, cap, blk, block_rows, own_hbm, key_hbm, sten_hbm, itp_hbm, w_hbm, d_hbm,
+                cy_hbm, c0_hbm, cx_hbm, w_out, v_out, first_out, last_out, *rest):
+    cy_outs, rest = rest[:-11], rest[-11:]
+    own_ref, key_ref, sten_ref, itp_ref, w_ref, d_ref, cy_ref, slot_v, slot_s, sems, sem = rest
+    width = c0_hbm.shape[2]
+    pairs = [
+        (own_hbm, own_ref), (key_hbm, key_ref), (sten_hbm, sten_ref), (itp_hbm, itp_ref),
+        (w_hbm, w_ref), (d_hbm, d_ref), (cy_hbm, cy_ref),
+        (c0_hbm.at[:, :, pl.ds(0, SEG)], first_out.at[pl.ds(0, F)]),
+        (cx_hbm.at[:, pl.ds(0, SEG)], first_out.at[F]),
+        (c0_hbm.at[:, :, pl.ds(width - SEG, SEG)], last_out.at[pl.ds(0, F)]),
+        (cx_hbm.at[:, pl.ds(width - SEG, SEG)], last_out.at[F]),
+    ]
+    loads = [pltpu.make_async_copy(*pair, sems.at[i]) for i, pair in enumerate(pairs)]
+    for load in loads:
+        load.start()
+
+    def clear(o, carry):
+        start = pl.multiple_of(o * block_rows, 8)
+        w_out[pl.ds(start, block_rows), :] = jnp.zeros((block_rows, SEG), jnp.float32)
+        start = pl.multiple_of(o * cap, 8)
+        v_out[pl.ds(start, cap), :] = jnp.zeros((cap, SEG), jnp.float32)
+        return carry
+
+    lax.fori_loop(0, groups, clear, 0)
+
+    for load in loads[:4]:
+        load.wait()
     chunks = own_ref.shape[0]
     nb = cap // blk
     own = own_ref[...]
@@ -68,28 +95,10 @@
     totals = mxu(flag(same), tallies)
     rank = sum(masks[o] * ranks[o * chunks:(o + 1) * chunks] for o in range(groups))
     rank = rank.astype(jnp.int32)
-    slot_v[...] = own * block_rows + rank
+    slot_v[:chunks] = own * block_rows + rank
+    slot_v[chunks:] = own * cap + rank
     copy = pltpu.make_async_copy(slot_v, slot_s, sem)
     copy.start()
-
-    def clear(o, carry):
-        start = pl.multiple_of(o * block_rows, 8)
-        out_ref[pl.ds(start, block_rows), :] = jnp.zeros((block_rows, SEG), jnp.float32)
-        return carry
-
-    lax.fori_loop(0, groups, clear, 0)
-
-    width = cy_out.shape[2] - SEG
-    columns = cy_ref.shape[1]
-    cy = cy_ref[...]
-    cy = jnp.where(iota(cy.shape, 1) == columns - 1, 0.0, cy)
-    empty = jnp.zeros((cy.shape[0], SEG), jnp.float32)
-    for q in range(columns // width):
-        low, top = q * width, (q + 1) * width
-        cy_out[q, :, :width] = cy[:, low:top]
-        before = cy[:, low - SEG:low] if low > 0 else empty
-        after = cy[:, top:top + SEG] if top < columns else empty
-        cy_out[q, :, width:] = ends_tile(before, after)
 
     log = blk.bit_length() - 1
     place = own * nb + (rank >> log)
@@ -109,10 +118,25 @@
     shares = meta[:tall] + meta[tall:2 * tall] + meta[2 * tall:3 * tall]
     targets = meta[3 * tall:4 * tall] * LX + meta[4 * tall:]
     for o in range(groups):
-        base = o * block_rows + 2 * cap
-        out_ref[base:base + nb, :] = shares[o * nb:(o + 1) * nb]
-        out_ref[base + nb:base + 2 * nb, :] = targets[o * nb:(o + 1) * nb]
-        out_ref[base + 2 * nb:base + 2 * nb + 1, :] = totals[o * chunks:o * chunks + 1]
+        base = o * block_rows + cap
+        w_out[base:base + nb, :] = shares[o * nb:(o + 1) * nb]
+        w_out[base + nb:base + 2 * nb, :] = targets[o * nb:(o + 1) * nb]
+        w_out[base + 2 * nb:base + 2 * nb + 1, :] = totals[o * chunks:o * chunks + 1]
+
+    for load in loads[4:]:
+        load.wait()
+    columns = cy_ref.shape[1]
+    cy = cy_ref[...]
+    cy_ref[...] = jnp.where(iota(cy.shape, 1) == columns - 1, 0.0, cy)
+    me = lax.axis_index("px")
+    for k, cy_out in enumerate(cy_outs):
+        q = me ^ k
+        low = pl.multiple_of(q * width, SEG)
+        cy_out[:, :width] = cy_ref[:, pl.ds(low, width)]
+        before = cy_ref[:, pl.ds(pl.multiple_of(jnp.maximum(low - SEG, 0), SEG), SEG)]
+        after = cy_ref[:, pl.ds(pl.multiple_of(jnp.minimum(low + width, columns - SEG), SEG), SEG)]
+        cy_out[:, width:] = ends_tile(jnp.where(q > 0, before, 0.0),
+                                      jnp.where(q < len(cy_outs) - 1, after, 0.0))
 
     copy.wait()
 
@@ -120,38 +144,30 @@
         start = pl.multiple_of(g * 8, 8)
         weights = w_ref[pl.ds(start, 8), :]
         products = weights * d_ref[pl.ds(start, 8), :]
+        line, lane = g // 16, (g % 16) * 8
         for i in range(8):
-            slot = slot_s[g // 16, (g % 16) * 8 + i]
-            out_ref[pl.ds(slot, 1), :] = weights[i:i + 1]
-            out_ref[pl.ds(slot + cap, 1), :] = products[i:i + 1]
+            w_out[pl.ds(slot_s[line, lane + i], 1), :] = weights[i:i + 1]
+            v_out[pl.ds(slot_s[chunks + line, lane + i], 1), :] = products[i:i + 1]
         return carry
 
     lax.fori_loop(0, w_ref.shape[0] // 8, place_rows, 0)
 
 
-def gather_kernel(groups, cap, blk, block_rows, in_ref, out_ref, acc_ref):
+def sum_rows(groups, cap, blk, block_rows, w_ref, acc_ref, terms):
     nb = cap // blk
     acc_ref[...] = jnp.zeros_like(acc_ref)
 
     def block(index, carry):
         source, part = index // nb, index % nb
         base = pl.multiple_of(source * block_rows, 8)
-        count = in_ref[pl.ds(base + 2 * cap + 2 * nb, 1), :][0, 0]
+        count = w_ref[pl.ds(base + cap + 2 * nb, 1), :][0, 0]
 
         @pl.when(count > (part * blk).astype(jnp.float32))
         def _():
-            share = in_ref[pl.ds(base + 2 * cap + part, 1), :]
-            target = in_ref[pl.ds(base + 2 * cap + nb + part, 1), :][:, :blk]
+            share = w_ref[pl.ds(base + cap + part, 1), :]
+            target = w_ref[pl.ds(base + cap + nb + part, 1), :][:, :blk]
             upper = jnp.broadcast_to(share, (SEG, SEG)).T[:blk]
-            lower = 1.0 - upper
-            start = pl.multiple_of(base + part * blk, 8)
-            weights = in_ref[pl.ds(start, blk), :]
-            start = pl.multiple_of(base + cap + part * blk, 8)
-            products = in_ref[pl.ds(start, blk), :]
-            lower_w, upper_w = lower * weights, upper * weights
-            values = jnp.concatenate(
-                [lower * lower_w, upper * lower_w, upper * upper_w,
-                 lower * products, upper * products], axis=1)
+            values = jnp.concatenate(terms(source, part, upper), axis=1)
             hit = flag(iota((ROWS, blk), 0).astype(jnp.float32) == target)
             acc_ref[...] += mxu(
                 jnp.concatenate([hit, hit], axis=1),
@@ -161,23 +177,55 @@
 
     lax.fori_loop(0, groups * nb, block, 0)
 
-    width = out_ref.shape[3] - SEG
+
+def cut_parts(stage_ref, outs):
+    width = outs[0].shape[2] - SEG
     per = width // SEG
-    empty = jnp.zeros((LX, SEG), jnp.float32)
-    fields = (
-        acc_ref[:, :SEG] + pltpu.roll(acc_ref[:, 2 * SEG:3 * SEG], 1, 0),
-        acc_ref[:, SEG:2 * SEG],
-        acc_ref[:, 3 * SEG:4 * SEG] + pltpu.roll(acc_ref[:, 4 * SEG:], 1, 0),
-    )
-    for channel, values in enumerate(fields):
-        for f in range(F):
-            tiles = [values[(f * NB + b) * LX:(f * NB + b + 1) * LX] for b in range(NB)]
-            for q in range(NB // per):
+    me = lax.axis_index("px")
+    for k, out in enumerate(outs):
+        q = me ^ k
+        for channel in range(stage_ref.shape[0]):
+            for f in range(F):
+                def tile(b):
+                    start = pl.multiple_of((f * NB + b) * LX, LX)
+                    return stage_ref[channel, pl.ds(start, LX), :]
+
+                to = out.at[channel * F + f]
                 for j in range(per):
-                    out_ref[q, channel * F + f, :, j * SEG:(j + 1) * SEG] = tiles[q * per + j]
-                before = tiles[q * per - 1] if q > 0 else empty
-                after = tiles[(q + 1) * per] if (q + 1) * per < NB else empty
-                out_ref[q, channel * F + f, :, width:] = ends_tile(before, after)
+                    to[:, j * SEG:(j + 1) * SEG] = tile(q * per + j)
+                before = tile(jnp.maximum(q * per - 1, 0))
+                after = tile(jnp.minimum(q * per + per, NB - 1))
+                to[:, width:] = ends_tile(jnp.where(q > 0, before, 0.0),
+                                          jnp.where(q < len(outs) - 1, after, 0.0))
+
+
+def weights_kernel(groups, cap, blk, block_rows, w_ref, tie_ref, *rest):
+    outs, acc_ref, stage_ref = rest[:-2], rest[-2], rest[-1]
+
+    def terms(source, part, upper):
+        lower = 1.0 - upper
+        start = pl.multiple_of(source * block_rows + part * blk, 8)
+        weights = w_ref[pl.ds(start, blk), :]
+        lower_w, upper_w = lower * weights, upper * weights
+        return [lower * lower_w, upper * lower_w, upper * upper_w]
+
+    sum_rows(groups, cap, blk, block_rows, w_ref, acc_ref, terms)
+    stage_ref[0] = acc_ref[:, :SEG] + pltpu.roll(acc_ref[:, 2 * SEG:], 1, 0)
+    stage_ref[1] = acc_ref[:, SEG:2 * SEG]
+    cut_parts(stage_ref, outs)
+
+
+def products_kernel(groups, cap, blk, block_rows, w_ref, v_ref, tie_ref, *rest):
+    outs, acc_ref, stage_ref = rest[:-2], rest[-2], rest[-1]
+
+    def terms(source, part, upper):
+        start = pl.multiple_of(source * cap + part * blk, 8)
+        products = v_ref[pl.ds(start, blk), :]
+        return [(1.0 - upper) * products, upper * products]
+
+    sum_rows(groups, cap, blk, block_rows, w_ref, acc_ref, terms)
+    stage_ref[0] = acc_ref[:, :SEG] + pltpu.roll(acc_ref[:, SEG:], 1, 0)
+    cut_parts(stage_ref, outs)
 
 
 def sweep_x_into(to_ref, from_ref, cx_ref, plus_ref=None, sign=1.0):
@@ -195,10 +243,12 @@
         to_ref[lines, :] = sweep(from_ref[lines, :], cy_ref[lines, :], 1)
 
 
-def start_kernel(c0_ref, cx_ref, prev_ref, next_ref, cy_ref, c0_out, cx_out, cy_out, u_out):
+def start_kernel(c0_ref, cx_ref, prev_ref, next_ref, *rest):
+    cy_refs, (c0_out, cx_out, cy_out, u_out) = rest[:-4], rest[-4:]
     width = c0_ref.shape[2]
-    for p in range(cy_ref.shape[0]):
-        cy_out[p * LX:(p + 1) * LX, :] = cy_ref[p]
+    me = lax.axis_index("px")
+    for k, cy_ref in enumerate(cy_refs):
+        cy_out[pl.ds(pl.multiple_of((me ^ k) * LX, LX), LX), :] = cy_ref[...]
     last = cx_ref.shape[0] - 1
     cx_out[:, :width] = cx_ref[...]
     cx_out[:, width:] = ends_tile(prev_ref[F], next_ref[F])
@@ -210,13 +260,17 @@
         sweep_y_into(u_out.at[f], u_out.at[f], cy_out)
 
 
-def solve_kernel(obs_ref, c0_ref, cx_ref, cy_ref, u_ref, r_out, q_out, qq_out, dots_out,
-                 vec, coef, work):
+def solve_kernel(spans, c0_ref, cx_ref, cy_ref, u_ref, *rest):
+    side_refs, sum_refs = rest[:spans], rest[spans:2 * spans]
+    r_out, q_out, qq_out, dots_out, vec, coef, work = rest[2 * spans:]
     width = r_out.shape[2]
-    parts = obs_ref.shape[0]
-    for p in range(parts):
-        for channel in range(3 * F):
-            coef[channel, p * LX:(p + 1) * LX, :] = obs_ref[p, channel]
+    me = lax.axis_index("px")
+    for k in range(spans):
+        rows = pl.ds(pl.multiple_of((me ^ k) * LX, LX), LX)
+        for channel in range(2 * F):
+            coef[channel, rows, :] = side_refs[k][channel]
+        for f in range(F):
+            coef[2 * F + f, rows, :] = sum_refs[k][f]
 
     def normal(f, values, tile):
         size = values.shape[0]
@@ -286,19 +340,24 @@
         residual_out[f] = r - first_weight * q + both * qq_ref[f]
 
 
-def call(kernel, out_shape, scratch=(), in_specs=None):
+def call(kernel, out_shape, scratch=(), in_specs=None, work=0, limit=VMEM_BYTES):
     params = {} if in_specs is None else {"in_specs": in_specs}
     return pl.pallas_call(
         kernel,
         out_shape=out_shape,
         scratch_shapes=list(scratch),
-        compiler_params=pltpu.CompilerParams(vmem_limit_bytes=VMEM_BYTES),
+        compiler_params=pltpu.CompilerParams(vmem_limit_bytes=limit),
+        cost_estimate=pl.CostEstimate(flops=work, bytes_accessed=work, transcendentals=0),
         **params,
     )
 
 
 def f32(*shape):
     return jax.ShapeDtypeStruct(shape, jnp.float32)
+
+
+def vmem(*shape, kind=jnp.float32):
+    return pltpu.VMEM(shape, kind)
 
 
 def shards(
@@ -309,48 +368,73 @@
     cap = 3 * rows // groups
     blk = SEG if cap % SEG == 0 else HALF
     nb = cap // blk
-    block_rows = 2 * cap + -(-(2 * nb + 1) // 8) * 8
+    block_rows = cap + -(-(2 * nb + 1) // 8) * 8
     chunks = rows // SEG
     nx, width = control_start.shape[2], control_start.shape[3]
     ext = width + SEG
     c0, cx = control_start[:, 0], coef_x[0]
-
-    packed, cy_parts = call(
-        functools.partial(pack_kernel, groups, cap, blk, block_rows),
-        (f32(groups * block_rows, SEG), f32(spans, LX, ext)),
-        [pltpu.VMEM((chunks, SEG), jnp.int32), pltpu.SMEM((chunks, SEG), jnp.int32),
+    hbm, any_space, local = (pl.BlockSpec(memory_space=s) for s in (pltpu.HBM, pl.ANY, pltpu.VMEM))
+    layout = (groups, cap, blk, block_rows)
+    ints = vmem(chunks, SEG, kind=jnp.int32)
+
+    def partners(parts):
+        moves = [[(i, i ^ k) for i in range(spans)] for k in range(spans)]
+        return [parts[0]] + [lax.ppermute(parts[k], "px", moves[k]) for k in range(1, spans)]
+
+    w_packed, v_packed, first, last, *cy_parts = call(
+        functools.partial(pack_kernel, *layout),
+        (f32(groups * block_rows, SEG), f32(groups * cap, SEG), f32(F + 1, nx, SEG),
+         f32(F + 1, nx, SEG)) + (f32(LX, ext),) * spans,
+        [ints, ints, ints, vmem(chunks, SEG), vmem(rows, SEG), vmem(rows, SEG),
+         vmem(*coef_y.shape[1:]), vmem(2 * chunks, SEG, kind=jnp.int32),
+         pltpu.SMEM((2 * chunks, SEG), jnp.int32), pltpu.SemaphoreType.DMA((11,)),
          pltpu.SemaphoreType.DMA],
+        [hbm] * 9,
+        limit=PACK_BYTES,
     )(
         obs_owner.reshape(chunks, SEG), cell_key.reshape(chunks, SEG),
         stencil.reshape(chunks, SEG), interp.reshape(chunks, SEG),
-        obs_weight, innovation, coef_y[0],
+        obs_weight, innovation, coef_y[0], c0, cx,
     )
-    arrived = lax.all_to_all(packed, "py", split_axis=0, concat_axis=0, tiled=True)
-
-    cy_lines = lax.all_to_all(cy_parts, "px", split_axis=0, concat_axis=0, tiled=True)
-    fields = jnp.concatenate([c0, cx[None]], axis=0)
+    w_arrived = lax.all_to_all(w_packed, "py", split_axis=0, concat_axis=0, tiled=True)
+
     steps = [(i, i + 1) for i in range(spans - 1)]
-    from_prev = lax.ppermute(fields[:, :, -SEG:], "px", steps)
-    from_next = lax.ppermute(fields[:, :, :SEG], "px", [(j, i) for i, j in steps])
+    from_prev = lax.ppermute(last, "px", steps)
+    from_next = lax.ppermute(first, "px", [(j, i) for i, j in steps])
     c0_ext, cx_ext, cy_ext, u_ext = call(
         start_kernel,
         (f32(F, nx, ext), f32(nx, ext), f32(nx, ext), f32(F, nx, ext)),
-    )(c0, cx, from_prev, from_next, cy_lines)
-
-    obs_parts = call(
-        functools.partial(gather_kernel, groups, cap, blk, block_rows),
-        f32(spans, 3 * F, LX, ext),
-        [pltpu.VMEM((ROWS, 5 * SEG), jnp.float32)],
-    )(arrived)
-    obs_fields = lax.all_to_all(obs_parts, "px", split_axis=0, concat_axis=0, tiled=True)
+        work=10_000_000,
+    )(c0, cx, from_prev, from_next, *partners(cy_parts))
+
+    w_arrived, v_packed = lax.optimization_barrier((w_arrived, v_packed))
+    v_arrived = lax.all_to_all(v_packed, "py", split_axis=0, concat_axis=0, tiled=True)
+    side_parts = call(
+        functools.partial(weights_kernel, *layout),
+        (f32(2 * F, LX, ext),) * spans,
+        [vmem(ROWS, 3 * SEG), vmem(2, ROWS, SEG)],
+        [local, any_space],
+        work=20_000_000,
+    )(w_arrived, cx_ext)
+    side_parts = partners(side_parts)
+    sum_parts = call(
+        functools.partial(products_kernel, *layout),
+        (f32(F, LX, ext),) * spans,
+        [vmem(ROWS, 2 * SEG), vmem(1, ROWS, SEG)],
+        [local, local, any_space],
+        work=10_000_000,
+    )(w_arrived, v_arrived, side_parts[0])
+    sum_parts = partners(sum_parts)
 
     r, q, qq, dots = call(
-        solve_kernel,
-        (f32(F, nx, width),) * 3 + (f32(groups * spans, 8, SEG),),
-        [pltpu.VMEM((3, F, nx, ext), jnp.float32), pltpu.VMEM((3 * F, nx, ext), jnp.float32),
-         pltpu.VMEM((nx, ext), jnp.float32)],
-    )(obs_fields, c0_ext, cx_ext, cy_ext, u_ext)
-    dots = lax.all_to_all(dots, ("px", "py"), split_axis=0, concat_axis=0, tiled=True)
+        functools.partial(solve_kernel, spans),
+        (f32(F, nx, width),) * 3 + (f32(spans, 8, SEG),),
+        [vmem(3, F, nx, ext), vmem(3 * F, nx, ext), vmem(nx, ext)],
+        work=20_000_000,
+    )(c0_ext, cx_ext, cy_ext, u_ext, *side_parts, *sum_parts)
+    dots = lax.all_to_all(dots, "px", split_axis=0, concat_axis=0, tiled=True)
+    dots = jnp.broadcast_to(jnp.sum(dots, axis=0), (groups, 8, SEG))
+    dots = lax.all_to_all(dots, "py", split_axis=0, concat_axis=0, tiled=True)
     control, residual = call(finish_kernel, (f32(F, nx, width),) * 2)(dots, c0, r, q, qq)
     return control[:, None], residual[:, None]
 

time: 148 us -> 137 us (0.926)
  blocking collectives: 95.8 us -> 64.1 us
  waiting for transfers between devices: 5.74 us -> 21.6 us
  Pallas kernels: 24.2 us -> 32.2 us
  local copies, waits for them, and re-layouts: 7.6 us -> 2.53 us
  starting transfers between devices: 11.7 us -> 14.8 us
    all_to_all x2 -> x3, blocking collectives: 95.8 us -> 64.1 us  [the longest x1 45.7 us: shards(): lax.all_to_all(w_packed, 'py', split_axis=0, concat_axis=0, tiled=True)]
    all_to_all x2 -> x1, waiting for transfers between devices: 3.16 us -> 13.4 us  [shards(): lax.all_to_all(v_packed, 'py', split_axis=0, concat_axis=0, tiled=True)]
    pallas_call x3 -> x4, Pallas kernels: 20.7 us -> 29.7 us  [the longest x1 9.17 us: shards(): call(functools.partial(solve_kernel, spans), (f32(F, nx, width),) * 3 + (...]
    ppermute x2 -> x11, starting transfers between devices: 4.1 us -> 11.1 us  [the longest x9 8.55 us: partners(): lax.ppermute(parts[k], 'px', moves[k])]
    ppermute x2 -> x11, waiting for transfers between devices: 2.58 us -> 8.15 us  [the longest x9 8.14 us: partners(): lax.ppermute(parts[k], 'px', moves[k])]
    unnamed x22 -> x30, local copies, waits for them, and re-layouts: 7.6 us -> 2.53 us
    all_to_all x2 -> x1, starting transfers between devices: 7.61 us -> 3.71 us  [shards(): lax.all_to_all(v_packed, 'py', split_axis=0, concat_axis=0, tiled=True)]
  transfers between devices with their start and end apart: 4 -> 12, of which waited for: 2 -> 5; matrix products, arithmetic and copies ran while one was open for 1% -> 0% of each run, Pallas kernels for 7% -> 10%
where the time goes in v2:
time: 137 us; the launch traced here: 136 us
  blocking collectives  64.1 us (47%)
  Pallas kernels  32.2 us (24%)
  waiting for transfers between devices  21.6 us (16%)
  starting transfers between devices  14.8 us (11%)
  local copies, waits for them, and re-layouts  2.53 us (2%)
    all_to_all x1, blocking collectives, shards(): lax.all_to_all(w_packed, 'py', split_axis=0, concat_axis=0, tiled=True)  45.7 us
    all_to_all x1, waiting for transfers between devices, shards(): lax.all_to_all(v_packed, 'py', split_axis=0, concat_axis=0, tiled=True)  13.4 us
    all_to_all x1, blocking collectives, shards(): dots = lax.all_to_all(dots, 'py', split_axis=0, concat_axis=0, tiled=True)  12.1 us
    pallas_call x1, Pallas kernels, shards(): call(functools.partial(solve_kernel, spans), (f32(F, nx, width),) * 3 + (...  9.17 us
    ppermute x9, starting transfers between devices, partners(): lax.ppermute(parts[k], 'px', moves[k])  8.55 us
    pallas_call x1, Pallas kernels, shards(): call(functools.partial(pack_kernel, *layout), (f32(groups * block_rows, S...  8.48 us
    ppermute x9, waiting for transfers between devices, partners(): lax.ppermute(parts[k], 'px', moves[k])  8.14 us
    pallas_call x1, Pallas kernels, shards(): call(functools.partial(weights_kernel, *layout), (f32(2 * F, LX, ext),) *...  6.83 us
  transfers between devices with their start and end apart: 12, of which 5 were waited for; matrix products, arithmetic and copies ran while one was open for 0% of the time, Pallas kernels for 10%

profile of v2, /device:TPU:0, one launch (start us, length us, event | category | flops | bytes accessed | tf_op | source)
XLA Modules:
  0.0 136.1 jit_solution(12973268764275103274)
XLA Ops:
  0.6 8.5 %shard_map.104 = (f32[3136,128]{1,0:T(8,128)}, f32[3072,128]{1,0:T(8,128)}, f32[3,64,128]{2,1,0:T(8,128)}, f32[3,64,128]{2,1,0:T(8,128)}, f32[16,640]{1,0:T(8,12...) custom-call(s32[8,128]{1,0:T(8,128)} %bitcast.28, s32[8,128]{1,0:T(8,128)} %bitcast.29, ...), custom_call_target="tpu_custom_call" | custom-call | tf_op jit(solution)/shard_map/pallas_call | solution.py:384
  9.1 45.7 %all_to_all.33 = f32[8,392,128]{2,1,0:T(8,128)S(1)} all-to-all(f32[8,392,128]{2,1,0:T(8,128)} %bitcast.25), channel_id=1, replica_groups=mesh['px'=4,'py'=8] {'py'}, dimensions={0} | all-to-all | bytes 3211264 | tf_op jit(solution)/shard_map/all_to_all | solution.py:399
  54.9 3.7 %all-to-all-start.1 = ((f32[8,384,128]{2,1,0:T(8,128)}), f32[8,384,128]{2,1,0:T(8,128)S(1)}, u32[]{:S(2)}, u32[]{:S(2)}) async-start(f32[8,384,128]{2,1,0:T(8,128)} %bitcast.26), calls=%async_computation.1 | async-start | bytes 3145728 | tf_op jit(solution)/shard_map/all_to_all | solution.py:411
  58.6 1.3 collective-permute-start
  59.9 1.3 collective-permute-start.1
  61.2 2.9 %collective-permute-start.2 = (f32[16,640]{1,0:T(8,128)}, f32[16,640]{1,0:T(8,128)S(1)}, u32[]{:S(2)}, u32[]{:S(2)}) collective-permute-start(f32[16,640]{1,0:T(8,128)} %get-tuple-element.33), channel_id=1, source_target_pairs={{0,8},{8,0},{16,24},{24,16},{1,9},{9,1},{17,25},{25,17},{2,10},{10... | collective-permute-start | bytes 122888 | tf_op jit(solution)/shard_map/ppermute | solution.py:382
  64.1 1.7 %collective-permute-start.3 = (f32[16,640]{1,0:T(8,128)}, f32[16,640]{1,0:T(8,128)S(1)}, u32[]{:S(2)}, u32[]{:S(2)}) collective-permute-start(f32[16,640]{1,0:T(8,128)} %get-tuple-element.34), channel_id=1, source_target_pairs={{0,16},{8,24},{16,0},{24,8},{1,17},{9,25},{17,1},{25,9},{2,18},{10... | collective-permute-start | bytes 122888 | tf_op jit(solution)/shard_map/ppermute | solution.py:382
  65.9 3.7 %collective-permute-done.3.rest_2_ = f32[16,640]{1,0:T(8,128)S(1)} collective-permute-done((f32[16,640]{1,0:T(8,128)}, f32[16,640]{1,0:T(8,128)S(1)}, u32[]{:S(2)}, u32[]{:S(2)}) %collective-permute-start.3) | collective-permute-done | bytes 40992 | tf_op jit(solution)/shard_map/ppermute | solution.py:382
  69.8 0.9 copy-done.6
  70.7 1.3 shard_map.105
  72.0 6.8 %shard_map.106 = (f32[4,16,640]{2,1,0:T(8,128)S(1)}, f32[4,16,640]{2,1,0:T(8,128)}, f32[4,16,640]{2,1,0:T(8,128)}, f32[4,16,640]{2,1,0:T(8,128)}) custom-call(f32[3136,128]{1,0:T(8,128)S(1)} %bitcast.17, f32[64,640]{1,0:T(8,128)S(1)} %get-tuple-element.37.tie_ref.cx_ref), custom_call_target="tpu_custom_call" | custom-call | flops 20000000 | bytes 20000000 | tf_op jit(solution)/shard_map/pallas_call | solution.py:412
  78.8 0.7 copy-done.1
  79.5 0.5 collective-permute-start.5
  80.0 1.4 %collective-permute-start.7 = (f32[4,16,640]{2,1,0:T(8,128)}, f32[4,16,640]{2,1,0:T(8,128)}, u32[]{:S(2)}, u32[]{:S(2)}) collective-permute-start(f32[4,16,640]{2,1,0:T(8,128)} %get-tuple-element.46), channel_id=1, source_target_pairs={{0,24},{8,16},{16,8},{24,0},{1,25},{9,17},{17,9},{25,1},{2,26},{10... | collective-permute-start | bytes 491528 | tf_op jit(solution)/shard_map/ppermute | solution.py:382
  81.4 13.4 %all-to-all-done.1 = f32[8,384,128]{2,1,0:T(8,128)S(1)} async-done(((f32[8,384,128]{2,1,0:T(8,128)}), f32[8,384,128]{2,1,0:T(8,128)S(1)}, u32[]{:S(2)}, u32[]{:S(2)}) %all-to-all-start.1) | async-done | bytes 1572896 | tf_op jit(solution)/shard_map/all_to_all | solution.py:411
  94.8 0.9 copy-done.2
  95.7 5.2 %shard_map.107 = (f32[2,16,640]{2,1,0:T(8,128)S(1)}, f32[2,16,640]{2,1,0:T(8,128)S(1)}, f32[2,16,640]{2,1,0:T(8,128)S(1)}, f32[2,16,640]{2,1,0:T(8,128)S(1)}) custom-call(f32[3136,128]{1,0:T(8,128)S(1)} %bitcast.18, f32[3072,128]{1,0:T(8,128)S(1)} %bitcast.19, f32[4,16,640]{2,1,0:T(8,128)S(1)} %copy-done.2), custom_call_target="tpu_custom_call" | custom-call | flops 10000000 | bytes 10000000 | tf_op jit(solution)/shard_map/pallas_call | solution.py:420
  101.4 1.5 %collective-permute-start.10 = (f32[2,16,640]{2,1,0:T(8,128)S(1)}, f32[2,16,640]{2,1,0:T(8,128)S(1)}, u32[]{:S(2)}, u32[]{:S(2)}) collective-permute-start(f32[2,16,640]{2,1,0:T(8,128)S(1)} %get-tuple-element.51), channel_id=1, source_target_pairs={{0,24},{8,16},{16,8},{24,0},{1,25},{9,17},{17,9},{25,1},{2,26},{10... | collective-permute-start | bytes 245768 | tf_op jit(solution)/shard_map/ppermute | solution.py:382
  102.9 3.4 %collective-permute-done.9.rest_6_ = f32[2,16,640]{2,1,0:T(8,128)S(1)} collective-permute-done((f32[2,16,640]{2,1,0:T(8,128)S(1)}, f32[2,16,640]{2,1,0:T(8,128)S(1)}, u32[]{:S(2)}, u32[]{:S(2)}) %collective-permute-start.9) | collective-permute-done | bytes 81952 | tf_op jit(solution)/shard_map/ppermute | solution.py:382
  106.3 0.8 collective-permute-done.10.rest_7_
  107.2 9.2 %shard_map.108 = (f32[2,64,512]{2,1,0:T(8,128)S(1)}, f32[2,64,512]{2,1,0:T(8,128)S(1)}, f32[2,64,512]{2,1,0:T(8,128)S(1)}, f32[4,8,128]{2,1,0:T(8,128)S(1)}) custom-call(f32[2,64,640]{2,1,0:T(8,128)S(1)} %copy-done.8, f32[64,640]{1,0:T(8,128)S(1)} %copy-done.5, f32[64,640]{1,0:T(8,128)S(1)} %copy-done.12, f32[2,64,640]{2,1,0:T(8,128)S(1)} %copy-done.10, ...), custom_call_target="tpu_custom_call" | custom-call | flops 20000000 | bytes 20000000 | tf_op jit(solution)/shard_map/pallas_call | solution.py:429
  116.4 6.2 %all_to_all.34 = f32[4,8,128]{2,1,0:T(8,128)S(1)} all-to-all(f32[4,8,128]{2,1,0:T(8,128)S(1)} %get-tuple-element.52), channel_id=1, replica_groups=mesh['px'=4,'py'=8] {'px'}, dimensions={0} | all-to-all | bytes 32768 | tf_op jit(solution)/shard_map/all_to_all | solution.py:435
  122.6 12.1 %all_to_all.35.dots_ref = f32[8,8,128]{2,1,0:T(8,128)S(1)} all-to-all(f32[8,8,128]{2,1,0:T(8,128)S(1)} %broadcast_in_dim.9), channel_id=1, replica_groups=mesh['px'=4,'py'=8] {'py'}, dimensions={0} | all-to-all | bytes 65536 | tf_op jit(solution)/shard_map/all_to_all | solution.py:437
  134.7 1.3 shard_map.109
  (41 shorter events, 0.7 us)
Async XLA Ops:
  54.9 11.0 %copy-start.14 = (f32[16,640]{1,0:T(8,128)S(1)}, f32[16,640]{1,0:T(8,128)}, u32[]{:S(2)}) copy-start(f32[16,640]{1,0:T(8,128)} %get-tuple-element.35) | copy-start | bytes 122884
  54.9 14.9 %copy-start = (f32[2,1,64,512]{3,2,1,0:T(8,128)S(1)}, f32[2,1,64,512]{3,2,1,0:T(8,128)}, u32[]{:S(2)}) copy-start(f32[2,1,64,512]{3,2,1,0:T(8,128)} %param.9) | copy-start | bytes 786436
  54.9 14.9 %copy-start.13 = (f32[16,640]{1,0:T(8,128)S(1)}, f32[16,640]{1,0:T(8,128)}, u32[]{:S(2)}) copy-start(f32[16,640]{1,0:T(8,128)} %get-tuple-element.32.rest_0_) | copy-start | bytes 122884
  54.9 39.9 %all-to-all-start.1 = ((f32[8,384,128]{2,1,0:T(8,128)}), f32[8,384,128]{2,1,0:T(8,128)S(1)}, u32[]{:S(2)}, u32[]{:S(2)}) async-start(f32[8,384,128]{2,1,0:T(8,128)} %bitcast.26), calls=%async_computation.1 | async-start | bytes 3145728 | tf_op jit(solution)/shard_map/all_to_all | solution.py:411
  58.6 11.2 %collective-permute-start = (f32[3,64,128]{2,1,0:T(8,128)}, f32[3,64,128]{2,1,0:T(8,128)S(1)}, u32[]{:S(2)}, u32[]{:S(2)}) collective-permute-start(f32[3,64,128]{2,1,0:T(8,128)} %get-tuple-element.30), channel_id=1, source_target_pairs={{0,8},{8,16},{16,24},{1,9},{9,17},{17,25},{2,10},{10,18},{18,26},{... | collective-permute-start | bytes 294920 | tf_op jit(solution)/shard_map/ppermute | solution.py:402
  59.9 9.9 %collective-permute-start.1 = (f32[3,64,128]{2,1,0:T(8,128)}, f32[3,64,128]{2,1,0:T(8,128)S(1)}, u32[]{:S(2)}, u32[]{:S(2)}) collective-permute-start(f32[3,64,128]{2,1,0:T(8,128)} %get-tuple-element.31), channel_id=1, source_target_pairs={{8,0},{16,8},{24,16},{9,1},{17,9},{25,17},{10,2},{18,10},{26,18},{... | collective-permute-start | bytes 294920 | tf_op jit(solution)/shard_map/ppermute | solution.py:403
  61.2 4.7 %collective-permute-start.2 = (f32[16,640]{1,0:T(8,128)}, f32[16,640]{1,0:T(8,128)S(1)}, u32[]{:S(2)}, u32[]{:S(2)}) collective-permute-start(f32[16,640]{1,0:T(8,128)} %get-tuple-element.33), channel_id=1, source_target_pairs={{0,8},{8,0},{16,24},{24,16},{1,9},{9,1},{17,25},{25,17},{2,10},{10... | collective-permute-start | bytes 122888 | tf_op jit(solution)/shard_map/ppermute | solution.py:382
  64.1 5.5 %collective-permute-start.3 = (f32[16,640]{1,0:T(8,128)}, f32[16,640]{1,0:T(8,128)S(1)}, u32[]{:S(2)}, u32[]{:S(2)}) collective-permute-start(f32[16,640]{1,0:T(8,128)} %get-tuple-element.34), channel_id=1, source_target_pairs={{0,16},{8,24},{16,0},{24,8},{1,17},{9,25},{17,1},{25,9},{2,18},{10... | collective-permute-start | bytes 122888 | tf_op jit(solution)/shard_map/ppermute | solution.py:382
  65.8 3.9 %collective-permute-start.4 = (f32[16,640]{1,0:T(8,128)S(1)}, f32[16,640]{1,0:T(8,128)S(1)}, u32[]{:S(2)}, u32[]{:S(2)}) collective-permute-start(f32[16,640]{1,0:T(8,128)S(1)} %copy-done.14), channel_id=1, source_target_pairs={{0,24},{8,16},{16,8},{24,0},{1,25},{9,17},{17,9},{25,1},{2,26},{10... | collective-permute-start | bytes 122888 | tf_op jit(solution)/shard_map/ppermute | solution.py:382
  71.9 8.0 %copy-start.4 = (f32[64,640]{1,0:T(8,128)}, f32[64,640]{1,0:T(8,128)S(1)}, u32[]{:S(2)}) copy-start(f32[64,640]{1,0:T(8,128)S(1)} %get-tuple-element.37.tie_ref.cx_ref) | copy-start | bytes 491524
  71.9 8.0 %copy-start.7 = (f32[2,64,640]{2,1,0:T(8,128)}, f32[2,64,640]{2,1,0:T(8,128)S(1)}, u32[]{:S(2)}) copy-start(f32[2,64,640]{2,1,0:T(8,128)S(1)} %get-tuple-element.36.c0_ref) | copy-start | bytes 983044
  71.9 8.0 %copy-start.9 = (f32[2,64,640]{2,1,0:T(8,128)}, f32[2,64,640]{2,1,0:T(8,128)S(1)}, u32[]{:S(2)}) copy-start(f32[2,64,640]{2,1,0:T(8,128)S(1)} %get-tuple-element.39.u_ref) | copy-start | bytes 983044
  72.0 8.0 %copy-start.11 = (f32[64,640]{1,0:T(8,128)}, f32[64,640]{1,0:T(8,128)S(1)}, u32[]{:S(2)}) copy-start(f32[64,640]{1,0:T(8,128)S(1)} %get-tuple-element.38.cy_ref) | copy-start | bytes 491524
  79.5 21.9 %collective-permute-start.5 = (f32[4,16,640]{2,1,0:T(8,128)}, f32[4,16,640]{2,1,0:T(8,128)}, u32[]{:S(2)}, u32[]{:S(2)}) collective-permute-start(f32[4,16,640]{2,1,0:T(8,128)} %get-tuple-element.44), channel_id=1, source_target_pairs={{0,8},{8,0},{16,24},{24,16},{1,9},{9,1},{17,25},{25,17},{2,10},{10... | collective-permute-start | bytes 491528 | tf_op jit(solution)/shard_map/ppermute | solution.py:382
  80.0 22.9 %collective-permute-start.6 = (f32[4,16,640]{2,1,0:T(8,128)}, f32[4,16,640]{2,1,0:T(8,128)}, u32[]{:S(2)}, u32[]{:S(2)}) collective-permute-start(f32[4,16,640]{2,1,0:T(8,128)} %get-tuple-element.45), channel_id=1, source_target_pairs={{0,16},{8,24},{16,0},{24,8},{1,17},{9,25},{17,1},{25,9},{2,18},{10... | collective-permute-start | bytes 491528 | tf_op jit(solution)/shard_map/ppermute | solution.py:382
  80.0 22.9 %collective-permute-start.7 = (f32[4,16,640]{2,1,0:T(8,128)}, f32[4,16,640]{2,1,0:T(8,128)}, u32[]{:S(2)}, u32[]{:S(2)}) collective-permute-start(f32[4,16,640]{2,1,0:T(8,128)} %get-tuple-element.46), channel_id=1, source_target_pairs={{0,24},{8,16},{16,8},{24,0},{1,25},{9,17},{17,9},{25,1},{2,26},{10... | collective-permute-start | bytes 491528 | tf_op jit(solution)/shard_map/ppermute | solution.py:382
  95.7 11.4 %copy-start.3 = (f32[4,16,640]{2,1,0:T(8,128)S(1)}, f32[4,16,640]{2,1,0:T(8,128)}, u32[]{:S(2)}) copy-start(f32[4,16,640]{2,1,0:T(8,128)} %copy-done.1) | copy-start | bytes 491524
  95.7 11.4 %copy-start.5 = (f32[64,640]{1,0:T(8,128)S(1)}, f32[64,640]{1,0:T(8,128)}, u32[]{:S(2)}) copy-start(f32[64,640]{1,0:T(8,128)} %copy-done.4) | copy-start | bytes 491524
  95.7 11.4 %copy-start.8 = (f32[2,64,640]{2,1,0:T(8,128)S(1)}, f32[2,64,640]{2,1,0:T(8,128)}, u32[]{:S(2)}) copy-start(f32[2,64,640]{2,1,0:T(8,128)} %copy-done.7) | copy-start | bytes 983044
  95.7 11.4 %copy-start.10 = (f32[2,64,640]{2,1,0:T(8,128)S(1)}, f32[2,64,640]{2,1,0:T(8,128)}, u32[]{:S(2)}) copy-start(f32[2,64,640]{2,1,0:T(8,128)} %copy-done.9) | copy-start | bytes 983044
  95.7 11.4 %copy-start.12 = (f32[64,640]{1,0:T(8,128)S(1)}, f32[64,640]{1,0:T(8,128)}, u32[]{:S(2)}) copy-start(f32[64,640]{1,0:T(8,128)} %copy-done.11) | copy-start | bytes 491524
  100.9 2.0 %collective-permute-start.8 = (f32[2,16,640]{2,1,0:T(8,128)S(1)}, f32[2,16,640]{2,1,0:T(8,128)S(1)}, u32[]{:S(2)}, u32[]{:S(2)}) collective-permute-start(f32[2,16,640]{2,1,0:T(8,128)S(1)} %get-tuple-element.49), channel_id=1, source_target_pairs={{0,8},{8,0},{16,24},{24,16},{1,9},{9,1},{17,25},{25,17},{2,10},{10... | collective-permute-start | bytes 245768 | tf_op jit(solution)/shard_map/ppermute | solution.py:382
  101.0 5.3 %collective-permute-start.9 = (f32[2,16,640]{2,1,0:T(8,128)S(1)}, f32[2,16,640]{2,1,0:T(8,128)S(1)}, u32[]{:S(2)}, u32[]{:S(2)}) collective-permute-start(f32[2,16,640]{2,1,0:T(8,128)S(1)} %get-tuple-element.50), channel_id=1, source_target_pairs={{0,16},{8,24},{16,0},{24,8},{1,17},{9,25},{17,1},{25,9},{2,18},{10... | collective-permute-start | bytes 245768 | tf_op jit(solution)/shard_map/ppermute | solution.py:382
  101.4 5.8 %collective-permute-start.10 = (f32[2,16,640]{2,1,0:T(8,128)S(1)}, f32[2,16,640]{2,1,0:T(8,128)S(1)}, u32[]{:S(2)}, u32[]{:S(2)}) collective-permute-start(f32[2,16,640]{2,1,0:T(8,128)S(1)} %get-tuple-element.51), channel_id=1, source_target_pairs={{0,24},{8,16},{16,8},{24,0},{1,25},{9,17},{17,9},{25,1},{2,26},{10... | collective-permute-start | bytes 245768 | tf_op jit(solution)/shard_map/ppermute | solution.py:382
  (3 other events, 2.5 us)

commit v3 on v2

--- a/solution.py
+++ b/solution.py
@@ -14,6 +14,9 @@
 LX = 16
 ROWS = F * NB * LX
 HALF = SEG // 2
+SPLIT = 16
+X_WIDTH = 256
+Y_LINES = 16
 VMEM_BYTES = 32 * 1024 * 1024
 PACK_BYTES = 60 * 1024 * 1024
 
@@ -51,28 +54,22 @@
     return values
 
 
-def pack_kernel(groups, cap, blk, block_rows, own_hbm, key_hbm, sten_hbm, itp_hbm, w_hbm, d_hbm,
-                cy_hbm, c0_hbm, cx_hbm, w_out, v_out, first_out, last_out, *rest):
-    cy_outs, rest = rest[:-11], rest[-11:]
-    own_ref, key_ref, sten_ref, itp_ref, w_ref, d_ref, cy_ref, slot_v, slot_s, sems, sem = rest
-    width = c0_hbm.shape[2]
-    pairs = [
-        (own_hbm, own_ref), (key_hbm, key_ref), (sten_hbm, sten_ref), (itp_hbm, itp_ref),
-        (w_hbm, w_ref), (d_hbm, d_ref), (cy_hbm, cy_ref),
-        (c0_hbm.at[:, :, pl.ds(0, SEG)], first_out.at[pl.ds(0, F)]),
-        (cx_hbm.at[:, pl.ds(0, SEG)], first_out.at[F]),
-        (c0_hbm.at[:, :, pl.ds(width - SEG, SEG)], last_out.at[pl.ds(0, F)]),
-        (cx_hbm.at[:, pl.ds(width - SEG, SEG)], last_out.at[F]),
-    ]
-    loads = [pltpu.make_async_copy(*pair, sems.at[i]) for i, pair in enumerate(pairs)]
-    for load in loads:
-        load.start()
+def start_copies(pairs, sems):
+    copies = [pltpu.make_async_copy(*pair, sems.at[i]) for i, pair in enumerate(pairs)]
+    for copy in copies:
+        copy.start()
+    return copies
+
+
+def pack_weights_kernel(groups, cap, blk, block_rows, own_hbm, key_hbm, sten_hbm, itp_hbm, w_hbm,
+                        w_out, slot_out, own_ref, key_ref, sten_ref, itp_ref, w_ref, slot_v,
+                        slot_s, sems, sem):
+    loads = start_copies([(own_hbm, own_ref), (key_hbm, key_ref), (sten_hbm, sten_ref),
+                          (itp_hbm, itp_ref), (w_hbm, w_ref)], sems)
 
     def clear(o, carry):
         start = pl.multiple_of(o * block_rows, 8)
         w_out[pl.ds(start, block_rows), :] = jnp.zeros((block_rows, SEG), jnp.float32)
-        start = pl.multiple_of(o * cap, 8)
-        v_out[pl.ds(start, cap), :] = jnp.zeros((cap, SEG), jnp.float32)
         return carry
 
     lax.fori_loop(0, groups, clear, 0)
@@ -92,11 +89,10 @@
     line, column = iota((high, high), 0), iota((high, high), 1)
     same = (line >> shift) == (column >> shift)
     ranks = within + mxu(flag(same & (column < line)), tallies)
-    totals = mxu(flag(same), tallies)
     rank = sum(masks[o] * ranks[o * chunks:(o + 1) * chunks] for o in range(groups))
     rank = rank.astype(jnp.int32)
-    slot_v[:chunks] = own * block_rows + rank
-    slot_v[chunks:] = own * cap + rank
+    slot_v[...] = own * block_rows + rank
+    slot_out[...] = own * cap + rank
     copy = pltpu.make_async_copy(slot_v, slot_s, sem)
     copy.start()
 
@@ -109,7 +105,7 @@
     for i in range(chunks):
         chosen = iota((tall, SEG), 0) == place[i:i + 1]
         parts = split_parts(itp[i:i + 1], 3)
-        parts += [key[i:i + 1].astype(jnp.bfloat16), sten[i:i + 1].astype(jnp.bfloat16)]
+        parts += [key[i:i + 1].astype(jnp.bfloat16), (sten[i:i + 1] + 1).astype(jnp.bfloat16)]
         left = [jnp.where(chosen, part.astype(jnp.float32), 0.0) for part in parts]
         right = flag(iota(square, 0) == lane[i:i + 1])
         meta = meta + lax.dot_general(
@@ -121,9 +117,40 @@
         base = o * block_rows + cap
         w_out[base:base + nb, :] = shares[o * nb:(o + 1) * nb]
         w_out[base + nb:base + 2 * nb, :] = targets[o * nb:(o + 1) * nb]
-        w_out[base + 2 * nb:base + 2 * nb + 1, :] = totals[o * chunks:o * chunks + 1]
-
-    for load in loads[4:]:
+
+    copy.wait()
+    loads[4].wait()
+
+    def place_rows(g, carry):
+        weights = w_ref[pl.ds(pl.multiple_of(g * 8, 8), 8), :]
+        line, lane = g // 16, (g % 16) * 8
+        for i in range(8):
+            w_out[pl.ds(slot_s[line, lane + i], 1), :] = weights[i:i + 1]
+        return carry
+
+    lax.fori_loop(0, w_ref.shape[0] // 8, place_rows, 0)
+
+
+def pack_products_kernel(groups, cap, slot_ref, w_hbm, d_hbm, cy_hbm, c0_hbm, cx_hbm, v_out,
+                         first_out, last_out, *rest):
+    cy_outs, (w_ref, d_ref, cy_ref, sems) = rest[:-4], rest[-4:]
+    width = c0_hbm.shape[2]
+    loads = start_copies([
+        (w_hbm, w_ref), (d_hbm, d_ref), (cy_hbm, cy_ref),
+        (c0_hbm.at[:, :, pl.ds(0, SEG)], first_out.at[pl.ds(0, F)]),
+        (cx_hbm.at[:, pl.ds(0, SEG)], first_out.at[F]),
+        (c0_hbm.at[:, :, pl.ds(width - SEG, SEG)], last_out.at[pl.ds(0, F)]),
+        (cx_hbm.at[:, pl.ds(width - SEG, SEG)], last_out.at[F]),
+    ], sems)
+
+    def clear(o, carry):
+        start = pl.multiple_of(o * cap, 8)
+        v_out[pl.ds(start, cap), :] = jnp.zeros((cap, SEG), jnp.float32)
+        return carry
+
+    lax.fori_loop(0, groups, clear, 0)
+
+    for load in loads:
         load.wait()
     columns = cy_ref.shape[1]
     cy = cy_ref[...]
@@ -138,16 +165,12 @@
         cy_out[:, width:] = ends_tile(jnp.where(q > 0, before, 0.0),
                                       jnp.where(q < len(cy_outs) - 1, after, 0.0))
 
-    copy.wait()
-
     def place_rows(g, carry):
         start = pl.multiple_of(g * 8, 8)
-        weights = w_ref[pl.ds(start, 8), :]
-        products = weights * d_ref[pl.ds(start, 8), :]
+        products = w_ref[pl.ds(start, 8), :] * d_ref[pl.ds(start, 8), :]
         line, lane = g // 16, (g % 16) * 8
         for i in range(8):
-            w_out[pl.ds(slot_s[line, lane + i], 1), :] = weights[i:i + 1]
-            v_out[pl.ds(slot_s[chunks + line, lane + i], 1), :] = products[i:i + 1]
+            v_out[pl.ds(slot_ref[line, lane + i], 1), :] = products[i:i + 1]
         return carry
 
     lax.fori_loop(0, w_ref.shape[0] // 8, place_rows, 0)
@@ -156,26 +179,22 @@
 def sum_rows(groups, cap, blk, block_rows, w_ref, acc_ref, terms):
     nb = cap // blk
     acc_ref[...] = jnp.zeros_like(acc_ref)
-
-    def block(index, carry):
-        source, part = index // nb, index % nb
-        base = pl.multiple_of(source * block_rows, 8)
-        count = w_ref[pl.ds(base + cap + 2 * nb, 1), :][0, 0]
-
-        @pl.when(count > (part * blk).astype(jnp.float32))
-        def _():
-            share = w_ref[pl.ds(base + cap + part, 1), :]
-            target = w_ref[pl.ds(base + cap + nb + part, 1), :][:, :blk]
-            upper = jnp.broadcast_to(share, (SEG, SEG)).T[:blk]
-            values = jnp.concatenate(terms(source, part, upper), axis=1)
-            hit = flag(iota((ROWS, blk), 0).astype(jnp.float32) == target)
-            acc_ref[...] += mxu(
-                jnp.concatenate([hit, hit], axis=1),
-                jnp.concatenate(split_parts(values, 2), axis=0))
-
-        return carry
-
-    lax.fori_loop(0, groups * nb, block, 0)
+    numbers = 1.0 + iota((ROWS, cap), 0).astype(jnp.float32)
+
+    def source_rows(source, carry):
+        start = pl.multiple_of(source * block_rows + cap, 8)
+        meta = w_ref[pl.ds(start, 8), :]
+        upper = jnp.concatenate(
+            [jnp.broadcast_to(meta[i:i + 1], (SEG, SEG)).T[:blk] for i in range(nb)], axis=0)
+        target = jnp.concatenate([meta[nb + i:nb + i + 1, :blk] for i in range(nb)], axis=1)
+        hit = flag(numbers == target)
+        values = jnp.concatenate(terms(source, upper), axis=1)
+        acc_ref[...] += mxu(
+            jnp.concatenate([hit, hit], axis=1),
+            jnp.concatenate(split_parts(values, 2), axis=0))
+        return carry
+
+    lax.fori_loop(0, groups, source_rows, 0, unroll=2)
 
 
 def cut_parts(stage_ref, outs):
@@ -202,10 +221,9 @@
 def weights_kernel(groups, cap, blk, block_rows, w_ref, tie_ref, *rest):
     outs, acc_ref, stage_ref = rest[:-2], rest[-2], rest[-1]
 
-    def terms(source, part, upper):
+    def terms(source, upper):
         lower = 1.0 - upper
-        start = pl.multiple_of(source * block_rows + part * blk, 8)
-        weights = w_ref[pl.ds(start, blk), :]
+        weights = w_ref[pl.ds(pl.multiple_of(source * block_rows, 8), cap), :]
         lower_w, upper_w = lower * weights, upper * weights
         return [lower * lower_w, upper * lower_w, upper * upper_w]
 
@@ -215,12 +233,11 @@
     cut_parts(stage_ref, outs)
 
 
-def products_kernel(groups, cap, blk, block_rows, w_ref, v_ref, tie_ref, *rest):
+def products_kernel(groups, cap, blk, block_rows, w_ref, v_ref, *rest):
     outs, acc_ref, stage_ref = rest[:-2], rest[-2], rest[-1]
 
-    def terms(source, part, upper):
-        start = pl.multiple_of(source * cap + part * blk, 8)
-        products = v_ref[pl.ds(start, blk), :]
+    def terms(source, upper):
+        products = v_ref[pl.ds(pl.multiple_of(source * cap, 8), cap), :]
         return [(1.0 - upper) * products, upper * products]
 
     sum_rows(groups, cap, blk, block_rows, w_ref, acc_ref, terms)
@@ -229,8 +246,9 @@
 
 
 def sweep_x_into(to_ref, from_ref, cx_ref, plus_ref=None, sign=1.0):
-    for low in range(0, cx_ref.shape[1], SEG):
-        tile = slice(low, low + SEG)
+    size = cx_ref.shape[1]
+    for low in range(0, size, X_WIDTH):
+        tile = slice(low, min(low + X_WIDTH, size))
         values = sweep(from_ref[:, tile], cx_ref[:, tile], 0)
         if plus_ref is not None:
             values = values + sign * plus_ref[:, tile]
@@ -238,8 +256,8 @@
 
 
 def sweep_y_into(to_ref, from_ref, cy_ref):
-    for low in range(0, cy_ref.shape[0], 8):
-        lines = slice(low, low + 8)
+    for low in range(0, cy_ref.shape[0], Y_LINES):
+        lines = slice(low, low + Y_LINES)
         to_ref[lines, :] = sweep(from_ref[lines, :], cy_ref[lines, :], 1)
 
 
@@ -313,18 +331,22 @@
                 qq = vec[2, f, low:low + 8, tile]
                 for i, product in enumerate((r * r, r * q, q * q, r * qq, q * qq)):
                     sums[i] = sums[i] + product
-    lines = [jnp.sum(s, axis=0, keepdims=True) for s in sums]
-    dots = jnp.concatenate(lines + [jnp.zeros((3, SEG), jnp.float32)], axis=0)
-    for device in range(dots_out.shape[0]):
-        dots_out[device] = dots
+    dots = jnp.zeros((1, SEG), jnp.float32)
+    for i, total in enumerate(sums):
+        line = jnp.sum(total, axis=0, keepdims=True)
+        for distance in (64, 32, 16):
+            line = line + pltpu.roll(line, distance, 1)
+        dots = jnp.where(iota((1, SEG), 1) // SPLIT == i, line, dots)
+    dots_out[...] = jnp.broadcast_to(dots, dots_out.shape)
 
 
 def finish_kernel(dots_ref, c0_ref, r_ref, q_ref, qq_ref, control_out, residual_out):
     dots = jnp.sum(dots_ref[...], axis=0)
-    rr, rq, qq2, rqq, qqq = (dots[i:i + 1] for i in range(5))
+    lane = iota((1, SEG), 1)
+    rr, rq, qq2, rqq, qqq = (pltpu.roll(dots, (SEG - i * SPLIT) % SEG, 1) for i in range(5))
 
     def total(line):
-        return jnp.sum(line, axis=1, keepdims=True)
+        return jnp.sum(jnp.where(lane < SPLIT, line, 0.0), axis=1, keepdims=True)
 
     rr_sum = total(rr)
     alpha = rr_sum / total(rq)
@@ -368,12 +390,13 @@
     cap = 3 * rows // groups
     blk = SEG if cap % SEG == 0 else HALF
     nb = cap // blk
-    block_rows = cap + -(-(2 * nb + 1) // 8) * 8
+    block_rows = cap + -(-2 * nb // 8) * 8
     chunks = rows // SEG
     nx, width = control_start.shape[2], control_start.shape[3]
     ext = width + SEG
     c0, cx = control_start[:, 0], coef_x[0]
-    hbm, any_space, local = (pl.BlockSpec(memory_space=s) for s in (pltpu.HBM, pl.ANY, pltpu.VMEM))
+    hbm, any_space, local, scalars = (
+        pl.BlockSpec(memory_space=s) for s in (pltpu.HBM, pl.ANY, pltpu.VMEM, pltpu.SMEM))
     layout = (groups, cap, blk, block_rows)
     ints = vmem(chunks, SEG, kind=jnp.int32)
 
@@ -381,21 +404,28 @@
         moves = [[(i, i ^ k) for i in range(spans)] for k in range(spans)]
         return [parts[0]] + [lax.ppermute(parts[k], "px", moves[k]) for k in range(1, spans)]
 
-    w_packed, v_packed, first, last, *cy_parts = call(
-        functools.partial(pack_kernel, *layout),
-        (f32(groups * block_rows, SEG), f32(groups * cap, SEG), f32(F + 1, nx, SEG),
-         f32(F + 1, nx, SEG)) + (f32(LX, ext),) * spans,
-        [ints, ints, ints, vmem(chunks, SEG), vmem(rows, SEG), vmem(rows, SEG),
-         vmem(*coef_y.shape[1:]), vmem(2 * chunks, SEG, kind=jnp.int32),
-         pltpu.SMEM((2 * chunks, SEG), jnp.int32), pltpu.SemaphoreType.DMA((11,)),
+    w_packed, slots = call(
+        functools.partial(pack_weights_kernel, *layout),
+        (f32(groups * block_rows, SEG), jax.ShapeDtypeStruct((chunks, SEG), jnp.int32)),
+        [ints, ints, ints, vmem(chunks, SEG), vmem(rows, SEG), ints,
+         pltpu.SMEM((chunks, SEG), jnp.int32), pltpu.SemaphoreType.DMA((5,)),
          pltpu.SemaphoreType.DMA],
-        [hbm] * 9,
+        [hbm] * 5,
         limit=PACK_BYTES,
     )(
         obs_owner.reshape(chunks, SEG), cell_key.reshape(chunks, SEG),
-        stencil.reshape(chunks, SEG), interp.reshape(chunks, SEG),
-        obs_weight, innovation, coef_y[0], c0, cx,
+        stencil.reshape(chunks, SEG), interp.reshape(chunks, SEG), obs_weight,
     )
+    v_packed, first, last, *cy_parts = call(
+        functools.partial(pack_products_kernel, groups, cap),
+        (f32(groups * cap, SEG), f32(F + 1, nx, SEG), f32(F + 1, nx, SEG))
+        + (f32(LX, ext),) * spans,
+        [vmem(rows, SEG), vmem(rows, SEG), vmem(*coef_y.shape[1:]),
+         pltpu.SemaphoreType.DMA((7,))],
+        [scalars] + [hbm] * 5,
+        work=20_000_000,
+        limit=PACK_BYTES,
+    )(slots, obs_weight, innovation, coef_y[0], c0, cx)
     w_arrived = lax.all_to_all(w_packed, "py", split_axis=0, concat_axis=0, tiled=True)
 
     steps = [(i, i + 1) for i in range(spans - 1)]
@@ -421,20 +451,17 @@
         functools.partial(products_kernel, *layout),
         (f32(F, LX, ext),) * spans,
         [vmem(ROWS, 2 * SEG), vmem(1, ROWS, SEG)],
-        [local, local, any_space],
         work=10_000_000,
-    )(w_arrived, v_arrived, side_parts[0])
+    )(w_arrived, v_arrived)
     sum_parts = partners(sum_parts)
 
     r, q, qq, dots = call(
         functools.partial(solve_kernel, spans),
-        (f32(F, nx, width),) * 3 + (f32(spans, 8, SEG),),
+        (f32(F, nx, width),) * 3 + (f32(groups * spans, 1, SEG),),
         [vmem(3, F, nx, ext), vmem(3 * F, nx, ext), vmem(nx, ext)],
         work=20_000_000,
     )(c0_ext, cx_ext, cy_ext, u_ext, *side_parts, *sum_parts)
-    dots = lax.all_to_all(dots, "px", split_axis=0, concat_axis=0, tiled=True)
-    dots = jnp.broadcast_to(jnp.sum(dots, axis=0), (groups, 8, SEG))
-    dots = lax.all_to_all(dots, "py", split_axis=0, concat_axis=0, tiled=True)
+    dots = lax.all_to_all(dots, ("px", "py"), split_axis=0, concat_axis=0, tiled=True)
     control, residual = call(finish_kernel, (f32(F, nx, width),) * 2)(dots, c0, r, q, qq)
     return control[:, None], residual[:, None]
 

time: 137 us -> 124 us (0.905)
  blocking collectives: 64.1 us -> 10.4 us
  waiting for transfers between devices: 21.6 us -> 55.1 us
  starting transfers between devices: 14.8 us -> 22 us
    all_to_all x3 -> x1, blocking collectives: 64.1 us -> 10.4 us  [shards(): lax.all_to_all(dots, ('px', 'py'), split_axis=0, concat_axis=0, tiled=True)]
    all_to_all x0 -> x1, waiting for transfers between devices: none -> 30.9 us  [shards(): lax.all_to_all(w_packed, 'py', split_axis=0, concat_axis=0, tiled=True)]
    all_to_all x0 -> x1, starting transfers between devices: none -> 7.26 us  [shards(): lax.all_to_all(w_packed, 'py', split_axis=0, concat_axis=0, tiled=True)]
    pallas_call x1 -> x2, Pallas kernels: 8.48 us -> 13.1 us  [the longest x1 6.79 us: shards(): call(functools.partial(pack_products_kernel, groups, cap), (f32(groups *...]
    all_to_all x1, waiting for transfers between devices: 13.4 us -> 15.9 us  [shards(): lax.all_to_all(v_packed, 'py', split_axis=0, concat_axis=0, tiled=True)]
    pallas_call x1, Pallas kernels: 5.17 us -> 3.07 us  [shards(): call(functools.partial(products_kernel, *layout), (f32(F, LX, ext),) * sp...]
    pallas_call x1, Pallas kernels: 6.83 us -> 5.24 us  [shards(): call(functools.partial(weights_kernel, *layout), (f32(2 * F, LX, ext),) *...]
  transfers between devices with their start and end apart: 12 -> 13, of which waited for: 5 -> 6; matrix products, arithmetic and copies ran while one was open for 0% -> 0% of each run, Pallas kernels for 10% -> 13%
where the time goes in v3:
time: 124 us; the launch traced here: 123 us
  waiting for transfers between devices  55.1 us (44%)
  Pallas kernels  33.4 us (27%)
  starting transfers between devices  22 us (18%)
  blocking collectives  10.4 us (8%)
  local copies, waits for them, and re-layouts  1.62 us (1%)
    all_to_all x1, waiting for transfers between devices, shards(): lax.all_to_all(w_packed, 'py', split_axis=0, concat_axis=0, tiled=True)  30.9 us
    all_to_all x1, waiting for transfers between devices, shards(): lax.all_to_all(v_packed, 'py', split_axis=0, concat_axis=0, tiled=True)  15.9 us
    all_to_all x1, blocking collectives, shards(): lax.all_to_all(dots, ('px', 'py'), split_axis=0, concat_axis=0, tiled=True)  10.4 us
    pallas_call x1, Pallas kernels, shards(): call(functools.partial(solve_kernel, spans), (f32(F, nx, width),) * 3 + (...  9.52 us
    ppermute x9, waiting for transfers between devices, partners(): lax.ppermute(parts[k], 'px', moves[k])  8.29 us
    ppermute x9, starting transfers between devices, partners(): lax.ppermute(parts[k], 'px', moves[k])  8.21 us
    all_to_all x1, starting transfers between devices, shards(): lax.all_to_all(w_packed, 'py', split_axis=0, concat_axis=0, tiled=True)  7.26 us
    pallas_call x1, Pallas kernels, shards(): call(functools.partial(pack_products_kernel, groups, cap), (f32(groups *...  6.79 us
  transfers between devices with their start and end apart: 13, of which 6 were waited for; matrix products, arithmetic and copies ran while one was open for 0% of the time, Pallas kernels for 13%

profile of v3, /device:TPU:0, one launch (start us, length us, event | category | flops | bytes accessed | tf_op | source)
XLA Modules:
  0.0 123.4 jit_solution(3259514941576991803)
XLA Ops:
  0.6 6.3 %shard_map.104 = (f32[3136,128]{1,0:T(8,128)}, s32[8,128]{1,0:T(8,128)}) custom-call(s32[8,128]{1,0:T(8,128)} %bitcast.28, s32[8,128]{1,0:T(8,128)} %bitcast.29, s32[8,128]{1,0:T(8,128)} %bitcast.30, f32[8,128]{1,0:T(8,128)} %bitcast.31, f32[1024,128]{1,0:T(8,128)} %w_hbm.3), custom_call_target="tpu_custom_call" | custom-call | tf_op jit(solution)/shard_map/pallas_call | solution.py:407
  6.9 7.3 %all-to-all-start = ((f32[8,392,128]{2,1,0:T(8,128)}), f32[8,392,128]{2,1,0:T(8,128)S(1)}, u32[]{:S(2)}, u32[]{:S(2)}) async-start(f32[8,392,128]{2,1,0:T(8,128)} %bitcast.25), calls=%async_computation | async-start | bytes 3211264 | tf_op jit(solution)/shard_map/all_to_all | solution.py:429
  14.2 6.8 %shard_map.105 = (f32[3072,128]{1,0:T(8,128)}, f32[3,64,128]{2,1,0:T(8,128)}, f32[3,64,128]{2,1,0:T(8,128)}, f32[16,640]{1,0:T(8,128)}, f32[16,640]{1,0:T(8,128)}, /*index=5*/f32[16,640]{1,0:T(8,128)}, f32[16,640]{1,0:T(8,128)}) custom-call(s32[8,128]{1,0:T(8,128)} %get-tuple-element.31.slot_ref, f32[1024,128]{1,0:T(8,128)} %w_hbm.3, f32[1024,128]{1,0:T(8,128)} %d_hbm.1, ...), custom_call_target="tpu_custom_call" | custom-call | flops 20000000 | bytes 20000000 | tf_op jit(solution)/shard_map/pallas_call | solution.py:419
  21.0 30.9 %all-to-all-done = f32[8,392,128]{2,1,0:T(8,128)S(1)} async-done(((f32[8,392,128]{2,1,0:T(8,128)}), f32[8,392,128]{2,1,0:T(8,128)S(1)}, u32[]{:S(2)}, u32[]{:S(2)}) %all-to-all-start) | async-done | bytes 1605664 | tf_op jit(solution)/shard_map/all_to_all | solution.py:429
  51.9 3.6 %all-to-all-start.1 = ((f32[8,384,128]{2,1,0:T(8,128)}), f32[8,384,128]{2,1,0:T(8,128)S(1)}, u32[]{:S(2)}, u32[]{:S(2)}) async-start(f32[8,384,128]{2,1,0:T(8,128)} %bitcast.26), calls=%async_computation.1 | async-start | bytes 3145728 | tf_op jit(solution)/shard_map/all_to_all | solution.py:441
  55.5 1.6 %collective-permute-start = (f32[3,64,128]{2,1,0:T(8,128)}, f32[3,64,128]{2,1,0:T(8,128)S(1)}, u32[]{:S(2)}, u32[]{:S(2)}) collective-permute-start(f32[3,64,128]{2,1,0:T(8,128)} %get-tuple-element.32), channel_id=1, source_target_pairs={{0,8},{8,16},{16,24},{1,9},{9,17},{17,25},{2,10},{10,18},{18,26},{... | collective-permute-start | bytes 294920 | tf_op jit(solution)/shard_map/ppermute | solution.py:432
  57.2 1.3 %collective-permute-start.1 = (f32[3,64,128]{2,1,0:T(8,128)}, f32[3,64,128]{2,1,0:T(8,128)S(1)}, u32[]{:S(2)}, u32[]{:S(2)}) collective-permute-start(f32[3,64,128]{2,1,0:T(8,128)} %get-tuple-element.33), channel_id=1, source_target_pairs={{8,0},{16,8},{24,16},{9,1},{17,9},{25,17},{10,2},{18,10},{26,18},{... | collective-permute-start | bytes 294920 | tf_op jit(solution)/shard_map/ppermute | solution.py:433
  58.5 2.6 %collective-permute-start.2 = (f32[16,640]{1,0:T(8,128)}, f32[16,640]{1,0:T(8,128)S(1)}, u32[]{:S(2)}, u32[]{:S(2)}) collective-permute-start(f32[16,640]{1,0:T(8,128)} %get-tuple-element.35), channel_id=1, source_target_pairs={{0,8},{8,0},{16,24},{24,16},{1,9},{9,1},{17,25},{25,17},{2,10},{10... | collective-permute-start | bytes 122888 | tf_op jit(solution)/shard_map/ppermute | solution.py:405
  61.1 1.7 %collective-permute-start.3 = (f32[16,640]{1,0:T(8,128)}, f32[16,640]{1,0:T(8,128)S(1)}, u32[]{:S(2)}, u32[]{:S(2)}) collective-permute-start(f32[16,640]{1,0:T(8,128)} %get-tuple-element.36), channel_id=1, source_target_pairs={{0,16},{8,24},{16,0},{24,8},{1,17},{9,25},{17,1},{25,9},{2,18},{10... | collective-permute-start | bytes 122888 | tf_op jit(solution)/shard_map/ppermute | solution.py:405
  62.8 3.7 %collective-permute-done.3.rest_2_ = f32[16,640]{1,0:T(8,128)S(1)} collective-permute-done((f32[16,640]{1,0:T(8,128)}, f32[16,640]{1,0:T(8,128)S(1)}, u32[]{:S(2)}, u32[]{:S(2)}) %collective-permute-start.3) | collective-permute-done | bytes 40992 | tf_op jit(solution)/shard_map/ppermute | solution.py:405
  66.7 0.9 copy-done.3
  67.6 1.3 %shard_map.106 = (f32[2,64,640]{2,1,0:T(8,128)S(1)}, f32[64,640]{1,0:T(8,128)S(1)}, f32[64,640]{1,0:T(8,128)S(1)}, f32[2,64,640]{2,1,0:T(8,128)S(1)}) custom-call(f32[2,64,512]{2,1,0:T(8,128)S(1)} %bitcast.21, f32[64,512]{1,0:T(8,128)S(1)} %bitcast.24, f32[3,64,128]{2,1,0:T(8,128)S(1)} %collective-permute-done.prev_ref, ...), custom_call_target="tpu_custom_call" | custom-call | flops 10000000 | bytes 10000000 | tf_op jit(solution)/shard_map/pallas_call | solution.py:434
  68.9 5.2 %shard_map.107 = (f32[4,16,640]{2,1,0:T(8,128)S(1)}, f32[4,16,640]{2,1,0:T(8,128)}, f32[4,16,640]{2,1,0:T(8,128)}, f32[4,16,640]{2,1,0:T(8,128)}) custom-call(f32[3136,128]{1,0:T(8,128)S(1)} %bitcast.17, f32[64,640]{1,0:T(8,128)S(1)} %get-tuple-element.39.tie_ref.cx_ref), custom_call_target="tpu_custom_call" | custom-call | flops 20000000 | bytes 20000000 | tf_op jit(solution)/shard_map/pallas_call | solution.py:442
  74.2 0.7 copy-done.10
  75.3 0.7 collective-permute-start.6
  76.0 0.7 collective-permute-start.7
  76.8 15.9 %all-to-all-done.1 = f32[8,384,128]{2,1,0:T(8,128)S(1)} async-done(((f32[8,384,128]{2,1,0:T(8,128)}), f32[8,384,128]{2,1,0:T(8,128)S(1)}, u32[]{:S(2)}, u32[]{:S(2)}) %all-to-all-start.1) | async-done | bytes 1572896 | tf_op jit(solution)/shard_map/all_to_all | solution.py:441
  92.7 3.1 %shard_map.108 = (f32[2,16,640]{2,1,0:T(8,128)S(1)}, f32[2,16,640]{2,1,0:T(8,128)S(1)}, f32[2,16,640]{2,1,0:T(8,128)S(1)}, f32[2,16,640]{2,1,0:T(8,128)S(1)}) custom-call(f32[3136,128]{1,0:T(8,128)S(1)} %bitcast.18, f32[3072,128]{1,0:T(8,128)S(1)} %bitcast.19), custom_call_target="tpu_custom_call" | custom-call | flops 10000000 | bytes 10000000 | tf_op jit(solution)/shard_map/pallas_call | solution.py:450
  95.9 1.6 %collective-permute-start.9 = (f32[2,16,640]{2,1,0:T(8,128)S(1)}, f32[2,16,640]{2,1,0:T(8,128)S(1)}, u32[]{:S(2)}, u32[]{:S(2)}) collective-permute-start(f32[2,16,640]{2,1,0:T(8,128)S(1)} %get-tuple-element.52), channel_id=1, source_target_pairs={{0,16},{8,24},{16,0},{24,8},{1,17},{9,25},{17,1},{25,9},{2,18},{10... | collective-permute-start | bytes 245768 | tf_op jit(solution)/shard_map/ppermute | solution.py:405
  97.8 3.3 %collective-permute-done.9.rest_6_ = f32[2,16,640]{2,1,0:T(8,128)S(1)} collective-permute-done((f32[2,16,640]{2,1,0:T(8,128)S(1)}, f32[2,16,640]{2,1,0:T(8,128)S(1)}, u32[]{:S(2)}, u32[]{:S(2)}) %collective-permute-start.9) | collective-permute-done | bytes 81952 | tf_op jit(solution)/shard_map/ppermute | solution.py:405
  101.0 1.1 collective-permute-done.10.rest_7_
  102.2 9.5 %shard_map.109 = (f32[2,64,512]{2,1,0:T(8,128)S(1)}, f32[2,64,512]{2,1,0:T(8,128)S(1)}, f32[2,64,512]{2,1,0:T(8,128)S(1)}, f32[32,1,128]{2,1,0:T(1,128)S(1)}) custom-call(f32[2,64,640]{2,1,0:T(8,128)S(1)} %copy-done.5, f32[64,640]{1,0:T(8,128)S(1)} %copy-done.2, f32[64,640]{1,0:T(8,128)S(1)} %copy-done.9, f32[2,64,640]{2,1,0:T(8,128)S(1)} %copy-done.7, ...), custom_call_target="tpu_custom_call" | custom-call | flops 20000000 | bytes 20000000 | tf_op jit(solution)/shard_map/pallas_call | solution.py:458
  111.7 10.4 %all_to_all.28.dots_ref = f32[32,1,128]{2,1,0:T(1,128)S(1)} all-to-all(f32[32,1,128]{2,1,0:T(1,128)S(1)} %get-tuple-element.54), channel_id=1, replica_groups=mesh['px'=4,'py'=8] {'px','py'}, dimensions={0} | all-to-all | bytes 32768 | tf_op jit(solution)/shard_map/all_to_all | solution.py:464
  122.2 1.2 shard_map.110
  (38 shorter events, 1.1 us)
Async XLA Ops:
  6.9 45.0 %all-to-all-start = ((f32[8,392,128]{2,1,0:T(8,128)}), f32[8,392,128]{2,1,0:T(8,128)S(1)}, u32[]{:S(2)}, u32[]{:S(2)}) async-start(f32[8,392,128]{2,1,0:T(8,128)} %bitcast.25), calls=%async_computation | async-start | bytes 3211264 | tf_op jit(solution)/shard_map/all_to_all | solution.py:429
  21.0 41.8 %copy-start.13 = (f32[16,640]{1,0:T(8,128)S(1)}, f32[16,640]{1,0:T(8,128)}, u32[]{:S(2)}) copy-start(f32[16,640]{1,0:T(8,128)} %get-tuple-element.37) | copy-start | bytes 122884
  21.0 45.7 %copy-start = (f32[2,1,64,512]{3,2,1,0:T(8,128)S(1)}, f32[2,1,64,512]{3,2,1,0:T(8,128)}, u32[]{:S(2)}) copy-start(f32[2,1,64,512]{3,2,1,0:T(8,128)} %param.9) | copy-start | bytes 786436
  21.0 45.7 %copy-start.12 = (f32[16,640]{1,0:T(8,128)S(1)}, f32[16,640]{1,0:T(8,128)}, u32[]{:S(2)}) copy-start(f32[16,640]{1,0:T(8,128)} %get-tuple-element.34.rest_0_) | copy-start | bytes 122884
  51.9 40.8 %all-to-all-start.1 = ((f32[8,384,128]{2,1,0:T(8,128)}), f32[8,384,128]{2,1,0:T(8,128)S(1)}, u32[]{:S(2)}, u32[]{:S(2)}) async-start(f32[8,384,128]{2,1,0:T(8,128)} %bitcast.26), calls=%async_computation.1 | async-start | bytes 3145728 | tf_op jit(solution)/shard_map/all_to_all | solution.py:441
  55.5 11.2 %collective-permute-start = (f32[3,64,128]{2,1,0:T(8,128)}, f32[3,64,128]{2,1,0:T(8,128)S(1)}, u32[]{:S(2)}, u32[]{:S(2)}) collective-permute-start(f32[3,64,128]{2,1,0:T(8,128)} %get-tuple-element.32), channel_id=1, source_target_pairs={{0,8},{8,16},{16,24},{1,9},{9,17},{17,25},{2,10},{10,18},{18,26},{... | collective-permute-start | bytes 294920 | tf_op jit(solution)/shard_map/ppermute | solution.py:432
  57.2 9.5 %collective-permute-start.1 = (f32[3,64,128]{2,1,0:T(8,128)}, f32[3,64,128]{2,1,0:T(8,128)S(1)}, u32[]{:S(2)}, u32[]{:S(2)}) collective-permute-start(f32[3,64,128]{2,1,0:T(8,128)} %get-tuple-element.33), channel_id=1, source_target_pairs={{8,0},{16,8},{24,16},{9,1},{17,9},{25,17},{10,2},{18,10},{26,18},{... | collective-permute-start | bytes 294920 | tf_op jit(solution)/shard_map/ppermute | solution.py:433
  58.5 4.4 %collective-permute-start.2 = (f32[16,640]{1,0:T(8,128)}, f32[16,640]{1,0:T(8,128)S(1)}, u32[]{:S(2)}, u32[]{:S(2)}) collective-permute-start(f32[16,640]{1,0:T(8,128)} %get-tuple-element.35), channel_id=1, source_target_pairs={{0,8},{8,0},{16,24},{24,16},{1,9},{9,1},{17,25},{25,17},{2,10},{10... | collective-permute-start | bytes 122888 | tf_op jit(solution)/shard_map/ppermute | solution.py:405
  61.1 5.5 %collective-permute-start.3 = (f32[16,640]{1,0:T(8,128)}, f32[16,640]{1,0:T(8,128)S(1)}, u32[]{:S(2)}, u32[]{:S(2)}) collective-permute-start(f32[16,640]{1,0:T(8,128)} %get-tuple-element.36), channel_id=1, source_target_pairs={{0,16},{8,24},{16,0},{24,8},{1,17},{9,25},{17,1},{25,9},{2,18},{10... | collective-permute-start | bytes 122888 | tf_op jit(solution)/shard_map/ppermute | solution.py:405
  62.8 3.9 %collective-permute-start.4 = (f32[16,640]{1,0:T(8,128)S(1)}, f32[16,640]{1,0:T(8,128)S(1)}, u32[]{:S(2)}, u32[]{:S(2)}) collective-permute-start(f32[16,640]{1,0:T(8,128)S(1)} %copy-done.13), channel_id=1, source_target_pairs={{0,24},{8,16},{16,8},{24,0},{1,25},{9,17},{17,9},{25,1},{2,26},{10... | collective-permute-start | bytes 122888 | tf_op jit(solution)/shard_map/ppermute | solution.py:405
  68.9 7.2 %copy-start.1 = (f32[64,640]{1,0:T(8,128)}, f32[64,640]{1,0:T(8,128)S(1)}, u32[]{:S(2)}) copy-start(f32[64,640]{1,0:T(8,128)S(1)} %get-tuple-element.39.tie_ref.cx_ref) | copy-start | bytes 491524
  68.9 7.1 %copy-start.4 = (f32[2,64,640]{2,1,0:T(8,128)}, f32[2,64,640]{2,1,0:T(8,128)S(1)}, u32[]{:S(2)}) copy-start(f32[2,64,640]{2,1,0:T(8,128)S(1)} %get-tuple-element.38.c0_ref) | copy-start | bytes 983044
  68.9 7.1 %copy-start.6 = (f32[2,64,640]{2,1,0:T(8,128)}, f32[2,64,640]{2,1,0:T(8,128)S(1)}, u32[]{:S(2)}) copy-start(f32[2,64,640]{2,1,0:T(8,128)S(1)} %get-tuple-element.41.u_ref) | copy-start | bytes 983044
  74.8 22.6 %collective-permute-start.5 = (f32[4,16,640]{2,1,0:T(8,128)}, f32[4,16,640]{2,1,0:T(8,128)}, u32[]{:S(2)}, u32[]{:S(2)}) collective-permute-start(f32[4,16,640]{2,1,0:T(8,128)} %get-tuple-element.46), channel_id=1, source_target_pairs={{0,8},{8,0},{16,24},{24,16},{1,9},{9,1},{17,25},{25,17},{2,10},{10... | collective-permute-start | bytes 491528 | tf_op jit(solution)/shard_map/ppermute | solution.py:405
  75.3 22.4 %collective-permute-start.6 = (f32[4,16,640]{2,1,0:T(8,128)}, f32[4,16,640]{2,1,0:T(8,128)}, u32[]{:S(2)}, u32[]{:S(2)}) collective-permute-start(f32[4,16,640]{2,1,0:T(8,128)} %get-tuple-element.47), channel_id=1, source_target_pairs={{0,16},{8,24},{16,0},{24,8},{1,17},{9,25},{17,1},{25,9},{2,18},{10... | collective-permute-start | bytes 491528 | tf_op jit(solution)/shard_map/ppermute | solution.py:405
  76.0 21.7 %collective-permute-start.7 = (f32[4,16,640]{2,1,0:T(8,128)}, f32[4,16,640]{2,1,0:T(8,128)}, u32[]{:S(2)}, u32[]{:S(2)}) collective-permute-start(f32[4,16,640]{2,1,0:T(8,128)} %get-tuple-element.48), channel_id=1, source_target_pairs={{0,24},{8,16},{16,8},{24,0},{1,25},{9,17},{17,9},{25,1},{2,26},{10... | collective-permute-start | bytes 491528 | tf_op jit(solution)/shard_map/ppermute | solution.py:405
  92.7 9.5 %copy-start.2 = (f32[64,640]{1,0:T(8,128)S(1)}, f32[64,640]{1,0:T(8,128)}, u32[]{:S(2)}) copy-start(f32[64,640]{1,0:T(8,128)} %copy-done.1) | copy-start | bytes 491524
  92.7 9.5 %copy-start.5 = (f32[2,64,640]{2,1,0:T(8,128)S(1)}, f32[2,64,640]{2,1,0:T(8,128)}, u32[]{:S(2)}) copy-start(f32[2,64,640]{2,1,0:T(8,128)} %copy-done.4) | copy-start | bytes 983044
  92.7 9.5 %copy-start.7 = (f32[2,64,640]{2,1,0:T(8,128)S(1)}, f32[2,64,640]{2,1,0:T(8,128)}, u32[]{:S(2)}) copy-start(f32[2,64,640]{2,1,0:T(8,128)} %copy-done.6) | copy-start | bytes 983044
  92.7 9.5 %copy-start.9 = (f32[64,640]{1,0:T(8,128)S(1)}, f32[64,640]{1,0:T(8,128)}, u32[]{:S(2)}) copy-start(f32[64,640]{1,0:T(8,128)} %copy-done.8) | copy-start | bytes 491524
  92.7 9.5 %copy-start.11 = (f32[4,16,640]{2,1,0:T(8,128)S(1)}, f32[4,16,640]{2,1,0:T(8,128)}, u32[]{:S(2)}) copy-start(f32[4,16,640]{2,1,0:T(8,128)} %copy-done.10) | copy-start | bytes 491524
  95.8 2.0 %collective-permute-start.8 = (f32[2,16,640]{2,1,0:T(8,128)S(1)}, f32[2,16,640]{2,1,0:T(8,128)S(1)}, u32[]{:S(2)}, u32[]{:S(2)}) collective-permute-start(f32[2,16,640]{2,1,0:T(8,128)S(1)} %get-tuple-element.51), channel_id=1, source_target_pairs={{0,8},{8,0},{16,24},{24,16},{1,9},{9,1},{17,25},{25,17},{2,10},{10... | collective-permute-start | bytes 245768 | tf_op jit(solution)/shard_map/ppermute | solution.py:405
  95.9 5.2 %collective-permute-start.9 = (f32[2,16,640]{2,1,0:T(8,128)S(1)}, f32[2,16,640]{2,1,0:T(8,128)S(1)}, u32[]{:S(2)}, u32[]{:S(2)}) collective-permute-start(f32[2,16,640]{2,1,0:T(8,128)S(1)} %get-tuple-element.52), channel_id=1, source_target_pairs={{0,16},{8,24},{16,0},{24,8},{1,17},{9,25},{17,1},{25,9},{2,18},{10... | collective-permute-start | bytes 245768 | tf_op jit(solution)/shard_map/ppermute | solution.py:405
  97.5 4.7 %collective-permute-start.10 = (f32[2,16,640]{2,1,0:T(8,128)S(1)}, f32[2,16,640]{2,1,0:T(8,128)S(1)}, u32[]{:S(2)}, u32[]{:S(2)}) collective-permute-start(f32[2,16,640]{2,1,0:T(8,128)S(1)} %get-tuple-element.53), channel_id=1, source_target_pairs={{0,24},{8,16},{16,8},{24,0},{1,25},{9,17},{17,9},{25,1},{2,26},{10... | collective-permute-start | bytes 245768 | tf_op jit(solution)/shard_map/ppermute | solution.py:405
  (3 other events, 8.7 us)

commit v4 on v3

v4 whole, which is shorter than its diff:
```python
import functools

import jax
import jax.numpy as jnp
from jax import lax
from jax.experimental import pallas as pl
from jax.experimental.pallas import tpu as pltpu
from jax.sharding import PartitionSpec as P

F = 2
SEG = 128
M = 4
NB = 16
LX = 16
ROWS = F * NB * LX
HALF = SEG // 2
SPLIT = 16
X_WIDTH = 256
Y_LINES = 16
VMEM_BYTES = 32 * 1024 * 1024
PACK_BYTES = 60 * 1024 * 1024


def iota(shape, axis):
    return lax.broadcasted_iota(jnp.int32, shape, axis)


def flag(condition, kind=jnp.bfloat16):
    return jnp.where(condition, 1.0, 0.0).astype(kind)


def mxu(left, right):
    return jnp.dot(left, right, preferred_element_type=jnp.float32)


def split_parts(values, count):
    parts = []
    for _ in range(count):
        part = values.astype(jnp.bfloat16)
        parts.append(part)
        values = values - part.astype(jnp.float32)
    return parts


def ends_tile(before, after):
    return jnp.where(iota(after.shape, after.ndim - 1) < HALF, after, before)


def sweep(values, coeffs, axis):
    size = values.shape[axis]
    for _ in range(M):
        flux = coeffs * (pltpu.roll(values, size - 1, axis) - values)
        values = values + flux - pltpu.roll(flux, 1, axis)
    return values


def start_copies(pairs, sems):
    copies = [pltpu.make_async_copy(*pair, sems.at[i]) for i, pair in enumerate(pairs)]
    for copy in copies:
        copy.start()
    return copies


def pack_weights_kernel(groups, cap, blk, block_rows, own_hbm, key_hbm, sten_hbm, itp_hbm, w_hbm,
                        *rest):
    half = groups // 2
    outs, rest = rest[:half], rest[half:]
    (slot_out, own_ref, key_ref, sten_ref, itp_ref, w_ref, buffer, slot_v, slot_s, sems, out_sems,
     sem) = rest
    loads = start_copies([(own_hbm, own_ref), (key_hbm, key_ref), (sten_hbm, sten_ref),
                          (itp_hbm, itp_ref), (w_hbm, w_ref)], sems)

    def clear(k, carry):
        start = pl.multiple_of(k * block_rows, 8)
        buffer[pl.ds(start, block_rows), :] = jnp.zeros((block_rows, SEG), jnp.float32)
        return carry

    lax.fori_loop(0, half, clear, 0)

    for load in loads[:4]:
        load.wait()
    chunks = own_ref.shape[0]
    nb = cap // blk
    own = own_ref[...]
    high = groups * chunks
    shift = chunks.bit_length() - 1
    masks = [flag(own == o, jnp.float32) for o in range(groups)]
    hits = jnp.concatenate(masks, axis=0).astype(jnp.bfloat16)
    square = (SEG, SEG)
    within = mxu(hits, flag(iota(square, 0) < iota(square, 1)))
    tallies = mxu(hits, jnp.ones(square, jnp.bfloat16)).astype(jnp.bfloat16)
    line, column = iota((high, high), 0), iota((high, high), 1)
    same = (line >> shift) == (column >> shift)
    ranks = within + mxu(flag(same & (column < line)), tallies)
    rank = sum(masks[o] * ranks[o * chunks:(o + 1) * chunks] for o in range(groups))
    rank = rank.astype(jnp.int32)
    relative = own ^ lax.axis_index("py")
    block, across = relative & (half - 1), relative >> (half.bit_length() - 1)
    slot_v[...] = block * block_rows + across * cap + rank
    slot_out[...] = (block * 2 + across) * cap + rank
    copy = pltpu.make_async_copy(slot_v, slot_s, sem)
    copy.start()

    log = blk.bit_length() - 1
    place = relative * nb + (rank >> log)
    lane = rank & (blk - 1)
    key, sten, itp = key_ref[...], sten_ref[...], itp_ref[...]
    tall = groups * nb
    meta = jnp.zeros((5 * tall, SEG), jnp.float32)
    for i in range(chunks):
        chosen = iota((tall, SEG), 0) == place[i:i + 1]
        parts = split_parts(itp[i:i + 1], 3)
        parts += [key[i:i + 1].astype(jnp.bfloat16), (sten[i:i + 1] + 1).astype(jnp.bfloat16)]
        left = [jnp.where(chosen, part.astype(jnp.float32), 0.0) for part in parts]
        right = flag(iota(square, 0) == lane[i:i + 1])
        meta = meta + lax.dot_general(
            jnp.concatenate(left, axis=0).astype(jnp.bfloat16), right,
            (((1,), (1,)), ((), ())), preferred_element_type=jnp.float32)
    shares = meta[:tall] + meta[tall:2 * tall] + meta[2 * tall:3 * tall]
    targets = meta[3 * tall:4 * tall] * LX + meta[4 * tall:]
    for v in range(groups):
        base = (v % half) * block_rows + 2 * cap + (v // half) * 2 * nb
        buffer[base:base + nb, :] = shares[v * nb:(v + 1) * nb]
        buffer[base + nb:base + 2 * nb, :] = targets[v * nb:(v + 1) * nb]

    copy.wait()
    loads[4].wait()

    def place_rows(g, carry):
        weights = w_ref[pl.ds(pl.multiple_of(g * 8, 8), 8), :]
        line, lane = g // 16, (g % 16) * 8
        for i in range(8):
            buffer[pl.ds(slot_s[line, lane + i], 1), :] = weights[i:i + 1]
        return carry

    lax.fori_loop(0, w_ref.shape[0] // 8, place_rows, 0)
    for store in start_copies([(buffer.at[pl.ds(k * block_rows, block_rows)], out)
                               for k, out in enumerate(outs)], out_sems):
        store.wait()


def pack_products_kernel(groups, cap, slot_ref, w_hbm, d_hbm, cy_hbm, c0_hbm, cx_hbm, *rest):
    half = groups // 2
    outs, (swap_out, w_ref, d_ref, cy_ref, first, last, buffer, sems, out_sems) = (
        rest[:half], rest[half:])
    width = c0_hbm.shape[2]
    loads = start_copies([
        (w_hbm, w_ref), (d_hbm, d_ref), (cy_hbm, cy_ref),
        (c0_hbm.at[:, :, pl.ds(0, SEG)], first.at[pl.ds(0, F)]),
        (cx_hbm.at[:, pl.ds(0, SEG)], first.at[F]),
        (c0_hbm.at[:, :, pl.ds(width - SEG, SEG)], last.at[pl.ds(0, F)]),
        (cx_hbm.at[:, pl.ds(width - SEG, SEG)], last.at[F]),
    ], sems)

    def clear(o, carry):
        start = pl.multiple_of(o * cap, 8)
        buffer[pl.ds(start, cap), :] = jnp.zeros((cap, SEG), jnp.float32)
        return carry

    lax.fori_loop(0, groups, clear, 0)

    for load in loads:
        load.wait()

    def place_rows(g, carry):
        start = pl.multiple_of(g * 8, 8)
        products = w_ref[pl.ds(start, 8), :] * d_ref[pl.ds(start, 8), :]
        line, lane = g // 16, (g % 16) * 8
        for i in range(8):
            buffer[pl.ds(slot_ref[line, lane + i], 1), :] = products[i:i + 1]
        return carry

    lax.fori_loop(0, w_ref.shape[0] // 8, place_rows, 0)
    stores = start_copies([(buffer.at[pl.ds(k * 2 * cap, 2 * cap)], out)
                           for k, out in enumerate(outs)], out_sems)
    columns = cy_ref.shape[1]
    cy = cy_ref[...]
    cy = jnp.where(iota(cy.shape, 1) == columns - 1, 0.0, cy)
    empty = jnp.zeros((LX, SEG), jnp.float32)
    me = lax.axis_index("px")
    nx = first.shape[1]
    for q in range(columns // width):
        low, top = q * width, (q + 1) * width
        tiles = [cy[:, t:t + SEG] for t in range(low, top, SEG)]
        before = cy[:, low - SEG:low] if low > 0 else empty
        after = cy[:, top:top + SEG] if top < columns else empty
        tiles.append(ends_tile(before, after))
        for t, tile in enumerate(tiles):
            swap_out[q, t * LX:(t + 1) * LX, :] = tile
        base = len(tiles) * LX
        for i in range(F + 1):
            swap_out[q, base + i * nx:base + (i + 1) * nx, :] = jnp.where(
                q < me, first[i], last[i])
    for store in stores:
        store.wait()


def sum_rows(cap, blk, metas, acc_ref, terms):
    nb = cap // blk
    numbers = 1.0 + iota((ROWS, cap), 0).astype(jnp.float32)
    for source, meta in enumerate(metas):
        upper = jnp.concatenate(
            [jnp.broadcast_to(meta[i:i + 1], (SEG, SEG)).T[:blk] for i in range(nb)], axis=0)
        target = jnp.concatenate([meta[nb + i:nb + i + 1, :blk] for i in range(nb)], axis=1)
        hit = flag(numbers == target)
        values = jnp.concatenate(terms(source, upper), axis=1)
        part = mxu(jnp.concatenate([hit, hit], axis=1),
                   jnp.concatenate(split_parts(values, 2), axis=0))
        if source:
            acc_ref[...] += part
        else:
            acc_ref[...] = part


def cut_part(rows_ref, to, f, q, spans):
    width = to.shape[1] - SEG
    per = width // SEG

    def tile(b):
        start = pl.multiple_of((f * NB + b) * LX, LX)
        return rows_ref[pl.ds(start, LX), :]

    for j in range(per):
        to[:, j * SEG:(j + 1) * SEG] = tile(q * per + j)
    before = tile(jnp.maximum(q * per - 1, 0))
    after = tile(jnp.minimum(q * per + per, NB - 1))
    to[:, width:] = ends_tile(jnp.where(q > 0, before, 0.0),
                              jnp.where(q < spans - 1, after, 0.0))


def weights_kernel(half, cap, blk, across, *rest):
    w_refs, (_, meta_out, out, acc_ref) = rest[:half], rest[half:]
    nb = cap // blk
    for k, w_ref in enumerate(w_refs):
        meta_out[k] = w_ref[2 * cap:, :]
    rows = slice(across * cap, (across + 1) * cap)

    def terms(source, upper):
        lower = 1.0 - upper
        weights = w_refs[source][rows, :]
        lower_w, upper_w = lower * weights, upper * weights
        return [lower * lower_w, upper * lower_w, upper * upper_w]

    low = 2 * cap + across * 2 * nb
    sum_rows(cap, blk, [w_ref[low:low + 2 * nb, :] for w_ref in w_refs], acc_ref, terms)
    out[0] = acc_ref[:, :SEG] + pltpu.roll(acc_ref[:, 2 * SEG:], 1, 0)
    out[1] = acc_ref[:, SEG:2 * SEG]


def sum_products(half, cap, blk, across, meta_ref, v_refs, acc_ref, sums_ref):
    nb = cap // blk
    rows = slice(across * cap, (across + 1) * cap)

    def terms(source, upper):
        products = v_refs[source][rows, :]
        return [(1.0 - upper) * products, upper * products]

    low = across * 2 * nb
    sum_rows(cap, blk, [meta_ref[k, low:low + 2 * nb, :] for k in range(half)], acc_ref, terms)
    sums_ref[...] = acc_ref[:, :SEG] + pltpu.roll(acc_ref[:, SEG:], 1, 0)


def products_across_kernel(half, cap, blk, meta_ref, *rest):
    v_refs, (*outs, acc_ref, sums_ref) = rest[:half], rest[half:]
    sum_products(half, cap, blk, 1, meta_ref, v_refs, acc_ref, sums_ref)
    me = lax.axis_index("px")
    for k, out in enumerate(outs):
        for f in range(F):
            cut_part(sums_ref, out.at[f], f, me ^ k, len(outs))


def products_kernel(half, cap, blk, meta_ref, side_ref, other_ref, *rest):
    v_refs, (out, acc_ref, sums_ref, side) = rest[:half], rest[half:]
    spans = out.shape[0]
    sum_products(half, cap, blk, 0, meta_ref, v_refs, acc_ref, sums_ref)
    side[...] = side_ref[...] + other_ref[...]
    for q in range(spans):
        for channel, rows_ref in enumerate((side.at[0], side.at[1], sums_ref)):
            for f in range(F):
                cut_part(rows_ref, out.at[q, channel * F + f], f, q, spans)


def sweep_x_into(to_ref, from_ref, cx_ref, plus_ref=None, sign=1.0):
    size = cx_ref.shape[1]
    for low in range(0, size, X_WIDTH):
        tile = slice(low, min(low + X_WIDTH, size))
        values = sweep(from_ref[:, tile], cx_ref[:, tile], 0)
        if plus_ref is not None:
            values = values + sign * plus_ref[:, tile]
        to_ref[:, tile] = values


def sweep_y_into(to_ref, from_ref, cy_ref):
    for low in range(0, cy_ref.shape[0], Y_LINES):
        lines = slice(low, low + Y_LINES)
        to_ref[lines, :] = sweep(from_ref[lines, :], cy_ref[lines, :], 1)


def start_kernel(c0_ref, cx_ref, swap_ref, c0_out, cx_out, cy_out, u_out):
    width = c0_ref.shape[2]
    nx = cx_ref.shape[0]
    spans, count = swap_ref.shape[0], cy_out.shape[1] // SEG
    me = lax.axis_index("px")
    for p in range(spans):
        for t in range(count):
            cy_out[p * LX:(p + 1) * LX, t * SEG:(t + 1) * SEG] = (
                swap_ref[p, t * LX:(t + 1) * LX, :])

    def beside(i):
        lines = slice(count * LX + i * nx, count * LX + (i + 1) * nx)
        before = swap_ref[jnp.maximum(me - 1, 0), lines, :]
        after = swap_ref[jnp.minimum(me + 1, spans - 1), lines, :]
        return ends_tile(jnp.where(me > 0, before, 0.0), jnp.where(me < spans - 1, after, 0.0))

    last = cx_ref.shape[0] - 1
    cx_out[:, :width] = cx_ref[...]
    cx_out[:, width:] = beside(F)
    cx_out[last:, :] = jnp.zeros((1, width + SEG), jnp.float32)
    for f in range(F):
        c0_out[f, :, :width] = c0_ref[f]
        c0_out[f, :, width:] = beside(f)
        sweep_x_into(u_out.at[f], c0_out.at[f], cx_out)
        sweep_y_into(u_out.at[f], u_out.at[f], cy_out)


def solve_kernel(spans, c0_ref, cx_ref, cy_ref, u_ref, obs_ref, *rest):
    sum_refs, (r_out, q_out, h_out, dots_out, vec, coef, work) = rest[:spans], rest[spans:]
    width = r_out.shape[2]
    for p in range(spans):
        for channel in range(3 * F):
            coef[channel, p * LX:(p + 1) * LX, :] = obs_ref[p, channel]
    me = lax.axis_index("px")
    for k in range(spans):
        rows = pl.ds(pl.multiple_of((me ^ k) * LX, LX), LX)
        for f in range(F):
            coef[2 * F + f, rows, :] += sum_refs[k][f]

    def normal(f, values, tile):
        size = values.shape[0]
        side = coef[F + f, :, tile]
        return (coef[f, :, tile] * values + side * pltpu.roll(values, size - 1, 0)
                + pltpu.roll(side * values, 1, 0))

    tiles = [slice(low, low + SEG) for low in range(0, width + SEG, SEG)]

    def first(f, carry):
        for tile in tiles:
            work[:, tile] = coef[2 * F + f, :, tile] - normal(f, u_ref[f, :, tile], tile)
        sweep_y_into(work, work, cy_ref)
        sweep_x_into(vec.at[0, f], work, cx_ref, c0_ref.at[f], -1.0)
        return carry

    lax.fori_loop(0, F, first, 0)

    def apply(f, carry):
        sweep_x_into(work, vec.at[0, f], cx_ref)
        sweep_y_into(work, work, cy_ref)
        for tile in tiles:
            work[:, tile] = normal(f, work[:, tile], tile)
        sweep_y_into(work, work, cy_ref)
        sweep_x_into(vec.at[1, f], work, cx_ref, vec.at[0, f])
        sweep_x_into(vec.at[2, f], vec.at[1, f], cx_ref)
        sweep_y_into(vec.at[2, f], vec.at[2, f], cy_ref)
        for tile in tiles:
            h_out[f, :, tile] = normal(f, vec[2, f, :, tile], tile)
        return carry

    lax.fori_loop(0, F, apply, 0)

    sums = [jnp.zeros((8, SEG), jnp.float32) for _ in range(4)]
    for f in range(F):
        r_out[f] = vec[0, f, :, :width]
        q_out[f] = vec[1, f, :, :width]
        for low in range(0, vec.shape[2], 8):
            for tile in tiles[:-1]:
                r = vec[0, f, low:low + 8, tile]
                q = vec[1, f, low:low + 8, tile]
                s = vec[2, f, low:low + 8, tile]
                for i, product in enumerate((r * r, r * q, q * q, s * h_out[f, low:low + 8, tile])):
                    sums[i] = sums[i] + product
    dots = jnp.zeros((1, SEG), jnp.float32)
    for i, total in enumerate(sums):
        line = jnp.sum(total, axis=0, keepdims=True)
        for distance in (64, 32, 16):
            line = line + pltpu.roll(line, distance, 1)
        dots = jnp.where(iota((1, SEG), 1) // SPLIT == i, line, dots)
    dots_out[...] = jnp.broadcast_to(dots, dots_out.shape)


def last_kernel(h_ref, q_ref, cx_ref, cy_ref, qq_out, work, other):
    width = qq_out.shape[2]

    def apply(f, carry):
        sweep_y_into(work, h_ref.at[f], cy_ref)
        sweep_x_into(other, work, cx_ref)
        qq_out[f] = q_ref[f] + other[:, :width]
        return carry

    lax.fori_loop(0, F, apply, 0)


def finish_kernel(dots_ref, c0_ref, r_ref, q_ref, qq_ref, control_out, residual_out):
    dots = jnp.sum(dots_ref[...], axis=0)
    lane = iota((1, SEG), 1)
    rr, rq, qq2, energy = (pltpu.roll(dots, (SEG - i * SPLIT) % SEG, 1) for i in range(4))

    def total(line):
        return jnp.sum(jnp.where(lane < SPLIT, line, 0.0), axis=1, keepdims=True)

    rr_sum = total(rr)
    alpha = rr_sum / total(rq)
    new_sum = total(rr - 2.0 * alpha * rq + alpha * alpha * qq2)
    more = 1.0 + new_sum / rr_sum
    curve = total(more * more * rq - 2.0 * more * alpha * qq2 + alpha * alpha * (qq2 + energy))
    second = new_sum / curve
    first_weight = alpha + second * more
    both = alpha * second
    for f in range(F):
        r, q = r_ref[f], q_ref[f]
        control_out[f] = c0_ref[f] + first_weight * r - both * q
        residual_out[f] = r - first_weight * q + both * qq_ref[f]


def call(kernel, out_shape, scratch=(), in_specs=None, out_specs=None, limit=VMEM_BYTES):
    params = {"in_specs": in_specs, "out_specs": out_specs}
    return pl.pallas_call(
        kernel,
        out_shape=out_shape,
        scratch_shapes=list(scratch),
        compiler_params=pltpu.CompilerParams(vmem_limit_bytes=limit),
        **{name: value for name, value in params.items() if value is not None},
    )


def f32(*shape):
    return jax.ShapeDtypeStruct(shape, jnp.float32)


def vmem(*shape, kind=jnp.float32):
    return pltpu.VMEM(shape, kind)


def shards(
    control_start, coef_x, coef_y, innovation, obs_weight, interp, obs_owner, cell_key, stencil
):
    groups, spans = lax.axis_size("py"), lax.axis_size("px")
    half = groups // 2
    rows = innovation.shape[0]
    cap = 3 * rows // groups
    blk = SEG if cap % SEG == 0 else HALF
    meta_rows = -(-4 * (cap // blk) // 8) * 8
    block_rows = 2 * cap + meta_rows
    chunks = rows // SEG
    nx, width = control_start.shape[2], control_start.shape[3]
    ext = width + SEG
    c0, cx = control_start[:, 0], coef_x[0]
    hbm, any_space, local, scalars = (
        pl.BlockSpec(memory_space=s) for s in (pltpu.HBM, pl.ANY, pltpu.VMEM, pltpu.SMEM))
    ints = vmem(chunks, SEG, kind=jnp.int32)
    dma = pltpu.SemaphoreType.DMA

    def to_half(block, k):
        return lax.ppermute(block, "py", [(i, i ^ k) for i in range(groups)])

    def across(parts):
        return [
            lax.ppermute(parts[k], ("px", "py"), [
                (i * groups + j, (i ^ k) * groups + (j ^ half))
                for i in range(spans) for j in range(groups)])
            for k in range(spans)]

    *w_blocks, slots = call(
        functools.partial(pack_weights_kernel, groups, cap, blk, block_rows),
        (f32(block_rows, SEG),) * half + (jax.ShapeDtypeStruct((chunks, SEG), jnp.int32),),
        [ints, ints, ints, vmem(chunks, SEG), vmem(rows, SEG), vmem(half * block_rows, SEG), ints,
         pltpu.SMEM((chunks, SEG), jnp.int32), dma((5,)), dma((half,)), dma],
        [hbm] * 5,
        (hbm,) * half + (local,),
        limit=PACK_BYTES,
    )(
        obs_owner.reshape(chunks, SEG), cell_key.reshape(chunks, SEG),
        stencil.reshape(chunks, SEG), interp.reshape(chunks, SEG), obs_weight,
    )
    *v_blocks, swap = call(
        functools.partial(pack_products_kernel, groups, cap),
        (f32(2 * cap, SEG),) * half + (f32(spans, LX * ext // SEG + (F + 1) * nx, SEG),),
        [vmem(rows, SEG), vmem(rows, SEG), vmem(*coef_y.shape[1:]), vmem(F + 1, nx, SEG),
         vmem(F + 1, nx, SEG), vmem(groups * cap, SEG), dma((7,)), dma((half,))],
        [scalars] + [hbm] * 5,
        (hbm,) * half + (local,),
        limit=PACK_BYTES,
    )(slots, obs_weight, innovation, coef_y[0], c0, cx)
    for k in range(1, half):
        w_blocks[k], v_blocks[k] = lax.optimization_barrier((to_half(w_blocks[k], k), v_blocks[k]))
        v_blocks[k] = to_half(v_blocks[k], k)

    swap = lax.all_to_all(swap, "px", split_axis=0, concat_axis=0, tiled=True)
    c0_ext, cx_ext, cy_ext, u_ext = call(
        start_kernel,
        (f32(F, nx, ext), f32(nx, ext), f32(nx, ext), f32(F, nx, ext)),
    )(c0, cx, swap)

    def sum_weights(side, tie):
        return call(
            functools.partial(weights_kernel, half, cap, blk, side),
            (f32(half, meta_rows, SEG), f32(2, ROWS, SEG)),
            [vmem(ROWS, 3 * SEG)],
            [local] * half + [any_space],
        )(*w_blocks, tie)

    meta, side_across = sum_weights(1, slots)
    side_across = to_half(side_across, half)
    _, side = sum_weights(0, cx_ext)
    sums_across = across(call(
        functools.partial(products_across_kernel, half, cap, blk),
        (f32(F, LX, ext),) * spans,
        [vmem(ROWS, 2 * SEG), vmem(ROWS, SEG)],
    )(meta, *v_blocks))
    parts = call(
        functools.partial(products_kernel, half, cap, blk),
        f32(spans, 3 * F, LX, ext),
        [vmem(ROWS, 2 * SEG), vmem(ROWS, SEG), vmem(2, ROWS, SEG)],
    )(meta, side, side_across, *v_blocks)
    parts = lax.all_to_all(parts, "px", split_axis=0, concat_axis=0, tiled=True)

    r, q, h, dots = call(
        functools.partial(solve_kernel, spans),
        (f32(F, nx, width),) * 2 + (f32(F, nx, ext), f32(groups * spans, 1, SEG)),
        [vmem(3, F, nx, ext), vmem(3 * F, nx, ext), vmem(nx, ext)],
    )(c0_ext, cx_ext, cy_ext, u_ext, parts, *sums_across)
    dots = lax.all_to_all(dots, ("px", "py"), split_axis=0, concat_axis=0, tiled=True)
    qq = call(last_kernel, f32(F, nx, width), [vmem(nx, ext)] * 2)(h, q, cx_ext, cy_ext)
    control, residual = call(finish_kernel, (f32(F, nx, width),) * 2)(dots, c0, r, q, qq)
    return control[:, None], residual[:, None]


def solution(mesh):
    return jax.shard_map(
        shards,
        mesh=mesh,
        in_specs=(
            P(None, "py", None, "px"),
            P("py", None, "px"),
            P("py", "px", None),
            P(("px", "py"), None),
            P(("px", "py"), None),
            P(("px", "py")),
            P(("px", "py"), None),
            P(("px", "py")),
            P(("px", "py")),
        ),
        out_specs=(P(None, "py", None, "px"), P(None, "py", None, "px")),
        check_vma=False,
    )
```

time: 124 us -> 117 us (0.944)
  blocking collectives: 10.4 us -> 0 us
  starting transfers between devices: 22 us -> 26.8 us
  waiting for transfers between devices: 55.1 us -> 50.8 us
  Pallas kernels: 33.4 us -> 37 us
    all_to_all x2 -> x3, waiting for transfers between devices: 46.8 us -> 11.1 us  [the longest x1 5.61 us: shards(): swap = lax.all_to_all(swap, 'px', split_axis=0, concat_axis=0, tiled=True)]
    ppermute x11, waiting for transfers between devices: 8.3 us -> 39.7 us  [the longest x7 27.3 us: to_half(): return lax.ppermute(block, 'py', [(i, i ^ k) for i in range(groups)])]
    all_to_all x1 -> x0, blocking collectives: 10.4 us -> none  [shards(): lax.all_to_all(dots, ('px', 'py'), split_axis=0, concat_axis=0, tiled=True)]
    ppermute x11, starting transfers between devices: 11.1 us -> 17.1 us  [the longest x7 10.9 us: to_half(): return lax.ppermute(block, 'py', [(i, i ^ k) for i in range(groups)])]
    pallas_call x5 -> x8, Pallas kernels: 30.9 us -> 34.5 us  [the longest x1 7.63 us: shards(): call(functools.partial(pack_products_kernel, groups, cap), (f32(2 * cap,...]
    all_to_all x2 -> x3, starting transfers between devices: 10.9 us -> 9.66 us  [the longest x1 3.6 us: shards(): swap = lax.all_to_all(swap, 'px', split_axis=0, concat_axis=0, tiled=True)]
  transfers between devices with their start and end apart: 13 -> 14, of which waited for: 6 -> 11; matrix products, arithmetic and copies ran while one was open for 0% -> 0% of each run, Pallas kernels for 13% -> 13%
where the time goes in v4:
time: 117 us
  waiting for transfers between devices  50.8 us (43%)
  Pallas kernels  37 us (32%)
  starting transfers between devices  26.8 us (23%)
  local copies, waits for them, and re-layouts  1.47 us (1%)
    ppermute x7, waiting for transfers between devices, to_half(): return lax.ppermute(block, 'py', [(i, i ^ k) for i in range(groups)])  27.3 us
    ppermute x4, waiting for transfers between devices, across(): lax.ppermute(parts[k], ('px', 'py'), [(i * groups + j, (i ^ k) * groups +...  12.4 us
    ppermute x7, starting transfers between devices, to_half(): return lax.ppermute(block, 'py', [(i, i ^ k) for i in range(groups)])  10.9 us
    pallas_call x1, Pallas kernels, shards(): call(functools.partial(pack_products_kernel, groups, cap), (f32(2 * cap,...  7.63 us
    pallas_call x1, Pallas kernels, shards(): call(functools.partial(solve_kernel, spans), (f32(F, nx, width),) * 2 + (...  7.47 us
    pallas_call x1, Pallas kernels, shards(): call(functools.partial(pack_weights_kernel, groups, cap, blk, block_rows)...  6.9 us
    ppermute x4, starting transfers between devices, across(): lax.ppermute(parts[k], ('px', 'py'), [(i * groups + j, (i ^ k) * groups +...  6.25 us
    all_to_all x1, waiting for transfers between devices, shards(): swap = lax.all_to_all(swap, 'px', split_axis=0, concat_axis=0, tiled=True)  5.61 us
  transfers between devices with their start and end apart: 14, of which 11 were waited for; matrix products, arithmetic and copies ran while one was open for 0% of the time, Pallas kernels for 13%

profile of v4, /device:TPU:0, one launch (start us, length us, event | category | flops | bytes accessed | tf_op | source)
XLA Modules:
  0.0 116.9 jit_solution(9475984200745109834)
XLA Ops:
  0.6 6.9 %shard_map.104 = (f32[784,128]{1,0:T(8,128)}, f32[784,128]{1,0:T(8,128)}, f32[784,128]{1,0:T(8,128)}, f32[784,128]{1,0:T(8,128)}, s32[8,128]{1,0:T(8,128)}) custom-call(s32[8,128]{1,0:T(8,128)} %bitcast.19, s32[8,128]{1,0:T(8,128)} %bitcast.20, s32[8,128]{1,0:T(8,128)} %bitcast.21, f32[8,128]{1,0:T(8,128)} %bitcast.22, f32[1024,128]{1,0:T(8,128)} %w_hbm.3), custom_call_target="tpu_custom_call" | custom-call | tf_op jit(solution)/shard_map/pallas_call | solution.py:472
  7.5 3.0 %collective-permute-start = (f32[784,128]{1,0:T(8,128)}, f32[784,128]{1,0:T(8,128)S(1)}, u32[]{:S(2)}, u32[]{:S(2)}) collective-permute-start(f32[784,128]{1,0:T(8,128)} %get-tuple-element.42), channel_id=1, source_target_pairs={{0,1},{1,0},{2,3},{3,2},{4,5},{5,4},{6,7},{7,6},{8,9},{9,8},{10,11... | collective-permute-start | bytes 1204232 | tf_op jit(solution)/shard_map/ppermute | solution.py:463
  12.1 7.6 %shard_map.105 = (f32[768,128]{1,0:T(8,128)}, f32[768,128]{1,0:T(8,128)}, f32[768,128]{1,0:T(8,128)}, f32[768,128]{1,0:T(8,128)}, f32[4,272,128]{2,1,0:T(8,128)}) custom-call(s32[8,128]{1,0:T(8,128)} %get-tuple-element.35.slot_ref.rest_4_, f32[1024,128]{1,0:T(8,128)} %w_hbm.3, f32[1024,128]{1,0:T(8,128)} %d_hbm.1, f32[16,2048]{1,0:T(8,128)} %bitcast.18, ...), custom_call_target="tpu_custom_call" | custom-call | tf_op jit(solution)/shard_map/pallas_call | solution.py:484
  20.0 2.9 %collective-permute-done.1.rest_2_ = f32[784,128]{1,0:T(8,128)S(1)} collective-permute-done((f32[784,128]{1,0:T(8,128)}, f32[784,128]{1,0:T(8,128)S(1)}, u32[]{:S(2)}, u32[]{:S(2)}) %collective-permute-start.1) | collective-permute-done | bytes 401440 | tf_op jit(solution)/shard_map/ppermute | solution.py:463
  23.0 6.9 %collective-permute-done.2.rest_3_ = f32[784,128]{1,0:T(8,128)S(1)} collective-permute-done((f32[784,128]{1,0:T(8,128)}, f32[784,128]{1,0:T(8,128)S(1)}, u32[]{:S(2)}, u32[]{:S(2)}) %collective-permute-start.2) | collective-permute-done | bytes 401440 | tf_op jit(solution)/shard_map/ppermute | solution.py:463
  29.9 2.7 %shard_map.107 = (f32[4,16,128]{2,1,0:T(8,128)S(1)}, f32[2,512,128]{2,1,0:T(8,128)}) custom-call(f32[784,128]{1,0:T(8,128)S(1)} %copy-done.1, f32[784,128]{1,0:T(8,128)S(1)} %collective-permute-done.rest_1_, f32[784,128]{1,0:T(8,128)S(1)} %collective-permute-done.1.rest_2_, f32[784,128]{1,0:T(8,128)S(1)} %collective-permute-done.2.rest_3_, ...), custom_call_target="tpu_custom_call" | custom-call | tf_op jit(solution)/shard_map/pallas_call | solution.py:504
  32.6 2.8 %collective-permute-start.3 = (f32[2,512,128]{2,1,0:T(8,128)}, f32[2,512,128]{2,1,0:T(8,128)}, u32[]{:S(2)}, u32[]{:S(2)}) collective-permute-start(f32[2,512,128]{2,1,0:T(8,128)} %get-tuple-element.53), channel_id=1, source_target_pairs={{0,4},{1,5},{2,6},{3,7},{4,0},{5,1},{6,2},{7,3},{8,12},{9,13},{10,... | collective-permute-start | bytes 1572872 | tf_op jit(solution)/shard_map/ppermute | solution.py:463
  35.4 3.6 %all-to-all-start = ((f32[4,272,128]{2,1,0:T(8,128)}), f32[4,272,128]{2,1,0:T(8,128)S(1)}, u32[]{:S(2)}, u32[]{:S(2)}) async-start(f32[4,272,128]{2,1,0:T(8,128)} %get-tuple-element.36), calls=%async_computation | async-start | bytes 1114112 | tf_op jit(solution)/shard_map/all_to_all | solution.py:497
  39.0 2.6 %collective-permute-start.6 = (f32[768,128]{1,0:T(8,128)}, f32[768,128]{1,0:T(8,128)S(1)}, u32[]{:S(2)}, u32[]{:S(2)}) collective-permute-start(f32[768,128]{1,0:T(8,128)} %get-tuple-element.57), channel_id=1, source_target_pairs={{0,3},{1,2},{2,1},{3,0},{4,7},{5,6},{6,5},{7,4},{8,11},{9,10},{10,... | collective-permute-start | bytes 1179656 | tf_op jit(solution)/shard_map/ppermute | solution.py:463
  42.5 5.6 %all-to-all-done.swap_ref = f32[4,272,128]{2,1,0:T(8,128)S(1)} async-done(((f32[4,272,128]{2,1,0:T(8,128)}), f32[4,272,128]{2,1,0:T(8,128)S(1)}, u32[]{:S(2)}, u32[]{:S(2)}) %all-to-all-start) | async-done | bytes 557088 | tf_op jit(solution)/shard_map/all_to_all | solution.py:497
  50.9 2.4 %shard_map.108 = (f32[4,16,128]{2,1,0:T(8,128)}, f32[2,512,128]{2,1,0:T(8,128)S(1)}) custom-call(f32[784,128]{1,0:T(8,128)S(1)} %copy-done.1, f32[784,128]{1,0:T(8,128)S(1)} %collective-permute-done.rest_1_, f32[784,128]{1,0:T(8,128)S(1)} %collective-permute-done.1.rest_2_, f32[784,128]{1,0:T(8,128)S(1)} %collective-permute-done.2.rest_3_, ...), custom_call_target="tpu_custom_call" | custom-call | tf_op jit(solution)/shard_map/pallas_call | solution.py:504
  53.3 8.9 %collective-permute-done.6.rest_3_ = f32[768,128]{1,0:T(8,128)S(1)} collective-permute-done((f32[768,128]{1,0:T(8,128)}, f32[768,128]{1,0:T(8,128)S(1)}, u32[]{:S(2)}, u32[]{:S(2)}) %collective-permute-start.6) | collective-permute-done | bytes 393248 | tf_op jit(solution)/shard_map/ppermute | solution.py:463
  62.2 8.2 %collective-permute-done.5.rest_2_ = f32[768,128]{1,0:T(8,128)} collective-permute-done((f32[768,128]{1,0:T(8,128)}, f32[768,128]{1,0:T(8,128)}, u32[]{:S(2)}, u32[]{:S(2)}) %collective-permute-start.5) | collective-permute-done | bytes 393248 | tf_op jit(solution)/shard_map/ppermute | solution.py:463
  70.5 3.4 %shard_map.109 = f32[4,6,16,640]{3,2,1,0:T(8,128)} custom-call(f32[4,16,128]{2,1,0:T(8,128)S(1)} %get-tuple-element.51.meta_ref, f32[2,512,128]{2,1,0:T(8,128)S(1)} %get-tuple-element.52.side_ref, f32[2,512,128]{2,1,0:T(8,128)} %collective-permute-done.3.other_ref, f32[768,128]{1,0:T(8,128)S(1)} %copy-done.2, f32[768,128]{1,0:T(8,128)} %collective-permute-done.4.rest_1_, ...), custom_call_target="tpu_custom_call" | custom-call | tf_op jit(solution)/shard_map/pallas_call | solution.py:519
  73.9 3.5 %all-to-all-start.1 = ((f32[4,6,16,640]{3,2,1,0:T(8,128)}), f32[4,6,16,640]{3,2,1,0:T(8,128)S(1)}, u32[]{:S(2)}, u32[]{:S(2)}) async-start(f32[4,6,16,640]{3,2,1,0:T(8,128)} %shard_map.109), calls=%async_computation.1 | async-start | bytes 1966080 | tf_op jit(solution)/shard_map/all_to_all | solution.py:524
  77.5 2.4 %shard_map.110 = (f32[2,16,640]{2,1,0:T(8,128)S(1)}, f32[2,16,640]{2,1,0:T(8,128)S(1)}, f32[2,16,640]{2,1,0:T(8,128)S(1)}, f32[2,16,640]{2,1,0:T(8,128)S(1)}) custom-call(f32[4,16,128]{2,1,0:T(8,128)S(1)} %get-tuple-element.51.meta_ref, f32[768,128]{1,0:T(8,128)S(1)} %copy-done.2, f32[768,128]{1,0:T(8,128)} %collective-permute-done.4.rest_1_, ...), custom_call_target="tpu_custom_call" | custom-call | tf_op jit(solution)/shard_map/pallas_call | solution.py:514
  80.3 2.4 %collective-permute-start.8 = (f32[2,16,640]{2,1,0:T(8,128)S(1)}, f32[2,16,640]{2,1,0:T(8,128)S(1)}, u32[]{:S(2)}, u32[]{:S(2)}) collective-permute-start(f32[2,16,640]{2,1,0:T(8,128)S(1)} %get-tuple-element.59), channel_id=1, source_target_pairs={{0,12},{1,13},{2,14},{3,15},{4,8},{5,9},{6,10},{7,11},{8,4},{9,5},... | collective-permute-start | bytes 245768 | tf_op jit(solution)/shard_map/ppermute | solution.py:467
  84.2 1.9 %collective-permute-start.10 = (f32[2,16,640]{2,1,0:T(8,128)S(1)}, f32[2,16,640]{2,1,0:T(8,128)S(1)}, u32[]{:S(2)}, u32[]{:S(2)}) collective-permute-start(f32[2,16,640]{2,1,0:T(8,128)S(1)} %get-tuple-element.61), channel_id=1, source_target_pairs={{0,28},{1,29},{2,30},{3,31},{4,24},{5,25},{6,26},{7,27},{8,20},{9,... | collective-permute-start | bytes 245768 | tf_op jit(solution)/shard_map/ppermute | solution.py:467
  86.1 6.2 %collective-permute-done.7.rest_0_ = f32[2,16,640]{2,1,0:T(8,128)S(1)} collective-permute-done((f32[2,16,640]{2,1,0:T(8,128)S(1)}, f32[2,16,640]{2,1,0:T(8,128)S(1)}, u32[]{:S(2)}, u32[]{:S(2)}) %collective-permute-start.7) | collective-permute-done | bytes 81952 | tf_op jit(solution)/shard_map/ppermute | solution.py:467
  92.3 1.7 %collective-permute-done.8.rest_1_ = f32[2,16,640]{2,1,0:T(8,128)S(1)} collective-permute-done((f32[2,16,640]{2,1,0:T(8,128)S(1)}, f32[2,16,640]{2,1,0:T(8,128)S(1)}, u32[]{:S(2)}, u32[]{:S(2)}) %collective-permute-start.8) | collective-permute-done | bytes 81952 | tf_op jit(solution)/shard_map/ppermute | solution.py:467
  94.0 3.0 %collective-permute-done.9.rest_2_ = f32[2,16,640]{2,1,0:T(8,128)S(1)} collective-permute-done((f32[2,16,640]{2,1,0:T(8,128)S(1)}, f32[2,16,640]{2,1,0:T(8,128)S(1)}, u32[]{:S(2)}, u32[]{:S(2)}) %collective-permute-start.9) | collective-permute-done | bytes 81952 | tf_op jit(solution)/shard_map/ppermute | solution.py:467
  98.6 7.5 %shard_map.111 = (f32[2,64,512]{2,1,0:T(8,128)S(1)}, f32[2,64,512]{2,1,0:T(8,128)S(1)}, f32[2,64,640]{2,1,0:T(8,128)S(1)}, f32[32,1,128]{2,1,0:T(1,128)}) custom-call(f32[2,64,640]{2,1,0:T(8,128)S(1)} %copy-done.7, f32[64,640]{1,0:T(8,128)S(1)} %get-tuple-element.38.rest_4_.cx_ref, f32[64,640]{1,0:T(8,128)S(1)} %copy-done.4, f32[2,64,640]{2,1,0:T(8,128)S(1)} %copy-done.9, ...), custom_call_target="tpu_custom_call" | custom-call | tf_op jit(solution)/shard_map/pallas_call | solution.py:526
  106.0 2.5 %all-to-all-start.2 = ((f32[32,1,128]{2,1,0:T(1,128)}), f32[32,1,128]{2,1,0:T(1,128)S(1)}, u32[]{:S(2)}, u32[]{:S(2)}) async-start(f32[32,1,128]{2,1,0:T(1,128)} %get-tuple-element.62), calls=%async_computation.2 | async-start | bytes 32768 | tf_op jit(solution)/shard_map/all_to_all | solution.py:531
  110.1 5.5 %all-to-all-done.2.dots_ref = f32[32,1,128]{2,1,0:T(1,128)S(1)} async-done(((f32[32,1,128]{2,1,0:T(1,128)}), f32[32,1,128]{2,1,0:T(1,128)S(1)}, u32[]{:S(2)}, u32[]{:S(2)}) %all-to-all-start.2) | async-done | bytes 16416 | tf_op jit(solution)/shard_map/all_to_all | solution.py:531
  (36 shorter events, 12.0 us)
Async XLA Ops:
  7.5 12.5 %collective-permute-start = (f32[784,128]{1,0:T(8,128)}, f32[784,128]{1,0:T(8,128)S(1)}, u32[]{:S(2)}, u32[]{:S(2)}) collective-permute-start(f32[784,128]{1,0:T(8,128)} %get-tuple-element.42), channel_id=1, source_target_pairs={{0,1},{1,0},{2,3},{3,2},{4,5},{5,4},{6,7},{7,6},{8,9},{9,8},{10,11... | collective-permute-start | bytes 1204232 | tf_op jit(solution)/shard_map/ppermute | solution.py:463
  10.5 12.4 %collective-permute-start.1 = (f32[784,128]{1,0:T(8,128)}, f32[784,128]{1,0:T(8,128)S(1)}, u32[]{:S(2)}, u32[]{:S(2)}) collective-permute-start(f32[784,128]{1,0:T(8,128)} %get-tuple-element.45), channel_id=1, source_target_pairs={{0,2},{1,3},{2,0},{3,1},{4,6},{5,7},{6,4},{7,5},{8,10},{9,11},{10,... | collective-permute-start | bytes 1204232 | tf_op jit(solution)/shard_map/ppermute | solution.py:463
  12.1 17.8 %collective-permute-start.2 = (f32[784,128]{1,0:T(8,128)}, f32[784,128]{1,0:T(8,128)S(1)}, u32[]{:S(2)}, u32[]{:S(2)}) collective-permute-start(f32[784,128]{1,0:T(8,128)} %get-tuple-element.48), channel_id=1, source_target_pairs={{0,3},{1,2},{2,1},{3,0},{4,7},{5,6},{6,5},{7,4},{8,11},{9,10},{10,... | collective-permute-start | bytes 1204232 | tf_op jit(solution)/shard_map/ppermute | solution.py:463
  12.1 17.8 %copy-start.1 = (f32[784,128]{1,0:T(8,128)S(1)}, f32[784,128]{1,0:T(8,128)}, u32[]{:S(2)}) copy-start(f32[784,128]{1,0:T(8,128)} %get-tuple-element.41.rest_0_) | copy-start | bytes 1204228
  19.8 10.2 %copy-start.10 = (s32[8,128]{1,0:T(8,128)S(1)}, s32[8,128]{1,0:T(8,128)}, u32[]{:S(2)}) copy-start(s32[8,128]{1,0:T(8,128)} %get-tuple-element.35.slot_ref.rest_4_) | copy-start | bytes 12292
  32.6 37.8 %collective-permute-start.3 = (f32[2,512,128]{2,1,0:T(8,128)}, f32[2,512,128]{2,1,0:T(8,128)}, u32[]{:S(2)}, u32[]{:S(2)}) collective-permute-start(f32[2,512,128]{2,1,0:T(8,128)} %get-tuple-element.53), channel_id=1, source_target_pairs={{0,4},{1,5},{2,6},{3,7},{4,0},{5,1},{6,2},{7,3},{8,12},{9,13},{10,... | collective-permute-start | bytes 1572872 | tf_op jit(solution)/shard_map/ppermute | solution.py:463
  35.4 12.8 %copy-start = (f32[2,1,64,512]{3,2,1,0:T(8,128)S(1)}, f32[2,1,64,512]{3,2,1,0:T(8,128)}, u32[]{:S(2)}) copy-start(f32[2,1,64,512]{3,2,1,0:T(8,128)} %param.9) | copy-start | bytes 786436
  35.4 12.8 %copy-start.5 = (f32[1,64,512]{2,1,0:T(8,128)S(1)}, f32[1,64,512]{2,1,0:T(8,128)}, u32[]{:S(2)}) copy-start(f32[1,64,512]{2,1,0:T(8,128)} %param.10) | copy-start | bytes 393220
  35.4 12.8 %all-to-all-start = ((f32[4,272,128]{2,1,0:T(8,128)}), f32[4,272,128]{2,1,0:T(8,128)S(1)}, u32[]{:S(2)}, u32[]{:S(2)}) async-start(f32[4,272,128]{2,1,0:T(8,128)} %get-tuple-element.36), calls=%async_computation | async-start | bytes 1114112 | tf_op jit(solution)/shard_map/all_to_all | solution.py:497
  39.0 23.2 %collective-permute-start.6 = (f32[768,128]{1,0:T(8,128)}, f32[768,128]{1,0:T(8,128)S(1)}, u32[]{:S(2)}, u32[]{:S(2)}) collective-permute-start(f32[768,128]{1,0:T(8,128)} %get-tuple-element.57), channel_id=1, source_target_pairs={{0,3},{1,2},{2,1},{3,0},{4,7},{5,6},{6,5},{7,4},{8,11},{9,10},{10,... | collective-permute-start | bytes 1179656 | tf_op jit(solution)/shard_map/ppermute | solution.py:463
  41.6 28.9 %collective-permute-start.5 = (f32[768,128]{1,0:T(8,128)}, f32[768,128]{1,0:T(8,128)}, u32[]{:S(2)}, u32[]{:S(2)}) collective-permute-start(f32[768,128]{1,0:T(8,128)} %get-tuple-element.56), channel_id=1, source_target_pairs={{0,2},{1,3},{2,0},{3,1},{4,6},{5,7},{6,4},{7,5},{8,10},{9,11},{10,... | collective-permute-start | bytes 1179656 | tf_op jit(solution)/shard_map/ppermute | solution.py:463
  42.0 28.4 %collective-permute-start.4 = (f32[768,128]{1,0:T(8,128)}, f32[768,128]{1,0:T(8,128)}, u32[]{:S(2)}, u32[]{:S(2)}) collective-permute-start(f32[768,128]{1,0:T(8,128)} %get-tuple-element.55), channel_id=1, source_target_pairs={{0,1},{1,0},{2,3},{3,2},{4,5},{5,4},{6,7},{7,6},{8,9},{9,8},{10,11... | collective-permute-start | bytes 1179656 | tf_op jit(solution)/shard_map/ppermute | solution.py:463
  50.2 0.7 copy-start.8
  50.9 2.4 %copy-start.3 = (f32[64,640]{1,0:T(8,128)}, f32[64,640]{1,0:T(8,128)S(1)}, u32[]{:S(2)}) copy-start(f32[64,640]{1,0:T(8,128)S(1)} %get-tuple-element.39.cy_ref) | copy-start | bytes 491524
  50.9 19.6 %copy-start.2 = (f32[768,128]{1,0:T(8,128)S(1)}, f32[768,128]{1,0:T(8,128)}, u32[]{:S(2)}) copy-start(f32[768,128]{1,0:T(8,128)} %get-tuple-element.54.rest_0_) | copy-start | bytes 1179652
  73.9 24.6 %all-to-all-start.1 = ((f32[4,6,16,640]{3,2,1,0:T(8,128)}), f32[4,6,16,640]{3,2,1,0:T(8,128)S(1)}, u32[]{:S(2)}, u32[]{:S(2)}) async-start(f32[4,6,16,640]{3,2,1,0:T(8,128)} %shard_map.109), calls=%async_computation.1 | async-start | bytes 1966080 | tf_op jit(solution)/shard_map/all_to_all | solution.py:524
  77.4 21.1 %copy-start.4 = (f32[64,640]{1,0:T(8,128)S(1)}, f32[64,640]{1,0:T(8,128)}, u32[]{:S(2)}) copy-start(f32[64,640]{1,0:T(8,128)} %copy-done.3) | copy-start | bytes 491524
  77.4 21.1 %copy-start.7 = (f32[2,64,640]{2,1,0:T(8,128)S(1)}, f32[2,64,640]{2,1,0:T(8,128)}, u32[]{:S(2)}) copy-start(f32[2,64,640]{2,1,0:T(8,128)} %copy-done.6) | copy-start | bytes 983044
  77.4 21.1 %copy-start.9 = (f32[2,64,640]{2,1,0:T(8,128)S(1)}, f32[2,64,640]{2,1,0:T(8,128)}, u32[]{:S(2)}) copy-start(f32[2,64,640]{2,1,0:T(8,128)} %copy-done.8) | copy-start | bytes 983044
  79.9 12.4 %collective-permute-start.7 = (f32[2,16,640]{2,1,0:T(8,128)S(1)}, f32[2,16,640]{2,1,0:T(8,128)S(1)}, u32[]{:S(2)}, u32[]{:S(2)}) collective-permute-start(f32[2,16,640]{2,1,0:T(8,128)S(1)} %get-tuple-element.58), channel_id=1, source_target_pairs={{0,4},{1,5},{2,6},{3,7},{4,0},{5,1},{6,2},{7,3},{8,12},{9,13},{10,... | collective-permute-start | bytes 245768 | tf_op jit(solution)/shard_map/ppermute | solution.py:467
  80.3 13.7 %collective-permute-start.8 = (f32[2,16,640]{2,1,0:T(8,128)S(1)}, f32[2,16,640]{2,1,0:T(8,128)S(1)}, u32[]{:S(2)}, u32[]{:S(2)}) collective-permute-start(f32[2,16,640]{2,1,0:T(8,128)S(1)} %get-tuple-element.59), channel_id=1, source_target_pairs={{0,12},{1,13},{2,14},{3,15},{4,8},{5,9},{6,10},{7,11},{8,4},{9,5},... | collective-permute-start | bytes 245768 | tf_op jit(solution)/shard_map/ppermute | solution.py:467
  82.6 14.3 %collective-permute-start.9 = (f32[2,16,640]{2,1,0:T(8,128)S(1)}, f32[2,16,640]{2,1,0:T(8,128)S(1)}, u32[]{:S(2)}, u32[]{:S(2)}) collective-permute-start(f32[2,16,640]{2,1,0:T(8,128)S(1)} %get-tuple-element.60), channel_id=1, source_target_pairs={{0,20},{1,21},{2,22},{3,23},{4,16},{5,17},{6,18},{7,19},{8,28},{9,... | collective-permute-start | bytes 245768 | tf_op jit(solution)/shard_map/ppermute | solution.py:467
  84.2 14.3 %collective-permute-start.10 = (f32[2,16,640]{2,1,0:T(8,128)S(1)}, f32[2,16,640]{2,1,0:T(8,128)S(1)}, u32[]{:S(2)}, u32[]{:S(2)}) collective-permute-start(f32[2,16,640]{2,1,0:T(8,128)S(1)} %get-tuple-element.61), channel_id=1, source_target_pairs={{0,28},{1,29},{2,30},{3,31},{4,24},{5,25},{6,26},{7,27},{8,20},{9,... | collective-permute-start | bytes 245768 | tf_op jit(solution)/shard_map/ppermute | solution.py:467
  106.0 9.6 %all-to-all-start.2 = ((f32[32,1,128]{2,1,0:T(1,128)}), f32[32,1,128]{2,1,0:T(1,128)S(1)}, u32[]{:S(2)}, u32[]{:S(2)}) async-start(f32[32,1,128]{2,1,0:T(1,128)} %get-tuple-element.62), calls=%async_computation.2 | async-start | bytes 32768 | tf_op jit(solution)/shard_map/all_to_all | solution.py:531
  (1 other events, 0.7 us)

commit v5 on v4

--- a/solution.py
+++ b/solution.py
@@ -229,7 +229,7 @@
 
 
 def weights_kernel(half, cap, blk, across, *rest):
-    w_refs, (_, meta_out, out, acc_ref) = rest[:half], rest[half:]
+    w_refs, (_, meta_out, diagonal_out, side_out, acc_ref) = rest[:half], rest[half:]
     nb = cap // blk
     for k, w_ref in enumerate(w_refs):
         meta_out[k] = w_ref[2 * cap:, :]
@@ -243,8 +243,8 @@
 
     low = 2 * cap + across * 2 * nb
     sum_rows(cap, blk, [w_ref[low:low + 2 * nb, :] for w_ref in w_refs], acc_ref, terms)
-    out[0] = acc_ref[:, :SEG] + pltpu.roll(acc_ref[:, 2 * SEG:], 1, 0)
-    out[1] = acc_ref[:, SEG:2 * SEG]
+    diagonal_out[...] = acc_ref[:, :SEG] + pltpu.roll(acc_ref[:, 2 * SEG:], 1, 0)
+    side_out[...] = acc_ref[:, SEG:2 * SEG]
 
 
 def sum_products(half, cap, blk, across, meta_ref, v_refs, acc_ref, sums_ref):
@@ -261,7 +261,8 @@
 
 
 def products_across_kernel(half, cap, blk, meta_ref, *rest):
-    v_refs, (*outs, acc_ref, sums_ref) = rest[:half], rest[half:]
+    v_refs, (meta_out, *outs, acc_ref, sums_ref) = rest[:half], rest[half:]
+    meta_out[...] = meta_ref[...]
     sum_products(half, cap, blk, 1, meta_ref, v_refs, acc_ref, sums_ref)
     me = lax.axis_index("px")
     for k, out in enumerate(outs):
@@ -269,11 +270,12 @@
             cut_part(sums_ref, out.at[f], f, me ^ k, len(outs))
 
 
-def products_kernel(half, cap, blk, meta_ref, side_ref, other_ref, *rest):
+def products_kernel(half, cap, blk, meta_ref, d_ref, e_ref, far_d_ref, far_e_ref, *rest):
     v_refs, (out, acc_ref, sums_ref, side) = rest[:half], rest[half:]
     spans = out.shape[0]
     sum_products(half, cap, blk, 0, meta_ref, v_refs, acc_ref, sums_ref)
-    side[...] = side_ref[...] + other_ref[...]
+    side[0] = d_ref[...] + far_d_ref[...]
+    side[1] = e_ref[...] + far_e_ref[...]
     for q in range(spans):
         for channel, rows_ref in enumerate((side.at[0], side.at[1], sums_ref)):
             for f in range(F):
@@ -296,7 +298,8 @@
         to_ref[lines, :] = sweep(from_ref[lines, :], cy_ref[lines, :], 1)
 
 
-def start_kernel(c0_ref, cx_ref, swap_ref, c0_out, cx_out, cy_out, u_out):
+def start_kernel(c0_ref, cx_ref, swap_ref, c0_out, cx_out, cy_out, u_out, token_out):
+    token_out[...] = jnp.zeros_like(token_out)
     width = c0_ref.shape[2]
     nx = cx_ref.shape[0]
     spans, count = swap_ref.shape[0], cy_out.shape[1] // SEG
@@ -454,8 +457,8 @@
     nx, width = control_start.shape[2], control_start.shape[3]
     ext = width + SEG
     c0, cx = control_start[:, 0], coef_x[0]
-    hbm, any_space, local, scalars = (
-        pl.BlockSpec(memory_space=s) for s in (pltpu.HBM, pl.ANY, pltpu.VMEM, pltpu.SMEM))
+    hbm, local, scalars = (
+        pl.BlockSpec(memory_space=s) for s in (pltpu.HBM, pltpu.VMEM, pltpu.SMEM))
     ints = vmem(chunks, SEG, kind=jnp.int32)
     dma = pltpu.SemaphoreType.DMA
 
@@ -490,37 +493,37 @@
         (hbm,) * half + (local,),
         limit=PACK_BYTES,
     )(slots, obs_weight, innovation, coef_y[0], c0, cx)
-    for k in range(1, half):
-        w_blocks[k], v_blocks[k] = lax.optimization_barrier((to_half(w_blocks[k], k), v_blocks[k]))
-        v_blocks[k] = to_half(v_blocks[k], k)
+    w_blocks[1:] = [to_half(w_blocks[k], k) for k in range(1, half)]
+    w_blocks[1], *v_blocks[1:] = lax.optimization_barrier((w_blocks[1], *v_blocks[1:]))
+    v_blocks[1:] = [to_half(v_blocks[k], k) for k in range(1, half)]
 
     swap = lax.all_to_all(swap, "px", split_axis=0, concat_axis=0, tiled=True)
-    c0_ext, cx_ext, cy_ext, u_ext = call(
+    c0_ext, cx_ext, cy_ext, u_ext, token = call(
         start_kernel,
-        (f32(F, nx, ext), f32(nx, ext), f32(nx, ext), f32(F, nx, ext)),
+        (f32(F, nx, ext), f32(nx, ext), f32(nx, ext), f32(F, nx, ext), f32(8, SEG)),
     )(c0, cx, swap)
 
-    def sum_weights(side, tie):
+    def sum_weights(side, token):
         return call(
             functools.partial(weights_kernel, half, cap, blk, side),
-            (f32(half, meta_rows, SEG), f32(2, ROWS, SEG)),
+            (f32(half, meta_rows, SEG),) + (f32(ROWS, SEG),) * 2,
             [vmem(ROWS, 3 * SEG)],
-            [local] * half + [any_space],
-        )(*w_blocks, tie)
-
-    meta, side_across = sum_weights(1, slots)
-    side_across = to_half(side_across, half)
-    _, side = sum_weights(0, cx_ext)
-    sums_across = across(call(
+        )(*w_blocks, token)
+
+    meta, *side_across = sum_weights(1, token)
+    side_across = [to_half(values, half) for values in side_across]
+    meta, *side = sum_weights(0, meta)
+    meta, *sums_across = call(
         functools.partial(products_across_kernel, half, cap, blk),
-        (f32(F, LX, ext),) * spans,
+        (f32(half, meta_rows, SEG),) + (f32(F, LX, ext),) * spans,
         [vmem(ROWS, 2 * SEG), vmem(ROWS, SEG)],
-    )(meta, *v_blocks))
+    )(meta, *v_blocks)
+    sums_across = across(sums_across)
     parts = call(
         functools.partial(products_kernel, half, cap, blk),
         f32(spans, 3 * F, LX, ext),
         [vmem(ROWS, 2 * SEG), vmem(ROWS, SEG), vmem(2, ROWS, SEG)],
-    )(meta, side, side_across, *v_blocks)
+    )(meta, *side, *side_across, *v_blocks)
     parts = lax.all_to_all(parts, "px", split_axis=0, concat_axis=0, tiled=True)
 
     r, q, h, dots = call(

time: 117 us -> 118 us (level)
  Pallas kernels: 37 us -> 35 us
  starting transfers between devices: 26.8 us -> 28.5 us
  waiting for transfers between devices: 50.8 us -> 52.1 us
    ppermute x7 -> x8, waiting for transfers between devices: 27.3 us -> 30.4 us  [to_half(): return lax.ppermute(block, 'py', [(i, i ^ k) for i in range(groups)])]
    all_to_all x1, waiting for transfers between devices: 5.61 us -> 3.95 us  [shards(): swap = lax.all_to_all(swap, 'px', split_axis=0, concat_axis=0, tiled=True)]
    pallas_call x2, Pallas kernels: 5.13 us -> 3.78 us  [sum_weights(): call(functools.partial(weights_kernel, half, cap, blk, side), (f32(half,...]
    ppermute x7 -> x8, starting transfers between devices: 10.9 us -> 11.3 us  [to_half(): return lax.ppermute(block, 'py', [(i, i ^ k) for i in range(groups)])]
  transfers between devices with their start and end apart: 14 -> 15, of which waited for: 11 -> 10; matrix products, arithmetic and copies ran while one was open for 0% -> 0% of each run, Pallas kernels for 13% -> 14%
where the time goes in v5:
time: 118 us; the launch traced here: 117 us
  waiting for transfers between devices  52.1 us (44%)
  Pallas kernels  35 us (30%)
  starting transfers between devices  28.5 us (24%)
    ppermute x8, waiting for transfers between devices, to_half(): return lax.ppermute(block, 'py', [(i, i ^ k) for i in range(groups)])  30.4 us
    ppermute x4, waiting for transfers between devices, across(): lax.ppermute(parts[k], ('px', 'py'), [(i * groups + j, (i ^ k) * groups +...  12.2 us
    ppermute x8, starting transfers between devices, to_half(): return lax.ppermute(block, 'py', [(i, i ^ k) for i in range(groups)])  11.3 us
    pallas_call x1, Pallas kernels, shards(): call(functools.partial(solve_kernel, spans), (f32(F, nx, width),) * 2 + (...  7.47 us
    pallas_call x1, Pallas kernels, shards(): call(functools.partial(pack_products_kernel, groups, cap), (f32(2 * cap,...  7.46 us
    pallas_call x1, Pallas kernels, shards(): call(functools.partial(pack_weights_kernel, groups, cap, blk, block_rows)...  6.91 us
    ppermute x4, starting transfers between devices, across(): lax.ppermute(parts[k], ('px', 'py'), [(i * groups + j, (i ^ k) * groups +...  6.25 us
    all_to_all x1, waiting for transfers between devices, shards(): lax.all_to_all(dots, ('px', 'py'), split_axis=0, concat_axis=0, tiled=True)  5.5 us
  transfers between devices with their start and end apart: 15, of which 10 were waited for; matrix products, arithmetic and copies ran while one was open for 0% of the time, Pallas kernels for 14%

profile of v5, /device:TPU:0, one launch (start us, length us, event | category | flops | bytes accessed | tf_op | source)
XLA Modules:
  0.0 117.2 jit_solution(10157715494159949353)
XLA Ops:
  0.6 6.9 %shard_map.104 = (f32[784,128]{1,0:T(8,128)}, f32[784,128]{1,0:T(8,128)}, f32[784,128]{1,0:T(8,128)}, f32[784,128]{1,0:T(8,128)}, s32[8,128]{1,0:T(8,128)}) custom-call(s32[8,128]{1,0:T(8,128)} %bitcast.19, s32[8,128]{1,0:T(8,128)} %bitcast.20, s32[8,128]{1,0:T(8,128)} %bitcast.21, f32[8,128]{1,0:T(8,128)} %bitcast.22, f32[1024,128]{1,0:T(8,128)} %w_hbm.3), custom_call_target="tpu_custom_call" | custom-call | tf_op jit(solution)/shard_map/pallas_call | solution.py:475
  7.6 3.0 %collective-permute-start = (f32[784,128]{1,0:T(8,128)}, f32[784,128]{1,0:T(8,128)S(1)}, u32[]{:S(2)}, u32[]{:S(2)}) collective-permute-start(f32[784,128]{1,0:T(8,128)} %get-tuple-element.45), channel_id=1, source_target_pairs={{0,1},{1,0},{2,3},{3,2},{4,5},{5,4},{6,7},{7,6},{8,9},{9,8},{10,11... | collective-permute-start | bytes 1204232 | tf_op jit(solution)/shard_map/ppermute | solution.py:466
  10.6 7.5 %shard_map.105 = (f32[768,128]{1,0:T(8,128)}, f32[768,128]{1,0:T(8,128)}, f32[768,128]{1,0:T(8,128)}, f32[768,128]{1,0:T(8,128)}, f32[4,272,128]{2,1,0:T(8,128)}) custom-call(s32[8,128]{1,0:T(8,128)} %get-tuple-element.38.slot_ref, f32[1024,128]{1,0:T(8,128)} %w_hbm.3, f32[1024,128]{1,0:T(8,128)} %d_hbm.1, f32[16,2048]{1,0:T(8,128)} %bitcast.18, ...), custom_call_target="tpu_custom_call" | custom-call | tf_op jit(solution)/shard_map/pallas_call | solution.py:487
  18.0 3.6 %all-to-all-start = ((f32[4,272,128]{2,1,0:T(8,128)}), f32[4,272,128]{2,1,0:T(8,128)S(1)}, u32[]{:S(2)}, u32[]{:S(2)}) async-start(f32[4,272,128]{2,1,0:T(8,128)} %get-tuple-element.39), calls=%async_computation | async-start | bytes 1114112 | tf_op jit(solution)/shard_map/all_to_all | solution.py:500
  21.7 1.6 %collective-permute-start.1 = (f32[784,128]{1,0:T(8,128)}, f32[784,128]{1,0:T(8,128)S(1)}, u32[]{:S(2)}, u32[]{:S(2)}) collective-permute-start(f32[784,128]{1,0:T(8,128)} %get-tuple-element.50), channel_id=1, source_target_pairs={{0,2},{1,3},{2,0},{3,1},{4,6},{5,7},{6,4},{7,5},{8,10},{9,11},{10,... | collective-permute-start | bytes 1204232 | tf_op jit(solution)/shard_map/ppermute | solution.py:466
  23.4 1.9 %collective-permute-start.3 = (f32[768,128]{1,0:T(8,128)}, f32[768,128]{1,0:T(8,128)S(1)}, u32[]{:S(2)}, u32[]{:S(2)}) collective-permute-start(f32[768,128]{1,0:T(8,128)} %get-tuple-element.56), channel_id=1, source_target_pairs={{0,1},{1,0},{2,3},{3,2},{4,5},{5,4},{6,7},{7,6},{8,9},{9,8},{10,11... | collective-permute-start | bytes 1179656 | tf_op jit(solution)/shard_map/ppermute | solution.py:466
  25.2 1.6 %collective-permute-start.4 = (f32[768,128]{1,0:T(8,128)}, f32[768,128]{1,0:T(8,128)S(1)}, u32[]{:S(2)}, u32[]{:S(2)}) collective-permute-start(f32[768,128]{1,0:T(8,128)} %get-tuple-element.57), channel_id=1, source_target_pairs={{0,2},{1,3},{2,0},{3,1},{4,6},{5,7},{6,4},{7,5},{8,10},{9,11},{10,... | collective-permute-start | bytes 1179656 | tf_op jit(solution)/shard_map/ppermute | solution.py:466
  26.9 4.0 %all-to-all-done.swap_ref = f32[4,272,128]{2,1,0:T(8,128)S(1)} async-done(((f32[4,272,128]{2,1,0:T(8,128)}), f32[4,272,128]{2,1,0:T(8,128)S(1)}, u32[]{:S(2)}, u32[]{:S(2)}) %all-to-all-start) | async-done | bytes 557088 | tf_op jit(solution)/shard_map/all_to_all | solution.py:500
  34.0 8.2 %collective-permute-done.2.rest_3_ = f32[784,128]{1,0:T(8,128)S(1)} collective-permute-done((f32[784,128]{1,0:T(8,128)}, f32[784,128]{1,0:T(8,128)S(1)}, u32[]{:S(2)}, u32[]{:S(2)}) %collective-permute-start.2) | collective-permute-done | bytes 401440 | tf_op jit(solution)/shard_map/ppermute | solution.py:466
  42.3 1.9 %shard_map.107 = (f32[4,16,128]{2,1,0:T(8,128)S(1)}, f32[512,128]{1,0:T(8,128)S(1)}, f32[512,128]{1,0:T(8,128)S(1)}) custom-call(f32[784,128]{1,0:T(8,128)S(1)} %copy-done.1, f32[784,128]{1,0:T(8,128)S(1)} %collective-permute-done.rest_1_, f32[784,128]{1,0:T(8,128)S(1)} %collective-permute-done.1.rest_2_, f32[784,128]{1,0:T(8,128)S(1)} %collective-permute-done.2.rest_3_, ...), custom_call_target="tpu_custom_call" | custom-call | tf_op jit(solution)/shard_map/pallas_call | solution.py:507
  44.2 3.0 %collective-permute-start.6 = (f32[512,128]{1,0:T(8,128)S(1)}, f32[512,128]{1,0:T(8,128)S(1)}, u32[]{:S(2)}, u32[]{:S(2)}) collective-permute-start(f32[512,128]{1,0:T(8,128)S(1)} %get-tuple-element.62), channel_id=1, source_target_pairs={{0,4},{1,5},{2,6},{3,7},{4,0},{5,1},{6,2},{7,3},{8,12},{9,13},{10,... | collective-permute-start | bytes 786440 | tf_op jit(solution)/shard_map/ppermute | solution.py:466
  47.3 1.9 %shard_map.108 = (f32[4,16,128]{2,1,0:T(8,128)S(1)}, f32[512,128]{1,0:T(8,128)S(1)}, f32[512,128]{1,0:T(8,128)S(1)}) custom-call(f32[784,128]{1,0:T(8,128)S(1)} %copy-done.1, f32[784,128]{1,0:T(8,128)S(1)} %collective-permute-done.rest_1_, f32[784,128]{1,0:T(8,128)S(1)} %collective-permute-done.1.rest_2_, f32[784,128]{1,0:T(8,128)S(1)} %collective-permute-done.2.rest_3_, ...), custom_call_target="tpu_custom_call" | custom-call | tf_op jit(solution)/shard_map/pallas_call | solution.py:507
  49.2 13.1 %collective-permute-done.4.rest_2_ = f32[768,128]{1,0:T(8,128)S(1)} collective-permute-done((f32[768,128]{1,0:T(8,128)}, f32[768,128]{1,0:T(8,128)S(1)}, u32[]{:S(2)}, u32[]{:S(2)}) %collective-permute-start.4) | collective-permute-done | bytes 393248 | tf_op jit(solution)/shard_map/ppermute | solution.py:466
  62.4 7.8 %collective-permute-done.5.rest_3_ = f32[768,128]{1,0:T(8,128)} collective-permute-done((f32[768,128]{1,0:T(8,128)}, f32[768,128]{1,0:T(8,128)}, u32[]{:S(2)}, u32[]{:S(2)}) %collective-permute-start.5) | collective-permute-done | bytes 393248 | tf_op jit(solution)/shard_map/ppermute | solution.py:466
  70.2 2.2 %shard_map.109 = (f32[4,16,128]{2,1,0:T(8,128)S(1)}, f32[2,16,640]{2,1,0:T(8,128)S(1)}, f32[2,16,640]{2,1,0:T(8,128)S(1)}, f32[2,16,640]{2,1,0:T(8,128)S(1)}, f32[2,16,640]{2,1,0:T(8,128)S(1)}) custom-call(f32[4,16,128]{2,1,0:T(8,128)S(1)} %get-tuple-element.54.meta_ref, f32[768,128]{1,0:T(8,128)S(1)} %copy-done.2, ...), custom_call_target="tpu_custom_call" | custom-call | tf_op jit(solution)/shard_map/pallas_call | solution.py:516
  72.4 3.1 %shard_map.110 = f32[4,6,16,640]{3,2,1,0:T(8,128)} custom-call(f32[4,16,128]{2,1,0:T(8,128)S(1)} %get-tuple-element.59.meta_ref, f32[512,128]{1,0:T(8,128)S(1)} %get-tuple-element.60.d_ref, f32[512,128]{1,0:T(8,128)S(1)} %get-tuple-element.61.e_ref, f32[512,128]{1,0:T(8,128)S(1)} %collective-permute-done.6.far_d_ref, ...), custom_call_target="tpu_custom_call" | custom-call | tf_op jit(solution)/shard_map/pallas_call | solution.py:522
  75.6 3.6 %all-to-all-start.1 = ((f32[4,6,16,640]{3,2,1,0:T(8,128)}), f32[4,6,16,640]{3,2,1,0:T(8,128)S(1)}, u32[]{:S(2)}, u32[]{:S(2)}) async-start(f32[4,6,16,640]{3,2,1,0:T(8,128)} %shard_map.110), calls=%async_computation.1 | async-start | bytes 1966080 | tf_op jit(solution)/shard_map/all_to_all | solution.py:527
  79.2 2.0 %collective-permute-start.8 = (f32[2,16,640]{2,1,0:T(8,128)S(1)}, f32[2,16,640]{2,1,0:T(8,128)S(1)}, u32[]{:S(2)}, u32[]{:S(2)}) collective-permute-start(f32[2,16,640]{2,1,0:T(8,128)S(1)} %get-tuple-element.64), channel_id=1, source_target_pairs={{0,4},{1,5},{2,6},{3,7},{4,0},{5,1},{6,2},{7,3},{8,12},{9,13},{10,... | collective-permute-start | bytes 245768 | tf_op jit(solution)/shard_map/ppermute | solution.py:470
  82.0 3.0 %collective-permute-start.10 = (f32[2,16,640]{2,1,0:T(8,128)S(1)}, f32[2,16,640]{2,1,0:T(8,128)S(1)}, u32[]{:S(2)}, u32[]{:S(2)}) collective-permute-start(f32[2,16,640]{2,1,0:T(8,128)S(1)} %get-tuple-element.66), channel_id=1, source_target_pairs={{0,20},{1,21},{2,22},{3,23},{4,16},{5,17},{6,18},{7,19},{8,28},{9,... | collective-permute-start | bytes 245768 | tf_op jit(solution)/shard_map/ppermute | solution.py:470
  85.5 7.0 %collective-permute-done.8.rest_0_ = f32[2,16,640]{2,1,0:T(8,128)S(1)} collective-permute-done((f32[2,16,640]{2,1,0:T(8,128)S(1)}, f32[2,16,640]{2,1,0:T(8,128)S(1)}, u32[]{:S(2)}, u32[]{:S(2)}) %collective-permute-start.8) | collective-permute-done | bytes 81952 | tf_op jit(solution)/shard_map/ppermute | solution.py:470
  93.3 3.9 %collective-permute-done.10.rest_2_ = f32[2,16,640]{2,1,0:T(8,128)S(1)} collective-permute-done((f32[2,16,640]{2,1,0:T(8,128)S(1)}, f32[2,16,640]{2,1,0:T(8,128)S(1)}, u32[]{:S(2)}, u32[]{:S(2)}) %collective-permute-start.10) | collective-permute-done | bytes 81952 | tf_op jit(solution)/shard_map/ppermute | solution.py:470
  97.7 7.5 %shard_map.111 = (f32[2,64,512]{2,1,0:T(8,128)S(1)}, f32[2,64,512]{2,1,0:T(8,128)S(1)}, f32[2,64,640]{2,1,0:T(8,128)S(1)}, f32[32,1,128]{2,1,0:T(1,128)}) custom-call(f32[2,64,640]{2,1,0:T(8,128)S(1)} %copy-done.7, f32[64,640]{1,0:T(8,128)S(1)} %get-tuple-element.41.cx_ref, f32[64,640]{1,0:T(8,128)S(1)} %copy-done.4, f32[2,64,640]{2,1,0:T(8,128)S(1)} %copy-done.9, ...), custom_call_target="tpu_custom_call" | custom-call | tf_op jit(solution)/shard_map/pallas_call | solution.py:529
  105.2 3.7 %all-to-all-start.2 = ((f32[32,1,128]{2,1,0:T(1,128)}), f32[32,1,128]{2,1,0:T(1,128)S(1)}, u32[]{:S(2)}, u32[]{:S(2)}) async-start(f32[32,1,128]{2,1,0:T(1,128)} %get-tuple-element.68), calls=%async_computation.2 | async-start | bytes 32768 | tf_op jit(solution)/shard_map/all_to_all | solution.py:534
  110.5 5.5 %all-to-all-done.2.dots_ref = f32[32,1,128]{2,1,0:T(1,128)S(1)} async-done(((f32[32,1,128]{2,1,0:T(1,128)}), f32[32,1,128]{2,1,0:T(1,128)S(1)}, u32[]{:S(2)}, u32[]{:S(2)}) %all-to-all-start.2) | async-done | bytes 16416 | tf_op jit(solution)/shard_map/all_to_all | solution.py:534
  (36 shorter events, 8.8 us)
Async XLA Ops:
  7.6 15.8 %collective-permute-start = (f32[784,128]{1,0:T(8,128)}, f32[784,128]{1,0:T(8,128)S(1)}, u32[]{:S(2)}, u32[]{:S(2)}) collective-permute-start(f32[784,128]{1,0:T(8,128)} %get-tuple-element.45), channel_id=1, source_target_pairs={{0,1},{1,0},{2,3},{3,2},{4,5},{5,4},{6,7},{7,6},{8,9},{9,8},{10,11... | collective-permute-start | bytes 1204232 | tf_op jit(solution)/shard_map/ppermute | solution.py:466
  18.0 12.8 %copy-start = (f32[2,1,64,512]{3,2,1,0:T(8,128)S(1)}, f32[2,1,64,512]{3,2,1,0:T(8,128)}, u32[]{:S(2)}) copy-start(f32[2,1,64,512]{3,2,1,0:T(8,128)} %param.9) | copy-start | bytes 786436
  18.0 12.8 %copy-start.5 = (f32[1,64,512]{2,1,0:T(8,128)S(1)}, f32[1,64,512]{2,1,0:T(8,128)}, u32[]{:S(2)}) copy-start(f32[1,64,512]{2,1,0:T(8,128)} %param.10) | copy-start | bytes 393220
  18.0 12.8 %all-to-all-start = ((f32[4,272,128]{2,1,0:T(8,128)}), f32[4,272,128]{2,1,0:T(8,128)S(1)}, u32[]{:S(2)}, u32[]{:S(2)}) async-start(f32[4,272,128]{2,1,0:T(8,128)} %get-tuple-element.39), calls=%async_computation | async-start | bytes 1114112 | tf_op jit(solution)/shard_map/all_to_all | solution.py:500
  21.7 12.4 %collective-permute-start.1 = (f32[784,128]{1,0:T(8,128)}, f32[784,128]{1,0:T(8,128)S(1)}, u32[]{:S(2)}, u32[]{:S(2)}) collective-permute-start(f32[784,128]{1,0:T(8,128)} %get-tuple-element.50), channel_id=1, source_target_pairs={{0,2},{1,3},{2,0},{3,1},{4,6},{5,7},{6,4},{7,5},{8,10},{9,11},{10,... | collective-permute-start | bytes 1204232 | tf_op jit(solution)/shard_map/ppermute | solution.py:466
  23.3 19.0 %collective-permute-start.2 = (f32[784,128]{1,0:T(8,128)}, f32[784,128]{1,0:T(8,128)S(1)}, u32[]{:S(2)}, u32[]{:S(2)}) collective-permute-start(f32[784,128]{1,0:T(8,128)} %get-tuple-element.51), channel_id=1, source_target_pairs={{0,3},{1,2},{2,1},{3,0},{4,7},{5,6},{6,5},{7,4},{8,11},{9,10},{10,... | collective-permute-start | bytes 1204232 | tf_op jit(solution)/shard_map/ppermute | solution.py:466
  23.4 18.9 %copy-start.1 = (f32[784,128]{1,0:T(8,128)S(1)}, f32[784,128]{1,0:T(8,128)}, u32[]{:S(2)}) copy-start(f32[784,128]{1,0:T(8,128)} %get-tuple-element.44.rest_0_) | copy-start | bytes 1204228
  23.4 25.9 %collective-permute-start.3 = (f32[768,128]{1,0:T(8,128)}, f32[768,128]{1,0:T(8,128)S(1)}, u32[]{:S(2)}, u32[]{:S(2)}) collective-permute-start(f32[768,128]{1,0:T(8,128)} %get-tuple-element.56), channel_id=1, source_target_pairs={{0,1},{1,0},{2,3},{3,2},{4,5},{5,4},{6,7},{7,6},{8,9},{9,8},{10,11... | collective-permute-start | bytes 1179656 | tf_op jit(solution)/shard_map/ppermute | solution.py:466
  25.2 37.1 %collective-permute-start.4 = (f32[768,128]{1,0:T(8,128)}, f32[768,128]{1,0:T(8,128)S(1)}, u32[]{:S(2)}, u32[]{:S(2)}) collective-permute-start(f32[768,128]{1,0:T(8,128)} %get-tuple-element.57), channel_id=1, source_target_pairs={{0,2},{1,3},{2,0},{3,1},{4,6},{5,7},{6,4},{7,5},{8,10},{9,11},{10,... | collective-permute-start | bytes 1179656 | tf_op jit(solution)/shard_map/ppermute | solution.py:466
  26.8 43.4 %collective-permute-start.5 = (f32[768,128]{1,0:T(8,128)}, f32[768,128]{1,0:T(8,128)}, u32[]{:S(2)}, u32[]{:S(2)}) collective-permute-start(f32[768,128]{1,0:T(8,128)} %get-tuple-element.58), channel_id=1, source_target_pairs={{0,3},{1,2},{2,1},{3,0},{4,7},{5,6},{6,5},{7,4},{8,11},{9,10},{10,... | collective-permute-start | bytes 1179656 | tf_op jit(solution)/shard_map/ppermute | solution.py:466
  32.9 11.3 %copy-start.3 = (f32[64,640]{1,0:T(8,128)}, f32[64,640]{1,0:T(8,128)S(1)}, u32[]{:S(2)}) copy-start(f32[64,640]{1,0:T(8,128)S(1)} %get-tuple-element.42.cy_ref) | copy-start | bytes 491524
  32.9 11.3 %copy-start.8 = (f32[2,64,640]{2,1,0:T(8,128)}, f32[2,64,640]{2,1,0:T(8,128)S(1)}, u32[]{:S(2)}) copy-start(f32[2,64,640]{2,1,0:T(8,128)S(1)} %get-tuple-element.43.u_ref) | copy-start | bytes 983044
  44.2 28.2 %collective-permute-start.6 = (f32[512,128]{1,0:T(8,128)S(1)}, f32[512,128]{1,0:T(8,128)S(1)}, u32[]{:S(2)}, u32[]{:S(2)}) collective-permute-start(f32[512,128]{1,0:T(8,128)S(1)} %get-tuple-element.62), channel_id=1, source_target_pairs={{0,4},{1,5},{2,6},{3,7},{4,0},{5,1},{6,2},{7,3},{8,12},{9,13},{10,... | collective-permute-start | bytes 786440 | tf_op jit(solution)/shard_map/ppermute | solution.py:466
  47.2 25.2 %collective-permute-start.7 = (f32[512,128]{1,0:T(8,128)S(1)}, f32[512,128]{1,0:T(8,128)S(1)}, u32[]{:S(2)}, u32[]{:S(2)}) collective-permute-start(f32[512,128]{1,0:T(8,128)S(1)} %get-tuple-element.63), channel_id=1, source_target_pairs={{0,4},{1,5},{2,6},{3,7},{4,0},{5,1},{6,2},{7,3},{8,12},{9,13},{10,... | collective-permute-start | bytes 786440 | tf_op jit(solution)/shard_map/ppermute | solution.py:466
  47.3 22.9 %copy-start.2 = (f32[768,128]{1,0:T(8,128)S(1)}, f32[768,128]{1,0:T(8,128)}, u32[]{:S(2)}) copy-start(f32[768,128]{1,0:T(8,128)} %get-tuple-element.55.rest_0_) | copy-start | bytes 1179652
  75.6 22.1 %copy-start.4 = (f32[64,640]{1,0:T(8,128)S(1)}, f32[64,640]{1,0:T(8,128)}, u32[]{:S(2)}) copy-start(f32[64,640]{1,0:T(8,128)} %copy-done.3) | copy-start | bytes 491524
  75.6 22.1 %copy-start.7 = (f32[2,64,640]{2,1,0:T(8,128)S(1)}, f32[2,64,640]{2,1,0:T(8,128)}, u32[]{:S(2)}) copy-start(f32[2,64,640]{2,1,0:T(8,128)} %copy-done.6) | copy-start | bytes 983044
  75.6 22.1 %copy-start.9 = (f32[2,64,640]{2,1,0:T(8,128)S(1)}, f32[2,64,640]{2,1,0:T(8,128)}, u32[]{:S(2)}) copy-start(f32[2,64,640]{2,1,0:T(8,128)} %copy-done.8) | copy-start | bytes 983044
  75.6 22.1 %all-to-all-start.1 = ((f32[4,6,16,640]{3,2,1,0:T(8,128)}), f32[4,6,16,640]{3,2,1,0:T(8,128)S(1)}, u32[]{:S(2)}, u32[]{:S(2)}) async-start(f32[4,6,16,640]{3,2,1,0:T(8,128)} %shard_map.110), calls=%async_computation.1 | async-start | bytes 1966080 | tf_op jit(solution)/shard_map/all_to_all | solution.py:527
  79.2 13.2 %collective-permute-start.8 = (f32[2,16,640]{2,1,0:T(8,128)S(1)}, f32[2,16,640]{2,1,0:T(8,128)S(1)}, u32[]{:S(2)}, u32[]{:S(2)}) collective-permute-start(f32[2,16,640]{2,1,0:T(8,128)S(1)} %get-tuple-element.64), channel_id=1, source_target_pairs={{0,4},{1,5},{2,6},{3,7},{4,0},{5,1},{6,2},{7,3},{8,12},{9,13},{10,... | collective-permute-start | bytes 245768 | tf_op jit(solution)/shard_map/ppermute | solution.py:470
  81.2 12.1 %collective-permute-start.9 = (f32[2,16,640]{2,1,0:T(8,128)S(1)}, f32[2,16,640]{2,1,0:T(8,128)S(1)}, u32[]{:S(2)}, u32[]{:S(2)}) collective-permute-start(f32[2,16,640]{2,1,0:T(8,128)S(1)} %get-tuple-element.65), channel_id=1, source_target_pairs={{0,12},{1,13},{2,14},{3,15},{4,8},{5,9},{6,10},{7,11},{8,4},{9,5},... | collective-permute-start | bytes 245768 | tf_op jit(solution)/shard_map/ppermute | solution.py:470
  82.0 15.2 %collective-permute-start.10 = (f32[2,16,640]{2,1,0:T(8,128)S(1)}, f32[2,16,640]{2,1,0:T(8,128)S(1)}, u32[]{:S(2)}, u32[]{:S(2)}) collective-permute-start(f32[2,16,640]{2,1,0:T(8,128)S(1)} %get-tuple-element.66), channel_id=1, source_target_pairs={{0,20},{1,21},{2,22},{3,23},{4,16},{5,17},{6,18},{7,19},{8,28},{9,... | collective-permute-start | bytes 245768 | tf_op jit(solution)/shard_map/ppermute | solution.py:470
  85.0 12.7 %collective-permute-start.11 = (f32[2,16,640]{2,1,0:T(8,128)S(1)}, f32[2,16,640]{2,1,0:T(8,128)S(1)}, u32[]{:S(2)}, u32[]{:S(2)}) collective-permute-start(f32[2,16,640]{2,1,0:T(8,128)S(1)} %get-tuple-element.67), channel_id=1, source_target_pairs={{0,28},{1,29},{2,30},{3,31},{4,24},{5,25},{6,26},{7,27},{8,20},{9,... | collective-permute-start | bytes 245768 | tf_op jit(solution)/shard_map/ppermute | solution.py:470
  105.2 10.8 %all-to-all-start.2 = ((f32[32,1,128]{2,1,0:T(1,128)}), f32[32,1,128]{2,1,0:T(1,128)S(1)}, u32[]{:S(2)}, u32[]{:S(2)}) async-start(f32[32,1,128]{2,1,0:T(1,128)} %get-tuple-element.68), calls=%async_computation.2 | async-start | bytes 32768 | tf_op jit(solution)/shard_map/all_to_all | solution.py:534
  (1 other events, 0.7 us)

commit v6 on v5

--- a/solution.py
+++ b/solution.py
@@ -431,6 +431,7 @@
         out_shape=out_shape,
         scratch_shapes=list(scratch),
         compiler_params=pltpu.CompilerParams(vmem_limit_bytes=limit),
+        cost_estimate=pl.CostEstimate(flops=1, bytes_accessed=1, transcendentals=0),
         **{name: value for name, value in params.items() if value is not None},
     )
 

time: 118 us -> 118 us (level)
  no operation moved by 1% of the time
where the time goes in v6:
time: 118 us; the launch traced here: 117 us
  waiting for transfers between devices  52.1 us (44%)
  Pallas kernels  35 us (30%)
  starting transfers between devices  28.5 us (24%)
    ppermute x8, waiting for transfers between devices, to_half(): return lax.ppermute(block, 'py', [(i, i ^ k) for i in range(groups)])  30.4 us
    ppermute x4, waiting for transfers between devices, across(): lax.ppermute(parts[k], ('px', 'py'), [(i * groups + j, (i ^ k) * groups +...  12.2 us
    ppermute x8, starting transfers between devices, to_half(): return lax.ppermute(block, 'py', [(i, i ^ k) for i in range(groups)])  11.3 us
    pallas_call x1, Pallas kernels, shards(): call(functools.partial(solve_kernel, spans), (f32(F, nx, width),) * 2 + (...  7.47 us
    pallas_call x1, Pallas kernels, shards(): call(functools.partial(pack_products_kernel, groups, cap), (f32(2 * cap,...  7.46 us
    pallas_call x1, Pallas kernels, shards(): call(functools.partial(pack_weights_kernel, groups, cap, blk, block_rows)...  6.91 us
    ppermute x4, starting transfers between devices, across(): lax.ppermute(parts[k], ('px', 'py'), [(i * groups + j, (i ^ k) * groups +...  6.25 us
    all_to_all x1, waiting for transfers between devices, shards(): lax.all_to_all(dots, ('px', 'py'), split_axis=0, concat_axis=0, tiled=True)  5.5 us
  transfers between devices with their start and end apart: 15, of which 10 were waited for; matrix products, arithmetic and copies ran while one was open for 0% of the time, Pallas kernels for 14%

profile of v6, /device:TPU:0, one launch (start us, length us, event | category | flops | bytes accessed | tf_op | source)
XLA Modules:
  0.0 117.2 jit_solution(10157715494159949353)
XLA Ops:
  0.6 6.9 %shard_map.104 = (f32[784,128]{1,0:T(8,128)}, f32[784,128]{1,0:T(8,128)}, f32[784,128]{1,0:T(8,128)}, f32[784,128]{1,0:T(8,128)}, s32[8,128]{1,0:T(8,128)}) custom-call(s32[8,128]{1,0:T(8,128)} %bitcast.19, s32[8,128]{1,0:T(8,128)} %bitcast.20, s32[8,128]{1,0:T(8,128)} %bitcast.21, f32[8,128]{1,0:T(8,128)} %bitcast.22, f32[1024,128]{1,0:T(8,128)} %w_hbm.3), custom_call_target="tpu_custom_call" | custom-call | flops 1 | bytes 1 | tf_op jit(solution)/shard_map/pallas_call | solution.py:476
  7.6 3.0 %collective-permute-start = (f32[784,128]{1,0:T(8,128)}, f32[784,128]{1,0:T(8,128)S(1)}, u32[]{:S(2)}, u32[]{:S(2)}) collective-permute-start(f32[784,128]{1,0:T(8,128)} %get-tuple-element.45), channel_id=1, source_target_pairs={{0,1},{1,0},{2,3},{3,2},{4,5},{5,4},{6,7},{7,6},{8,9},{9,8},{10,11... | collective-permute-start | bytes 1204232 | tf_op jit(solution)/shard_map/ppermute | solution.py:467
  10.6 7.5 %shard_map.105 = (f32[768,128]{1,0:T(8,128)}, f32[768,128]{1,0:T(8,128)}, f32[768,128]{1,0:T(8,128)}, f32[768,128]{1,0:T(8,128)}, f32[4,272,128]{2,1,0:T(8,128)}) custom-call(s32[8,128]{1,0:T(8,128)} %get-tuple-element.38.slot_ref, f32[1024,128]{1,0:T(8,128)} %w_hbm.3, f32[1024,128]{1,0:T(8,128)} %d_hbm.1, f32[16,2048]{1,0:T(8,128)} %bitcast.18, ...), custom_call_target="tpu_custom_call" | custom-call | flops 1 | bytes 1 | tf_op jit(solution)/shard_map/pallas_call | solution.py:488
  18.0 3.6 %all-to-all-start = ((f32[4,272,128]{2,1,0:T(8,128)}), f32[4,272,128]{2,1,0:T(8,128)S(1)}, u32[]{:S(2)}, u32[]{:S(2)}) async-start(f32[4,272,128]{2,1,0:T(8,128)} %get-tuple-element.39), calls=%async_computation | async-start | bytes 1114112 | tf_op jit(solution)/shard_map/all_to_all | solution.py:501
  21.7 1.6 %collective-permute-start.1 = (f32[784,128]{1,0:T(8,128)}, f32[784,128]{1,0:T(8,128)S(1)}, u32[]{:S(2)}, u32[]{:S(2)}) collective-permute-start(f32[784,128]{1,0:T(8,128)} %get-tuple-element.50), channel_id=1, source_target_pairs={{0,2},{1,3},{2,0},{3,1},{4,6},{5,7},{6,4},{7,5},{8,10},{9,11},{10,... | collective-permute-start | bytes 1204232 | tf_op jit(solution)/shard_map/ppermute | solution.py:467
  23.4 1.9 %collective-permute-start.3 = (f32[768,128]{1,0:T(8,128)}, f32[768,128]{1,0:T(8,128)S(1)}, u32[]{:S(2)}, u32[]{:S(2)}) collective-permute-start(f32[768,128]{1,0:T(8,128)} %get-tuple-element.56), channel_id=1, source_target_pairs={{0,1},{1,0},{2,3},{3,2},{4,5},{5,4},{6,7},{7,6},{8,9},{9,8},{10,11... | collective-permute-start | bytes 1179656 | tf_op jit(solution)/shard_map/ppermute | solution.py:467
  25.2 1.6 %collective-permute-start.4 = (f32[768,128]{1,0:T(8,128)}, f32[768,128]{1,0:T(8,128)S(1)}, u32[]{:S(2)}, u32[]{:S(2)}) collective-permute-start(f32[768,128]{1,0:T(8,128)} %get-tuple-element.57), channel_id=1, source_target_pairs={{0,2},{1,3},{2,0},{3,1},{4,6},{5,7},{6,4},{7,5},{8,10},{9,11},{10,... | collective-permute-start | bytes 1179656 | tf_op jit(solution)/shard_map/ppermute | solution.py:467
  26.9 4.0 %all-to-all-done.swap_ref = f32[4,272,128]{2,1,0:T(8,128)S(1)} async-done(((f32[4,272,128]{2,1,0:T(8,128)}), f32[4,272,128]{2,1,0:T(8,128)S(1)}, u32[]{:S(2)}, u32[]{:S(2)}) %all-to-all-start) | async-done | bytes 557088 | tf_op jit(solution)/shard_map/all_to_all | solution.py:501
  34.0 8.2 %collective-permute-done.2.rest_3_ = f32[784,128]{1,0:T(8,128)S(1)} collective-permute-done((f32[784,128]{1,0:T(8,128)}, f32[784,128]{1,0:T(8,128)S(1)}, u32[]{:S(2)}, u32[]{:S(2)}) %collective-permute-start.2) | collective-permute-done | bytes 401440 | tf_op jit(solution)/shard_map/ppermute | solution.py:467
  42.3 1.9 %shard_map.107 = (f32[4,16,128]{2,1,0:T(8,128)S(1)}, f32[512,128]{1,0:T(8,128)S(1)}, f32[512,128]{1,0:T(8,128)S(1)}) custom-call(f32[784,128]{1,0:T(8,128)S(1)} %copy-done.1, f32[784,128]{1,0:T(8,128)S(1)} %collective-permute-done.rest_1_, f32[784,128]{1,0:T(8,128)S(1)} %collective-permute-done.1.rest_2_, f32[784,128]{1,0:T(8,128)S(1)} %collective-permute-done.2.rest_3_, ...), custom_call_target="tpu_custom_call" | custom-call | flops 1 | bytes 1 | tf_op jit(solution)/shard_map/pallas_call | solution.py:508
  44.2 3.0 %collective-permute-start.6 = (f32[512,128]{1,0:T(8,128)S(1)}, f32[512,128]{1,0:T(8,128)S(1)}, u32[]{:S(2)}, u32[]{:S(2)}) collective-permute-start(f32[512,128]{1,0:T(8,128)S(1)} %get-tuple-element.62), channel_id=1, source_target_pairs={{0,4},{1,5},{2,6},{3,7},{4,0},{5,1},{6,2},{7,3},{8,12},{9,13},{10,... | collective-permute-start | bytes 786440 | tf_op jit(solution)/shard_map/ppermute | solution.py:467
  47.3 1.9 %shard_map.108 = (f32[4,16,128]{2,1,0:T(8,128)S(1)}, f32[512,128]{1,0:T(8,128)S(1)}, f32[512,128]{1,0:T(8,128)S(1)}) custom-call(f32[784,128]{1,0:T(8,128)S(1)} %copy-done.1, f32[784,128]{1,0:T(8,128)S(1)} %collective-permute-done.rest_1_, f32[784,128]{1,0:T(8,128)S(1)} %collective-permute-done.1.rest_2_, f32[784,128]{1,0:T(8,128)S(1)} %collective-permute-done.2.rest_3_, ...), custom_call_target="tpu_custom_call" | custom-call | flops 1 | bytes 1 | tf_op jit(solution)/shard_map/pallas_call | solution.py:508
  49.2 13.1 %collective-permute-done.4.rest_2_ = f32[768,128]{1,0:T(8,128)S(1)} collective-permute-done((f32[768,128]{1,0:T(8,128)}, f32[768,128]{1,0:T(8,128)S(1)}, u32[]{:S(2)}, u32[]{:S(2)}) %collective-permute-start.4) | collective-permute-done | bytes 393248 | tf_op jit(solution)/shard_map/ppermute | solution.py:467
  62.4 7.8 %collective-permute-done.5.rest_3_ = f32[768,128]{1,0:T(8,128)} collective-permute-done((f32[768,128]{1,0:T(8,128)}, f32[768,128]{1,0:T(8,128)}, u32[]{:S(2)}, u32[]{:S(2)}) %collective-permute-start.5) | collective-permute-done | bytes 393248 | tf_op jit(solution)/shard_map/ppermute | solution.py:467
  70.2 2.2 %shard_map.109 = (f32[4,16,128]{2,1,0:T(8,128)S(1)}, f32[2,16,640]{2,1,0:T(8,128)S(1)}, f32[2,16,640]{2,1,0:T(8,128)S(1)}, f32[2,16,640]{2,1,0:T(8,128)S(1)}, f32[2,16,640]{2,1,0:T(8,128)S(1)}) custom-call(f32[4,16,128]{2,1,0:T(8,128)S(1)} %get-tuple-element.54.meta_ref, f32[768,128]{1,0:T(8,128)S(1)} %copy-done.2, ...), custom_call_target="tpu_custom_call" | custom-call | flops 1 | bytes 1 | tf_op jit(solution)/shard_map/pallas_call | solution.py:517
  72.4 3.1 %shard_map.110 = f32[4,6,16,640]{3,2,1,0:T(8,128)} custom-call(f32[4,16,128]{2,1,0:T(8,128)S(1)} %get-tuple-element.59.meta_ref, f32[512,128]{1,0:T(8,128)S(1)} %get-tuple-element.60.d_ref, f32[512,128]{1,0:T(8,128)S(1)} %get-tuple-element.61.e_ref, f32[512,128]{1,0:T(8,128)S(1)} %collective-permute-done.6.far_d_ref, ...), custom_call_target="tpu_custom_call" | custom-call | flops 1 | bytes 1 | tf_op jit(solution)/shard_map/pallas_call | solution.py:523
  75.6 3.6 %all-to-all-start.1 = ((f32[4,6,16,640]{3,2,1,0:T(8,128)}), f32[4,6,16,640]{3,2,1,0:T(8,128)S(1)}, u32[]{:S(2)}, u32[]{:S(2)}) async-start(f32[4,6,16,640]{3,2,1,0:T(8,128)} %shard_map.110), calls=%async_computation.1 | async-start | bytes 1966080 | tf_op jit(solution)/shard_map/all_to_all | solution.py:528
  79.2 2.0 %collective-permute-start.8 = (f32[2,16,640]{2,1,0:T(8,128)S(1)}, f32[2,16,640]{2,1,0:T(8,128)S(1)}, u32[]{:S(2)}, u32[]{:S(2)}) collective-permute-start(f32[2,16,640]{2,1,0:T(8,128)S(1)} %get-tuple-element.64), channel_id=1, source_target_pairs={{0,4},{1,5},{2,6},{3,7},{4,0},{5,1},{6,2},{7,3},{8,12},{9,13},{10,... | collective-permute-start | bytes 245768 | tf_op jit(solution)/shard_map/ppermute | solution.py:471
  82.0 3.0 %collective-permute-start.10 = (f32[2,16,640]{2,1,0:T(8,128)S(1)}, f32[2,16,640]{2,1,0:T(8,128)S(1)}, u32[]{:S(2)}, u32[]{:S(2)}) collective-permute-start(f32[2,16,640]{2,1,0:T(8,128)S(1)} %get-tuple-element.66), channel_id=1, source_target_pairs={{0,20},{1,21},{2,22},{3,23},{4,16},{5,17},{6,18},{7,19},{8,28},{9,... | collective-permute-start | bytes 245768 | tf_op jit(solution)/shard_map/ppermute | solution.py:471
  85.5 7.0 %collective-permute-done.8.rest_0_ = f32[2,16,640]{2,1,0:T(8,128)S(1)} collective-permute-done((f32[2,16,640]{2,1,0:T(8,128)S(1)}, f32[2,16,640]{2,1,0:T(8,128)S(1)}, u32[]{:S(2)}, u32[]{:S(2)}) %collective-permute-start.8) | collective-permute-done | bytes 81952 | tf_op jit(solution)/shard_map/ppermute | solution.py:471
  93.3 3.9 %collective-permute-done.10.rest_2_ = f32[2,16,640]{2,1,0:T(8,128)S(1)} collective-permute-done((f32[2,16,640]{2,1,0:T(8,128)S(1)}, f32[2,16,640]{2,1,0:T(8,128)S(1)}, u32[]{:S(2)}, u32[]{:S(2)}) %collective-permute-start.10) | collective-permute-done | bytes 81952 | tf_op jit(solution)/shard_map/ppermute | solution.py:471
  97.7 7.5 %shard_map.111 = (f32[2,64,512]{2,1,0:T(8,128)S(1)}, f32[2,64,512]{2,1,0:T(8,128)S(1)}, f32[2,64,640]{2,1,0:T(8,128)S(1)}, f32[32,1,128]{2,1,0:T(1,128)}) custom-call(f32[2,64,640]{2,1,0:T(8,128)S(1)} %copy-done.7, f32[64,640]{1,0:T(8,128)S(1)} %get-tuple-element.41.cx_ref, f32[64,640]{1,0:T(8,128)S(1)} %copy-done.4, f32[2,64,640]{2,1,0:T(8,128)S(1)} %copy-done.9, ...), custom_call_target="tpu_custom_call" | custom-call | flops 1 | bytes 1 | tf_op jit(solution)/shard_map/pallas_call | solution.py:530
  105.2 3.7 %all-to-all-start.2 = ((f32[32,1,128]{2,1,0:T(1,128)}), f32[32,1,128]{2,1,0:T(1,128)S(1)}, u32[]{:S(2)}, u32[]{:S(2)}) async-start(f32[32,1,128]{2,1,0:T(1,128)} %get-tuple-element.68), calls=%async_computation.2 | async-start | bytes 32768 | tf_op jit(solution)/shard_map/all_to_all | solution.py:535
  110.5 5.5 %all-to-all-done.2.dots_ref = f32[32,1,128]{2,1,0:T(1,128)S(1)} async-done(((f32[32,1,128]{2,1,0:T(1,128)}), f32[32,1,128]{2,1,0:T(1,128)S(1)}, u32[]{:S(2)}, u32[]{:S(2)}) %all-to-all-start.2) | async-done | bytes 16416 | tf_op jit(solution)/shard_map/all_to_all | solution.py:535
  (36 shorter events, 8.8 us)
Async XLA Ops:
  7.6 15.8 %collective-permute-start = (f32[784,128]{1,0:T(8,128)}, f32[784,128]{1,0:T(8,128)S(1)}, u32[]{:S(2)}, u32[]{:S(2)}) collective-permute-start(f32[784,128]{1,0:T(8,128)} %get-tuple-element.45), channel_id=1, source_target_pairs={{0,1},{1,0},{2,3},{3,2},{4,5},{5,4},{6,7},{7,6},{8,9},{9,8},{10,11... | collective-permute-start | bytes 1204232 | tf_op jit(solution)/shard_map/ppermute | solution.py:467
  18.0 12.8 %copy-start = (f32[2,1,64,512]{3,2,1,0:T(8,128)S(1)}, f32[2,1,64,512]{3,2,1,0:T(8,128)}, u32[]{:S(2)}) copy-start(f32[2,1,64,512]{3,2,1,0:T(8,128)} %param.9) | copy-start | bytes 786436
  18.0 12.8 %copy-start.5 = (f32[1,64,512]{2,1,0:T(8,128)S(1)}, f32[1,64,512]{2,1,0:T(8,128)}, u32[]{:S(2)}) copy-start(f32[1,64,512]{2,1,0:T(8,128)} %param.10) | copy-start | bytes 393220
  18.0 12.8 %all-to-all-start = ((f32[4,272,128]{2,1,0:T(8,128)}), f32[4,272,128]{2,1,0:T(8,128)S(1)}, u32[]{:S(2)}, u32[]{:S(2)}) async-start(f32[4,272,128]{2,1,0:T(8,128)} %get-tuple-element.39), calls=%async_computation | async-start | bytes 1114112 | tf_op jit(solution)/shard_map/all_to_all | solution.py:501
  21.7 12.4 %collective-permute-start.1 = (f32[784,128]{1,0:T(8,128)}, f32[784,128]{1,0:T(8,128)S(1)}, u32[]{:S(2)}, u32[]{:S(2)}) collective-permute-start(f32[784,128]{1,0:T(8,128)} %get-tuple-element.50), channel_id=1, source_target_pairs={{0,2},{1,3},{2,0},{3,1},{4,6},{5,7},{6,4},{7,5},{8,10},{9,11},{10,... | collective-permute-start | bytes 1204232 | tf_op jit(solution)/shard_map/ppermute | solution.py:467
  23.3 19.0 %collective-permute-start.2 = (f32[784,128]{1,0:T(8,128)}, f32[784,128]{1,0:T(8,128)S(1)}, u32[]{:S(2)}, u32[]{:S(2)}) collective-permute-start(f32[784,128]{1,0:T(8,128)} %get-tuple-element.51), channel_id=1, source_target_pairs={{0,3},{1,2},{2,1},{3,0},{4,7},{5,6},{6,5},{7,4},{8,11},{9,10},{10,... | collective-permute-start | bytes 1204232 | tf_op jit(solution)/shard_map/ppermute | solution.py:467
  23.4 18.9 %copy-start.1 = (f32[784,128]{1,0:T(8,128)S(1)}, f32[784,128]{1,0:T(8,128)}, u32[]{:S(2)}) copy-start(f32[784,128]{1,0:T(8,128)} %get-tuple-element.44.rest_0_) | copy-start | bytes 1204228
  23.4 25.9 %collective-permute-start.3 = (f32[768,128]{1,0:T(8,128)}, f32[768,128]{1,0:T(8,128)S(1)}, u32[]{:S(2)}, u32[]{:S(2)}) collective-permute-start(f32[768,128]{1,0:T(8,128)} %get-tuple-element.56), channel_id=1, source_target_pairs={{0,1},{1,0},{2,3},{3,2},{4,5},{5,4},{6,7},{7,6},{8,9},{9,8},{10,11... | collective-permute-start | bytes 1179656 | tf_op jit(solution)/shard_map/ppermute | solution.py:467
  25.2 37.1 %collective-permute-start.4 = (f32[768,128]{1,0:T(8,128)}, f32[768,128]{1,0:T(8,128)S(1)}, u32[]{:S(2)}, u32[]{:S(2)}) collective-permute-start(f32[768,128]{1,0:T(8,128)} %get-tuple-element.57), channel_id=1, source_target_pairs={{0,2},{1,3},{2,0},{3,1},{4,6},{5,7},{6,4},{7,5},{8,10},{9,11},{10,... | collective-permute-start | bytes 1179656 | tf_op jit(solution)/shard_map/ppermute | solution.py:467
  26.8 43.4 %collective-permute-start.5 = (f32[768,128]{1,0:T(8,128)}, f32[768,128]{1,0:T(8,128)}, u32[]{:S(2)}, u32[]{:S(2)}) collective-permute-start(f32[768,128]{1,0:T(8,128)} %get-tuple-element.58), channel_id=1, source_target_pairs={{0,3},{1,2},{2,1},{3,0},{4,7},{5,6},{6,5},{7,4},{8,11},{9,10},{10,... | collective-permute-start | bytes 1179656 | tf_op jit(solution)/shard_map/ppermute | solution.py:467
  32.9 11.3 %copy-start.3 = (f32[64,640]{1,0:T(8,128)}, f32[64,640]{1,0:T(8,128)S(1)}, u32[]{:S(2)}) copy-start(f32[64,640]{1,0:T(8,128)S(1)} %get-tuple-element.42.cy_ref) | copy-start | bytes 491524
  32.9 11.3 %copy-start.8 = (f32[2,64,640]{2,1,0:T(8,128)}, f32[2,64,640]{2,1,0:T(8,128)S(1)}, u32[]{:S(2)}) copy-start(f32[2,64,640]{2,1,0:T(8,128)S(1)} %get-tuple-element.43.u_ref) | copy-start | bytes 983044
  44.2 28.2 %collective-permute-start.6 = (f32[512,128]{1,0:T(8,128)S(1)}, f32[512,128]{1,0:T(8,128)S(1)}, u32[]{:S(2)}, u32[]{:S(2)}) collective-permute-start(f32[512,128]{1,0:T(8,128)S(1)} %get-tuple-element.62), channel_id=1, source_target_pairs={{0,4},{1,5},{2,6},{3,7},{4,0},{5,1},{6,2},{7,3},{8,12},{9,13},{10,... | collective-permute-start | bytes 786440 | tf_op jit(solution)/shard_map/ppermute | solution.py:467
  47.2 25.2 %collective-permute-start.7 = (f32[512,128]{1,0:T(8,128)S(1)}, f32[512,128]{1,0:T(8,128)S(1)}, u32[]{:S(2)}, u32[]{:S(2)}) collective-permute-start(f32[512,128]{1,0:T(8,128)S(1)} %get-tuple-element.63), channel_id=1, source_target_pairs={{0,4},{1,5},{2,6},{3,7},{4,0},{5,1},{6,2},{7,3},{8,12},{9,13},{10,... | collective-permute-start | bytes 786440 | tf_op jit(solution)/shard_map/ppermute | solution.py:467
  47.3 22.9 %copy-start.2 = (f32[768,128]{1,0:T(8,128)S(1)}, f32[768,128]{1,0:T(8,128)}, u32[]{:S(2)}) copy-start(f32[768,128]{1,0:T(8,128)} %get-tuple-element.55.rest_0_) | copy-start | bytes 1179652
  75.6 22.1 %copy-start.4 = (f32[64,640]{1,0:T(8,128)S(1)}, f32[64,640]{1,0:T(8,128)}, u32[]{:S(2)}) copy-start(f32[64,640]{1,0:T(8,128)} %copy-done.3) | copy-start | bytes 491524
  75.6 22.1 %copy-start.7 = (f32[2,64,640]{2,1,0:T(8,128)S(1)}, f32[2,64,640]{2,1,0:T(8,128)}, u32[]{:S(2)}) copy-start(f32[2,64,640]{2,1,0:T(8,128)} %copy-done.6) | copy-start | bytes 983044
  75.6 22.1 %copy-start.9 = (f32[2,64,640]{2,1,0:T(8,128)S(1)}, f32[2,64,640]{2,1,0:T(8,128)}, u32[]{:S(2)}) copy-start(f32[2,64,640]{2,1,0:T(8,128)} %copy-done.8) | copy-start | bytes 983044
  75.6 22.1 %all-to-all-start.1 = ((f32[4,6,16,640]{3,2,1,0:T(8,128)}), f32[4,6,16,640]{3,2,1,0:T(8,128)S(1)}, u32[]{:S(2)}, u32[]{:S(2)}) async-start(f32[4,6,16,640]{3,2,1,0:T(8,128)} %shard_map.110), calls=%async_computation.1 | async-start | bytes 1966080 | tf_op jit(solution)/shard_map/all_to_all | solution.py:528
  79.2 13.2 %collective-permute-start.8 = (f32[2,16,640]{2,1,0:T(8,128)S(1)}, f32[2,16,640]{2,1,0:T(8,128)S(1)}, u32[]{:S(2)}, u32[]{:S(2)}) collective-permute-start(f32[2,16,640]{2,1,0:T(8,128)S(1)} %get-tuple-element.64), channel_id=1, source_target_pairs={{0,4},{1,5},{2,6},{3,7},{4,0},{5,1},{6,2},{7,3},{8,12},{9,13},{10,... | collective-permute-start | bytes 245768 | tf_op jit(solution)/shard_map/ppermute | solution.py:471
  81.2 12.1 %collective-permute-start.9 = (f32[2,16,640]{2,1,0:T(8,128)S(1)}, f32[2,16,640]{2,1,0:T(8,128)S(1)}, u32[]{:S(2)}, u32[]{:S(2)}) collective-permute-start(f32[2,16,640]{2,1,0:T(8,128)S(1)} %get-tuple-element.65), channel_id=1, source_target_pairs={{0,12},{1,13},{2,14},{3,15},{4,8},{5,9},{6,10},{7,11},{8,4},{9,5},... | collective-permute-start | bytes 245768 | tf_op jit(solution)/shard_map/ppermute | solution.py:471
  82.0 15.2 %collective-permute-start.10 = (f32[2,16,640]{2,1,0:T(8,128)S(1)}, f32[2,16,640]{2,1,0:T(8,128)S(1)}, u32[]{:S(2)}, u32[]{:S(2)}) collective-permute-start(f32[2,16,640]{2,1,0:T(8,128)S(1)} %get-tuple-element.66), channel_id=1, source_target_pairs={{0,20},{1,21},{2,22},{3,23},{4,16},{5,17},{6,18},{7,19},{8,28},{9,... | collective-permute-start | bytes 245768 | tf_op jit(solution)/shard_map/ppermute | solution.py:471
  85.0 12.7 %collective-permute-start.11 = (f32[2,16,640]{2,1,0:T(8,128)S(1)}, f32[2,16,640]{2,1,0:T(8,128)S(1)}, u32[]{:S(2)}, u32[]{:S(2)}) collective-permute-start(f32[2,16,640]{2,1,0:T(8,128)S(1)} %get-tuple-element.67), channel_id=1, source_target_pairs={{0,28},{1,29},{2,30},{3,31},{4,24},{5,25},{6,26},{7,27},{8,20},{9,... | collective-permute-start | bytes 245768 | tf_op jit(solution)/shard_map/ppermute | solution.py:471
  105.2 10.8 %all-to-all-start.2 = ((f32[32,1,128]{2,1,0:T(1,128)}), f32[32,1,128]{2,1,0:T(1,128)S(1)}, u32[]{:S(2)}, u32[]{:S(2)}) async-start(f32[32,1,128]{2,1,0:T(1,128)} %get-tuple-element.68), calls=%async_computation.2 | async-start | bytes 32768 | tf_op jit(solution)/shard_map/all_to_all | solution.py:535
  (1 other events, 0.7 us)

commit v7 on v5

--- a/solution.py
+++ b/solution.py
@@ -19,6 +19,8 @@
 Y_LINES = 16
 VMEM_BYTES = 32 * 1024 * 1024
 PACK_BYTES = 60 * 1024 * 1024
+FIRST = 100_000_000
+JOIN = 100_000_000
 
 
 def iota(shape, axis):
@@ -326,17 +328,23 @@
         sweep_y_into(u_out.at[f], u_out.at[f], cy_out)
 
 
-def solve_kernel(spans, c0_ref, cx_ref, cy_ref, u_ref, obs_ref, *rest):
-    sum_refs, (r_out, q_out, h_out, dots_out, vec, coef, work) = rest[:spans], rest[spans:]
+def join_kernel(spans, *rest):
+    parts, out = rest[:spans], rest[spans]
+    me = lax.axis_index("px")
+    for k, part in enumerate(parts):
+        for f in range(F):
+            out[f, pl.ds(pl.multiple_of((me ^ k) * LX, LX), LX), :] = part[f]
+
+
+def solve_kernel(c0_ref, cx_ref, cy_ref, u_ref, obs_ref, far_ref, r_out, q_out, h_out, dots_out,
+                 vec, coef, work):
     width = r_out.shape[2]
-    for p in range(spans):
-        for channel in range(3 * F):
-            coef[channel, p * LX:(p + 1) * LX, :] = obs_ref[p, channel]
-    me = lax.axis_index("px")
-    for k in range(spans):
-        rows = pl.ds(pl.multiple_of((me ^ k) * LX, LX), LX)
+    for p in range(obs_ref.shape[0]):
+        rows = slice(p * LX, (p + 1) * LX)
+        for channel in range(2 * F):
+            coef[channel, rows, :] = obs_ref[p, channel]
         for f in range(F):
-            coef[2 * F + f, rows, :] += sum_refs[k][f]
+            coef[2 * F + f, rows, :] = obs_ref[p, 2 * F + f] + far_ref[f, rows, :]
 
     def normal(f, values, tile):
         size = values.shape[0]
@@ -424,13 +432,15 @@
         residual_out[f] = r - first_weight * q + both * qq_ref[f]
 
 
-def call(kernel, out_shape, scratch=(), in_specs=None, out_specs=None, limit=VMEM_BYTES):
+def call(kernel, out_shape, scratch=(), in_specs=None, out_specs=None, limit=VMEM_BYTES,
+         weight=1):
     params = {"in_specs": in_specs, "out_specs": out_specs}
     return pl.pallas_call(
         kernel,
         out_shape=out_shape,
         scratch_shapes=list(scratch),
         compiler_params=pltpu.CompilerParams(vmem_limit_bytes=limit),
+        cost_estimate=pl.CostEstimate(flops=weight, bytes_accessed=weight, transcendentals=0),
         **{name: value for name, value in params.items() if value is not None},
     )
 
@@ -493,9 +503,9 @@
         (hbm,) * half + (local,),
         limit=PACK_BYTES,
     )(slots, obs_weight, innovation, coef_y[0], c0, cx)
-    w_blocks[1:] = [to_half(w_blocks[k], k) for k in range(1, half)]
-    w_blocks[1], *v_blocks[1:] = lax.optimization_barrier((w_blocks[1], *v_blocks[1:]))
-    v_blocks[1:] = [to_half(v_blocks[k], k) for k in range(1, half)]
+    for k in range(1, half):
+        w_blocks[k], v_blocks[k] = lax.optimization_barrier((to_half(w_blocks[k], k), v_blocks[k]))
+        v_blocks[k] = to_half(v_blocks[k], k)
 
     swap = lax.all_to_all(swap, "px", split_axis=0, concat_axis=0, tiled=True)
     c0_ext, cx_ext, cy_ext, u_ext, token = call(
@@ -503,22 +513,25 @@
         (f32(F, nx, ext), f32(nx, ext), f32(nx, ext), f32(F, nx, ext), f32(8, SEG)),
     )(c0, cx, swap)
 
-    def sum_weights(side, token):
+    def sum_weights(side, token, weight):
         return call(
             functools.partial(weights_kernel, half, cap, blk, side),
             (f32(half, meta_rows, SEG),) + (f32(ROWS, SEG),) * 2,
             [vmem(ROWS, 3 * SEG)],
+            weight=weight,
         )(*w_blocks, token)
 
-    meta, *side_across = sum_weights(1, token)
+    meta, *side_across = sum_weights(1, w_blocks[0], FIRST)
     side_across = [to_half(values, half) for values in side_across]
-    meta, *side = sum_weights(0, meta)
+    meta, *side = sum_weights(0, token, 1)
     meta, *sums_across = call(
         functools.partial(products_across_kernel, half, cap, blk),
         (f32(half, meta_rows, SEG),) + (f32(F, LX, ext),) * spans,
         [vmem(ROWS, 2 * SEG), vmem(ROWS, SEG)],
     )(meta, *v_blocks)
-    sums_across = across(sums_across)
+    far_sums = call(
+        functools.partial(join_kernel, spans), f32(F, nx, ext), weight=JOIN,
+    )(*across(sums_across))
     parts = call(
         functools.partial(products_kernel, half, cap, blk),
         f32(spans, 3 * F, LX, ext),
@@ -527,10 +540,10 @@
     parts = lax.all_to_all(parts, "px", split_axis=0, concat_axis=0, tiled=True)
 
     r, q, h, dots = call(
-        functools.partial(solve_kernel, spans),
+        solve_kernel,
         (f32(F, nx, width),) * 2 + (f32(F, nx, ext), f32(groups * spans, 1, SEG)),
         [vmem(3, F, nx, ext), vmem(3 * F, nx, ext), vmem(nx, ext)],
-    )(c0_ext, cx_ext, cy_ext, u_ext, parts, *sums_across)
+    )(c0_ext, cx_ext, cy_ext, u_ext, parts, far_sums)
     dots = lax.all_to_all(dots, ("px", "py"), split_axis=0, concat_axis=0, tiled=True)
     qq = call(last_kernel, f32(F, nx, width), [vmem(nx, ext)] * 2)(h, q, cx_ext, cy_ext)
     control, residual = call(finish_kernel, (f32(F, nx, width),) * 2)(dots, c0, r, q, qq)

time: 118 us -> 109 us (0.924)
  waiting for transfers between devices: 52.1 us -> 41.9 us
    ppermute x8, waiting for transfers between devices: 30.4 us -> 24.2 us  [to_half(): return lax.ppermute(block, 'py', [(i, i ^ k) for i in range(groups)])]
    all_to_all x1, waiting for transfers between devices: 3.95 us -> 0.01 us  [shards(): swap = lax.all_to_all(swap, 'px', split_axis=0, concat_axis=0, tiled=True)]
    pallas_call x1 -> x2, Pallas kernels: 7.47 us -> 7.46 us  [the longest x1 7.43 us: shards(): call(solve_kernel, (f32(F, nx, width),) * 2 + (f32(F, nx, ext), f32(group...]
  transfers between devices with their start and end apart: 15 -> 15, of which waited for: 10 -> 8; matrix products, arithmetic and copies ran while one was open for 0% -> 0% of each run, Pallas kernels for 14% -> 16%
where the time goes in v7:
time: 109 us; the launch traced here: 108 us
  waiting for transfers between devices  41.9 us (38%)
  Pallas kernels  36 us (33%)
  starting transfers between devices  28.2 us (26%)
  local copies, waits for them, and re-layouts  1.46 us (1%)
    ppermute x8, waiting for transfers between devices, to_half(): return lax.ppermute(block, 'py', [(i, i ^ k) for i in range(groups)])  24.2 us
    ppermute x4, waiting for transfers between devices, across(): lax.ppermute(parts[k], ('px', 'py'), [(i * groups + j, (i ^ k) * groups +...  12.1 us
    ppermute x8, starting transfers between devices, to_half(): return lax.ppermute(block, 'py', [(i, i ^ k) for i in range(groups)])  11 us
    pallas_call x1, Pallas kernels, shards(): call(functools.partial(pack_products_kernel, groups, cap), (f32(2 * cap,...  7.53 us
    pallas_call x1, Pallas kernels, shards(): call(solve_kernel, (f32(F, nx, width),) * 2 + (f32(F, nx, ext), f32(group...  7.43 us
    pallas_call x1, Pallas kernels, shards(): call(functools.partial(pack_weights_kernel, groups, cap, blk, block_rows)...  6.91 us
    ppermute x4, starting transfers between devices, across(): lax.ppermute(parts[k], ('px', 'py'), [(i * groups + j, (i ^ k) * groups +...  6.25 us
    all_to_all x1, waiting for transfers between devices, shards(): lax.all_to_all(dots, ('px', 'py'), split_axis=0, concat_axis=0, tiled=True)  5.5 us
  transfers between devices with their start and end apart: 15, of which 8 were waited for; matrix products, arithmetic and copies ran while one was open for 0% of the time, Pallas kernels for 16%

profile of v7, /device:TPU:0, one launch (start us, length us, event | category | flops | bytes accessed | tf_op | source)
XLA Modules:
  0.0 108.4 jit_solution(2137605501128117854)
XLA Ops:
  0.6 6.9 %shard_map.104 = (f32[784,128]{1,0:T(8,128)}, f32[784,128]{1,0:T(8,128)}, f32[784,128]{1,0:T(8,128)}, f32[784,128]{1,0:T(8,128)}, s32[8,128]{1,0:T(8,128)}) custom-call(s32[8,128]{1,0:T(8,128)} %bitcast.19, s32[8,128]{1,0:T(8,128)} %bitcast.20, s32[8,128]{1,0:T(8,128)} %bitcast.21, f32[8,128]{1,0:T(8,128)} %bitcast.22, f32[1024,128]{1,0:T(8,128)} %w_hbm.3), custom_call_target="tpu_custom_call" | custom-call | flops 1 | bytes 1 | tf_op jit(solution)/shard_map/pallas_call | solution.py:485
  7.5 3.0 %collective-permute-start = (f32[784,128]{1,0:T(8,128)}, f32[784,128]{1,0:T(8,128)S(1)}, u32[]{:S(2)}, u32[]{:S(2)}) collective-permute-start(f32[784,128]{1,0:T(8,128)} %get-tuple-element.46), channel_id=1, source_target_pairs={{0,1},{1,0},{2,3},{3,2},{4,5},{5,4},{6,7},{7,6},{8,9},{9,8},{10,11... | collective-permute-start | bytes 1204232 | tf_op jit(solution)/shard_map/ppermute | solution.py:476
  10.6 1.6 %collective-permute-start.1 = (f32[784,128]{1,0:T(8,128)}, f32[784,128]{1,0:T(8,128)S(1)}, u32[]{:S(2)}, u32[]{:S(2)}) collective-permute-start(f32[784,128]{1,0:T(8,128)} %get-tuple-element.49), channel_id=1, source_target_pairs={{0,2},{1,3},{2,0},{3,1},{4,6},{5,7},{6,4},{7,5},{8,10},{9,11},{10,... | collective-permute-start | bytes 1204232 | tf_op jit(solution)/shard_map/ppermute | solution.py:476
  12.1 7.5 %shard_map.105 = (f32[768,128]{1,0:T(8,128)}, f32[768,128]{1,0:T(8,128)}, f32[768,128]{1,0:T(8,128)}, f32[768,128]{1,0:T(8,128)}, f32[4,272,128]{2,1,0:T(8,128)}) custom-call(s32[8,128]{1,0:T(8,128)} %get-tuple-element.39.slot_ref, f32[1024,128]{1,0:T(8,128)} %w_hbm.3, f32[1024,128]{1,0:T(8,128)} %d_hbm.1, f32[16,2048]{1,0:T(8,128)} %bitcast.18, ...), custom_call_target="tpu_custom_call" | custom-call | flops 1 | bytes 1 | tf_op jit(solution)/shard_map/pallas_call | solution.py:497
  19.7 3.6 %all-to-all-start = ((f32[4,272,128]{2,1,0:T(8,128)}), f32[4,272,128]{2,1,0:T(8,128)S(1)}, u32[]{:S(2)}, u32[]{:S(2)}) async-start(f32[4,272,128]{2,1,0:T(8,128)} %get-tuple-element.40), calls=%async_computation | async-start | bytes 1114112 | tf_op jit(solution)/shard_map/all_to_all | solution.py:510
  23.3 6.6 %collective-permute-done.2.rest_3_ = f32[784,128]{1,0:T(8,128)S(1)} collective-permute-done((f32[784,128]{1,0:T(8,128)}, f32[784,128]{1,0:T(8,128)S(1)}, u32[]{:S(2)}, u32[]{:S(2)}) %collective-permute-start.2) | collective-permute-done | bytes 401440 | tf_op jit(solution)/shard_map/ppermute | solution.py:476
  29.9 2.7 %collective-permute-start.5 = (f32[768,128]{1,0:T(8,128)}, f32[768,128]{1,0:T(8,128)S(1)}, u32[]{:S(2)}, u32[]{:S(2)}) collective-permute-start(f32[768,128]{1,0:T(8,128)} %get-tuple-element.60), channel_id=1, source_target_pairs={{0,3},{1,2},{2,1},{3,0},{4,7},{5,6},{6,5},{7,4},{8,11},{9,10},{10,... | collective-permute-start | bytes 1179656 | tf_op jit(solution)/shard_map/ppermute | solution.py:476
  33.4 2.7 %shard_map.109 = (f32[4,16,128]{2,1,0:T(8,128)}, f32[512,128]{1,0:T(8,128)}, f32[512,128]{1,0:T(8,128)}) custom-call(f32[784,128]{1,0:T(8,128)S(1)} %copy-done, f32[784,128]{1,0:T(8,128)S(1)} %collective-permute-done.rest_1_, f32[784,128]{1,0:T(8,128)S(1)} %collective-permute-done.1.rest_2_, f32[784,128]{1,0:T(8,128)S(1)} %collective-permute-done.2.rest_3_, ...), custom_call_target="tpu_custom_call" | custom-call | flops 100000000 | bytes 100000000 | tf_op jit(solution)/shard_map/pallas_call | solution.py:517
  36.1 2.8 %collective-permute-start.6 = (f32[512,128]{1,0:T(8,128)}, f32[512,128]{1,0:T(8,128)}, u32[]{:S(2)}, u32[]{:S(2)}) collective-permute-start(f32[512,128]{1,0:T(8,128)} %get-tuple-element.64), channel_id=1, source_target_pairs={{0,4},{1,5},{2,6},{3,7},{4,0},{5,1},{6,2},{7,3},{8,12},{9,13},{10,... | collective-permute-start | bytes 786440 | tf_op jit(solution)/shard_map/ppermute | solution.py:476
  39.0 1.3 %shard_map.106 = (f32[2,64,640]{2,1,0:T(8,128)S(1)}, f32[64,640]{1,0:T(8,128)S(1)}, f32[64,640]{1,0:T(8,128)S(1)}, f32[2,64,640]{2,1,0:T(8,128)S(1)}, f32[8,128]{1,0:T(8,128)S(1)}) custom-call(f32[2,64,512]{2,1,0:T(8,128)S(1)} %bitcast.14, f32[64,512]{1,0:T(8,128)S(1)} %bitcast.17, f32[4,272,128]{2,1,0:T(8,128)S(1)} %all-to-all-done.swap_ref), custom_call_target="tpu_custom_call" | custom-call | flops 1 | bytes 1 | tf_op jit(solution)/shard_map/pallas_call | solution.py:511
  41.0 1.9 %shard_map.107 = (f32[4,16,128]{2,1,0:T(8,128)S(1)}, f32[512,128]{1,0:T(8,128)S(1)}, f32[512,128]{1,0:T(8,128)S(1)}) custom-call(f32[784,128]{1,0:T(8,128)S(1)} %copy-done, f32[784,128]{1,0:T(8,128)S(1)} %collective-permute-done.rest_1_, f32[784,128]{1,0:T(8,128)S(1)} %collective-permute-done.1.rest_2_, f32[784,128]{1,0:T(8,128)S(1)} %collective-permute-done.2.rest_3_, ...), custom_call_target="tpu_custom_call" | custom-call | flops 1 | bytes 1 | tf_op jit(solution)/shard_map/pallas_call | solution.py:517
  43.0 11.4 %collective-permute-done.5.rest_3_ = f32[768,128]{1,0:T(8,128)S(1)} collective-permute-done((f32[768,128]{1,0:T(8,128)}, f32[768,128]{1,0:T(8,128)S(1)}, u32[]{:S(2)}, u32[]{:S(2)}) %collective-permute-start.5) | collective-permute-done | bytes 393248 | tf_op jit(solution)/shard_map/ppermute | solution.py:476
  54.4 6.2 %collective-permute-done.4.rest_2_ = f32[768,128]{1,0:T(8,128)S(1)} collective-permute-done((f32[768,128]{1,0:T(8,128)}, f32[768,128]{1,0:T(8,128)S(1)}, u32[]{:S(2)}, u32[]{:S(2)}) %collective-permute-start.4) | collective-permute-done | bytes 393248 | tf_op jit(solution)/shard_map/ppermute | solution.py:476
  60.6 2.2 %shard_map.108 = (f32[4,16,128]{2,1,0:T(8,128)S(1)}, f32[2,16,640]{2,1,0:T(8,128)S(1)}, f32[2,16,640]{2,1,0:T(8,128)S(1)}, f32[2,16,640]{2,1,0:T(8,128)S(1)}, f32[2,16,640]{2,1,0:T(8,128)S(1)}) custom-call(f32[4,16,128]{2,1,0:T(8,128)S(1)} %get-tuple-element.56.meta_ref, f32[768,128]{1,0:T(8,128)S(1)} %copy-done.2, ...), custom_call_target="tpu_custom_call" | custom-call | flops 1 | bytes 1 | tf_op jit(solution)/shard_map/pallas_call | solution.py:527
  62.8 3.3 %shard_map.110 = f32[4,6,16,640]{3,2,1,0:T(8,128)} custom-call(f32[4,16,128]{2,1,0:T(8,128)S(1)} %get-tuple-element.61.meta_ref, f32[512,128]{1,0:T(8,128)S(1)} %get-tuple-element.62.d_ref, f32[512,128]{1,0:T(8,128)S(1)} %get-tuple-element.63.e_ref, f32[512,128]{1,0:T(8,128)} %collective-permute-done.6.far_d_ref, ...), custom_call_target="tpu_custom_call" | custom-call | flops 1 | bytes 1 | tf_op jit(solution)/shard_map/pallas_call | solution.py:535
  66.1 3.6 %all-to-all-start.1 = ((f32[4,6,16,640]{3,2,1,0:T(8,128)}), f32[4,6,16,640]{3,2,1,0:T(8,128)S(1)}, u32[]{:S(2)}, u32[]{:S(2)}) async-start(f32[4,6,16,640]{3,2,1,0:T(8,128)} %shard_map.110), calls=%async_computation.1 | async-start | bytes 1966080 | tf_op jit(solution)/shard_map/all_to_all | solution.py:540
  69.8 1.9 %collective-permute-start.8 = (f32[2,16,640]{2,1,0:T(8,128)S(1)}, f32[2,16,640]{2,1,0:T(8,128)S(1)}, u32[]{:S(2)}, u32[]{:S(2)}) collective-permute-start(f32[2,16,640]{2,1,0:T(8,128)S(1)} %get-tuple-element.66), channel_id=1, source_target_pairs={{0,4},{1,5},{2,6},{3,7},{4,0},{5,1},{6,2},{7,3},{8,12},{9,13},{10,... | collective-permute-start | bytes 245768 | tf_op jit(solution)/shard_map/ppermute | solution.py:480
  72.5 2.9 %collective-permute-start.10 = (f32[2,16,640]{2,1,0:T(8,128)S(1)}, f32[2,16,640]{2,1,0:T(8,128)S(1)}, u32[]{:S(2)}, u32[]{:S(2)}) collective-permute-start(f32[2,16,640]{2,1,0:T(8,128)S(1)} %get-tuple-element.68), channel_id=1, source_target_pairs={{0,20},{1,21},{2,22},{3,23},{4,16},{5,17},{6,18},{7,19},{8,28},{9,... | collective-permute-start | bytes 245768 | tf_op jit(solution)/shard_map/ppermute | solution.py:480
  76.1 7.0 %collective-permute-done.8.rest_0_ = f32[2,16,640]{2,1,0:T(8,128)S(1)} collective-permute-done((f32[2,16,640]{2,1,0:T(8,128)S(1)}, f32[2,16,640]{2,1,0:T(8,128)S(1)}, u32[]{:S(2)}, u32[]{:S(2)}) %collective-permute-start.8) | collective-permute-done | bytes 81952 | tf_op jit(solution)/shard_map/ppermute | solution.py:480
  83.8 4.0 %collective-permute-done.10.rest_2_ = f32[2,16,640]{2,1,0:T(8,128)S(1)} collective-permute-done((f32[2,16,640]{2,1,0:T(8,128)S(1)}, f32[2,16,640]{2,1,0:T(8,128)S(1)}, u32[]{:S(2)}, u32[]{:S(2)}) %collective-permute-start.10) | collective-permute-done | bytes 81952 | tf_op jit(solution)/shard_map/ppermute | solution.py:480
  88.3 7.4 %shard_map.112 = (f32[2,64,512]{2,1,0:T(8,128)S(1)}, f32[2,64,512]{2,1,0:T(8,128)S(1)}, f32[2,64,640]{2,1,0:T(8,128)S(1)}, f32[32,1,128]{2,1,0:T(1,128)}) custom-call(f32[2,64,640]{2,1,0:T(8,128)S(1)} %copy-done.7, f32[64,640]{1,0:T(8,128)S(1)} %get-tuple-element.42.cx_ref, f32[64,640]{1,0:T(8,128)S(1)} %copy-done.4, f32[2,64,640]{2,1,0:T(8,128)S(1)} %copy-done.9, ...), custom_call_target="tpu_custom_call" | custom-call | flops 1 | bytes 1 | tf_op jit(solution)/shard_map/pallas_call | solution.py:542
  96.4 3.7 %all-to-all-start.2 = ((f32[32,1,128]{2,1,0:T(1,128)}), f32[32,1,128]{2,1,0:T(1,128)S(1)}, u32[]{:S(2)}, u32[]{:S(2)}) async-start(f32[32,1,128]{2,1,0:T(1,128)} %get-tuple-element.70), calls=%async_computation.2 | async-start | bytes 32768 | tf_op jit(solution)/shard_map/all_to_all | solution.py:547
  100.1 1.5 %shard_map.113.qq_ref = f32[2,64,512]{2,1,0:T(8,128)S(1)} custom-call(f32[2,64,640]{2,1,0:T(8,128)S(1)} %get-tuple-element.73.h_ref, f32[2,64,512]{2,1,0:T(8,128)S(1)} %get-tuple-element.72.q_ref, f32[64,640]{1,0:T(8,128)S(1)} %get-tuple-element.42.cx_ref, f32[64,640]{1,0:T(8,128)S(1)} %copy-done.4), custom_call_target="tpu_custom_call" | custom-call | flops 1 | bytes 1 | tf_op jit(solution)/shard_map/pallas_call | solution.py:548
  101.6 5.5 %all-to-all-done.2.dots_ref = f32[32,1,128]{2,1,0:T(1,128)S(1)} async-done(((f32[32,1,128]{2,1,0:T(1,128)}), f32[32,1,128]{2,1,0:T(1,128)S(1)}, u32[]{:S(2)}, u32[]{:S(2)}) %all-to-all-start.2) | async-done | bytes 16416 | tf_op jit(solution)/shard_map/all_to_all | solution.py:547
  (41 shorter events, 6.4 us)
Async XLA Ops:
  7.5 15.8 %collective-permute-start = (f32[784,128]{1,0:T(8,128)}, f32[784,128]{1,0:T(8,128)S(1)}, u32[]{:S(2)}, u32[]{:S(2)}) collective-permute-start(f32[784,128]{1,0:T(8,128)} %get-tuple-element.46), channel_id=1, source_target_pairs={{0,1},{1,0},{2,3},{3,2},{4,5},{5,4},{6,7},{7,6},{8,9},{9,8},{10,11... | collective-permute-start | bytes 1204232 | tf_op jit(solution)/shard_map/ppermute | solution.py:476
  10.6 12.8 %collective-permute-start.1 = (f32[784,128]{1,0:T(8,128)}, f32[784,128]{1,0:T(8,128)S(1)}, u32[]{:S(2)}, u32[]{:S(2)}) collective-permute-start(f32[784,128]{1,0:T(8,128)} %get-tuple-element.49), channel_id=1, source_target_pairs={{0,2},{1,3},{2,0},{3,1},{4,6},{5,7},{6,4},{7,5},{8,10},{9,11},{10,... | collective-permute-start | bytes 1204232 | tf_op jit(solution)/shard_map/ppermute | solution.py:476
  12.1 17.8 %collective-permute-start.2 = (f32[784,128]{1,0:T(8,128)}, f32[784,128]{1,0:T(8,128)S(1)}, u32[]{:S(2)}, u32[]{:S(2)}) collective-permute-start(f32[784,128]{1,0:T(8,128)} %get-tuple-element.52), channel_id=1, source_target_pairs={{0,3},{1,2},{2,1},{3,0},{4,7},{5,6},{6,5},{7,4},{8,11},{9,10},{10,... | collective-permute-start | bytes 1204232 | tf_op jit(solution)/shard_map/ppermute | solution.py:476
  19.7 13.7 %copy-start = (f32[784,128]{1,0:T(8,128)S(1)}, f32[784,128]{1,0:T(8,128)}, u32[]{:S(2)}) copy-start(f32[784,128]{1,0:T(8,128)} %get-tuple-element.45.rest_0_.rest_4_) | copy-start | bytes 1204228
  19.7 19.3 %all-to-all-start = ((f32[4,272,128]{2,1,0:T(8,128)}), f32[4,272,128]{2,1,0:T(8,128)S(1)}, u32[]{:S(2)}, u32[]{:S(2)}) async-start(f32[4,272,128]{2,1,0:T(8,128)} %get-tuple-element.40), calls=%async_computation | async-start | bytes 1114112 | tf_op jit(solution)/shard_map/all_to_all | solution.py:510
  29.9 24.4 %collective-permute-start.5 = (f32[768,128]{1,0:T(8,128)}, f32[768,128]{1,0:T(8,128)S(1)}, u32[]{:S(2)}, u32[]{:S(2)}) collective-permute-start(f32[768,128]{1,0:T(8,128)} %get-tuple-element.60), channel_id=1, source_target_pairs={{0,3},{1,2},{2,1},{3,0},{4,7},{5,6},{6,5},{7,4},{8,11},{9,10},{10,... | collective-permute-start | bytes 1179656 | tf_op jit(solution)/shard_map/ppermute | solution.py:476
  32.6 28.0 %collective-permute-start.4 = (f32[768,128]{1,0:T(8,128)}, f32[768,128]{1,0:T(8,128)S(1)}, u32[]{:S(2)}, u32[]{:S(2)}) collective-permute-start(f32[768,128]{1,0:T(8,128)} %get-tuple-element.59), channel_id=1, source_target_pairs={{0,2},{1,3},{2,0},{3,1},{4,6},{5,7},{6,4},{7,5},{8,10},{9,11},{10,... | collective-permute-start | bytes 1179656 | tf_op jit(solution)/shard_map/ppermute | solution.py:476
  33.0 27.6 %collective-permute-start.3 = (f32[768,128]{1,0:T(8,128)}, f32[768,128]{1,0:T(8,128)}, u32[]{:S(2)}, u32[]{:S(2)}) collective-permute-start(f32[768,128]{1,0:T(8,128)} %get-tuple-element.58), channel_id=1, source_target_pairs={{0,1},{1,0},{2,3},{3,2},{4,5},{5,4},{6,7},{7,6},{8,9},{9,8},{10,11... | collective-permute-start | bytes 1179656 | tf_op jit(solution)/shard_map/ppermute | solution.py:476
  33.4 5.6 %copy-start.1 = (f32[2,1,64,512]{3,2,1,0:T(8,128)S(1)}, f32[2,1,64,512]{3,2,1,0:T(8,128)}, u32[]{:S(2)}) copy-start(f32[2,1,64,512]{3,2,1,0:T(8,128)} %param.9) | copy-start | bytes 786436
  33.4 5.6 %copy-start.5 = (f32[1,64,512]{2,1,0:T(8,128)S(1)}, f32[1,64,512]{2,1,0:T(8,128)}, u32[]{:S(2)}) copy-start(f32[1,64,512]{2,1,0:T(8,128)} %param.10) | copy-start | bytes 393220
  36.1 26.7 %collective-permute-start.6 = (f32[512,128]{1,0:T(8,128)}, f32[512,128]{1,0:T(8,128)}, u32[]{:S(2)}, u32[]{:S(2)}) collective-permute-start(f32[512,128]{1,0:T(8,128)} %get-tuple-element.64), channel_id=1, source_target_pairs={{0,4},{1,5},{2,6},{3,7},{4,0},{5,1},{6,2},{7,3},{8,12},{9,13},{10,... | collective-permute-start | bytes 786440 | tf_op jit(solution)/shard_map/ppermute | solution.py:476
  38.9 24.0 %collective-permute-start.7 = (f32[512,128]{1,0:T(8,128)}, f32[512,128]{1,0:T(8,128)}, u32[]{:S(2)}, u32[]{:S(2)}) collective-permute-start(f32[512,128]{1,0:T(8,128)} %get-tuple-element.65), channel_id=1, source_target_pairs={{0,4},{1,5},{2,6},{3,7},{4,0},{5,1},{6,2},{7,3},{8,12},{9,13},{10,... | collective-permute-start | bytes 786440 | tf_op jit(solution)/shard_map/ppermute | solution.py:476
  41.0 1.9 %copy-start.8 = (f32[2,64,640]{2,1,0:T(8,128)}, f32[2,64,640]{2,1,0:T(8,128)S(1)}, u32[]{:S(2)}) copy-start(f32[2,64,640]{2,1,0:T(8,128)S(1)} %get-tuple-element.44.u_ref) | copy-start | bytes 983044
  41.0 19.6 %copy-start.2 = (f32[768,128]{1,0:T(8,128)S(1)}, f32[768,128]{1,0:T(8,128)}, u32[]{:S(2)}) copy-start(f32[768,128]{1,0:T(8,128)} %get-tuple-element.57.rest_0_) | copy-start | bytes 1179652
  66.1 22.1 %copy-start.9 = (f32[2,64,640]{2,1,0:T(8,128)S(1)}, f32[2,64,640]{2,1,0:T(8,128)}, u32[]{:S(2)}) copy-start(f32[2,64,640]{2,1,0:T(8,128)} %copy-done.8) | copy-start | bytes 983044
  66.1 22.1 %all-to-all-start.1 = ((f32[4,6,16,640]{3,2,1,0:T(8,128)}), f32[4,6,16,640]{3,2,1,0:T(8,128)S(1)}, u32[]{:S(2)}, u32[]{:S(2)}) async-start(f32[4,6,16,640]{3,2,1,0:T(8,128)} %shard_map.110), calls=%async_computation.1 | async-start | bytes 1966080 | tf_op jit(solution)/shard_map/all_to_all | solution.py:540
  69.8 13.2 %collective-permute-start.8 = (f32[2,16,640]{2,1,0:T(8,128)S(1)}, f32[2,16,640]{2,1,0:T(8,128)S(1)}, u32[]{:S(2)}, u32[]{:S(2)}) collective-permute-start(f32[2,16,640]{2,1,0:T(8,128)S(1)} %get-tuple-element.66), channel_id=1, source_target_pairs={{0,4},{1,5},{2,6},{3,7},{4,0},{5,1},{6,2},{7,3},{8,12},{9,13},{10,... | collective-permute-start | bytes 245768 | tf_op jit(solution)/shard_map/ppermute | solution.py:480
  71.6 12.2 %collective-permute-start.9 = (f32[2,16,640]{2,1,0:T(8,128)S(1)}, f32[2,16,640]{2,1,0:T(8,128)S(1)}, u32[]{:S(2)}, u32[]{:S(2)}) collective-permute-start(f32[2,16,640]{2,1,0:T(8,128)S(1)} %get-tuple-element.67), channel_id=1, source_target_pairs={{0,12},{1,13},{2,14},{3,15},{4,8},{5,9},{6,10},{7,11},{8,4},{9,5},... | collective-permute-start | bytes 245768 | tf_op jit(solution)/shard_map/ppermute | solution.py:480
  72.5 15.3 %collective-permute-start.10 = (f32[2,16,640]{2,1,0:T(8,128)S(1)}, f32[2,16,640]{2,1,0:T(8,128)S(1)}, u32[]{:S(2)}, u32[]{:S(2)}) collective-permute-start(f32[2,16,640]{2,1,0:T(8,128)S(1)} %get-tuple-element.68), channel_id=1, source_target_pairs={{0,20},{1,21},{2,22},{3,23},{4,16},{5,17},{6,18},{7,19},{8,28},{9,... | collective-permute-start | bytes 245768 | tf_op jit(solution)/shard_map/ppermute | solution.py:480
  75.4 12.9 %copy-start.4 = (f32[64,640]{1,0:T(8,128)S(1)}, f32[64,640]{1,0:T(8,128)}, u32[]{:S(2)}) copy-start(f32[64,640]{1,0:T(8,128)} %copy-done.3) | copy-start | bytes 491524
  75.4 12.9 %copy-start.7 = (f32[2,64,640]{2,1,0:T(8,128)S(1)}, f32[2,64,640]{2,1,0:T(8,128)}, u32[]{:S(2)}) copy-start(f32[2,64,640]{2,1,0:T(8,128)} %copy-done.6) | copy-start | bytes 983044
  75.4 12.8 %collective-permute-start.11 = (f32[2,16,640]{2,1,0:T(8,128)S(1)}, f32[2,16,640]{2,1,0:T(8,128)S(1)}, u32[]{:S(2)}, u32[]{:S(2)}) collective-permute-start(f32[2,16,640]{2,1,0:T(8,128)S(1)} %get-tuple-element.69), channel_id=1, source_target_pairs={{0,28},{1,29},{2,30},{3,31},{4,24},{5,25},{6,26},{7,27},{8,20},{9,... | collective-permute-start | bytes 245768 | tf_op jit(solution)/shard_map/ppermute | solution.py:480
  96.4 10.7 %all-to-all-start.2 = ((f32[32,1,128]{2,1,0:T(1,128)}), f32[32,1,128]{2,1,0:T(1,128)S(1)}, u32[]{:S(2)}, u32[]{:S(2)}) async-start(f32[32,1,128]{2,1,0:T(1,128)} %get-tuple-element.70), calls=%async_computation.2 | async-start | bytes 32768 | tf_op jit(solution)/shard_map/all_to_all | solution.py:547
  100.1 7.0 %copy-start.11 = (f32[2,64,512]{2,1,0:T(8,128)S(1)}, f32[2,64,512]{2,1,0:T(8,128)}, u32[]{:S(2)}) copy-start(f32[2,64,512]{2,1,0:T(8,128)} %copy-done.10) | copy-start | bytes 786436
  (3 other events, 3.3 us)

commit v8 on v7

--- a/solution.py
+++ b/solution.py
@@ -20,7 +20,7 @@
 VMEM_BYTES = 32 * 1024 * 1024
 PACK_BYTES = 60 * 1024 * 1024
 FIRST = 100_000_000
-JOIN = 100_000_000
+JOIN = 400_000_000
 
 
 def iota(shape, axis):
@@ -231,7 +231,7 @@
 
 
 def weights_kernel(half, cap, blk, across, *rest):
-    w_refs, (_, meta_out, diagonal_out, side_out, acc_ref) = rest[:half], rest[half:]
+    w_refs, (_, meta_out, out, acc_ref) = rest[:half], rest[half:]
     nb = cap // blk
     for k, w_ref in enumerate(w_refs):
         meta_out[k] = w_ref[2 * cap:, :]
@@ -245,8 +245,8 @@
 
     low = 2 * cap + across * 2 * nb
     sum_rows(cap, blk, [w_ref[low:low + 2 * nb, :] for w_ref in w_refs], acc_ref, terms)
-    diagonal_out[...] = acc_ref[:, :SEG] + pltpu.roll(acc_ref[:, 2 * SEG:], 1, 0)
-    side_out[...] = acc_ref[:, SEG:2 * SEG]
+    out[0] = acc_ref[:, :SEG] + pltpu.roll(acc_ref[:, 2 * SEG:], 1, 0)
+    out[1] = acc_ref[:, SEG:2 * SEG]
 
 
 def sum_products(half, cap, blk, across, meta_ref, v_refs, acc_ref, sums_ref):
@@ -272,12 +272,11 @@
             cut_part(sums_ref, out.at[f], f, me ^ k, len(outs))
 
 
-def products_kernel(half, cap, blk, meta_ref, d_ref, e_ref, far_d_ref, far_e_ref, *rest):
+def products_kernel(half, cap, blk, meta_ref, side_ref, far_ref, *rest):
     v_refs, (out, acc_ref, sums_ref, side) = rest[:half], rest[half:]
     spans = out.shape[0]
     sum_products(half, cap, blk, 0, meta_ref, v_refs, acc_ref, sums_ref)
-    side[0] = d_ref[...] + far_d_ref[...]
-    side[1] = e_ref[...] + far_e_ref[...]
+    side[...] = side_ref[...] + far_ref[...]
     for q in range(spans):
         for channel, rows_ref in enumerate((side.at[0], side.at[1], sums_ref)):
             for f in range(F):
@@ -516,14 +515,14 @@
     def sum_weights(side, token, weight):
         return call(
             functools.partial(weights_kernel, half, cap, blk, side),
-            (f32(half, meta_rows, SEG),) + (f32(ROWS, SEG),) * 2,
+            (f32(half, meta_rows, SEG), f32(2, ROWS, SEG)),
             [vmem(ROWS, 3 * SEG)],
             weight=weight,
         )(*w_blocks, token)
 
-    meta, *side_across = sum_weights(1, w_blocks[0], FIRST)
-    side_across = [to_half(values, half) for values in side_across]
-    meta, *side = sum_weights(0, token, 1)
+    meta, far_side = sum_weights(1, w_blocks[0], FIRST)
+    far_side = to_half(far_side, half)
+    meta, side = sum_weights(0, token, 1)
     meta, *sums_across = call(
         functools.partial(products_across_kernel, half, cap, blk),
         (f32(half, meta_rows, SEG),) + (f32(F, LX, ext),) * spans,
@@ -536,7 +535,7 @@
         functools.partial(products_kernel, half, cap, blk),
         f32(spans, 3 * F, LX, ext),
         [vmem(ROWS, 2 * SEG), vmem(ROWS, SEG), vmem(2, ROWS, SEG)],
-    )(meta, *side, *side_across, *v_blocks)
+    )(meta, side, far_side, *v_blocks)
     parts = lax.all_to_all(parts, "px", split_axis=0, concat_axis=0, tiled=True)
 
     r, q, h, dots = call(

time: 109 us -> 117 us (1.073)
  waiting for transfers between devices: 41.9 us -> 51.9 us
  starting transfers between devices: 28.2 us -> 26.8 us
    all_to_all x1, waiting for transfers between devices: 0.01 us -> 5.61 us  [shards(): swap = lax.all_to_all(swap, 'px', split_axis=0, concat_axis=0, tiled=True)]
    ppermute x8 -> x7, waiting for transfers between devices: 24.2 us -> 28.4 us  [to_half(): return lax.ppermute(block, 'py', [(i, i ^ k) for i in range(groups)])]
    ppermute x8 -> x7, starting transfers between devices: 11 us -> 10.9 us  [to_half(): return lax.ppermute(block, 'py', [(i, i ^ k) for i in range(groups)])]
  transfers between devices with their start and end apart: 15 -> 14, of which waited for: 8 -> 11; matrix products, arithmetic and copies ran while one was open for 0% -> 0% of each run, Pallas kernels for 16% -> 12%
where the time goes in v8:
time: 117 us
  waiting for transfers between devices  51.9 us (44%)
  Pallas kernels  36.1 us (31%)
  starting transfers between devices  26.8 us (23%)
  local copies, waits for them, and re-layouts  1.45 us (1%)
    ppermute x7, waiting for transfers between devices, to_half(): return lax.ppermute(block, 'py', [(i, i ^ k) for i in range(groups)])  28.4 us
    ppermute x4, waiting for transfers between devices, across(): lax.ppermute(parts[k], ('px', 'py'), [(i * groups + j, (i ^ k) * groups +...  12.4 us
    ppermute x7, starting transfers between devices, to_half(): return lax.ppermute(block, 'py', [(i, i ^ k) for i in range(groups)])  10.9 us
    pallas_call x1, Pallas kernels, shards(): call(functools.partial(pack_products_kernel, groups, cap), (f32(2 * cap,...  7.64 us
    pallas_call x1, Pallas kernels, shards(): call(solve_kernel, (f32(F, nx, width),) * 2 + (f32(F, nx, ext), f32(group...  7.43 us
    pallas_call x1, Pallas kernels, shards(): call(functools.partial(pack_weights_kernel, groups, cap, blk, block_rows)...  6.9 us
    ppermute x4, starting transfers between devices, across(): lax.ppermute(parts[k], ('px', 'py'), [(i * groups + j, (i ^ k) * groups +...  6.25 us
    all_to_all x1, waiting for transfers between devices, shards(): swap = lax.all_to_all(swap, 'px', split_axis=0, concat_axis=0, tiled=True)  5.61 us
  transfers between devices with their start and end apart: 14, of which 11 were waited for; matrix products, arithmetic and copies ran while one was open for 0% of the time, Pallas kernels for 12%

profile of v8, /device:TPU:0, one launch (start us, length us, event | category | flops | bytes accessed | tf_op | source)
XLA Modules:
  0.0 117.1 jit_solution(4848875028391115849)
XLA Ops:
  0.6 6.9 %shard_map.104 = (f32[784,128]{1,0:T(8,128)}, f32[784,128]{1,0:T(8,128)}, f32[784,128]{1,0:T(8,128)}, f32[784,128]{1,0:T(8,128)}, s32[8,128]{1,0:T(8,128)}) custom-call(s32[8,128]{1,0:T(8,128)} %bitcast.19, s32[8,128]{1,0:T(8,128)} %bitcast.20, s32[8,128]{1,0:T(8,128)} %bitcast.21, f32[8,128]{1,0:T(8,128)} %bitcast.22, f32[1024,128]{1,0:T(8,128)} %w_hbm.3), custom_call_target="tpu_custom_call" | custom-call | flops 1 | bytes 1 | tf_op jit(solution)/shard_map/pallas_call | solution.py:484
  7.5 3.0 %collective-permute-start = (f32[784,128]{1,0:T(8,128)}, f32[784,128]{1,0:T(8,128)S(1)}, u32[]{:S(2)}, u32[]{:S(2)}) collective-permute-start(f32[784,128]{1,0:T(8,128)} %get-tuple-element.44), channel_id=1, source_target_pairs={{0,1},{1,0},{2,3},{3,2},{4,5},{5,4},{6,7},{7,6},{8,9},{9,8},{10,11... | collective-permute-start | bytes 1204232 | tf_op jit(solution)/shard_map/ppermute | solution.py:475
  12.1 7.6 %shard_map.105 = (f32[768,128]{1,0:T(8,128)}, f32[768,128]{1,0:T(8,128)}, f32[768,128]{1,0:T(8,128)}, f32[768,128]{1,0:T(8,128)}, f32[4,272,128]{2,1,0:T(8,128)}) custom-call(s32[8,128]{1,0:T(8,128)} %get-tuple-element.37.slot_ref, f32[1024,128]{1,0:T(8,128)} %w_hbm.3, f32[1024,128]{1,0:T(8,128)} %d_hbm.1, f32[16,2048]{1,0:T(8,128)} %bitcast.18, ...), custom_call_target="tpu_custom_call" | custom-call | flops 1 | bytes 1 | tf_op jit(solution)/shard_map/pallas_call | solution.py:496
  20.0 2.9 %collective-permute-done.1.rest_2_ = f32[784,128]{1,0:T(8,128)S(1)} collective-permute-done((f32[784,128]{1,0:T(8,128)}, f32[784,128]{1,0:T(8,128)S(1)}, u32[]{:S(2)}, u32[]{:S(2)}) %collective-permute-start.1) | collective-permute-done | bytes 401440 | tf_op jit(solution)/shard_map/ppermute | solution.py:475
  23.0 6.9 %collective-permute-done.2.rest_3_ = f32[784,128]{1,0:T(8,128)S(1)} collective-permute-done((f32[784,128]{1,0:T(8,128)}, f32[784,128]{1,0:T(8,128)S(1)}, u32[]{:S(2)}, u32[]{:S(2)}) %collective-permute-start.2) | collective-permute-done | bytes 401440 | tf_op jit(solution)/shard_map/ppermute | solution.py:475
  29.9 2.7 %shard_map.109 = (f32[4,16,128]{2,1,0:T(8,128)}, f32[2,512,128]{2,1,0:T(8,128)}) custom-call(f32[784,128]{1,0:T(8,128)S(1)} %copy-done, f32[784,128]{1,0:T(8,128)S(1)} %collective-permute-done.rest_1_, f32[784,128]{1,0:T(8,128)S(1)} %collective-permute-done.1.rest_2_, f32[784,128]{1,0:T(8,128)S(1)} %collective-permute-done.2.rest_3_, f32[784,128]{1,0:T(8,128)S(1)} %copy-done), custom_call_target="tpu_custom_call" | custom-call | flops 100000000 | bytes 100000000 | tf_op jit(solution)/shard_map/pallas_call | solution.py:516
  32.6 2.8 %collective-permute-start.6 = (f32[2,512,128]{2,1,0:T(8,128)}, f32[2,512,128]{2,1,0:T(8,128)}, u32[]{:S(2)}, u32[]{:S(2)}) collective-permute-start(f32[2,512,128]{2,1,0:T(8,128)} %get-tuple-element.61), channel_id=1, source_target_pairs={{0,4},{1,5},{2,6},{3,7},{4,0},{5,1},{6,2},{7,3},{8,12},{9,13},{10,... | collective-permute-start | bytes 1572872 | tf_op jit(solution)/shard_map/ppermute | solution.py:475
  35.4 3.6 %all-to-all-start = ((f32[4,272,128]{2,1,0:T(8,128)}), f32[4,272,128]{2,1,0:T(8,128)S(1)}, u32[]{:S(2)}, u32[]{:S(2)}) async-start(f32[4,272,128]{2,1,0:T(8,128)} %get-tuple-element.38), calls=%async_computation | async-start | bytes 1114112 | tf_op jit(solution)/shard_map/all_to_all | solution.py:509
  39.0 2.6 %collective-permute-start.5 = (f32[768,128]{1,0:T(8,128)}, f32[768,128]{1,0:T(8,128)S(1)}, u32[]{:S(2)}, u32[]{:S(2)}) collective-permute-start(f32[768,128]{1,0:T(8,128)} %get-tuple-element.58), channel_id=1, source_target_pairs={{0,3},{1,2},{2,1},{3,0},{4,7},{5,6},{6,5},{7,4},{8,11},{9,10},{10,... | collective-permute-start | bytes 1179656 | tf_op jit(solution)/shard_map/ppermute | solution.py:475
  42.5 5.6 %all-to-all-done.swap_ref = f32[4,272,128]{2,1,0:T(8,128)S(1)} async-done(((f32[4,272,128]{2,1,0:T(8,128)}), f32[4,272,128]{2,1,0:T(8,128)S(1)}, u32[]{:S(2)}, u32[]{:S(2)}) %all-to-all-start) | async-done | bytes 557088 | tf_op jit(solution)/shard_map/all_to_all | solution.py:509
  50.2 1.9 %shard_map.107 = (f32[4,16,128]{2,1,0:T(8,128)S(1)}, f32[2,512,128]{2,1,0:T(8,128)S(1)}) custom-call(f32[784,128]{1,0:T(8,128)S(1)} %copy-done, f32[784,128]{1,0:T(8,128)S(1)} %collective-permute-done.rest_1_, f32[784,128]{1,0:T(8,128)S(1)} %collective-permute-done.1.rest_2_, f32[784,128]{1,0:T(8,128)S(1)} %collective-permute-done.2.rest_3_, ...), custom_call_target="tpu_custom_call" | custom-call | flops 1 | bytes 1 | tf_op jit(solution)/shard_map/pallas_call | solution.py:516
  52.1 10.1 %collective-permute-done.5.rest_3_ = f32[768,128]{1,0:T(8,128)S(1)} collective-permute-done((f32[768,128]{1,0:T(8,128)}, f32[768,128]{1,0:T(8,128)S(1)}, u32[]{:S(2)}, u32[]{:S(2)}) %collective-permute-start.5) | collective-permute-done | bytes 393248 | tf_op jit(solution)/shard_map/ppermute | solution.py:475
  62.2 8.1 %collective-permute-done.4.rest_2_ = f32[768,128]{1,0:T(8,128)S(1)} collective-permute-done((f32[768,128]{1,0:T(8,128)}, f32[768,128]{1,0:T(8,128)S(1)}, u32[]{:S(2)}, u32[]{:S(2)}) %collective-permute-start.4) | collective-permute-done | bytes 393248 | tf_op jit(solution)/shard_map/ppermute | solution.py:475
  70.3 2.2 %shard_map.108 = (f32[4,16,128]{2,1,0:T(8,128)S(1)}, f32[2,16,640]{2,1,0:T(8,128)S(1)}, f32[2,16,640]{2,1,0:T(8,128)S(1)}, f32[2,16,640]{2,1,0:T(8,128)S(1)}, f32[2,16,640]{2,1,0:T(8,128)S(1)}) custom-call(f32[4,16,128]{2,1,0:T(8,128)S(1)} %get-tuple-element.54.meta_ref, f32[768,128]{1,0:T(8,128)S(1)} %copy-done.2, ...), custom_call_target="tpu_custom_call" | custom-call | flops 1 | bytes 1 | tf_op jit(solution)/shard_map/pallas_call | solution.py:526
  72.6 3.3 %shard_map.110 = f32[4,6,16,640]{3,2,1,0:T(8,128)} custom-call(f32[4,16,128]{2,1,0:T(8,128)S(1)} %get-tuple-element.59.meta_ref, f32[2,512,128]{2,1,0:T(8,128)S(1)} %get-tuple-element.60.side_ref, f32[2,512,128]{2,1,0:T(8,128)} %collective-permute-done.6.far_ref, f32[768,128]{1,0:T(8,128)S(1)} %copy-done.2, f32[768,128]{1,0:T(8,128)} %collective-permute-done.3.rest_1_, ...), custom_call_target="tpu_custom_call" | custom-call | flops 1 | bytes 1 | tf_op jit(solution)/shard_map/pallas_call | solution.py:534
  75.9 3.5 %all-to-all-start.1 = ((f32[4,6,16,640]{3,2,1,0:T(8,128)}), f32[4,6,16,640]{3,2,1,0:T(8,128)S(1)}, u32[]{:S(2)}, u32[]{:S(2)}) async-start(f32[4,6,16,640]{3,2,1,0:T(8,128)} %shard_map.110), calls=%async_computation.1 | async-start | bytes 1966080 | tf_op jit(solution)/shard_map/all_to_all | solution.py:539
  79.9 2.2 %collective-permute-start.8 = (f32[2,16,640]{2,1,0:T(8,128)S(1)}, f32[2,16,640]{2,1,0:T(8,128)S(1)}, u32[]{:S(2)}, u32[]{:S(2)}) collective-permute-start(f32[2,16,640]{2,1,0:T(8,128)S(1)} %get-tuple-element.63), channel_id=1, source_target_pairs={{0,12},{1,13},{2,14},{3,15},{4,8},{5,9},{6,10},{7,11},{8,4},{9,5},... | collective-permute-start | bytes 245768 | tf_op jit(solution)/shard_map/ppermute | solution.py:479
  83.7 1.9 %collective-permute-start.10 = (f32[2,16,640]{2,1,0:T(8,128)S(1)}, f32[2,16,640]{2,1,0:T(8,128)S(1)}, u32[]{:S(2)}, u32[]{:S(2)}) collective-permute-start(f32[2,16,640]{2,1,0:T(8,128)S(1)} %get-tuple-element.65), channel_id=1, source_target_pairs={{0,28},{1,29},{2,30},{3,31},{4,24},{5,25},{6,26},{7,27},{8,20},{9,... | collective-permute-start | bytes 245768 | tf_op jit(solution)/shard_map/ppermute | solution.py:479
  85.6 6.1 %collective-permute-done.7.rest_0_ = f32[2,16,640]{2,1,0:T(8,128)S(1)} collective-permute-done((f32[2,16,640]{2,1,0:T(8,128)S(1)}, f32[2,16,640]{2,1,0:T(8,128)S(1)}, u32[]{:S(2)}, u32[]{:S(2)}) %collective-permute-start.7) | collective-permute-done | bytes 81952 | tf_op jit(solution)/shard_map/ppermute | solution.py:479
  91.8 1.7 %collective-permute-done.8.rest_1_ = f32[2,16,640]{2,1,0:T(8,128)S(1)} collective-permute-done((f32[2,16,640]{2,1,0:T(8,128)S(1)}, f32[2,16,640]{2,1,0:T(8,128)S(1)}, u32[]{:S(2)}, u32[]{:S(2)}) %collective-permute-start.8) | collective-permute-done | bytes 81952 | tf_op jit(solution)/shard_map/ppermute | solution.py:479
  93.4 3.0 %collective-permute-done.9.rest_2_ = f32[2,16,640]{2,1,0:T(8,128)S(1)} collective-permute-done((f32[2,16,640]{2,1,0:T(8,128)S(1)}, f32[2,16,640]{2,1,0:T(8,128)S(1)}, u32[]{:S(2)}, u32[]{:S(2)}) %collective-permute-start.9) | collective-permute-done | bytes 81952 | tf_op jit(solution)/shard_map/ppermute | solution.py:479
  98.1 7.4 %shard_map.112 = (f32[2,64,512]{2,1,0:T(8,128)S(1)}, f32[2,64,512]{2,1,0:T(8,128)S(1)}, f32[2,64,640]{2,1,0:T(8,128)S(1)}, f32[32,1,128]{2,1,0:T(1,128)}) custom-call(f32[2,64,640]{2,1,0:T(8,128)S(1)} %copy-done.7, f32[64,640]{1,0:T(8,128)S(1)} %get-tuple-element.40.cx_ref, f32[64,640]{1,0:T(8,128)S(1)} %copy-done.4, f32[2,64,640]{2,1,0:T(8,128)S(1)} %copy-done.9, ...), custom_call_target="tpu_custom_call" | custom-call | flops 1 | bytes 1 | tf_op jit(solution)/shard_map/pallas_call | solution.py:541
  106.2 2.5 %all-to-all-start.2 = ((f32[32,1,128]{2,1,0:T(1,128)}), f32[32,1,128]{2,1,0:T(1,128)S(1)}, u32[]{:S(2)}, u32[]{:S(2)}) async-start(f32[32,1,128]{2,1,0:T(1,128)} %get-tuple-element.66), calls=%async_computation.2 | async-start | bytes 32768 | tf_op jit(solution)/shard_map/all_to_all | solution.py:546
  110.3 5.5 %all-to-all-done.2.dots_ref = f32[32,1,128]{2,1,0:T(1,128)S(1)} async-done(((f32[32,1,128]{2,1,0:T(1,128)}), f32[32,1,128]{2,1,0:T(1,128)S(1)}, u32[]{:S(2)}, u32[]{:S(2)}) %all-to-all-start.2) | async-done | bytes 16416 | tf_op jit(solution)/shard_map/all_to_all | solution.py:546
  (39 shorter events, 12.1 us)
Async XLA Ops:
  7.5 12.5 %collective-permute-start = (f32[784,128]{1,0:T(8,128)}, f32[784,128]{1,0:T(8,128)S(1)}, u32[]{:S(2)}, u32[]{:S(2)}) collective-permute-start(f32[784,128]{1,0:T(8,128)} %get-tuple-element.44), channel_id=1, source_target_pairs={{0,1},{1,0},{2,3},{3,2},{4,5},{5,4},{6,7},{7,6},{8,9},{9,8},{10,11... | collective-permute-start | bytes 1204232 | tf_op jit(solution)/shard_map/ppermute | solution.py:475
  10.5 12.4 %collective-permute-start.1 = (f32[784,128]{1,0:T(8,128)}, f32[784,128]{1,0:T(8,128)S(1)}, u32[]{:S(2)}, u32[]{:S(2)}) collective-permute-start(f32[784,128]{1,0:T(8,128)} %get-tuple-element.47), channel_id=1, source_target_pairs={{0,2},{1,3},{2,0},{3,1},{4,6},{5,7},{6,4},{7,5},{8,10},{9,11},{10,... | collective-permute-start | bytes 1204232 | tf_op jit(solution)/shard_map/ppermute | solution.py:475
  12.1 17.8 %collective-permute-start.2 = (f32[784,128]{1,0:T(8,128)}, f32[784,128]{1,0:T(8,128)S(1)}, u32[]{:S(2)}, u32[]{:S(2)}) collective-permute-start(f32[784,128]{1,0:T(8,128)} %get-tuple-element.50), channel_id=1, source_target_pairs={{0,3},{1,2},{2,1},{3,0},{4,7},{5,6},{6,5},{7,4},{8,11},{9,10},{10,... | collective-permute-start | bytes 1204232 | tf_op jit(solution)/shard_map/ppermute | solution.py:475
  12.1 17.8 %copy-start = (f32[784,128]{1,0:T(8,128)S(1)}, f32[784,128]{1,0:T(8,128)}, u32[]{:S(2)}) copy-start(f32[784,128]{1,0:T(8,128)} %get-tuple-element.43.rest_0_.rest_4_) | copy-start | bytes 1204228
  32.6 39.9 %collective-permute-start.6 = (f32[2,512,128]{2,1,0:T(8,128)}, f32[2,512,128]{2,1,0:T(8,128)}, u32[]{:S(2)}, u32[]{:S(2)}) collective-permute-start(f32[2,512,128]{2,1,0:T(8,128)} %get-tuple-element.61), channel_id=1, source_target_pairs={{0,4},{1,5},{2,6},{3,7},{4,0},{5,1},{6,2},{7,3},{8,12},{9,13},{10,... | collective-permute-start | bytes 1572872 | tf_op jit(solution)/shard_map/ppermute | solution.py:475
  35.4 12.8 %copy-start.1 = (f32[2,1,64,512]{3,2,1,0:T(8,128)S(1)}, f32[2,1,64,512]{3,2,1,0:T(8,128)}, u32[]{:S(2)}) copy-start(f32[2,1,64,512]{3,2,1,0:T(8,128)} %param.9) | copy-start | bytes 786436
  35.4 12.8 %copy-start.5 = (f32[1,64,512]{2,1,0:T(8,128)S(1)}, f32[1,64,512]{2,1,0:T(8,128)}, u32[]{:S(2)}) copy-start(f32[1,64,512]{2,1,0:T(8,128)} %param.10) | copy-start | bytes 393220
  35.4 12.8 %all-to-all-start = ((f32[4,272,128]{2,1,0:T(8,128)}), f32[4,272,128]{2,1,0:T(8,128)S(1)}, u32[]{:S(2)}, u32[]{:S(2)}) async-start(f32[4,272,128]{2,1,0:T(8,128)} %get-tuple-element.38), calls=%async_computation | async-start | bytes 1114112 | tf_op jit(solution)/shard_map/all_to_all | solution.py:509
  39.0 23.2 %collective-permute-start.5 = (f32[768,128]{1,0:T(8,128)}, f32[768,128]{1,0:T(8,128)S(1)}, u32[]{:S(2)}, u32[]{:S(2)}) collective-permute-start(f32[768,128]{1,0:T(8,128)} %get-tuple-element.58), channel_id=1, source_target_pairs={{0,3},{1,2},{2,1},{3,0},{4,7},{5,6},{6,5},{7,4},{8,11},{9,10},{10,... | collective-permute-start | bytes 1179656 | tf_op jit(solution)/shard_map/ppermute | solution.py:475
  41.5 28.8 %collective-permute-start.4 = (f32[768,128]{1,0:T(8,128)}, f32[768,128]{1,0:T(8,128)S(1)}, u32[]{:S(2)}, u32[]{:S(2)}) collective-permute-start(f32[768,128]{1,0:T(8,128)} %get-tuple-element.57), channel_id=1, source_target_pairs={{0,2},{1,3},{2,0},{3,1},{4,6},{5,7},{6,4},{7,5},{8,10},{9,11},{10,... | collective-permute-start | bytes 1179656 | tf_op jit(solution)/shard_map/ppermute | solution.py:475
  42.0 28.3 %collective-permute-start.3 = (f32[768,128]{1,0:T(8,128)}, f32[768,128]{1,0:T(8,128)}, u32[]{:S(2)}, u32[]{:S(2)}) collective-permute-start(f32[768,128]{1,0:T(8,128)} %get-tuple-element.56), channel_id=1, source_target_pairs={{0,1},{1,0},{2,3},{3,2},{4,5},{5,4},{6,7},{7,6},{8,9},{9,8},{10,11... | collective-permute-start | bytes 1179656 | tf_op jit(solution)/shard_map/ppermute | solution.py:475
  50.1 1.9 %copy-start.3 = (f32[64,640]{1,0:T(8,128)}, f32[64,640]{1,0:T(8,128)S(1)}, u32[]{:S(2)}) copy-start(f32[64,640]{1,0:T(8,128)S(1)} %get-tuple-element.41.cy_ref) | copy-start | bytes 491524
  50.1 1.9 %copy-start.8 = (f32[2,64,640]{2,1,0:T(8,128)}, f32[2,64,640]{2,1,0:T(8,128)S(1)}, u32[]{:S(2)}) copy-start(f32[2,64,640]{2,1,0:T(8,128)S(1)} %get-tuple-element.42.u_ref) | copy-start | bytes 983044
  50.1 20.2 %copy-start.2 = (f32[768,128]{1,0:T(8,128)S(1)}, f32[768,128]{1,0:T(8,128)}, u32[]{:S(2)}) copy-start(f32[768,128]{1,0:T(8,128)} %get-tuple-element.55.rest_0_) | copy-start | bytes 1179652
  75.9 22.2 %all-to-all-start.1 = ((f32[4,6,16,640]{3,2,1,0:T(8,128)}), f32[4,6,16,640]{3,2,1,0:T(8,128)S(1)}, u32[]{:S(2)}, u32[]{:S(2)}) async-start(f32[4,6,16,640]{3,2,1,0:T(8,128)} %shard_map.110), calls=%async_computation.1 | async-start | bytes 1966080 | tf_op jit(solution)/shard_map/all_to_all | solution.py:539
  79.4 12.4 %collective-permute-start.7 = (f32[2,16,640]{2,1,0:T(8,128)S(1)}, f32[2,16,640]{2,1,0:T(8,128)S(1)}, u32[]{:S(2)}, u32[]{:S(2)}) collective-permute-start(f32[2,16,640]{2,1,0:T(8,128)S(1)} %get-tuple-element.62), channel_id=1, source_target_pairs={{0,4},{1,5},{2,6},{3,7},{4,0},{5,1},{6,2},{7,3},{8,12},{9,13},{10,... | collective-permute-start | bytes 245768 | tf_op jit(solution)/shard_map/ppermute | solution.py:479
  79.9 13.6 %collective-permute-start.8 = (f32[2,16,640]{2,1,0:T(8,128)S(1)}, f32[2,16,640]{2,1,0:T(8,128)S(1)}, u32[]{:S(2)}, u32[]{:S(2)}) collective-permute-start(f32[2,16,640]{2,1,0:T(8,128)S(1)} %get-tuple-element.63), channel_id=1, source_target_pairs={{0,12},{1,13},{2,14},{3,15},{4,8},{5,9},{6,10},{7,11},{8,4},{9,5},... | collective-permute-start | bytes 245768 | tf_op jit(solution)/shard_map/ppermute | solution.py:479
  82.1 14.3 %collective-permute-start.9 = (f32[2,16,640]{2,1,0:T(8,128)S(1)}, f32[2,16,640]{2,1,0:T(8,128)S(1)}, u32[]{:S(2)}, u32[]{:S(2)}) collective-permute-start(f32[2,16,640]{2,1,0:T(8,128)S(1)} %get-tuple-element.64), channel_id=1, source_target_pairs={{0,20},{1,21},{2,22},{3,23},{4,16},{5,17},{6,18},{7,19},{8,28},{9,... | collective-permute-start | bytes 245768 | tf_op jit(solution)/shard_map/ppermute | solution.py:479
  83.7 14.3 %copy-start.4 = (f32[64,640]{1,0:T(8,128)S(1)}, f32[64,640]{1,0:T(8,128)}, u32[]{:S(2)}) copy-start(f32[64,640]{1,0:T(8,128)} %copy-done.3) | copy-start | bytes 491524
  83.7 14.4 %copy-start.7 = (f32[2,64,640]{2,1,0:T(8,128)S(1)}, f32[2,64,640]{2,1,0:T(8,128)}, u32[]{:S(2)}) copy-start(f32[2,64,640]{2,1,0:T(8,128)} %copy-done.6) | copy-start | bytes 983044
  83.7 14.4 %copy-start.9 = (f32[2,64,640]{2,1,0:T(8,128)S(1)}, f32[2,64,640]{2,1,0:T(8,128)}, u32[]{:S(2)}) copy-start(f32[2,64,640]{2,1,0:T(8,128)} %copy-done.8) | copy-start | bytes 983044
  83.7 14.3 %collective-permute-start.10 = (f32[2,16,640]{2,1,0:T(8,128)S(1)}, f32[2,16,640]{2,1,0:T(8,128)S(1)}, u32[]{:S(2)}, u32[]{:S(2)}) collective-permute-start(f32[2,16,640]{2,1,0:T(8,128)S(1)} %get-tuple-element.65), channel_id=1, source_target_pairs={{0,28},{1,29},{2,30},{3,31},{4,24},{5,25},{6,26},{7,27},{8,20},{9,... | collective-permute-start | bytes 245768 | tf_op jit(solution)/shard_map/ppermute | solution.py:479
  106.2 9.6 %all-to-all-start.2 = ((f32[32,1,128]{2,1,0:T(1,128)}), f32[32,1,128]{2,1,0:T(1,128)S(1)}, u32[]{:S(2)}, u32[]{:S(2)}) async-start(f32[32,1,128]{2,1,0:T(1,128)} %get-tuple-element.66), calls=%async_computation.2 | async-start | bytes 32768 | tf_op jit(solution)/shard_map/all_to_all | solution.py:546
  108.8 7.0 %copy-start.11 = (f32[2,64,512]{2,1,0:T(8,128)S(1)}, f32[2,64,512]{2,1,0:T(8,128)}, u32[]{:S(2)}) copy-start(f32[2,64,512]{2,1,0:T(8,128)} %copy-done.10) | copy-start | bytes 786436
  (2 other events, 1.4 us)

commit v9 on v7

--- a/solution.py
+++ b/solution.py
@@ -141,18 +141,10 @@
         store.wait()
 
 
-def pack_products_kernel(groups, cap, slot_ref, w_hbm, d_hbm, cy_hbm, c0_hbm, cx_hbm, *rest):
+def pack_products_kernel(groups, cap, slot_ref, w_hbm, d_hbm, *rest):
     half = groups // 2
-    outs, (swap_out, w_ref, d_ref, cy_ref, first, last, buffer, sems, out_sems) = (
-        rest[:half], rest[half:])
-    width = c0_hbm.shape[2]
-    loads = start_copies([
-        (w_hbm, w_ref), (d_hbm, d_ref), (cy_hbm, cy_ref),
-        (c0_hbm.at[:, :, pl.ds(0, SEG)], first.at[pl.ds(0, F)]),
-        (cx_hbm.at[:, pl.ds(0, SEG)], first.at[F]),
-        (c0_hbm.at[:, :, pl.ds(width - SEG, SEG)], last.at[pl.ds(0, F)]),
-        (cx_hbm.at[:, pl.ds(width - SEG, SEG)], last.at[F]),
-    ], sems)
+    outs, (w_ref, d_ref, buffer, sems, out_sems) = rest[:half], rest[half:]
+    loads = start_copies([(w_hbm, w_ref), (d_hbm, d_ref)], sems)
 
     def clear(o, carry):
         start = pl.multiple_of(o * cap, 8)
@@ -173,8 +165,21 @@
         return carry
 
     lax.fori_loop(0, w_ref.shape[0] // 8, place_rows, 0)
-    stores = start_copies([(buffer.at[pl.ds(k * 2 * cap, 2 * cap)], out)
-                           for k, out in enumerate(outs)], out_sems)
+    for store in start_copies([(buffer.at[pl.ds(k * 2 * cap, 2 * cap)], out)
+                               for k, out in enumerate(outs)], out_sems):
+        store.wait()
+
+
+def pack_swap_kernel(_, cy_hbm, c0_hbm, cx_hbm, swap_out, cy_ref, first, last, sems):
+    width = c0_hbm.shape[2]
+    for load in start_copies([
+        (cy_hbm, cy_ref),
+        (c0_hbm.at[:, :, pl.ds(0, SEG)], first.at[pl.ds(0, F)]),
+        (cx_hbm.at[:, pl.ds(0, SEG)], first.at[F]),
+        (c0_hbm.at[:, :, pl.ds(width - SEG, SEG)], last.at[pl.ds(0, F)]),
+        (cx_hbm.at[:, pl.ds(width - SEG, SEG)], last.at[F]),
+    ], sems):
+        load.wait()
     columns = cy_ref.shape[1]
     cy = cy_ref[...]
     cy = jnp.where(iota(cy.shape, 1) == columns - 1, 0.0, cy)
@@ -193,8 +198,6 @@
         for i in range(F + 1):
             swap_out[q, base + i * nx:base + (i + 1) * nx, :] = jnp.where(
                 q < me, first[i], last[i])
-    for store in stores:
-        store.wait()
 
 
 def sum_rows(cap, blk, metas, acc_ref, terms):
@@ -494,19 +497,25 @@
         obs_owner.reshape(chunks, SEG), cell_key.reshape(chunks, SEG),
         stencil.reshape(chunks, SEG), interp.reshape(chunks, SEG), obs_weight,
     )
-    *v_blocks, swap = call(
+    v_blocks = list(call(
         functools.partial(pack_products_kernel, groups, cap),
-        (f32(2 * cap, SEG),) * half + (f32(spans, LX * ext // SEG + (F + 1) * nx, SEG),),
-        [vmem(rows, SEG), vmem(rows, SEG), vmem(*coef_y.shape[1:]), vmem(F + 1, nx, SEG),
-         vmem(F + 1, nx, SEG), vmem(groups * cap, SEG), dma((7,)), dma((half,))],
-        [scalars] + [hbm] * 5,
-        (hbm,) * half + (local,),
+        (f32(2 * cap, SEG),) * half,
+        [vmem(rows, SEG), vmem(rows, SEG), vmem(groups * cap, SEG), dma((2,)), dma((half,))],
+        [scalars] + [hbm] * 2,
+        (hbm,) * half,
         limit=PACK_BYTES,
-    )(slots, obs_weight, innovation, coef_y[0], c0, cx)
-    for k in range(1, half):
-        w_blocks[k], v_blocks[k] = lax.optimization_barrier((to_half(w_blocks[k], k), v_blocks[k]))
-        v_blocks[k] = to_half(v_blocks[k], k)
-
+    )(slots, obs_weight, innovation))
+    w_blocks[1:] = [to_half(w_blocks[k], k) for k in range(1, half)]
+    w_blocks[1], *v_blocks[1:] = lax.optimization_barrier((w_blocks[1], *v_blocks[1:]))
+    v_blocks[1:] = [to_half(v_blocks[k], k) for k in range(1, half)]
+
+    swap = call(
+        pack_swap_kernel,
+        f32(spans, LX * ext // SEG + (F + 1) * nx, SEG),
+        [vmem(*coef_y.shape[1:]), vmem(F + 1, nx, SEG), vmem(F + 1, nx, SEG), dma((5,))],
+        [local] + [hbm] * 3,
+        limit=PACK_BYTES,
+    )(slots, coef_y[0], c0, cx)
     swap = lax.all_to_all(swap, "px", split_axis=0, concat_axis=0, tiled=True)
     c0_ext, cx_ext, cy_ext, u_ext, token = call(
         start_kernel,

time: 109 us -> 106 us (0.972)
  waiting for transfers between devices: 41.9 us -> 37.7 us
  Pallas kernels: 36 us -> 37.8 us
    ppermute x8, waiting for transfers between devices: 24.2 us -> 20 us  [to_half(): return lax.ppermute(block, 'py', [(i, i ^ k) for i in range(groups)])]
    pallas_call x0 -> x1, Pallas kernels: none -> 2.55 us  [shards(): call(pack_swap_kernel, f32(spans, LX * ext // SEG + (F + 1) * nx, SEG), [...]
  transfers between devices with their start and end apart: 15 -> 15, of which waited for: 8 -> 8; matrix products, arithmetic and copies ran while one was open for 0% -> 0% of each run, Pallas kernels for 16% -> 18%
where the time goes in v9:
time: 106 us
  Pallas kernels  37.8 us (36%)
  waiting for transfers between devices  37.7 us (36%)
  starting transfers between devices  28.2 us (27%)
  local copies, waits for them, and re-layouts  1.46 us (1%)
    ppermute x8, waiting for transfers between devices, to_half(): return lax.ppermute(block, 'py', [(i, i ^ k) for i in range(groups)])  20 us
    ppermute x4, waiting for transfers between devices, across(): lax.ppermute(parts[k], ('px', 'py'), [(i * groups + j, (i ^ k) * groups +...  12.2 us
    ppermute x8, starting transfers between devices, to_half(): return lax.ppermute(block, 'py', [(i, i ^ k) for i in range(groups)])  11.1 us
    pallas_call x1, Pallas kernels, shards(): call(solve_kernel, (f32(F, nx, width),) * 2 + (f32(F, nx, ext), f32(group...  7.43 us
    pallas_call x1, Pallas kernels, shards(): call(functools.partial(pack_weights_kernel, groups, cap, blk, block_rows)...  6.91 us
    pallas_call x1, Pallas kernels, shards(): call(functools.partial(pack_products_kernel, groups, cap), (f32(2 * cap,...  6.75 us
    ppermute x4, starting transfers between devices, across(): lax.ppermute(parts[k], ('px', 'py'), [(i * groups + j, (i ^ k) * groups +...  6.25 us
    all_to_all x1, waiting for transfers between devices, shards(): lax.all_to_all(dots, ('px', 'py'), split_axis=0, concat_axis=0, tiled=True)  5.5 us
  transfers between devices with their start and end apart: 15, of which 8 were waited for; matrix products, arithmetic and copies ran while one was open for 0% of the time, Pallas kernels for 18%

profile of v9, /device:TPU:0, one launch (start us, length us, event | category | flops | bytes accessed | tf_op | source)
XLA Modules:
  0.0 106.0 jit_solution(1112612412025078377)
XLA Ops:
  0.6 6.9 %shard_map.104 = (f32[784,128]{1,0:T(8,128)}, f32[784,128]{1,0:T(8,128)}, f32[784,128]{1,0:T(8,128)}, f32[784,128]{1,0:T(8,128)}, s32[8,128]{1,0:T(8,128)}) custom-call(s32[8,128]{1,0:T(8,128)} %bitcast.19, s32[8,128]{1,0:T(8,128)} %bitcast.20, s32[8,128]{1,0:T(8,128)} %bitcast.21, f32[8,128]{1,0:T(8,128)} %bitcast.22, f32[1024,128]{1,0:T(8,128)} %w_hbm.3), custom_call_target="tpu_custom_call" | custom-call | flops 1 | bytes 1 | tf_op jit(solution)/shard_map/pallas_call | solution.py:488
  7.5 3.0 %collective-permute-start = (f32[784,128]{1,0:T(8,128)}, f32[784,128]{1,0:T(8,128)S(1)}, u32[]{:S(2)}, u32[]{:S(2)}) collective-permute-start(f32[784,128]{1,0:T(8,128)} %get-tuple-element.42), channel_id=1, source_target_pairs={{0,1},{1,0},{2,3},{3,2},{4,5},{5,4},{6,7},{7,6},{8,9},{9,8},{10,11... | collective-permute-start | bytes 1204232 | tf_op jit(solution)/shard_map/ppermute | solution.py:479
  10.6 1.6 %collective-permute-start.1 = (f32[784,128]{1,0:T(8,128)}, f32[784,128]{1,0:T(8,128)S(1)}, u32[]{:S(2)}, u32[]{:S(2)}) collective-permute-start(f32[784,128]{1,0:T(8,128)} %get-tuple-element.47), channel_id=1, source_target_pairs={{0,2},{1,3},{2,0},{3,1},{4,6},{5,7},{6,4},{7,5},{8,10},{9,11},{10,... | collective-permute-start | bytes 1204232 | tf_op jit(solution)/shard_map/ppermute | solution.py:479
  12.1 2.5 %shard_map.105 = f32[4,272,128]{2,1,0:T(8,128)} custom-call(s32[8,128]{1,0:T(8,128)} %get-tuple-element.36._.slot_ref, f32[16,2048]{1,0:T(8,128)} %bitcast.18, f32[2,64,512]{2,1,0:T(8,128)} %bitcast.13, f32[64,512]{1,0:T(8,128)} %bitcast.16), custom_call_target="tpu_custom_call" | custom-call | flops 1 | bytes 1 | tf_op jit(solution)/shard_map/pallas_call | solution.py:512
  14.7 3.5 %all-to-all-start = ((f32[4,272,128]{2,1,0:T(8,128)}), f32[4,272,128]{2,1,0:T(8,128)S(1)}, u32[]{:S(2)}, u32[]{:S(2)}) async-start(f32[4,272,128]{2,1,0:T(8,128)} %shard_map.105), calls=%async_computation | async-start | bytes 1114112 | tf_op jit(solution)/shard_map/all_to_all | solution.py:519
  18.2 6.8 %shard_map.107 = (f32[768,128]{1,0:T(8,128)}, f32[768,128]{1,0:T(8,128)}, f32[768,128]{1,0:T(8,128)}, f32[768,128]{1,0:T(8,128)}) custom-call(s32[8,128]{1,0:T(8,128)} %get-tuple-element.36._.slot_ref, f32[1024,128]{1,0:T(8,128)} %w_hbm.3, f32[1024,128]{1,0:T(8,128)} %d_hbm.1), custom_call_target="tpu_custom_call" | custom-call | flops 1 | bytes 1 | tf_op jit(solution)/shard_map/pallas_call | solution.py:500
  25.0 2.0 %collective-permute-start.3 = (f32[768,128]{1,0:T(8,128)}, f32[768,128]{1,0:T(8,128)S(1)}, u32[]{:S(2)}, u32[]{:S(2)}) collective-permute-start(f32[768,128]{1,0:T(8,128)} %get-tuple-element.52), channel_id=1, source_target_pairs={{0,1},{1,0},{2,3},{3,2},{4,5},{5,4},{6,7},{7,6},{8,9},{9,8},{10,11... | collective-permute-start | bytes 1179656 | tf_op jit(solution)/shard_map/ppermute | solution.py:479
  26.9 1.6 %collective-permute-start.4 = (f32[768,128]{1,0:T(8,128)}, f32[768,128]{1,0:T(8,128)S(1)}, u32[]{:S(2)}, u32[]{:S(2)}) collective-permute-start(f32[768,128]{1,0:T(8,128)} %get-tuple-element.53), channel_id=1, source_target_pairs={{0,2},{1,3},{2,0},{3,1},{4,6},{5,7},{6,4},{7,5},{8,10},{9,11},{10,... | collective-permute-start | bytes 1179656 | tf_op jit(solution)/shard_map/ppermute | solution.py:479
  28.5 1.5 %collective-permute-done.2.rest_3_ = f32[784,128]{1,0:T(8,128)S(1)} collective-permute-done((f32[784,128]{1,0:T(8,128)}, f32[784,128]{1,0:T(8,128)S(1)}, u32[]{:S(2)}, u32[]{:S(2)}) %collective-permute-start.2) | collective-permute-done | bytes 401440 | tf_op jit(solution)/shard_map/ppermute | solution.py:479
  30.1 2.7 %shard_map.110 = (f32[4,16,128]{2,1,0:T(8,128)}, f32[512,128]{1,0:T(8,128)}, f32[512,128]{1,0:T(8,128)}) custom-call(f32[784,128]{1,0:T(8,128)S(1)} %copy-done, f32[784,128]{1,0:T(8,128)S(1)} %collective-permute-done.rest_1_, f32[784,128]{1,0:T(8,128)S(1)} %collective-permute-done.1.rest_2_, f32[784,128]{1,0:T(8,128)S(1)} %collective-permute-done.2.rest_3_, ...), custom_call_target="tpu_custom_call" | custom-call | flops 100000000 | bytes 100000000 | tf_op jit(solution)/shard_map/pallas_call | solution.py:526
  32.7 2.8 %collective-permute-start.6 = (f32[512,128]{1,0:T(8,128)}, f32[512,128]{1,0:T(8,128)}, u32[]{:S(2)}, u32[]{:S(2)}) collective-permute-start(f32[512,128]{1,0:T(8,128)} %get-tuple-element.58), channel_id=1, source_target_pairs={{0,4},{1,5},{2,6},{3,7},{4,0},{5,1},{6,2},{7,3},{8,12},{9,13},{10,... | collective-permute-start | bytes 786440 | tf_op jit(solution)/shard_map/ppermute | solution.py:479
  37.7 1.9 %shard_map.108 = (f32[4,16,128]{2,1,0:T(8,128)S(1)}, f32[512,128]{1,0:T(8,128)S(1)}, f32[512,128]{1,0:T(8,128)S(1)}) custom-call(f32[784,128]{1,0:T(8,128)S(1)} %copy-done, f32[784,128]{1,0:T(8,128)S(1)} %collective-permute-done.rest_1_, f32[784,128]{1,0:T(8,128)S(1)} %collective-permute-done.1.rest_2_, f32[784,128]{1,0:T(8,128)S(1)} %collective-permute-done.2.rest_3_, ...), custom_call_target="tpu_custom_call" | custom-call | flops 1 | bytes 1 | tf_op jit(solution)/shard_map/pallas_call | solution.py:526
  39.6 10.7 %collective-permute-done.4.rest_2_ = f32[768,128]{1,0:T(8,128)S(1)} collective-permute-done((f32[768,128]{1,0:T(8,128)}, f32[768,128]{1,0:T(8,128)S(1)}, u32[]{:S(2)}, u32[]{:S(2)}) %collective-permute-start.4) | collective-permute-done | bytes 393248 | tf_op jit(solution)/shard_map/ppermute | solution.py:479
  50.3 7.8 %collective-permute-done.5.rest_3_ = f32[768,128]{1,0:T(8,128)} collective-permute-done((f32[768,128]{1,0:T(8,128)}, f32[768,128]{1,0:T(8,128)}, u32[]{:S(2)}, u32[]{:S(2)}) %collective-permute-start.5) | collective-permute-done | bytes 393248 | tf_op jit(solution)/shard_map/ppermute | solution.py:479
  58.1 2.2 %shard_map.109 = (f32[4,16,128]{2,1,0:T(8,128)S(1)}, f32[2,16,640]{2,1,0:T(8,128)S(1)}, f32[2,16,640]{2,1,0:T(8,128)S(1)}, f32[2,16,640]{2,1,0:T(8,128)S(1)}, f32[2,16,640]{2,1,0:T(8,128)S(1)}) custom-call(f32[4,16,128]{2,1,0:T(8,128)S(1)} %get-tuple-element.50.meta_ref, f32[768,128]{1,0:T(8,128)S(1)} %copy-done.2, ...), custom_call_target="tpu_custom_call" | custom-call | flops 1 | bytes 1 | tf_op jit(solution)/shard_map/pallas_call | solution.py:536
  60.4 3.3 %shard_map.111 = f32[4,6,16,640]{3,2,1,0:T(8,128)} custom-call(f32[4,16,128]{2,1,0:T(8,128)S(1)} %get-tuple-element.55.meta_ref, f32[512,128]{1,0:T(8,128)S(1)} %get-tuple-element.56.d_ref, f32[512,128]{1,0:T(8,128)S(1)} %get-tuple-element.57.e_ref, f32[512,128]{1,0:T(8,128)} %collective-permute-done.6.far_d_ref, ...), custom_call_target="tpu_custom_call" | custom-call | flops 1 | bytes 1 | tf_op jit(solution)/shard_map/pallas_call | solution.py:544
  63.7 3.6 %all-to-all-start.1 = ((f32[4,6,16,640]{3,2,1,0:T(8,128)}), f32[4,6,16,640]{3,2,1,0:T(8,128)S(1)}, u32[]{:S(2)}, u32[]{:S(2)}) async-start(f32[4,6,16,640]{3,2,1,0:T(8,128)} %shard_map.111), calls=%async_computation.1 | async-start | bytes 1966080 | tf_op jit(solution)/shard_map/all_to_all | solution.py:549
  67.3 1.9 %collective-permute-start.8 = (f32[2,16,640]{2,1,0:T(8,128)S(1)}, f32[2,16,640]{2,1,0:T(8,128)S(1)}, u32[]{:S(2)}, u32[]{:S(2)}) collective-permute-start(f32[2,16,640]{2,1,0:T(8,128)S(1)} %get-tuple-element.60), channel_id=1, source_target_pairs={{0,4},{1,5},{2,6},{3,7},{4,0},{5,1},{6,2},{7,3},{8,12},{9,13},{10,... | collective-permute-start | bytes 245768 | tf_op jit(solution)/shard_map/ppermute | solution.py:483
  70.0 3.0 %collective-permute-start.10 = (f32[2,16,640]{2,1,0:T(8,128)S(1)}, f32[2,16,640]{2,1,0:T(8,128)S(1)}, u32[]{:S(2)}, u32[]{:S(2)}) collective-permute-start(f32[2,16,640]{2,1,0:T(8,128)S(1)} %get-tuple-element.62), channel_id=1, source_target_pairs={{0,20},{1,21},{2,22},{3,23},{4,16},{5,17},{6,18},{7,19},{8,28},{9,... | collective-permute-start | bytes 245768 | tf_op jit(solution)/shard_map/ppermute | solution.py:483
  73.6 7.0 %collective-permute-done.8.rest_0_ = f32[2,16,640]{2,1,0:T(8,128)S(1)} collective-permute-done((f32[2,16,640]{2,1,0:T(8,128)S(1)}, f32[2,16,640]{2,1,0:T(8,128)S(1)}, u32[]{:S(2)}, u32[]{:S(2)}) %collective-permute-start.8) | collective-permute-done | bytes 81952 | tf_op jit(solution)/shard_map/ppermute | solution.py:483
  81.3 4.0 %collective-permute-done.10.rest_2_ = f32[2,16,640]{2,1,0:T(8,128)S(1)} collective-permute-done((f32[2,16,640]{2,1,0:T(8,128)S(1)}, f32[2,16,640]{2,1,0:T(8,128)S(1)}, u32[]{:S(2)}, u32[]{:S(2)}) %collective-permute-start.10) | collective-permute-done | bytes 81952 | tf_op jit(solution)/shard_map/ppermute | solution.py:483
  85.8 7.4 %shard_map.113 = (f32[2,64,512]{2,1,0:T(8,128)S(1)}, f32[2,64,512]{2,1,0:T(8,128)S(1)}, f32[2,64,640]{2,1,0:T(8,128)S(1)}, f32[32,1,128]{2,1,0:T(1,128)}) custom-call(f32[2,64,640]{2,1,0:T(8,128)S(1)} %copy-done.7, f32[64,640]{1,0:T(8,128)S(1)} %get-tuple-element.38.cx_ref, f32[64,640]{1,0:T(8,128)S(1)} %copy-done.4, f32[2,64,640]{2,1,0:T(8,128)S(1)} %copy-done.9, ...), custom_call_target="tpu_custom_call" | custom-call | flops 1 | bytes 1 | tf_op jit(solution)/shard_map/pallas_call | solution.py:551
  94.0 3.7 %all-to-all-start.2 = ((f32[32,1,128]{2,1,0:T(1,128)}), f32[32,1,128]{2,1,0:T(1,128)S(1)}, u32[]{:S(2)}, u32[]{:S(2)}) async-start(f32[32,1,128]{2,1,0:T(1,128)} %get-tuple-element.64), calls=%async_computation.2 | async-start | bytes 32768 | tf_op jit(solution)/shard_map/all_to_all | solution.py:556
  99.2 5.5 %all-to-all-done.2.dots_ref = f32[32,1,128]{2,1,0:T(1,128)S(1)} async-done(((f32[32,1,128]{2,1,0:T(1,128)}), f32[32,1,128]{2,1,0:T(1,128)S(1)}, u32[]{:S(2)}, u32[]{:S(2)}) %all-to-all-start.2) | async-done | bytes 16416 | tf_op jit(solution)/shard_map/all_to_all | solution.py:556
  (42 shorter events, 8.3 us)
Async XLA Ops:
  7.5 17.4 %collective-permute-start = (f32[784,128]{1,0:T(8,128)}, f32[784,128]{1,0:T(8,128)S(1)}, u32[]{:S(2)}, u32[]{:S(2)}) collective-permute-start(f32[784,128]{1,0:T(8,128)} %get-tuple-element.42), channel_id=1, source_target_pairs={{0,1},{1,0},{2,3},{3,2},{4,5},{5,4},{6,7},{7,6},{8,9},{9,8},{10,11... | collective-permute-start | bytes 1204232 | tf_op jit(solution)/shard_map/ppermute | solution.py:479
  10.6 18.0 %collective-permute-start.1 = (f32[784,128]{1,0:T(8,128)}, f32[784,128]{1,0:T(8,128)S(1)}, u32[]{:S(2)}, u32[]{:S(2)}) collective-permute-start(f32[784,128]{1,0:T(8,128)} %get-tuple-element.47), channel_id=1, source_target_pairs={{0,2},{1,3},{2,0},{3,1},{4,6},{5,7},{6,4},{7,5},{8,10},{9,11},{10,... | collective-permute-start | bytes 1204232 | tf_op jit(solution)/shard_map/ppermute | solution.py:479
  12.1 17.9 %collective-permute-start.2 = (f32[784,128]{1,0:T(8,128)}, f32[784,128]{1,0:T(8,128)S(1)}, u32[]{:S(2)}, u32[]{:S(2)}) collective-permute-start(f32[784,128]{1,0:T(8,128)} %get-tuple-element.48), channel_id=1, source_target_pairs={{0,3},{1,2},{2,1},{3,0},{4,7},{5,6},{6,5},{7,4},{8,11},{9,10},{10,... | collective-permute-start | bytes 1204232 | tf_op jit(solution)/shard_map/ppermute | solution.py:479
  14.7 21.0 %all-to-all-start = ((f32[4,272,128]{2,1,0:T(8,128)}), f32[4,272,128]{2,1,0:T(8,128)S(1)}, u32[]{:S(2)}, u32[]{:S(2)}) async-start(f32[4,272,128]{2,1,0:T(8,128)} %shard_map.105), calls=%async_computation | async-start | bytes 1114112 | tf_op jit(solution)/shard_map/all_to_all | solution.py:519
  18.2 11.9 %copy-start = (f32[784,128]{1,0:T(8,128)S(1)}, f32[784,128]{1,0:T(8,128)}, u32[]{:S(2)}) copy-start(f32[784,128]{1,0:T(8,128)} %get-tuple-element.41.rest_0_.rest_4_) | copy-start | bytes 1204228
  25.0 14.6 %collective-permute-start.3 = (f32[768,128]{1,0:T(8,128)}, f32[768,128]{1,0:T(8,128)S(1)}, u32[]{:S(2)}, u32[]{:S(2)}) collective-permute-start(f32[768,128]{1,0:T(8,128)} %get-tuple-element.52), channel_id=1, source_target_pairs={{0,1},{1,0},{2,3},{3,2},{4,5},{5,4},{6,7},{7,6},{8,9},{9,8},{10,11... | collective-permute-start | bytes 1179656 | tf_op jit(solution)/shard_map/ppermute | solution.py:479
  26.9 23.4 %collective-permute-start.4 = (f32[768,128]{1,0:T(8,128)}, f32[768,128]{1,0:T(8,128)S(1)}, u32[]{:S(2)}, u32[]{:S(2)}) collective-permute-start(f32[768,128]{1,0:T(8,128)} %get-tuple-element.53), channel_id=1, source_target_pairs={{0,2},{1,3},{2,0},{3,1},{4,6},{5,7},{6,4},{7,5},{8,10},{9,11},{10,... | collective-permute-start | bytes 1179656 | tf_op jit(solution)/shard_map/ppermute | solution.py:479
  28.5 29.6 %collective-permute-start.5 = (f32[768,128]{1,0:T(8,128)}, f32[768,128]{1,0:T(8,128)}, u32[]{:S(2)}, u32[]{:S(2)}) collective-permute-start(f32[768,128]{1,0:T(8,128)} %get-tuple-element.54), channel_id=1, source_target_pairs={{0,3},{1,2},{2,1},{3,0},{4,7},{5,6},{6,5},{7,4},{8,11},{9,10},{10,... | collective-permute-start | bytes 1179656 | tf_op jit(solution)/shard_map/ppermute | solution.py:479
  30.0 5.6 %copy-start.1 = (f32[2,1,64,512]{3,2,1,0:T(8,128)S(1)}, f32[2,1,64,512]{3,2,1,0:T(8,128)}, u32[]{:S(2)}) copy-start(f32[2,1,64,512]{3,2,1,0:T(8,128)} %param.9) | copy-start | bytes 786436
  30.0 5.6 %copy-start.5 = (f32[1,64,512]{2,1,0:T(8,128)S(1)}, f32[1,64,512]{2,1,0:T(8,128)}, u32[]{:S(2)}) copy-start(f32[1,64,512]{2,1,0:T(8,128)} %param.10) | copy-start | bytes 393220
  32.7 27.6 %collective-permute-start.6 = (f32[512,128]{1,0:T(8,128)}, f32[512,128]{1,0:T(8,128)}, u32[]{:S(2)}, u32[]{:S(2)}) collective-permute-start(f32[512,128]{1,0:T(8,128)} %get-tuple-element.58), channel_id=1, source_target_pairs={{0,4},{1,5},{2,6},{3,7},{4,0},{5,1},{6,2},{7,3},{8,12},{9,13},{10,... | collective-permute-start | bytes 786440 | tf_op jit(solution)/shard_map/ppermute | solution.py:479
  35.5 24.9 %collective-permute-start.7 = (f32[512,128]{1,0:T(8,128)}, f32[512,128]{1,0:T(8,128)}, u32[]{:S(2)}, u32[]{:S(2)}) collective-permute-start(f32[512,128]{1,0:T(8,128)} %get-tuple-element.59), channel_id=1, source_target_pairs={{0,4},{1,5},{2,6},{3,7},{4,0},{5,1},{6,2},{7,3},{8,12},{9,13},{10,... | collective-permute-start | bytes 786440 | tf_op jit(solution)/shard_map/ppermute | solution.py:479
  37.7 1.9 %copy-start.8 = (f32[2,64,640]{2,1,0:T(8,128)}, f32[2,64,640]{2,1,0:T(8,128)S(1)}, u32[]{:S(2)}) copy-start(f32[2,64,640]{2,1,0:T(8,128)S(1)} %get-tuple-element.40.u_ref) | copy-start | bytes 983044
  37.7 20.4 %copy-start.2 = (f32[768,128]{1,0:T(8,128)S(1)}, f32[768,128]{1,0:T(8,128)}, u32[]{:S(2)}) copy-start(f32[768,128]{1,0:T(8,128)} %get-tuple-element.51.rest_0_) | copy-start | bytes 1179652
  63.7 22.1 %copy-start.9 = (f32[2,64,640]{2,1,0:T(8,128)S(1)}, f32[2,64,640]{2,1,0:T(8,128)}, u32[]{:S(2)}) copy-start(f32[2,64,640]{2,1,0:T(8,128)} %copy-done.8) | copy-start | bytes 983044
  63.7 22.1 %all-to-all-start.1 = ((f32[4,6,16,640]{3,2,1,0:T(8,128)}), f32[4,6,16,640]{3,2,1,0:T(8,128)S(1)}, u32[]{:S(2)}, u32[]{:S(2)}) async-start(f32[4,6,16,640]{3,2,1,0:T(8,128)} %shard_map.111), calls=%async_computation.1 | async-start | bytes 1966080 | tf_op jit(solution)/shard_map/all_to_all | solution.py:549
  67.3 13.2 %collective-permute-start.8 = (f32[2,16,640]{2,1,0:T(8,128)S(1)}, f32[2,16,640]{2,1,0:T(8,128)S(1)}, u32[]{:S(2)}, u32[]{:S(2)}) collective-permute-start(f32[2,16,640]{2,1,0:T(8,128)S(1)} %get-tuple-element.60), channel_id=1, source_target_pairs={{0,4},{1,5},{2,6},{3,7},{4,0},{5,1},{6,2},{7,3},{8,12},{9,13},{10,... | collective-permute-start | bytes 245768 | tf_op jit(solution)/shard_map/ppermute | solution.py:483
  69.2 12.1 %collective-permute-start.9 = (f32[2,16,640]{2,1,0:T(8,128)S(1)}, f32[2,16,640]{2,1,0:T(8,128)S(1)}, u32[]{:S(2)}, u32[]{:S(2)}) collective-permute-start(f32[2,16,640]{2,1,0:T(8,128)S(1)} %get-tuple-element.61), channel_id=1, source_target_pairs={{0,12},{1,13},{2,14},{3,15},{4,8},{5,9},{6,10},{7,11},{8,4},{9,5},... | collective-permute-start | bytes 245768 | tf_op jit(solution)/shard_map/ppermute | solution.py:483
  70.0 15.3 %collective-permute-start.10 = (f32[2,16,640]{2,1,0:T(8,128)S(1)}, f32[2,16,640]{2,1,0:T(8,128)S(1)}, u32[]{:S(2)}, u32[]{:S(2)}) collective-permute-start(f32[2,16,640]{2,1,0:T(8,128)S(1)} %get-tuple-element.62), channel_id=1, source_target_pairs={{0,20},{1,21},{2,22},{3,23},{4,16},{5,17},{6,18},{7,19},{8,28},{9,... | collective-permute-start | bytes 245768 | tf_op jit(solution)/shard_map/ppermute | solution.py:483
  73.0 12.8 %copy-start.4 = (f32[64,640]{1,0:T(8,128)S(1)}, f32[64,640]{1,0:T(8,128)}, u32[]{:S(2)}) copy-start(f32[64,640]{1,0:T(8,128)} %copy-done.3) | copy-start | bytes 491524
  73.0 12.8 %copy-start.7 = (f32[2,64,640]{2,1,0:T(8,128)S(1)}, f32[2,64,640]{2,1,0:T(8,128)}, u32[]{:S(2)}) copy-start(f32[2,64,640]{2,1,0:T(8,128)} %copy-done.6) | copy-start | bytes 983044
  73.0 12.7 %collective-permute-start.11 = (f32[2,16,640]{2,1,0:T(8,128)S(1)}, f32[2,16,640]{2,1,0:T(8,128)S(1)}, u32[]{:S(2)}, u32[]{:S(2)}) collective-permute-start(f32[2,16,640]{2,1,0:T(8,128)S(1)} %get-tuple-element.63), channel_id=1, source_target_pairs={{0,28},{1,29},{2,30},{3,31},{4,24},{5,25},{6,26},{7,27},{8,20},{9,... | collective-permute-start | bytes 245768 | tf_op jit(solution)/shard_map/ppermute | solution.py:483
  94.0 10.8 %all-to-all-start.2 = ((f32[32,1,128]{2,1,0:T(1,128)}), f32[32,1,128]{2,1,0:T(1,128)S(1)}, u32[]{:S(2)}, u32[]{:S(2)}) async-start(f32[32,1,128]{2,1,0:T(1,128)} %get-tuple-element.64), calls=%async_computation.2 | async-start | bytes 32768 | tf_op jit(solution)/shard_map/all_to_all | solution.py:556
  97.7 7.0 %copy-start.11 = (f32[2,64,512]{2,1,0:T(8,128)S(1)}, f32[2,64,512]{2,1,0:T(8,128)}, u32[]{:S(2)}) copy-start(f32[2,64,512]{2,1,0:T(8,128)} %copy-done.10) | copy-start | bytes 786436
  (3 other events, 3.3 us)

commit v10 on v9

--- a/solution.py
+++ b/solution.py
@@ -15,7 +15,6 @@
 ROWS = F * NB * LX
 HALF = SEG // 2
 SPLIT = 16
-X_WIDTH = 256
 Y_LINES = 16
 VMEM_BYTES = 32 * 1024 * 1024
 PACK_BYTES = 60 * 1024 * 1024
@@ -46,14 +45,6 @@
 
 def ends_tile(before, after):
     return jnp.where(iota(after.shape, after.ndim - 1) < HALF, after, before)
-
-
-def sweep(values, coeffs, axis):
-    size = values.shape[axis]
-    for _ in range(M):
-        flux = coeffs * (pltpu.roll(values, size - 1, axis) - values)
-        values = values + flux - pltpu.roll(flux, 1, axis)
-    return values
 
 
 def start_copies(pairs, sems):
@@ -218,19 +209,17 @@
 
 
 def cut_part(rows_ref, to, f, q, spans):
-    width = to.shape[1] - SEG
-    per = width // SEG
+    per = to.shape[0] - 1
 
     def tile(b):
         start = pl.multiple_of((f * NB + b) * LX, LX)
         return rows_ref[pl.ds(start, LX), :]
 
     for j in range(per):
-        to[:, j * SEG:(j + 1) * SEG] = tile(q * per + j)
+        to[j] = tile(q * per + j)
     before = tile(jnp.maximum(q * per - 1, 0))
     after = tile(jnp.minimum(q * per + per, NB - 1))
-    to[:, width:] = ends_tile(jnp.where(q > 0, before, 0.0),
-                              jnp.where(q < spans - 1, after, 0.0))
+    to[per] = ends_tile(jnp.where(q > 0, before, 0.0), jnp.where(q < spans - 1, after, 0.0))
 
 
 def weights_kernel(half, cap, blk, across, *rest):
@@ -265,19 +254,14 @@
     sums_ref[...] = acc_ref[:, :SEG] + pltpu.roll(acc_ref[:, SEG:], 1, 0)
 
 
-def products_across_kernel(half, cap, blk, meta_ref, *rest):
-    v_refs, (meta_out, *outs, acc_ref, sums_ref) = rest[:half], rest[half:]
-    meta_out[...] = meta_ref[...]
-    sum_products(half, cap, blk, 1, meta_ref, v_refs, acc_ref, sums_ref)
+def products_kernel(half, cap, blk, meta_ref, d_ref, e_ref, far_d_ref, far_e_ref, *rest):
+    v_refs, (out, *far_outs, acc_ref, sums_ref, far_ref, side) = rest[:half], rest[half:]
+    spans = out.shape[0]
+    sum_products(half, cap, blk, 1, meta_ref, v_refs, acc_ref, far_ref)
     me = lax.axis_index("px")
-    for k, out in enumerate(outs):
+    for k, far_out in enumerate(far_outs):
         for f in range(F):
-            cut_part(sums_ref, out.at[f], f, me ^ k, len(outs))
-
-
-def products_kernel(half, cap, blk, meta_ref, d_ref, e_ref, far_d_ref, far_e_ref, *rest):
-    v_refs, (out, acc_ref, sums_ref, side) = rest[:half], rest[half:]
-    spans = out.shape[0]
+            cut_part(far_ref, far_out.at[f], f, me ^ k, spans)
     sum_products(half, cap, blk, 0, meta_ref, v_refs, acc_ref, sums_ref)
     side[0] = d_ref[...] + far_d_ref[...]
     side[1] = e_ref[...] + far_e_ref[...]
@@ -287,32 +271,72 @@
                 cut_part(rows_ref, out.at[q, channel * F + f], f, q, spans)
 
 
+def x_lines(nx):
+    return [pl.ds(i, 8, stride=nx // 8) for i in range(nx // 8)]
+
+
+def next_line(lines):
+    return lines[1:] + [pltpu.roll(lines[0], 7, 0)]
+
+
+def previous_line(lines):
+    return [pltpu.roll(lines[-1], 1, 0)] + lines[:-1]
+
+
 def sweep_x_into(to_ref, from_ref, cx_ref, plus_ref=None, sign=1.0):
-    size = cx_ref.shape[1]
-    for low in range(0, size, X_WIDTH):
-        tile = slice(low, min(low + X_WIDTH, size))
-        values = sweep(from_ref[:, tile], cx_ref[:, tile], 0)
-        if plus_ref is not None:
-            values = values + sign * plus_ref[:, tile]
-        to_ref[:, tile] = values
+    picks = x_lines(cx_ref.shape[1])
+    for t in range(cx_ref.shape[0]):
+        values = [from_ref[t, pick, :] for pick in picks]
+        coeffs = [cx_ref[t, pick, :] for pick in picks]
+        for _ in range(M):
+            flux = [c * (b - a) for c, a, b in zip(coeffs, values, next_line(values))]
+            values = [a + f - g for a, f, g in zip(values, flux, previous_line(flux))]
+        for pick, value in zip(picks, values):
+            if plus_ref is not None:
+                value = value + sign * plus_ref[t, pick, :]
+            to_ref[t, pick, :] = value
 
 
 def sweep_y_into(to_ref, from_ref, cy_ref):
-    for low in range(0, cy_ref.shape[0], Y_LINES):
+    tiles, nx, _ = cy_ref.shape
+    lane = iota((Y_LINES, SEG), 1)
+    for low in range(0, nx, Y_LINES):
         lines = slice(low, low + Y_LINES)
-        to_ref[lines, :] = sweep(from_ref[lines, :], cy_ref[lines, :], 1)
+        values = [from_ref[t, lines, :] for t in range(tiles)]
+        coeffs = [cy_ref[t, lines, :] for t in range(tiles)]
+        for _ in range(M):
+            moved = [pltpu.roll(value, SEG - 1, 1) for value in values]
+            after = [jnp.where(lane == SEG - 1, b, a) for a, b in zip(moved, moved[1:] + moved[:1])]
+            flux = [c * (b - a) for c, a, b in zip(coeffs, values, after)]
+            moved = [pltpu.roll(value, 1, 1) for value in flux]
+            before = [jnp.where(lane == 0, a, b) for a, b in zip(moved[-1:] + moved[:-1], moved)]
+            values = [a + f - g for a, f, g in zip(values, flux, before)]
+        for t, value in enumerate(values):
+            to_ref[t, lines, :] = value
+
+
+def normal_into(to_ref, from_ref, diagonal_ref, side_ref, base_ref=None):
+    tiles, nx, _ = diagonal_ref.shape
+    picks = x_lines(nx)
+    for t in range(tiles):
+        values = [from_ref[t, pick, :] for pick in picks]
+        sides = [side_ref[t, pick, :] for pick in picks]
+        low = previous_line([e * a for e, a in zip(sides, values)])
+        for i, (pick, after) in enumerate(zip(picks, next_line(values))):
+            result = diagonal_ref[t, pick, :] * values[i] + sides[i] * after + low[i]
+            if base_ref is not None:
+                result = base_ref[t, pick, :] - result
+            to_ref[t, pick, :] = result
 
 
 def start_kernel(c0_ref, cx_ref, swap_ref, c0_out, cx_out, cy_out, u_out, token_out):
     token_out[...] = jnp.zeros_like(token_out)
-    width = c0_ref.shape[2]
     nx = cx_ref.shape[0]
-    spans, count = swap_ref.shape[0], cy_out.shape[1] // SEG
+    spans, count = swap_ref.shape[0], cy_out.shape[0]
     me = lax.axis_index("px")
     for p in range(spans):
         for t in range(count):
-            cy_out[p * LX:(p + 1) * LX, t * SEG:(t + 1) * SEG] = (
-                swap_ref[p, t * LX:(t + 1) * LX, :])
+            cy_out[t, p * LX:(p + 1) * LX, :] = swap_ref[p, t * LX:(t + 1) * LX, :]
 
     def beside(i):
         lines = slice(count * LX + i * nx, count * LX + (i + 1) * nx)
@@ -320,13 +344,15 @@
         after = swap_ref[jnp.minimum(me + 1, spans - 1), lines, :]
         return ends_tile(jnp.where(me > 0, before, 0.0), jnp.where(me < spans - 1, after, 0.0))
 
-    last = cx_ref.shape[0] - 1
-    cx_out[:, :width] = cx_ref[...]
-    cx_out[:, width:] = beside(F)
-    cx_out[last:, :] = jnp.zeros((1, width + SEG), jnp.float32)
+    for t in range(count - 1):
+        tile = slice(t * SEG, (t + 1) * SEG)
+        cx_out[t] = cx_ref[:, tile]
+        for f in range(F):
+            c0_out[f, t] = c0_ref[f, :, tile]
+    cx_out[count - 1] = beside(F)
+    cx_out[:, nx - 1:, :] = jnp.zeros((count, 1, SEG), jnp.float32)
     for f in range(F):
-        c0_out[f, :, :width] = c0_ref[f]
-        c0_out[f, :, width:] = beside(f)
+        c0_out[f, count - 1] = beside(f)
         sweep_x_into(u_out.at[f], c0_out.at[f], cx_out)
         sweep_y_into(u_out.at[f], u_out.at[f], cy_out)
 
@@ -335,62 +361,48 @@
     parts, out = rest[:spans], rest[spans]
     me = lax.axis_index("px")
     for k, part in enumerate(parts):
+        rows = pl.ds(pl.multiple_of((me ^ k) * LX, LX), LX)
         for f in range(F):
-            out[f, pl.ds(pl.multiple_of((me ^ k) * LX, LX), LX), :] = part[f]
+            for t in range(out.shape[1]):
+                out[f, t, rows, :] = part[f, t]
 
 
 def solve_kernel(c0_ref, cx_ref, cy_ref, u_ref, obs_ref, far_ref, r_out, q_out, h_out, dots_out,
                  vec, coef, work):
-    width = r_out.shape[2]
     for p in range(obs_ref.shape[0]):
         rows = slice(p * LX, (p + 1) * LX)
         for channel in range(2 * F):
-            coef[channel, rows, :] = obs_ref[p, channel]
+            coef[channel, :, rows, :] = obs_ref[p, channel]
         for f in range(F):
-            coef[2 * F + f, rows, :] = obs_ref[p, 2 * F + f] + far_ref[f, rows, :]
-
-    def normal(f, values, tile):
-        size = values.shape[0]
-        side = coef[F + f, :, tile]
-        return (coef[f, :, tile] * values + side * pltpu.roll(values, size - 1, 0)
-                + pltpu.roll(side * values, 1, 0))
-
-    tiles = [slice(low, low + SEG) for low in range(0, width + SEG, SEG)]
-
-    def first(f, carry):
-        for tile in tiles:
-            work[:, tile] = coef[2 * F + f, :, tile] - normal(f, u_ref[f, :, tile], tile)
+            coef[2 * F + f, :, rows, :] = obs_ref[p, 2 * F + f] + far_ref[f, :, rows, :]
+
+    def solve_field(f, carry):
+        field = (coef.at[f], coef.at[F + f])
+        normal_into(work, u_ref.at[f], *field, coef.at[2 * F + f])
         sweep_y_into(work, work, cy_ref)
         sweep_x_into(vec.at[0, f], work, cx_ref, c0_ref.at[f], -1.0)
-        return carry
-
-    lax.fori_loop(0, F, first, 0)
-
-    def apply(f, carry):
         sweep_x_into(work, vec.at[0, f], cx_ref)
         sweep_y_into(work, work, cy_ref)
-        for tile in tiles:
-            work[:, tile] = normal(f, work[:, tile], tile)
+        normal_into(work, work, *field)
         sweep_y_into(work, work, cy_ref)
         sweep_x_into(vec.at[1, f], work, cx_ref, vec.at[0, f])
         sweep_x_into(vec.at[2, f], vec.at[1, f], cx_ref)
         sweep_y_into(vec.at[2, f], vec.at[2, f], cy_ref)
-        for tile in tiles:
-            h_out[f, :, tile] = normal(f, vec[2, f, :, tile], tile)
+        normal_into(h_out.at[f], vec.at[2, f], *field)
         return carry
 
-    lax.fori_loop(0, F, apply, 0)
-
+    lax.fori_loop(0, F, solve_field, 0)
+
+    tiles, nx = vec.shape[2] - 1, vec.shape[3]
     sums = [jnp.zeros((8, SEG), jnp.float32) for _ in range(4)]
     for f in range(F):
-        r_out[f] = vec[0, f, :, :width]
-        q_out[f] = vec[1, f, :, :width]
-        for low in range(0, vec.shape[2], 8):
-            for tile in tiles[:-1]:
-                r = vec[0, f, low:low + 8, tile]
-                q = vec[1, f, low:low + 8, tile]
-                s = vec[2, f, low:low + 8, tile]
-                for i, product in enumerate((r * r, r * q, q * q, s * h_out[f, low:low + 8, tile])):
+        for t in range(tiles):
+            r_out[f, :, t * SEG:(t + 1) * SEG] = vec[0, f, t]
+            q_out[f, :, t * SEG:(t + 1) * SEG] = vec[1, f, t]
+            for low in range(0, nx, 8):
+                lines = slice(low, low + 8)
+                r, q, s = (vec[i, f, t, lines, :] for i in range(3))
+                for i, product in enumerate((r * r, r * q, q * q, s * h_out[f, t, lines, :])):
                     sums[i] = sums[i] + product
     dots = jnp.zeros((1, SEG), jnp.float32)
     for i, total in enumerate(sums):
@@ -401,13 +413,13 @@
     dots_out[...] = jnp.broadcast_to(dots, dots_out.shape)
 
 
-def last_kernel(h_ref, q_ref, cx_ref, cy_ref, qq_out, work, other):
-    width = qq_out.shape[2]
-
+def last_kernel(h_ref, q_ref, cx_ref, cy_ref, qq_out, work):
     def apply(f, carry):
         sweep_y_into(work, h_ref.at[f], cy_ref)
-        sweep_x_into(other, work, cx_ref)
-        qq_out[f] = q_ref[f] + other[:, :width]
+        sweep_x_into(work, work, cx_ref)
+        for t in range(work.shape[0] - 1):
+            tile = slice(t * SEG, (t + 1) * SEG)
+            qq_out[f, :, tile] = q_ref[f, :, tile] + work[t]
         return carry
 
     lax.fori_loop(0, F, apply, 0)
@@ -468,7 +480,7 @@
     block_rows = 2 * cap + meta_rows
     chunks = rows // SEG
     nx, width = control_start.shape[2], control_start.shape[3]
-    ext = width + SEG
+    tiles = width // SEG + 1
     c0, cx = control_start[:, 0], coef_x[0]
     hbm, local, scalars = (
         pl.BlockSpec(memory_space=s) for s in (pltpu.HBM, pltpu.VMEM, pltpu.SMEM))
@@ -511,7 +523,7 @@
 
     swap = call(
         pack_swap_kernel,
-        f32(spans, LX * ext // SEG + (F + 1) * nx, SEG),
+        f32(spans, LX * tiles + (F + 1) * nx, SEG),
         [vmem(*coef_y.shape[1:]), vmem(F + 1, nx, SEG), vmem(F + 1, nx, SEG), dma((5,))],
         [local] + [hbm] * 3,
         limit=PACK_BYTES,
@@ -519,7 +531,8 @@
     swap = lax.all_to_all(swap, "px", split_axis=0, concat_axis=0, tiled=True)
     c0_ext, cx_ext, cy_ext, u_ext, token = call(
         start_kernel,
-        (f32(F, nx, ext), f32(nx, ext), f32(nx, ext), f32(F, nx, ext), f32(8, SEG)),
+        (f32(F, tiles, nx, SEG), f32(tiles, nx, SEG), f32(tiles, nx, SEG), f32(F, tiles, nx, SEG),
+         f32(8, SEG)),
     )(c0, cx, swap)
 
     def sum_weights(side, token, weight):
@@ -533,28 +546,23 @@
     meta, *side_across = sum_weights(1, w_blocks[0], FIRST)
     side_across = [to_half(values, half) for values in side_across]
     meta, *side = sum_weights(0, token, 1)
-    meta, *sums_across = call(
-        functools.partial(products_across_kernel, half, cap, blk),
-        (f32(half, meta_rows, SEG),) + (f32(F, LX, ext),) * spans,
-        [vmem(ROWS, 2 * SEG), vmem(ROWS, SEG)],
-    )(meta, *v_blocks)
+    parts, *sums_across = call(
+        functools.partial(products_kernel, half, cap, blk),
+        (f32(spans, 3 * F, tiles, LX, SEG),) + (f32(F, tiles, LX, SEG),) * spans,
+        [vmem(ROWS, 2 * SEG), vmem(ROWS, SEG), vmem(ROWS, SEG), vmem(2, ROWS, SEG)],
+    )(meta, *side, *side_across, *v_blocks)
     far_sums = call(
-        functools.partial(join_kernel, spans), f32(F, nx, ext), weight=JOIN,
+        functools.partial(join_kernel, spans), f32(F, tiles, nx, SEG), weight=JOIN,
     )(*across(sums_across))
-    parts = call(
-        functools.partial(products_kernel, half, cap, blk),
-        f32(spans, 3 * F, LX, ext),
-        [vmem(ROWS, 2 * SEG), vmem(ROWS, SEG), vmem(2, ROWS, SEG)],
-    )(meta, *side, *side_across, *v_blocks)
     parts = lax.all_to_all(parts, "px", split_axis=0, concat_axis=0, tiled=True)
 
     r, q, h, dots = call(
         solve_kernel,
-        (f32(F, nx, width),) * 2 + (f32(F, nx, ext), f32(groups * spans, 1, SEG)),
-        [vmem(3, F, nx, ext), vmem(3 * F, nx, ext), vmem(nx, ext)],
+        (f32(F, nx, width),) * 2 + (f32(F, tiles, nx, SEG), f32(groups * spans, 1, SEG)),
+        [vmem(3, F, tiles, nx, SEG), vmem(3 * F, tiles, nx, SEG), vmem(tiles, nx, SEG)],
     )(c0_ext, cx_ext, cy_ext, u_ext, parts, far_sums)
     dots = lax.all_to_all(dots, ("px", "py"), split_axis=0, concat_axis=0, tiled=True)
-    qq = call(last_kernel, f32(F, nx, width), [vmem(nx, ext)] * 2)(h, q, cx_ext, cy_ext)
+    qq = call(last_kernel, f32(F, nx, width), [vmem(tiles, nx, SEG)])(h, q, cx_ext, cy_ext)
     control, residual = call(finish_kernel, (f32(F, nx, width),) * 2)(dots, c0, r, q, qq)
     return control[:, None], residual[:, None]
 

time: 106 us -> 105 us (level)
    pallas_call x7 -> x6, Pallas kernels: 18.3 us -> 17.3 us  [the longest x1 7.64 us: shards(): call(solve_kernel, (f32(F, nx, width),) * 2 + (f32(F, tiles, nx, SEG), f3...]
  transfers between devices with their start and end apart: 15 -> 15, of which waited for: 8 -> 8; matrix products, arithmetic and copies ran while one was open for 0% -> 0% of each run, Pallas kernels for 18% -> 16%
where the time goes in v10:
time: 105 us
  waiting for transfers between devices  38.4 us (37%)
  Pallas kernels  36.8 us (35%)
  starting transfers between devices  28.3 us (27%)
    ppermute x8, waiting for transfers between devices, to_half(): return lax.ppermute(block, 'py', [(i, i ^ k) for i in range(groups)])  20.1 us
    ppermute x4, waiting for transfers between devices, across(): lax.ppermute(parts[k], ('px', 'py'), [(i * groups + j, (i ^ k) * groups +...  12.8 us
    ppermute x8, starting transfers between devices, to_half(): return lax.ppermute(block, 'py', [(i, i ^ k) for i in range(groups)])  11.1 us
    pallas_call x1, Pallas kernels, shards(): call(solve_kernel, (f32(F, nx, width),) * 2 + (f32(F, tiles, nx, SEG), f3...  7.64 us
    pallas_call x1, Pallas kernels, shards(): call(functools.partial(pack_weights_kernel, groups, cap, blk, block_rows)...  6.91 us
    ppermute x4, starting transfers between devices, across(): lax.ppermute(parts[k], ('px', 'py'), [(i * groups + j, (i ^ k) * groups +...  6.79 us
    pallas_call x1, Pallas kernels, shards(): call(functools.partial(pack_products_kernel, groups, cap), (f32(2 * cap,...  6.76 us
    all_to_all x1, waiting for transfers between devices, shards(): lax.all_to_all(dots, ('px', 'py'), split_axis=0, concat_axis=0, tiled=True)  5.51 us
  transfers between devices with their start and end apart: 15, of which 8 were waited for; matrix products, arithmetic and copies ran while one was open for 0% of the time, Pallas kernels for 16%

profile of v10, /device:TPU:0, one launch (start us, length us, event | category | flops | bytes accessed | tf_op | source)
XLA Modules:
  0.0 105.1 jit_solution(6186423334544671020)
XLA Ops:
  0.6 6.9 %shard_map.104 = (f32[784,128]{1,0:T(8,128)}, f32[784,128]{1,0:T(8,128)}, f32[784,128]{1,0:T(8,128)}, f32[784,128]{1,0:T(8,128)}, s32[8,128]{1,0:T(8,128)}) custom-call(s32[8,128]{1,0:T(8,128)} %bitcast.19, s32[8,128]{1,0:T(8,128)} %bitcast.20, s32[8,128]{1,0:T(8,128)} %bitcast.21, f32[8,128]{1,0:T(8,128)} %bitcast.22, f32[1024,128]{1,0:T(8,128)} %w_hbm.3), custom_call_target="tpu_custom_call" | custom-call | flops 1 | bytes 1 | tf_op jit(solution)/shard_map/pallas_call | solution.py:500
  7.5 3.0 %collective-permute-start = (f32[784,128]{1,0:T(8,128)}, f32[784,128]{1,0:T(8,128)S(1)}, u32[]{:S(2)}, u32[]{:S(2)}) collective-permute-start(f32[784,128]{1,0:T(8,128)} %get-tuple-element.42), channel_id=1, source_target_pairs={{0,1},{1,0},{2,3},{3,2},{4,5},{5,4},{6,7},{7,6},{8,9},{9,8},{10,11... | collective-permute-start | bytes 1204232 | tf_op jit(solution)/shard_map/ppermute | solution.py:491
  10.6 1.6 %collective-permute-start.1 = (f32[784,128]{1,0:T(8,128)}, f32[784,128]{1,0:T(8,128)S(1)}, u32[]{:S(2)}, u32[]{:S(2)}) collective-permute-start(f32[784,128]{1,0:T(8,128)} %get-tuple-element.47), channel_id=1, source_target_pairs={{0,2},{1,3},{2,0},{3,1},{4,6},{5,7},{6,4},{7,5},{8,10},{9,11},{10,... | collective-permute-start | bytes 1204232 | tf_op jit(solution)/shard_map/ppermute | solution.py:491
  12.1 2.5 %shard_map.105 = f32[4,272,128]{2,1,0:T(8,128)} custom-call(s32[8,128]{1,0:T(8,128)} %get-tuple-element.36._.slot_ref, f32[16,2048]{1,0:T(8,128)} %bitcast.18, f32[2,64,512]{2,1,0:T(8,128)} %bitcast.13, f32[64,512]{1,0:T(8,128)} %bitcast.16), custom_call_target="tpu_custom_call" | custom-call | flops 1 | bytes 1 | tf_op jit(solution)/shard_map/pallas_call | solution.py:524
  14.7 3.5 %all-to-all-start = ((f32[4,272,128]{2,1,0:T(8,128)}), f32[4,272,128]{2,1,0:T(8,128)S(1)}, u32[]{:S(2)}, u32[]{:S(2)}) async-start(f32[4,272,128]{2,1,0:T(8,128)} %shard_map.105), calls=%async_computation | async-start | bytes 1114112 | tf_op jit(solution)/shard_map/all_to_all | solution.py:531
  18.2 6.8 %shard_map.107 = (f32[768,128]{1,0:T(8,128)}, f32[768,128]{1,0:T(8,128)}, f32[768,128]{1,0:T(8,128)}, f32[768,128]{1,0:T(8,128)}) custom-call(s32[8,128]{1,0:T(8,128)} %get-tuple-element.36._.slot_ref, f32[1024,128]{1,0:T(8,128)} %w_hbm.3, f32[1024,128]{1,0:T(8,128)} %d_hbm.1), custom_call_target="tpu_custom_call" | custom-call | flops 1 | bytes 1 | tf_op jit(solution)/shard_map/pallas_call | solution.py:512
  24.9 2.0 %collective-permute-start.5 = (f32[768,128]{1,0:T(8,128)}, f32[768,128]{1,0:T(8,128)S(1)}, u32[]{:S(2)}, u32[]{:S(2)}) collective-permute-start(f32[768,128]{1,0:T(8,128)} %get-tuple-element.56), channel_id=1, source_target_pairs={{0,1},{1,0},{2,3},{3,2},{4,5},{5,4},{6,7},{7,6},{8,9},{9,8},{10,11... | collective-permute-start | bytes 1179656 | tf_op jit(solution)/shard_map/ppermute | solution.py:491
  26.9 1.6 %collective-permute-start.6 = (f32[768,128]{1,0:T(8,128)}, f32[768,128]{1,0:T(8,128)}, u32[]{:S(2)}, u32[]{:S(2)}) collective-permute-start(f32[768,128]{1,0:T(8,128)} %get-tuple-element.57), channel_id=1, source_target_pairs={{0,2},{1,3},{2,0},{3,1},{4,6},{5,7},{6,4},{7,5},{8,10},{9,11},{10,... | collective-permute-start | bytes 1179656 | tf_op jit(solution)/shard_map/ppermute | solution.py:491
  28.5 1.6 %collective-permute-done.2.rest_3_ = f32[784,128]{1,0:T(8,128)S(1)} collective-permute-done((f32[784,128]{1,0:T(8,128)}, f32[784,128]{1,0:T(8,128)S(1)}, u32[]{:S(2)}, u32[]{:S(2)}) %collective-permute-start.2) | collective-permute-done | bytes 401440 | tf_op jit(solution)/shard_map/ppermute | solution.py:491
  30.1 2.7 %shard_map.109 = (f32[4,16,128]{2,1,0:T(8,128)}, f32[512,128]{1,0:T(8,128)}, f32[512,128]{1,0:T(8,128)}) custom-call(f32[784,128]{1,0:T(8,128)S(1)} %copy-done, f32[784,128]{1,0:T(8,128)S(1)} %collective-permute-done.rest_1_, f32[784,128]{1,0:T(8,128)S(1)} %collective-permute-done.1.rest_2_, f32[784,128]{1,0:T(8,128)S(1)} %collective-permute-done.2.rest_3_, ...), custom_call_target="tpu_custom_call" | custom-call | flops 100000000 | bytes 100000000 | tf_op jit(solution)/shard_map/pallas_call | solution.py:539
  32.8 2.8 %collective-permute-start.3 = (f32[512,128]{1,0:T(8,128)}, f32[512,128]{1,0:T(8,128)}, u32[]{:S(2)}, u32[]{:S(2)}) collective-permute-start(f32[512,128]{1,0:T(8,128)} %get-tuple-element.53), channel_id=1, source_target_pairs={{0,4},{1,5},{2,6},{3,7},{4,0},{5,1},{6,2},{7,3},{8,12},{9,13},{10,... | collective-permute-start | bytes 786440 | tf_op jit(solution)/shard_map/ppermute | solution.py:491
  37.6 1.9 %shard_map.108 = (f32[4,16,128]{2,1,0:T(8,128)S(1)}, f32[512,128]{1,0:T(8,128)S(1)}, f32[512,128]{1,0:T(8,128)S(1)}) custom-call(f32[784,128]{1,0:T(8,128)S(1)} %copy-done, f32[784,128]{1,0:T(8,128)S(1)} %collective-permute-done.rest_1_, f32[784,128]{1,0:T(8,128)S(1)} %collective-permute-done.1.rest_2_, f32[784,128]{1,0:T(8,128)S(1)} %collective-permute-done.2.rest_3_, ...), custom_call_target="tpu_custom_call" | custom-call | flops 1 | bytes 1 | tf_op jit(solution)/shard_map/pallas_call | solution.py:539
  39.6 12.8 %collective-permute-done.3.far_d_ref = f32[512,128]{1,0:T(8,128)} collective-permute-done((f32[512,128]{1,0:T(8,128)}, f32[512,128]{1,0:T(8,128)}, u32[]{:S(2)}, u32[]{:S(2)}) %collective-permute-start.3) | collective-permute-done | bytes 262176 | tf_op jit(solution)/shard_map/ppermute | solution.py:491
  52.3 5.1 %collective-permute-done.4.far_e_ref = f32[512,128]{1,0:T(8,128)} collective-permute-done((f32[512,128]{1,0:T(8,128)}, f32[512,128]{1,0:T(8,128)}, u32[]{:S(2)}, u32[]{:S(2)}) %collective-permute-start.4) | collective-permute-done | bytes 262176 | tf_op jit(solution)/shard_map/ppermute | solution.py:491
  58.1 4.4 %shard_map.110 = (f32[4,6,5,16,128]{4,3,2,1,0:T(8,128)}, f32[2,5,16,128]{3,2,1,0:T(8,128)S(1)}, f32[2,5,16,128]{3,2,1,0:T(8,128)S(1)}, f32[2,5,16,128]{3,2,1,0:T(8,128)S(1)}, f32[2,5,16,128]{3,2,1,0:T(8,128)S(1)}) custom-call(f32[4,16,128]{2,1,0:T(8,128)S(1)} %get-tuple-element.50.meta_ref, f32[512,128]{1,0:T(8,128)S(1)} %get-tuple-element.51.d_ref, ...), custom_call_target="tpu_custom_call" | custom-call | flops 1 | bytes 1 | tf_op jit(solution)/shard_map/pallas_call | solution.py:549
  62.5 3.5 %all-to-all-start.1 = ((f32[4,6,5,16,128]{4,3,2,1,0:T(8,128)}), f32[4,6,5,16,128]{4,3,2,1,0:T(8,128)S(1)}, u32[]{:S(2)}, u32[]{:S(2)}) async-start(f32[4,6,5,16,128]{4,3,2,1,0:T(8,128)} %get-tuple-element.59), calls=%async_computation.1 | async-start | bytes 1966080 | tf_op jit(solution)/shard_map/all_to_all | solution.py:557
  66.0 2.8 %collective-permute-start.8 = (f32[2,5,16,128]{3,2,1,0:T(8,128)S(1)}, f32[2,5,16,128]{3,2,1,0:T(8,128)S(1)}, u32[]{:S(2)}, u32[]{:S(2)}) collective-permute-start(f32[2,5,16,128]{3,2,1,0:T(8,128)S(1)} %get-tuple-element.60), channel_id=1, source_target_pairs={{0,4},{1,5},{2,6},{3,7},{4,0},{5,1},{6,2},{7,3},{8,12},{9,13},{10,... | collective-permute-start | bytes 245768 | tf_op jit(solution)/shard_map/ppermute | solution.py:495
  68.8 3.7 %collective-permute-start.10 = (f32[2,5,16,128]{3,2,1,0:T(8,128)S(1)}, f32[2,5,16,128]{3,2,1,0:T(8,128)S(1)}, u32[]{:S(2)}, u32[]{:S(2)}) collective-permute-start(f32[2,5,16,128]{3,2,1,0:T(8,128)S(1)} %get-tuple-element.62), channel_id=1, source_target_pairs={{0,20},{1,21},{2,22},{3,23},{4,16},{5,17},{6,18},{7,19},{8,28},{9,... | collective-permute-start | bytes 245768 | tf_op jit(solution)/shard_map/ppermute | solution.py:495
  72.8 8.2 %collective-permute-done.9.rest_1_ = f32[2,5,16,128]{3,2,1,0:T(8,128)S(1)} collective-permute-done((f32[2,5,16,128]{3,2,1,0:T(8,128)S(1)}, f32[2,5,16,128]{3,2,1,0:T(8,128)S(1)}, u32[]{:S(2)}, u32[]{:S(2)}) %collective-permute-start.9) | collective-permute-done | bytes 81952 | tf_op jit(solution)/shard_map/ppermute | solution.py:495
  81.0 2.9 %collective-permute-done.10.rest_2_ = f32[2,5,16,128]{3,2,1,0:T(8,128)S(1)} collective-permute-done((f32[2,5,16,128]{3,2,1,0:T(8,128)S(1)}, f32[2,5,16,128]{3,2,1,0:T(8,128)S(1)}, u32[]{:S(2)}, u32[]{:S(2)}) %collective-permute-start.10) | collective-permute-done | bytes 81952 | tf_op jit(solution)/shard_map/ppermute | solution.py:495
  83.9 1.8 %collective-permute-done.11.rest_3_ = f32[2,5,16,128]{3,2,1,0:T(8,128)S(1)} collective-permute-done((f32[2,5,16,128]{3,2,1,0:T(8,128)S(1)}, f32[2,5,16,128]{3,2,1,0:T(8,128)S(1)}, u32[]{:S(2)}, u32[]{:S(2)}) %collective-permute-start.11) | collective-permute-done | bytes 81952 | tf_op jit(solution)/shard_map/ppermute | solution.py:495
  85.7 7.6 %shard_map.112 = (f32[2,64,512]{2,1,0:T(8,128)S(1)}, f32[2,64,512]{2,1,0:T(8,128)S(1)}, f32[2,5,64,128]{3,2,1,0:T(8,128)S(1)}, f32[32,1,128]{2,1,0:T(1,128)}) custom-call(f32[2,5,64,128]{3,2,1,0:T(8,128)S(1)} %copy-done.5, f32[5,64,128]{2,1,0:T(8,128)S(1)} %get-tuple-element.38.cx_ref, f32[5,64,128]{2,1,0:T(8,128)S(1)} %get-tuple-element.39.cy_ref, ...), custom_call_target="tpu_custom_call" | custom-call | flops 1 | bytes 1 | tf_op jit(solution)/shard_map/pallas_call | solution.py:559
  93.3 3.5 %all-to-all-start.2 = ((f32[32,1,128]{2,1,0:T(1,128)}), f32[32,1,128]{2,1,0:T(1,128)S(1)}, u32[]{:S(2)}, u32[]{:S(2)}) async-start(f32[32,1,128]{2,1,0:T(1,128)} %get-tuple-element.64), calls=%async_computation.2 | async-start | bytes 32768 | tf_op jit(solution)/shard_map/all_to_all | solution.py:564
  98.3 5.5 %all-to-all-done.2.dots_ref = f32[32,1,128]{2,1,0:T(1,128)S(1)} async-done(((f32[32,1,128]{2,1,0:T(1,128)}), f32[32,1,128]{2,1,0:T(1,128)S(1)}, u32[]{:S(2)}, u32[]{:S(2)}) %all-to-all-start.2) | async-done | bytes 16416 | tf_op jit(solution)/shard_map/all_to_all | solution.py:564
  (33 shorter events, 6.0 us)
Async XLA Ops:
  7.5 17.4 %collective-permute-start = (f32[784,128]{1,0:T(8,128)}, f32[784,128]{1,0:T(8,128)S(1)}, u32[]{:S(2)}, u32[]{:S(2)}) collective-permute-start(f32[784,128]{1,0:T(8,128)} %get-tuple-element.42), channel_id=1, source_target_pairs={{0,1},{1,0},{2,3},{3,2},{4,5},{5,4},{6,7},{7,6},{8,9},{9,8},{10,11... | collective-permute-start | bytes 1204232 | tf_op jit(solution)/shard_map/ppermute | solution.py:491
  10.6 17.9 %collective-permute-start.1 = (f32[784,128]{1,0:T(8,128)}, f32[784,128]{1,0:T(8,128)S(1)}, u32[]{:S(2)}, u32[]{:S(2)}) collective-permute-start(f32[784,128]{1,0:T(8,128)} %get-tuple-element.47), channel_id=1, source_target_pairs={{0,2},{1,3},{2,0},{3,1},{4,6},{5,7},{6,4},{7,5},{8,10},{9,11},{10,... | collective-permute-start | bytes 1204232 | tf_op jit(solution)/shard_map/ppermute | solution.py:491
  12.1 17.9 %collective-permute-start.2 = (f32[784,128]{1,0:T(8,128)}, f32[784,128]{1,0:T(8,128)S(1)}, u32[]{:S(2)}, u32[]{:S(2)}) collective-permute-start(f32[784,128]{1,0:T(8,128)} %get-tuple-element.48), channel_id=1, source_target_pairs={{0,3},{1,2},{2,1},{3,0},{4,7},{5,6},{6,5},{7,4},{8,11},{9,10},{10,... | collective-permute-start | bytes 1204232 | tf_op jit(solution)/shard_map/ppermute | solution.py:491
  14.7 21.0 %all-to-all-start = ((f32[4,272,128]{2,1,0:T(8,128)}), f32[4,272,128]{2,1,0:T(8,128)S(1)}, u32[]{:S(2)}, u32[]{:S(2)}) async-start(f32[4,272,128]{2,1,0:T(8,128)} %shard_map.105), calls=%async_computation | async-start | bytes 1114112 | tf_op jit(solution)/shard_map/all_to_all | solution.py:531
  18.2 11.9 %copy-start = (f32[784,128]{1,0:T(8,128)S(1)}, f32[784,128]{1,0:T(8,128)}, u32[]{:S(2)}) copy-start(f32[784,128]{1,0:T(8,128)} %get-tuple-element.41.rest_0_.rest_4_) | copy-start | bytes 1204228
  24.9 32.5 %collective-permute-start.5 = (f32[768,128]{1,0:T(8,128)}, f32[768,128]{1,0:T(8,128)S(1)}, u32[]{:S(2)}, u32[]{:S(2)}) collective-permute-start(f32[768,128]{1,0:T(8,128)} %get-tuple-element.56), channel_id=1, source_target_pairs={{0,1},{1,0},{2,3},{3,2},{4,5},{5,4},{6,7},{7,6},{8,9},{9,8},{10,11... | collective-permute-start | bytes 1179656 | tf_op jit(solution)/shard_map/ppermute | solution.py:491
  26.9 30.5 %collective-permute-start.6 = (f32[768,128]{1,0:T(8,128)}, f32[768,128]{1,0:T(8,128)}, u32[]{:S(2)}, u32[]{:S(2)}) collective-permute-start(f32[768,128]{1,0:T(8,128)} %get-tuple-element.57), channel_id=1, source_target_pairs={{0,2},{1,3},{2,0},{3,1},{4,6},{5,7},{6,4},{7,5},{8,10},{9,11},{10,... | collective-permute-start | bytes 1179656 | tf_op jit(solution)/shard_map/ppermute | solution.py:491
  28.5 29.6 %collective-permute-start.7 = (f32[768,128]{1,0:T(8,128)}, f32[768,128]{1,0:T(8,128)}, u32[]{:S(2)}, u32[]{:S(2)}) collective-permute-start(f32[768,128]{1,0:T(8,128)} %get-tuple-element.58), channel_id=1, source_target_pairs={{0,3},{1,2},{2,1},{3,0},{4,7},{5,6},{6,5},{7,4},{8,11},{9,10},{10,... | collective-permute-start | bytes 1179656 | tf_op jit(solution)/shard_map/ppermute | solution.py:491
  30.1 5.6 %copy-start.1 = (f32[2,1,64,512]{3,2,1,0:T(8,128)S(1)}, f32[2,1,64,512]{3,2,1,0:T(8,128)}, u32[]{:S(2)}) copy-start(f32[2,1,64,512]{3,2,1,0:T(8,128)} %param.9) | copy-start | bytes 786436
  30.1 5.6 %copy-start.2 = (f32[1,64,512]{2,1,0:T(8,128)S(1)}, f32[1,64,512]{2,1,0:T(8,128)}, u32[]{:S(2)}) copy-start(f32[1,64,512]{2,1,0:T(8,128)} %param.10) | copy-start | bytes 393220
  32.8 19.6 %collective-permute-start.3 = (f32[512,128]{1,0:T(8,128)}, f32[512,128]{1,0:T(8,128)}, u32[]{:S(2)}, u32[]{:S(2)}) collective-permute-start(f32[512,128]{1,0:T(8,128)} %get-tuple-element.53), channel_id=1, source_target_pairs={{0,4},{1,5},{2,6},{3,7},{4,0},{5,1},{6,2},{7,3},{8,12},{9,13},{10,... | collective-permute-start | bytes 786440 | tf_op jit(solution)/shard_map/ppermute | solution.py:491
  35.5 21.9 %collective-permute-start.4 = (f32[512,128]{1,0:T(8,128)}, f32[512,128]{1,0:T(8,128)}, u32[]{:S(2)}, u32[]{:S(2)}) collective-permute-start(f32[512,128]{1,0:T(8,128)} %get-tuple-element.54), channel_id=1, source_target_pairs={{0,4},{1,5},{2,6},{3,7},{4,0},{5,1},{6,2},{7,3},{8,12},{9,13},{10,... | collective-permute-start | bytes 786440 | tf_op jit(solution)/shard_map/ppermute | solution.py:491
  36.9 0.7 copy-start.6
  37.6 1.9 %copy-start.4 = (f32[2,5,64,128]{3,2,1,0:T(8,128)}, f32[2,5,64,128]{3,2,1,0:T(8,128)S(1)}, u32[]{:S(2)}) copy-start(f32[2,5,64,128]{3,2,1,0:T(8,128)S(1)} %get-tuple-element.37.c0_ref) | copy-start | bytes 983044
  37.6 20.5 %copy-start.3 = (f32[768,128]{1,0:T(8,128)S(1)}, f32[768,128]{1,0:T(8,128)}, u32[]{:S(2)}) copy-start(f32[768,128]{1,0:T(8,128)} %get-tuple-element.55.rest_0_) | copy-start | bytes 1179652
  62.5 23.2 %all-to-all-start.1 = ((f32[4,6,5,16,128]{4,3,2,1,0:T(8,128)}), f32[4,6,5,16,128]{4,3,2,1,0:T(8,128)S(1)}, u32[]{:S(2)}, u32[]{:S(2)}) async-start(f32[4,6,5,16,128]{4,3,2,1,0:T(8,128)} %get-tuple-element.59), calls=%async_computation.1 | async-start | bytes 1966080 | tf_op jit(solution)/shard_map/all_to_all | solution.py:557
  66.0 6.8 %collective-permute-start.8 = (f32[2,5,16,128]{3,2,1,0:T(8,128)S(1)}, f32[2,5,16,128]{3,2,1,0:T(8,128)S(1)}, u32[]{:S(2)}, u32[]{:S(2)}) collective-permute-start(f32[2,5,16,128]{3,2,1,0:T(8,128)S(1)} %get-tuple-element.60), channel_id=1, source_target_pairs={{0,4},{1,5},{2,6},{3,7},{4,0},{5,1},{6,2},{7,3},{8,12},{9,13},{10,... | collective-permute-start | bytes 245768 | tf_op jit(solution)/shard_map/ppermute | solution.py:495
  68.8 12.2 %collective-permute-start.9 = (f32[2,5,16,128]{3,2,1,0:T(8,128)S(1)}, f32[2,5,16,128]{3,2,1,0:T(8,128)S(1)}, u32[]{:S(2)}, u32[]{:S(2)}) collective-permute-start(f32[2,5,16,128]{3,2,1,0:T(8,128)S(1)} %get-tuple-element.61), channel_id=1, source_target_pairs={{0,12},{1,13},{2,14},{3,15},{4,8},{5,9},{6,10},{7,11},{8,4},{9,5},... | collective-permute-start | bytes 245768 | tf_op jit(solution)/shard_map/ppermute | solution.py:495
  68.8 15.0 %collective-permute-start.10 = (f32[2,5,16,128]{3,2,1,0:T(8,128)S(1)}, f32[2,5,16,128]{3,2,1,0:T(8,128)S(1)}, u32[]{:S(2)}, u32[]{:S(2)}) collective-permute-start(f32[2,5,16,128]{3,2,1,0:T(8,128)S(1)} %get-tuple-element.62), channel_id=1, source_target_pairs={{0,20},{1,21},{2,22},{3,23},{4,16},{5,17},{6,18},{7,19},{8,28},{9,... | collective-permute-start | bytes 245768 | tf_op jit(solution)/shard_map/ppermute | solution.py:495
  72.5 13.1 %copy-start.5 = (f32[2,5,64,128]{3,2,1,0:T(8,128)S(1)}, f32[2,5,64,128]{3,2,1,0:T(8,128)}, u32[]{:S(2)}) copy-start(f32[2,5,64,128]{3,2,1,0:T(8,128)} %copy-done.4) | copy-start | bytes 983044
  72.5 13.1 %copy-start.7 = (f32[2,5,64,128]{3,2,1,0:T(8,128)S(1)}, f32[2,5,64,128]{3,2,1,0:T(8,128)}, u32[]{:S(2)}) copy-start(f32[2,5,64,128]{3,2,1,0:T(8,128)} %copy-done.6) | copy-start | bytes 983044
  72.5 13.1 %collective-permute-start.11 = (f32[2,5,16,128]{3,2,1,0:T(8,128)S(1)}, f32[2,5,16,128]{3,2,1,0:T(8,128)S(1)}, u32[]{:S(2)}, u32[]{:S(2)}) collective-permute-start(f32[2,5,16,128]{3,2,1,0:T(8,128)S(1)} %get-tuple-element.63), channel_id=1, source_target_pairs={{0,28},{1,29},{2,30},{3,31},{4,24},{5,25},{6,26},{7,27},{8,20},{9,... | collective-permute-start | bytes 245768 | tf_op jit(solution)/shard_map/ppermute | solution.py:495
  93.3 10.5 %all-to-all-start.2 = ((f32[32,1,128]{2,1,0:T(1,128)}), f32[32,1,128]{2,1,0:T(1,128)S(1)}, u32[]{:S(2)}, u32[]{:S(2)}) async-start(f32[32,1,128]{2,1,0:T(1,128)} %get-tuple-element.64), calls=%async_computation.2 | async-start | bytes 32768 | tf_op jit(solution)/shard_map/all_to_all | solution.py:564

commit v11 on v10

--- a/solution.py
+++ b/solution.py
@@ -15,6 +15,7 @@
 ROWS = F * NB * LX
 HALF = SEG // 2
 SPLIT = 16
+X_TILES = 2
 Y_LINES = 16
 VMEM_BYTES = 32 * 1024 * 1024
 PACK_BYTES = 60 * 1024 * 1024
@@ -275,61 +276,80 @@
     return [pl.ds(i, 8, stride=nx // 8) for i in range(nx // 8)]
 
 
-def next_line(lines):
-    return lines[1:] + [pltpu.roll(lines[0], 7, 0)]
-
-
-def previous_line(lines):
-    return [pltpu.roll(lines[-1], 1, 0)] + lines[:-1]
-
-
-def sweep_x_into(to_ref, from_ref, cx_ref, plus_ref=None, sign=1.0):
-    picks = x_lines(cx_ref.shape[1])
-    for t in range(cx_ref.shape[0]):
-        values = [from_ref[t, pick, :] for pick in picks]
-        coeffs = [cx_ref[t, pick, :] for pick in picks]
+def sweep_x_into(to_refs, from_refs, cx_ref, plus_refs=None, sign=1.0):
+    tiles, nx, _ = cx_ref.shape
+    picks = x_lines(nx)
+    for start in range(0, tiles, X_TILES):
+        group = range(start, min(start + X_TILES, tiles))
+        chains = [(i, t) for t in group for i in range(len(from_refs))]
+        coeffs = {t: [cx_ref[t, pick, :] for pick in picks] for t in group}
+        wrapped = {t: pltpu.roll(coeffs[t][-1], 1, 0) for t in group}
+        fields = {(i, t): [from_refs[i][t, pick, :] for pick in picks] for i, t in chains}
         for _ in range(M):
-            flux = [c * (b - a) for c, a, b in zip(coeffs, values, next_line(values))]
-            values = [a + f - g for a, f, g in zip(values, flux, previous_line(flux))]
-        for pick, value in zip(picks, values):
-            if plus_ref is not None:
-                value = value + sign * plus_ref[t, pick, :]
-            to_ref[t, pick, :] = value
-
-
-def sweep_y_into(to_ref, from_ref, cy_ref):
+            for i, t in chains:
+                values = fields[i, t]
+                after = values[1:] + [pltpu.roll(values[0], 7, 0)]
+                low = wrapped[t] * (values[0] - pltpu.roll(values[-1], 1, 0))
+                flux = [c * (b - a) for c, a, b in zip(coeffs[t], values, after)]
+                fields[i, t] = [a + f - g for a, f, g in zip(values, flux, [low] + flux[:-1])]
+        for i, t in chains:
+            for pick, value in zip(picks, fields[i, t]):
+                if plus_refs is not None:
+                    value = value + sign * plus_refs[i][t, pick, :]
+                to_refs[i][t, pick, :] = value
+
+
+def sweep_y_into(to_refs, from_refs, cy_ref):
     tiles, nx, _ = cy_ref.shape
     lane = iota((Y_LINES, SEG), 1)
+
+    def next_cells(values):
+        moved = [pltpu.roll(value, SEG - 1, 1) for value in values]
+        return [jnp.where(lane == SEG - 1, b, a) for a, b in zip(moved, moved[1:] + moved[:1])]
+
+    def previous_cells(values):
+        moved = [pltpu.roll(value, 1, 1) for value in values]
+        return [jnp.where(lane == 0, a, b) for a, b in zip(moved[-1:] + moved[:-1], moved)]
+
     for low in range(0, nx, Y_LINES):
         lines = slice(low, low + Y_LINES)
-        values = [from_ref[t, lines, :] for t in range(tiles)]
         coeffs = [cy_ref[t, lines, :] for t in range(tiles)]
+        coeffs_low = previous_cells(coeffs)
+        fields = [[ref[t, lines, :] for t in range(tiles)] for ref in from_refs]
         for _ in range(M):
-            moved = [pltpu.roll(value, SEG - 1, 1) for value in values]
-            after = [jnp.where(lane == SEG - 1, b, a) for a, b in zip(moved, moved[1:] + moved[:1])]
-            flux = [c * (b - a) for c, a, b in zip(coeffs, values, after)]
-            moved = [pltpu.roll(value, 1, 1) for value in flux]
-            before = [jnp.where(lane == 0, a, b) for a, b in zip(moved[-1:] + moved[:-1], moved)]
-            values = [a + f - g for a, f, g in zip(values, flux, before)]
-        for t, value in enumerate(values):
-            to_ref[t, lines, :] = value
-
-
-def normal_into(to_ref, from_ref, diagonal_ref, side_ref, base_ref=None):
-    tiles, nx, _ = diagonal_ref.shape
+            for i, values in enumerate(fields):
+                after, before = next_cells(values), previous_cells(values)
+                fields[i] = [
+                    a + c * (b - a) - d * (a - e)
+                    for a, b, c, d, e in zip(values, after, coeffs, coeffs_low, before)]
+        for to_ref, values in zip(to_refs, fields):
+            for t, value in enumerate(values):
+                to_ref[t, lines, :] = value
+
+
+def normal_into(to_refs, from_refs, diagonal_refs, side_refs, base_refs=None):
+    tiles, nx, _ = from_refs[0].shape
     picks = x_lines(nx)
     for t in range(tiles):
-        values = [from_ref[t, pick, :] for pick in picks]
-        sides = [side_ref[t, pick, :] for pick in picks]
-        low = previous_line([e * a for e, a in zip(sides, values)])
-        for i, (pick, after) in enumerate(zip(picks, next_line(values))):
-            result = diagonal_ref[t, pick, :] * values[i] + sides[i] * after + low[i]
-            if base_ref is not None:
-                result = base_ref[t, pick, :] - result
-            to_ref[t, pick, :] = result
-
-
-def start_kernel(c0_ref, cx_ref, swap_ref, c0_out, cx_out, cy_out, u_out, token_out):
+        for i, from_ref in enumerate(from_refs):
+            values = [from_ref[t, pick, :] for pick in picks]
+            sides = [side_refs[i][t, pick, :] for pick in picks]
+            low = [e * a for e, a in zip(sides, values)]
+            low = [pltpu.roll(low[-1], 1, 0)] + low[:-1]
+            after = values[1:] + [pltpu.roll(values[0], 7, 0)]
+            for line, pick in enumerate(picks):
+                result = (diagonal_refs[i][t, pick, :] * values[line] + sides[line] * after[line]
+                          + low[line])
+                if base_refs is not None:
+                    result = base_refs[i][t, pick, :] - result
+                to_refs[i][t, pick, :] = result
+
+
+def of_fields(ref, start=0):
+    return [ref.at[start + f] for f in range(F)]
+
+
+def start_kernel(c0_ref, cx_ref, swap_ref, c0_out, cx_out, cy_out, u_out, token_out, work):
     token_out[...] = jnp.zeros_like(token_out)
     nx = cx_ref.shape[0]
     spans, count = swap_ref.shape[0], cy_out.shape[0]
@@ -353,8 +373,8 @@
     cx_out[:, nx - 1:, :] = jnp.zeros((count, 1, SEG), jnp.float32)
     for f in range(F):
         c0_out[f, count - 1] = beside(f)
-        sweep_x_into(u_out.at[f], c0_out.at[f], cx_out)
-        sweep_y_into(u_out.at[f], u_out.at[f], cy_out)
+    sweep_x_into(of_fields(work), of_fields(c0_out), cx_out)
+    sweep_y_into(of_fields(u_out), of_fields(work), cy_out)
 
 
 def join_kernel(spans, *rest):
@@ -376,22 +396,20 @@
         for f in range(F):
             coef[2 * F + f, :, rows, :] = obs_ref[p, 2 * F + f] + far_ref[f, :, rows, :]
 
-    def solve_field(f, carry):
-        field = (coef.at[f], coef.at[F + f])
-        normal_into(work, u_ref.at[f], *field, coef.at[2 * F + f])
-        sweep_y_into(work, work, cy_ref)
-        sweep_x_into(vec.at[0, f], work, cx_ref, c0_ref.at[f], -1.0)
-        sweep_x_into(work, vec.at[0, f], cx_ref)
-        sweep_y_into(work, work, cy_ref)
-        normal_into(work, work, *field)
-        sweep_y_into(work, work, cy_ref)
-        sweep_x_into(vec.at[1, f], work, cx_ref, vec.at[0, f])
-        sweep_x_into(vec.at[2, f], vec.at[1, f], cx_ref)
-        sweep_y_into(vec.at[2, f], vec.at[2, f], cy_ref)
-        normal_into(h_out.at[f], vec.at[2, f], *field)
-        return carry
-
-    lax.fori_loop(0, F, solve_field, 0)
+    sides = (of_fields(coef), of_fields(coef, F))
+    one, two, r, q, s, h = (of_fields(ref) for ref in (
+        work.at[0], work.at[1], vec.at[0], vec.at[1], vec.at[2], h_out))
+    normal_into(one, of_fields(u_ref), *sides, of_fields(coef, 2 * F))
+    sweep_y_into(two, one, cy_ref)
+    sweep_x_into(r, two, cx_ref, of_fields(c0_ref), -1.0)
+    sweep_x_into(one, r, cx_ref)
+    sweep_y_into(two, one, cy_ref)
+    normal_into(one, two, *sides)
+    sweep_y_into(two, one, cy_ref)
+    sweep_x_into(q, two, cx_ref, r)
+    sweep_x_into(one, q, cx_ref)
+    sweep_y_into(s, one, cy_ref)
+    normal_into(h, s, *sides)
 
     tiles, nx = vec.shape[2] - 1, vec.shape[3]
     sums = [jnp.zeros((8, SEG), jnp.float32) for _ in range(4)]
@@ -414,15 +432,12 @@
 
 
 def last_kernel(h_ref, q_ref, cx_ref, cy_ref, qq_out, work):
-    def apply(f, carry):
-        sweep_y_into(work, h_ref.at[f], cy_ref)
-        sweep_x_into(work, work, cx_ref)
-        for t in range(work.shape[0] - 1):
+    sweep_y_into(of_fields(work.at[0]), of_fields(h_ref), cy_ref)
+    sweep_x_into(of_fields(work.at[1]), of_fields(work.at[0]), cx_ref)
+    for f in range(F):
+        for t in range(work.shape[2] - 1):
             tile = slice(t * SEG, (t + 1) * SEG)
-            qq_out[f, :, tile] = q_ref[f, :, tile] + work[t]
-        return carry
-
-    lax.fori_loop(0, F, apply, 0)
+            qq_out[f, :, tile] = q_ref[f, :, tile] + work[1, f, t]
 
 
 def finish_kernel(dots_ref, c0_ref, r_ref, q_ref, qq_ref, control_out, residual_out):
@@ -533,6 +548,7 @@
         start_kernel,
         (f32(F, tiles, nx, SEG), f32(tiles, nx, SEG), f32(tiles, nx, SEG), f32(F, tiles, nx, SEG),
          f32(8, SEG)),
+        [vmem(F, tiles, nx, SEG)],
     )(c0, cx, swap)
 
     def sum_weights(side, token, weight):
@@ -559,10 +575,11 @@
     r, q, h, dots = call(
         solve_kernel,
         (f32(F, nx, width),) * 2 + (f32(F, tiles, nx, SEG), f32(groups * spans, 1, SEG)),
-        [vmem(3, F, tiles, nx, SEG), vmem(3 * F, tiles, nx, SEG), vmem(tiles, nx, SEG)],
+        [vmem(3, F, tiles, nx, SEG), vmem(3 * F, tiles, nx, SEG), vmem(2, F, tiles, nx, SEG)],
     )(c0_ext, cx_ext, cy_ext, u_ext, parts, far_sums)
     dots = lax.all_to_all(dots, ("px", "py"), split_axis=0, concat_axis=0, tiled=True)
-    qq = call(last_kernel, f32(F, nx, width), [vmem(tiles, nx, SEG)])(h, q, cx_ext, cy_ext)
+    qq = call(last_kernel, f32(F, nx, width), [vmem(2, F, tiles, nx, SEG)])(
+        h, q, cx_ext, cy_ext)
     control, residual = call(finish_kernel, (f32(F, nx, width),) * 2)(dots, c0, r, q, qq)
     return control[:, None], residual[:, None]
 

time: 105 us -> 105 us (level)
  no operation moved by 1% of the time
where the time goes in v11:
time: 105 us
  waiting for transfers between devices  38 us (36%)
  Pallas kernels  37 us (35%)
  starting transfers between devices  28.3 us (27%)
    ppermute x8, waiting for transfers between devices, to_half(): return lax.ppermute(block, 'py', [(i, i ^ k) for i in range(groups)])  19.8 us
    ppermute x4, waiting for transfers between devices, across(): lax.ppermute(parts[k], ('px', 'py'), [(i * groups + j, (i ^ k) * groups +...  12.8 us
    ppermute x8, starting transfers between devices, to_half(): return lax.ppermute(block, 'py', [(i, i ^ k) for i in range(groups)])  11.1 us
    pallas_call x1, Pallas kernels, shards(): call(solve_kernel, (f32(F, nx, width),) * 2 + (f32(F, tiles, nx, SEG), f3...  7.52 us
    pallas_call x1, Pallas kernels, shards(): call(functools.partial(pack_weights_kernel, groups, cap, blk, block_rows)...  6.91 us
    pallas_call x1, Pallas kernels, shards(): call(functools.partial(pack_products_kernel, groups, cap), (f32(2 * cap,...  6.76 us
    ppermute x4, starting transfers between devices, across(): lax.ppermute(parts[k], ('px', 'py'), [(i * groups + j, (i ^ k) * groups +...  6.63 us
    all_to_all x1, waiting for transfers between devices, shards(): lax.all_to_all(dots, ('px', 'py'), split_axis=0, concat_axis=0, tiled=True)  5.46 us
  transfers between devices with their start and end apart: 15, of which 8 were waited for; matrix products, arithmetic and copies ran while one was open for 0% of the time, Pallas kernels for 16%

profile of v11, /device:TPU:0, one launch (start us, length us, event | category | flops | bytes accessed | tf_op | source)
XLA Modules:
  0.0 104.9 jit_solution(6846769801284521081)
XLA Ops:
  0.6 6.9 %shard_map.104 = (f32[784,128]{1,0:T(8,128)}, f32[784,128]{1,0:T(8,128)}, f32[784,128]{1,0:T(8,128)}, f32[784,128]{1,0:T(8,128)}, s32[8,128]{1,0:T(8,128)}) custom-call(s32[8,128]{1,0:T(8,128)} %bitcast.19, s32[8,128]{1,0:T(8,128)} %bitcast.20, s32[8,128]{1,0:T(8,128)} %bitcast.21, f32[8,128]{1,0:T(8,128)} %bitcast.22, f32[1024,128]{1,0:T(8,128)} %w_hbm.3), custom_call_target="tpu_custom_call" | custom-call | flops 1 | bytes 1 | tf_op jit(solution)/shard_map/pallas_call | solution.py:515
  7.5 3.0 %collective-permute-start = (f32[784,128]{1,0:T(8,128)}, f32[784,128]{1,0:T(8,128)S(1)}, u32[]{:S(2)}, u32[]{:S(2)}) collective-permute-start(f32[784,128]{1,0:T(8,128)} %get-tuple-element.42), channel_id=1, source_target_pairs={{0,1},{1,0},{2,3},{3,2},{4,5},{5,4},{6,7},{7,6},{8,9},{9,8},{10,11... | collective-permute-start | bytes 1204232 | tf_op jit(solution)/shard_map/ppermute | solution.py:506
  10.6 1.6 %collective-permute-start.1 = (f32[784,128]{1,0:T(8,128)}, f32[784,128]{1,0:T(8,128)S(1)}, u32[]{:S(2)}, u32[]{:S(2)}) collective-permute-start(f32[784,128]{1,0:T(8,128)} %get-tuple-element.47), channel_id=1, source_target_pairs={{0,2},{1,3},{2,0},{3,1},{4,6},{5,7},{6,4},{7,5},{8,10},{9,11},{10,... | collective-permute-start | bytes 1204232 | tf_op jit(solution)/shard_map/ppermute | solution.py:506
  12.1 2.5 %shard_map.105 = f32[4,272,128]{2,1,0:T(8,128)} custom-call(s32[8,128]{1,0:T(8,128)} %get-tuple-element.36._.slot_ref, f32[16,2048]{1,0:T(8,128)} %bitcast.18, f32[2,64,512]{2,1,0:T(8,128)} %bitcast.13, f32[64,512]{1,0:T(8,128)} %bitcast.16), custom_call_target="tpu_custom_call" | custom-call | flops 1 | bytes 1 | tf_op jit(solution)/shard_map/pallas_call | solution.py:539
  14.7 3.5 %all-to-all-start = ((f32[4,272,128]{2,1,0:T(8,128)}), f32[4,272,128]{2,1,0:T(8,128)S(1)}, u32[]{:S(2)}, u32[]{:S(2)}) async-start(f32[4,272,128]{2,1,0:T(8,128)} %shard_map.105), calls=%async_computation | async-start | bytes 1114112 | tf_op jit(solution)/shard_map/all_to_all | solution.py:546
  18.2 6.8 %shard_map.107 = (f32[768,128]{1,0:T(8,128)}, f32[768,128]{1,0:T(8,128)}, f32[768,128]{1,0:T(8,128)}, f32[768,128]{1,0:T(8,128)}) custom-call(s32[8,128]{1,0:T(8,128)} %get-tuple-element.36._.slot_ref, f32[1024,128]{1,0:T(8,128)} %w_hbm.3, f32[1024,128]{1,0:T(8,128)} %d_hbm.1), custom_call_target="tpu_custom_call" | custom-call | flops 1 | bytes 1 | tf_op jit(solution)/shard_map/pallas_call | solution.py:527
  24.9 2.0 %collective-permute-start.5 = (f32[768,128]{1,0:T(8,128)}, f32[768,128]{1,0:T(8,128)S(1)}, u32[]{:S(2)}, u32[]{:S(2)}) collective-permute-start(f32[768,128]{1,0:T(8,128)} %get-tuple-element.56), channel_id=1, source_target_pairs={{0,1},{1,0},{2,3},{3,2},{4,5},{5,4},{6,7},{7,6},{8,9},{9,8},{10,11... | collective-permute-start | bytes 1179656 | tf_op jit(solution)/shard_map/ppermute | solution.py:506
  26.9 1.6 %collective-permute-start.6 = (f32[768,128]{1,0:T(8,128)}, f32[768,128]{1,0:T(8,128)}, u32[]{:S(2)}, u32[]{:S(2)}) collective-permute-start(f32[768,128]{1,0:T(8,128)} %get-tuple-element.57), channel_id=1, source_target_pairs={{0,2},{1,3},{2,0},{3,1},{4,6},{5,7},{6,4},{7,5},{8,10},{9,11},{10,... | collective-permute-start | bytes 1179656 | tf_op jit(solution)/shard_map/ppermute | solution.py:506
  30.1 2.7 %shard_map.109 = (f32[4,16,128]{2,1,0:T(8,128)}, f32[512,128]{1,0:T(8,128)}, f32[512,128]{1,0:T(8,128)}) custom-call(f32[784,128]{1,0:T(8,128)S(1)} %copy-done, f32[784,128]{1,0:T(8,128)S(1)} %collective-permute-done.rest_1_, f32[784,128]{1,0:T(8,128)S(1)} %collective-permute-done.1.rest_2_, f32[784,128]{1,0:T(8,128)S(1)} %collective-permute-done.2.rest_3_, ...), custom_call_target="tpu_custom_call" | custom-call | flops 100000000 | bytes 100000000 | tf_op jit(solution)/shard_map/pallas_call | solution.py:555
  32.8 2.8 %collective-permute-start.3 = (f32[512,128]{1,0:T(8,128)}, f32[512,128]{1,0:T(8,128)}, u32[]{:S(2)}, u32[]{:S(2)}) collective-permute-start(f32[512,128]{1,0:T(8,128)} %get-tuple-element.53), channel_id=1, source_target_pairs={{0,4},{1,5},{2,6},{3,7},{4,0},{5,1},{6,2},{7,3},{8,12},{9,13},{10,... | collective-permute-start | bytes 786440 | tf_op jit(solution)/shard_map/ppermute | solution.py:506
  38.0 1.9 %shard_map.108 = (f32[4,16,128]{2,1,0:T(8,128)S(1)}, f32[512,128]{1,0:T(8,128)S(1)}, f32[512,128]{1,0:T(8,128)S(1)}) custom-call(f32[784,128]{1,0:T(8,128)S(1)} %copy-done, f32[784,128]{1,0:T(8,128)S(1)} %collective-permute-done.rest_1_, f32[784,128]{1,0:T(8,128)S(1)} %collective-permute-done.1.rest_2_, f32[784,128]{1,0:T(8,128)S(1)} %collective-permute-done.2.rest_3_, ...), custom_call_target="tpu_custom_call" | custom-call | flops 1 | bytes 1 | tf_op jit(solution)/shard_map/pallas_call | solution.py:555
  39.9 12.4 %collective-permute-done.3.far_d_ref = f32[512,128]{1,0:T(8,128)} collective-permute-done((f32[512,128]{1,0:T(8,128)}, f32[512,128]{1,0:T(8,128)}, u32[]{:S(2)}, u32[]{:S(2)}) %collective-permute-start.3) | collective-permute-done | bytes 262176 | tf_op jit(solution)/shard_map/ppermute | solution.py:506
  52.3 5.1 %collective-permute-done.4.far_e_ref = f32[512,128]{1,0:T(8,128)} collective-permute-done((f32[512,128]{1,0:T(8,128)}, f32[512,128]{1,0:T(8,128)}, u32[]{:S(2)}, u32[]{:S(2)}) %collective-permute-start.4) | collective-permute-done | bytes 262176 | tf_op jit(solution)/shard_map/ppermute | solution.py:506
  58.1 4.4 %shard_map.110 = (f32[4,6,5,16,128]{4,3,2,1,0:T(8,128)}, f32[2,5,16,128]{3,2,1,0:T(8,128)S(1)}, f32[2,5,16,128]{3,2,1,0:T(8,128)S(1)}, f32[2,5,16,128]{3,2,1,0:T(8,128)S(1)}, f32[2,5,16,128]{3,2,1,0:T(8,128)S(1)}) custom-call(f32[4,16,128]{2,1,0:T(8,128)S(1)} %get-tuple-element.50.meta_ref, f32[512,128]{1,0:T(8,128)S(1)} %get-tuple-element.51.d_ref, ...), custom_call_target="tpu_custom_call" | custom-call | flops 1 | bytes 1 | tf_op jit(solution)/shard_map/pallas_call | solution.py:565
  62.5 3.7 %all-to-all-start.1 = ((f32[4,6,5,16,128]{4,3,2,1,0:T(8,128)}), f32[4,6,5,16,128]{4,3,2,1,0:T(8,128)S(1)}, u32[]{:S(2)}, u32[]{:S(2)}) async-start(f32[4,6,5,16,128]{4,3,2,1,0:T(8,128)} %get-tuple-element.59), calls=%async_computation.1 | async-start | bytes 1966080 | tf_op jit(solution)/shard_map/all_to_all | solution.py:573
  66.2 2.8 %collective-permute-start.8 = (f32[2,5,16,128]{3,2,1,0:T(8,128)S(1)}, f32[2,5,16,128]{3,2,1,0:T(8,128)S(1)}, u32[]{:S(2)}, u32[]{:S(2)}) collective-permute-start(f32[2,5,16,128]{3,2,1,0:T(8,128)S(1)} %get-tuple-element.60), channel_id=1, source_target_pairs={{0,4},{1,5},{2,6},{3,7},{4,0},{5,1},{6,2},{7,3},{8,12},{9,13},{10,... | collective-permute-start | bytes 245768 | tf_op jit(solution)/shard_map/ppermute | solution.py:510
  69.0 3.6 %collective-permute-start.10 = (f32[2,5,16,128]{3,2,1,0:T(8,128)S(1)}, f32[2,5,16,128]{3,2,1,0:T(8,128)S(1)}, u32[]{:S(2)}, u32[]{:S(2)}) collective-permute-start(f32[2,5,16,128]{3,2,1,0:T(8,128)S(1)} %get-tuple-element.62), channel_id=1, source_target_pairs={{0,20},{1,21},{2,22},{3,23},{4,16},{5,17},{6,18},{7,19},{8,28},{9,... | collective-permute-start | bytes 245768 | tf_op jit(solution)/shard_map/ppermute | solution.py:510
  72.8 8.2 %collective-permute-done.9.rest_1_ = f32[2,5,16,128]{3,2,1,0:T(8,128)S(1)} collective-permute-done((f32[2,5,16,128]{3,2,1,0:T(8,128)S(1)}, f32[2,5,16,128]{3,2,1,0:T(8,128)S(1)}, u32[]{:S(2)}, u32[]{:S(2)}) %collective-permute-start.9) | collective-permute-done | bytes 81952 | tf_op jit(solution)/shard_map/ppermute | solution.py:510
  81.0 2.9 %collective-permute-done.10.rest_2_ = f32[2,5,16,128]{3,2,1,0:T(8,128)S(1)} collective-permute-done((f32[2,5,16,128]{3,2,1,0:T(8,128)S(1)}, f32[2,5,16,128]{3,2,1,0:T(8,128)S(1)}, u32[]{:S(2)}, u32[]{:S(2)}) %collective-permute-start.10) | collective-permute-done | bytes 81952 | tf_op jit(solution)/shard_map/ppermute | solution.py:510
  83.9 1.8 %collective-permute-done.11.rest_3_ = f32[2,5,16,128]{3,2,1,0:T(8,128)S(1)} collective-permute-done((f32[2,5,16,128]{3,2,1,0:T(8,128)S(1)}, f32[2,5,16,128]{3,2,1,0:T(8,128)S(1)}, u32[]{:S(2)}, u32[]{:S(2)}) %collective-permute-start.11) | collective-permute-done | bytes 81952 | tf_op jit(solution)/shard_map/ppermute | solution.py:510
  85.7 7.5 %shard_map.112 = (f32[2,64,512]{2,1,0:T(8,128)S(1)}, f32[2,64,512]{2,1,0:T(8,128)S(1)}, f32[2,5,64,128]{3,2,1,0:T(8,128)S(1)}, f32[32,1,128]{2,1,0:T(1,128)}) custom-call(f32[2,5,64,128]{3,2,1,0:T(8,128)S(1)} %copy-done.5, f32[5,64,128]{2,1,0:T(8,128)S(1)} %get-tuple-element.38.cx_ref, f32[5,64,128]{2,1,0:T(8,128)S(1)} %get-tuple-element.39.cy_ref, ...), custom_call_target="tpu_custom_call" | custom-call | flops 1 | bytes 1 | tf_op jit(solution)/shard_map/pallas_call | solution.py:575
  93.2 3.5 %all-to-all-start.2 = ((f32[32,1,128]{2,1,0:T(1,128)}), f32[32,1,128]{2,1,0:T(1,128)S(1)}, u32[]{:S(2)}, u32[]{:S(2)}) async-start(f32[32,1,128]{2,1,0:T(1,128)} %get-tuple-element.64), calls=%async_computation.2 | async-start | bytes 32768 | tf_op jit(solution)/shard_map/all_to_all | solution.py:580
  96.7 1.6 %shard_map.113.qq_ref = f32[2,64,512]{2,1,0:T(8,128)S(1)} custom-call(f32[2,5,64,128]{3,2,1,0:T(8,128)S(1)} %get-tuple-element.67.h_ref, f32[2,64,512]{2,1,0:T(8,128)S(1)} %get-tuple-element.66.q_ref, f32[5,64,128]{2,1,0:T(8,128)S(1)} %get-tuple-element.38.cx_ref, f32[5,64,128]{2,1,0:T(8,128)S(1)} %get-tuple-element.39.cy_ref), custom_call_target="tpu_custom_call" | custom-call | flops 1 | bytes 1 | tf_op jit(solution)/shard_map/pallas_call | solution.py:581
  98.3 5.5 %all-to-all-done.2.dots_ref = f32[32,1,128]{2,1,0:T(1,128)S(1)} async-done(((f32[32,1,128]{2,1,0:T(1,128)}), f32[32,1,128]{2,1,0:T(1,128)S(1)}, u32[]{:S(2)}, u32[]{:S(2)}) %all-to-all-start.2) | async-done | bytes 16416 | tf_op jit(solution)/shard_map/all_to_all | solution.py:580
  (33 shorter events, 6.3 us)
Async XLA Ops:
  7.5 17.4 %collective-permute-start = (f32[784,128]{1,0:T(8,128)}, f32[784,128]{1,0:T(8,128)S(1)}, u32[]{:S(2)}, u32[]{:S(2)}) collective-permute-start(f32[784,128]{1,0:T(8,128)} %get-tuple-element.42), channel_id=1, source_target_pairs={{0,1},{1,0},{2,3},{3,2},{4,5},{5,4},{6,7},{7,6},{8,9},{9,8},{10,11... | collective-permute-start | bytes 1204232 | tf_op jit(solution)/shard_map/ppermute | solution.py:506
  10.6 17.9 %collective-permute-start.1 = (f32[784,128]{1,0:T(8,128)}, f32[784,128]{1,0:T(8,128)S(1)}, u32[]{:S(2)}, u32[]{:S(2)}) collective-permute-start(f32[784,128]{1,0:T(8,128)} %get-tuple-element.47), channel_id=1, source_target_pairs={{0,2},{1,3},{2,0},{3,1},{4,6},{5,7},{6,4},{7,5},{8,10},{9,11},{10,... | collective-permute-start | bytes 1204232 | tf_op jit(solution)/shard_map/ppermute | solution.py:506
  12.1 17.9 %collective-permute-start.2 = (f32[784,128]{1,0:T(8,128)}, f32[784,128]{1,0:T(8,128)S(1)}, u32[]{:S(2)}, u32[]{:S(2)}) collective-permute-start(f32[784,128]{1,0:T(8,128)} %get-tuple-element.48), channel_id=1, source_target_pairs={{0,3},{1,2},{2,1},{3,0},{4,7},{5,6},{6,5},{7,4},{8,11},{9,10},{10,... | collective-permute-start | bytes 1204232 | tf_op jit(solution)/shard_map/ppermute | solution.py:506
  14.7 21.0 %all-to-all-start = ((f32[4,272,128]{2,1,0:T(8,128)}), f32[4,272,128]{2,1,0:T(8,128)S(1)}, u32[]{:S(2)}, u32[]{:S(2)}) async-start(f32[4,272,128]{2,1,0:T(8,128)} %shard_map.105), calls=%async_computation | async-start | bytes 1114112 | tf_op jit(solution)/shard_map/all_to_all | solution.py:546
  18.2 11.9 %copy-start = (f32[784,128]{1,0:T(8,128)S(1)}, f32[784,128]{1,0:T(8,128)}, u32[]{:S(2)}) copy-start(f32[784,128]{1,0:T(8,128)} %get-tuple-element.41.rest_0_.rest_4_) | copy-start | bytes 1204228
  24.9 32.5 %collective-permute-start.5 = (f32[768,128]{1,0:T(8,128)}, f32[768,128]{1,0:T(8,128)S(1)}, u32[]{:S(2)}, u32[]{:S(2)}) collective-permute-start(f32[768,128]{1,0:T(8,128)} %get-tuple-element.56), channel_id=1, source_target_pairs={{0,1},{1,0},{2,3},{3,2},{4,5},{5,4},{6,7},{7,6},{8,9},{9,8},{10,11... | collective-permute-start | bytes 1179656 | tf_op jit(solution)/shard_map/ppermute | solution.py:506
  26.9 30.5 %collective-permute-start.6 = (f32[768,128]{1,0:T(8,128)}, f32[768,128]{1,0:T(8,128)}, u32[]{:S(2)}, u32[]{:S(2)}) collective-permute-start(f32[768,128]{1,0:T(8,128)} %get-tuple-element.57), channel_id=1, source_target_pairs={{0,2},{1,3},{2,0},{3,1},{4,6},{5,7},{6,4},{7,5},{8,10},{9,11},{10,... | collective-permute-start | bytes 1179656 | tf_op jit(solution)/shard_map/ppermute | solution.py:506
  28.5 29.6 %collective-permute-start.7 = (f32[768,128]{1,0:T(8,128)}, f32[768,128]{1,0:T(8,128)}, u32[]{:S(2)}, u32[]{:S(2)}) collective-permute-start(f32[768,128]{1,0:T(8,128)} %get-tuple-element.58), channel_id=1, source_target_pairs={{0,3},{1,2},{2,1},{3,0},{4,7},{5,6},{6,5},{7,4},{8,11},{9,10},{10,... | collective-permute-start | bytes 1179656 | tf_op jit(solution)/shard_map/ppermute | solution.py:506
  30.1 5.6 %copy-start.1 = (f32[2,1,64,512]{3,2,1,0:T(8,128)S(1)}, f32[2,1,64,512]{3,2,1,0:T(8,128)}, u32[]{:S(2)}) copy-start(f32[2,1,64,512]{3,2,1,0:T(8,128)} %param.9) | copy-start | bytes 786436
  30.1 5.6 %copy-start.2 = (f32[1,64,512]{2,1,0:T(8,128)S(1)}, f32[1,64,512]{2,1,0:T(8,128)}, u32[]{:S(2)}) copy-start(f32[1,64,512]{2,1,0:T(8,128)} %param.10) | copy-start | bytes 393220
  32.8 19.6 %collective-permute-start.3 = (f32[512,128]{1,0:T(8,128)}, f32[512,128]{1,0:T(8,128)}, u32[]{:S(2)}, u32[]{:S(2)}) collective-permute-start(f32[512,128]{1,0:T(8,128)} %get-tuple-element.53), channel_id=1, source_target_pairs={{0,4},{1,5},{2,6},{3,7},{4,0},{5,1},{6,2},{7,3},{8,12},{9,13},{10,... | collective-permute-start | bytes 786440 | tf_op jit(solution)/shard_map/ppermute | solution.py:506
  35.5 21.9 %collective-permute-start.4 = (f32[512,128]{1,0:T(8,128)}, f32[512,128]{1,0:T(8,128)}, u32[]{:S(2)}, u32[]{:S(2)}) collective-permute-start(f32[512,128]{1,0:T(8,128)} %get-tuple-element.54), channel_id=1, source_target_pairs={{0,4},{1,5},{2,6},{3,7},{4,0},{5,1},{6,2},{7,3},{8,12},{9,13},{10,... | collective-permute-start | bytes 786440 | tf_op jit(solution)/shard_map/ppermute | solution.py:506
  37.2 0.7 copy-start.6
  38.0 1.9 %copy-start.4 = (f32[2,5,64,128]{3,2,1,0:T(8,128)}, f32[2,5,64,128]{3,2,1,0:T(8,128)S(1)}, u32[]{:S(2)}) copy-start(f32[2,5,64,128]{3,2,1,0:T(8,128)S(1)} %get-tuple-element.37.c0_ref) | copy-start | bytes 983044
  38.0 20.1 %copy-start.3 = (f32[768,128]{1,0:T(8,128)S(1)}, f32[768,128]{1,0:T(8,128)}, u32[]{:S(2)}) copy-start(f32[768,128]{1,0:T(8,128)} %get-tuple-element.55.rest_0_) | copy-start | bytes 1179652
  62.5 23.2 %all-to-all-start.1 = ((f32[4,6,5,16,128]{4,3,2,1,0:T(8,128)}), f32[4,6,5,16,128]{4,3,2,1,0:T(8,128)S(1)}, u32[]{:S(2)}, u32[]{:S(2)}) async-start(f32[4,6,5,16,128]{4,3,2,1,0:T(8,128)} %get-tuple-element.59), calls=%async_computation.1 | async-start | bytes 1966080 | tf_op jit(solution)/shard_map/all_to_all | solution.py:573
  66.2 6.6 %collective-permute-start.8 = (f32[2,5,16,128]{3,2,1,0:T(8,128)S(1)}, f32[2,5,16,128]{3,2,1,0:T(8,128)S(1)}, u32[]{:S(2)}, u32[]{:S(2)}) collective-permute-start(f32[2,5,16,128]{3,2,1,0:T(8,128)S(1)} %get-tuple-element.60), channel_id=1, source_target_pairs={{0,4},{1,5},{2,6},{3,7},{4,0},{5,1},{6,2},{7,3},{8,12},{9,13},{10,... | collective-permute-start | bytes 245768 | tf_op jit(solution)/shard_map/ppermute | solution.py:510
  69.0 12.0 %collective-permute-start.9 = (f32[2,5,16,128]{3,2,1,0:T(8,128)S(1)}, f32[2,5,16,128]{3,2,1,0:T(8,128)S(1)}, u32[]{:S(2)}, u32[]{:S(2)}) collective-permute-start(f32[2,5,16,128]{3,2,1,0:T(8,128)S(1)} %get-tuple-element.61), channel_id=1, source_target_pairs={{0,12},{1,13},{2,14},{3,15},{4,8},{5,9},{6,10},{7,11},{8,4},{9,5},... | collective-permute-start | bytes 245768 | tf_op jit(solution)/shard_map/ppermute | solution.py:510
  69.0 14.9 %collective-permute-start.10 = (f32[2,5,16,128]{3,2,1,0:T(8,128)S(1)}, f32[2,5,16,128]{3,2,1,0:T(8,128)S(1)}, u32[]{:S(2)}, u32[]{:S(2)}) collective-permute-start(f32[2,5,16,128]{3,2,1,0:T(8,128)S(1)} %get-tuple-element.62), channel_id=1, source_target_pairs={{0,20},{1,21},{2,22},{3,23},{4,16},{5,17},{6,18},{7,19},{8,28},{9,... | collective-permute-start | bytes 245768 | tf_op jit(solution)/shard_map/ppermute | solution.py:510
  72.5 13.1 %copy-start.5 = (f32[2,5,64,128]{3,2,1,0:T(8,128)S(1)}, f32[2,5,64,128]{3,2,1,0:T(8,128)}, u32[]{:S(2)}) copy-start(f32[2,5,64,128]{3,2,1,0:T(8,128)} %copy-done.4) | copy-start | bytes 983044
  72.5 13.1 %copy-start.7 = (f32[2,5,64,128]{3,2,1,0:T(8,128)S(1)}, f32[2,5,64,128]{3,2,1,0:T(8,128)}, u32[]{:S(2)}) copy-start(f32[2,5,64,128]{3,2,1,0:T(8,128)} %copy-done.6) | copy-start | bytes 983044
  72.5 13.1 %collective-permute-start.11 = (f32[2,5,16,128]{3,2,1,0:T(8,128)S(1)}, f32[2,5,16,128]{3,2,1,0:T(8,128)S(1)}, u32[]{:S(2)}, u32[]{:S(2)}) collective-permute-start(f32[2,5,16,128]{3,2,1,0:T(8,128)S(1)} %get-tuple-element.63), channel_id=1, source_target_pairs={{0,28},{1,29},{2,30},{3,31},{4,24},{5,25},{6,26},{7,27},{8,20},{9,... | collective-permute-start | bytes 245768 | tf_op jit(solution)/shard_map/ppermute | solution.py:510
  93.2 10.5 %all-to-all-start.2 = ((f32[32,1,128]{2,1,0:T(1,128)}), f32[32,1,128]{2,1,0:T(1,128)S(1)}, u32[]{:S(2)}, u32[]{:S(2)}) async-start(f32[32,1,128]{2,1,0:T(1,128)} %get-tuple-element.64), calls=%async_computation.2 | async-start | bytes 32768 | tf_op jit(solution)/shard_map/all_to_all | solution.py:580

commit v12 on v11

--- a/solution.py
+++ b/solution.py
@@ -15,7 +15,6 @@
 ROWS = F * NB * LX
 HALF = SEG // 2
 SPLIT = 16
-X_TILES = 2
 Y_LINES = 16
 VMEM_BYTES = 32 * 1024 * 1024
 PACK_BYTES = 60 * 1024 * 1024
@@ -279,24 +278,25 @@
 def sweep_x_into(to_refs, from_refs, cx_ref, plus_refs=None, sign=1.0):
     tiles, nx, _ = cx_ref.shape
     picks = x_lines(nx)
-    for start in range(0, tiles, X_TILES):
-        group = range(start, min(start + X_TILES, tiles))
-        chains = [(i, t) for t in group for i in range(len(from_refs))]
-        coeffs = {t: [cx_ref[t, pick, :] for pick in picks] for t in group}
-        wrapped = {t: pltpu.roll(coeffs[t][-1], 1, 0) for t in group}
-        fields = {(i, t): [from_refs[i][t, pick, :] for pick in picks] for i, t in chains}
+
+    def sweep_tile(t, carry):
+        coeffs = [cx_ref[t, pick, :] for pick in picks]
+        wrapped = pltpu.roll(coeffs[-1], 1, 0)
+        fields = [[ref[t, pick, :] for pick in picks] for ref in from_refs]
         for _ in range(M):
-            for i, t in chains:
-                values = fields[i, t]
+            for i, values in enumerate(fields):
                 after = values[1:] + [pltpu.roll(values[0], 7, 0)]
-                low = wrapped[t] * (values[0] - pltpu.roll(values[-1], 1, 0))
-                flux = [c * (b - a) for c, a, b in zip(coeffs[t], values, after)]
-                fields[i, t] = [a + f - g for a, f, g in zip(values, flux, [low] + flux[:-1])]
-        for i, t in chains:
-            for pick, value in zip(picks, fields[i, t]):
+                low = wrapped * (values[0] - pltpu.roll(values[-1], 1, 0))
+                flux = [c * (b - a) for c, a, b in zip(coeffs, values, after)]
+                fields[i] = [a + f - g for a, f, g in zip(values, flux, [low] + flux[:-1])]
+        for i, values in enumerate(fields):
+            for pick, value in zip(picks, values):
                 if plus_refs is not None:
                     value = value + sign * plus_refs[i][t, pick, :]
                 to_refs[i][t, pick, :] = value
+        return carry
+
+    lax.fori_loop(0, tiles, sweep_tile, 0)
 
 
 def sweep_y_into(to_refs, from_refs, cy_ref):
@@ -311,26 +311,28 @@
         moved = [pltpu.roll(value, 1, 1) for value in values]
         return [jnp.where(lane == 0, a, b) for a, b in zip(moved[-1:] + moved[:-1], moved)]
 
-    for low in range(0, nx, Y_LINES):
-        lines = slice(low, low + Y_LINES)
+    def sweep_lines(group, carry):
+        lines = pl.ds(pl.multiple_of(group * Y_LINES, Y_LINES), Y_LINES)
         coeffs = [cy_ref[t, lines, :] for t in range(tiles)]
-        coeffs_low = previous_cells(coeffs)
         fields = [[ref[t, lines, :] for t in range(tiles)] for ref in from_refs]
         for _ in range(M):
             for i, values in enumerate(fields):
-                after, before = next_cells(values), previous_cells(values)
+                flux = [c * (b - a) for c, a, b in zip(coeffs, values, next_cells(values))]
                 fields[i] = [
-                    a + c * (b - a) - d * (a - e)
-                    for a, b, c, d, e in zip(values, after, coeffs, coeffs_low, before)]
+                    a + f - g for a, f, g in zip(values, flux, previous_cells(flux))]
         for to_ref, values in zip(to_refs, fields):
             for t, value in enumerate(values):
                 to_ref[t, lines, :] = value
+        return carry
+
+    lax.fori_loop(0, nx // Y_LINES, sweep_lines, 0)
 
 
 def normal_into(to_refs, from_refs, diagonal_refs, side_refs, base_refs=None):
     tiles, nx, _ = from_refs[0].shape
     picks = x_lines(nx)
-    for t in range(tiles):
+
+    def tile(t, carry):
         for i, from_ref in enumerate(from_refs):
             values = [from_ref[t, pick, :] for pick in picks]
             sides = [side_refs[i][t, pick, :] for pick in picks]
@@ -343,6 +345,9 @@
                 if base_refs is not None:
                     result = base_refs[i][t, pick, :] - result
                 to_refs[i][t, pick, :] = result
+        return carry
+
+    lax.fori_loop(0, tiles, tile, 0)
 
 
 def of_fields(ref, start=0):
@@ -412,16 +417,21 @@
     normal_into(h, s, *sides)
 
     tiles, nx = vec.shape[2] - 1, vec.shape[3]
-    sums = [jnp.zeros((8, SEG), jnp.float32) for _ in range(4)]
     for f in range(F):
         for t in range(tiles):
             r_out[f, :, t * SEG:(t + 1) * SEG] = vec[0, f, t]
             q_out[f, :, t * SEG:(t + 1) * SEG] = vec[1, f, t]
-            for low in range(0, nx, 8):
-                lines = slice(low, low + 8)
-                r, q, s = (vec[i, f, t, lines, :] for i in range(3))
-                for i, product in enumerate((r * r, r * q, q * q, s * h_out[f, t, lines, :])):
-                    sums[i] = sums[i] + product
+
+    def products(index, sums):
+        f, t = index // tiles, index % tiles
+        for low in range(0, nx, 8):
+            lines = slice(low, low + 8)
+            r, q, s = (vec[i, f, t, lines, :] for i in range(3))
+            terms = (r * r, r * q, q * q, s * h_out[f, t, lines, :])
+            sums = tuple(a + b for a, b in zip(sums, terms))
+        return sums
+
+    sums = lax.fori_loop(0, F * tiles, products, (jnp.zeros((8, SEG), jnp.float32),) * 4)
     dots = jnp.zeros((1, SEG), jnp.float32)
     for i, total in enumerate(sums):
         line = jnp.sum(total, axis=0, keepdims=True)

time: 105 us -> 110 us (1.048)
  Pallas kernels: 37 us -> 44.6 us
  waiting for transfers between devices: 38 us -> 35.6 us
    pallas_call x1, Pallas kernels: 7.52 us -> 12.7 us  [shards(): call(solve_kernel, (f32(F, nx, width),) * 2 + (f32(F, tiles, nx, SEG), f3...]
    ppermute x8, waiting for transfers between devices: 19.8 us -> 18.5 us  [to_half(): return lax.ppermute(block, 'py', [(i, i ^ k) for i in range(groups)])]
    pallas_call x1, Pallas kernels: 1.53 us -> 2.78 us  [shards(): call(start_kernel, (f32(F, tiles, nx, SEG), f32(tiles, nx, SEG), f32(tile...]
    all_to_all x1, waiting for transfers between devices: 5.46 us -> 4.28 us  [shards(): lax.all_to_all(dots, ('px', 'py'), split_axis=0, concat_axis=0, tiled=True)]
    pallas_call x1, Pallas kernels: 1.58 us -> 2.75 us  [shards(): call(last_kernel, f32(F, nx, width), [vmem(2, F, tiles, nx, SEG)])]
  transfers between devices with their start and end apart: 15 -> 15, of which waited for: 8 -> 8; matrix products, arithmetic and copies ran while one was open for 0% -> 0% of each run, Pallas kernels for 16% -> 18%
where the time goes in v12:
time: 110 us
  Pallas kernels  44.6 us (41%)
  waiting for transfers between devices  35.6 us (32%)
  starting transfers between devices  28.3 us (26%)
    ppermute x8, waiting for transfers between devices, to_half(): return lax.ppermute(block, 'py', [(i, i ^ k) for i in range(groups)])  18.5 us
    ppermute x4, waiting for transfers between devices, across(): lax.ppermute(parts[k], ('px', 'py'), [(i * groups + j, (i ^ k) * groups +...  12.8 us
    pallas_call x1, Pallas kernels, shards(): call(solve_kernel, (f32(F, nx, width),) * 2 + (f32(F, tiles, nx, SEG), f3...  12.7 us
    ppermute x8, starting transfers between devices, to_half(): return lax.ppermute(block, 'py', [(i, i ^ k) for i in range(groups)])  11.1 us
    pallas_call x1, Pallas kernels, shards(): call(functools.partial(pack_weights_kernel, groups, cap, blk, block_rows)...  6.91 us
    ppermute x4, starting transfers between devices, across(): lax.ppermute(parts[k], ('px', 'py'), [(i * groups + j, (i ^ k) * groups +...  6.79 us
    pallas_call x1, Pallas kernels, shards(): call(functools.partial(pack_products_kernel, groups, cap), (f32(2 * cap,...  6.76 us
    pallas_call x2, Pallas kernels, sum_weights(): call(functools.partial(weights_kernel, half, cap, blk, side), (f32(half,...  4.57 us
  transfers between devices with their start and end apart: 15, of which 8 were waited for; matrix products, arithmetic and copies ran while one was open for 0% of the time, Pallas kernels for 18%

profile of v12, /device:TPU:0, one launch (start us, length us, event | category | flops | bytes accessed | tf_op | source)
XLA Modules:
  0.0 110.1 jit_solution(6377843270412655989)
XLA Ops:
  0.6 6.9 %shard_map.104 = (f32[784,128]{1,0:T(8,128)}, f32[784,128]{1,0:T(8,128)}, f32[784,128]{1,0:T(8,128)}, f32[784,128]{1,0:T(8,128)}, s32[8,128]{1,0:T(8,128)}) custom-call(s32[8,128]{1,0:T(8,128)} %bitcast.19, s32[8,128]{1,0:T(8,128)} %bitcast.20, s32[8,128]{1,0:T(8,128)} %bitcast.21, f32[8,128]{1,0:T(8,128)} %bitcast.22, f32[1024,128]{1,0:T(8,128)} %w_hbm.3), custom_call_target="tpu_custom_call" | custom-call | flops 1 | bytes 1 | tf_op jit(solution)/shard_map/pallas_call | solution.py:525
  7.5 3.0 %collective-permute-start = (f32[784,128]{1,0:T(8,128)}, f32[784,128]{1,0:T(8,128)S(1)}, u32[]{:S(2)}, u32[]{:S(2)}) collective-permute-start(f32[784,128]{1,0:T(8,128)} %get-tuple-element.42), channel_id=1, source_target_pairs={{0,1},{1,0},{2,3},{3,2},{4,5},{5,4},{6,7},{7,6},{8,9},{9,8},{10,11... | collective-permute-start | bytes 1204232 | tf_op jit(solution)/shard_map/ppermute | solution.py:516
  10.6 1.6 %collective-permute-start.1 = (f32[784,128]{1,0:T(8,128)}, f32[784,128]{1,0:T(8,128)S(1)}, u32[]{:S(2)}, u32[]{:S(2)}) collective-permute-start(f32[784,128]{1,0:T(8,128)} %get-tuple-element.47), channel_id=1, source_target_pairs={{0,2},{1,3},{2,0},{3,1},{4,6},{5,7},{6,4},{7,5},{8,10},{9,11},{10,... | collective-permute-start | bytes 1204232 | tf_op jit(solution)/shard_map/ppermute | solution.py:516
  12.1 2.5 %shard_map.105 = f32[4,272,128]{2,1,0:T(8,128)} custom-call(s32[8,128]{1,0:T(8,128)} %get-tuple-element.36._.slot_ref, f32[16,2048]{1,0:T(8,128)} %bitcast.18, f32[2,64,512]{2,1,0:T(8,128)} %bitcast.13, f32[64,512]{1,0:T(8,128)} %bitcast.16), custom_call_target="tpu_custom_call" | custom-call | flops 1 | bytes 1 | tf_op jit(solution)/shard_map/pallas_call | solution.py:549
  14.7 3.5 %all-to-all-start = ((f32[4,272,128]{2,1,0:T(8,128)}), f32[4,272,128]{2,1,0:T(8,128)S(1)}, u32[]{:S(2)}, u32[]{:S(2)}) async-start(f32[4,272,128]{2,1,0:T(8,128)} %shard_map.105), calls=%async_computation | async-start | bytes 1114112 | tf_op jit(solution)/shard_map/all_to_all | solution.py:556
  18.2 6.8 %shard_map.107 = (f32[768,128]{1,0:T(8,128)}, f32[768,128]{1,0:T(8,128)}, f32[768,128]{1,0:T(8,128)}, f32[768,128]{1,0:T(8,128)}) custom-call(s32[8,128]{1,0:T(8,128)} %get-tuple-element.36._.slot_ref, f32[1024,128]{1,0:T(8,128)} %w_hbm.3, f32[1024,128]{1,0:T(8,128)} %d_hbm.1), custom_call_target="tpu_custom_call" | custom-call | flops 1 | bytes 1 | tf_op jit(solution)/shard_map/pallas_call | solution.py:537
  24.9 2.0 %collective-permute-start.5 = (f32[768,128]{1,0:T(8,128)}, f32[768,128]{1,0:T(8,128)S(1)}, u32[]{:S(2)}, u32[]{:S(2)}) collective-permute-start(f32[768,128]{1,0:T(8,128)} %get-tuple-element.56), channel_id=1, source_target_pairs={{0,1},{1,0},{2,3},{3,2},{4,5},{5,4},{6,7},{7,6},{8,9},{9,8},{10,11... | collective-permute-start | bytes 1179656 | tf_op jit(solution)/shard_map/ppermute | solution.py:516
  30.1 2.7 %shard_map.109 = (f32[4,16,128]{2,1,0:T(8,128)}, f32[512,128]{1,0:T(8,128)}, f32[512,128]{1,0:T(8,128)}) custom-call(f32[784,128]{1,0:T(8,128)S(1)} %copy-done, f32[784,128]{1,0:T(8,128)S(1)} %collective-permute-done.rest_1_, f32[784,128]{1,0:T(8,128)S(1)} %collective-permute-done.1.rest_2_, f32[784,128]{1,0:T(8,128)S(1)} %collective-permute-done.2.rest_3_, ...), custom_call_target="tpu_custom_call" | custom-call | flops 100000000 | bytes 100000000 | tf_op jit(solution)/shard_map/pallas_call | solution.py:565
  32.8 2.8 %collective-permute-start.3 = (f32[512,128]{1,0:T(8,128)}, f32[512,128]{1,0:T(8,128)}, u32[]{:S(2)}, u32[]{:S(2)}) collective-permute-start(f32[512,128]{1,0:T(8,128)} %get-tuple-element.53), channel_id=1, source_target_pairs={{0,4},{1,5},{2,6},{3,7},{4,0},{5,1},{6,2},{7,3},{8,12},{9,13},{10,... | collective-permute-start | bytes 786440 | tf_op jit(solution)/shard_map/ppermute | solution.py:516
  35.7 2.8 %shard_map.106 = (f32[2,5,64,128]{3,2,1,0:T(8,128)S(1)}, f32[5,64,128]{2,1,0:T(8,128)S(1)}, f32[5,64,128]{2,1,0:T(8,128)S(1)}, f32[2,5,64,128]{3,2,1,0:T(8,128)S(1)}, f32[8,128]{1,0:T(8,128)S(1)}) custom-call(f32[2,64,512]{2,1,0:T(8,128)S(1)} %bitcast.14, f32[64,512]{1,0:T(8,128)S(1)} %bitcast.17, f32[4,272,128]{2,1,0:T(8,128)S(1)} %all-to-all-done.swap_ref), custom_call_target="tpu_custom_call" | custom-call | flops 1 | bytes 1 | tf_op jit(solution)/shard_map/pallas_call | solution.py:557
  39.2 1.9 %shard_map.108 = (f32[4,16,128]{2,1,0:T(8,128)S(1)}, f32[512,128]{1,0:T(8,128)S(1)}, f32[512,128]{1,0:T(8,128)S(1)}) custom-call(f32[784,128]{1,0:T(8,128)S(1)} %copy-done, f32[784,128]{1,0:T(8,128)S(1)} %collective-permute-done.rest_1_, f32[784,128]{1,0:T(8,128)S(1)} %collective-permute-done.1.rest_2_, f32[784,128]{1,0:T(8,128)S(1)} %collective-permute-done.2.rest_3_, ...), custom_call_target="tpu_custom_call" | custom-call | flops 1 | bytes 1 | tf_op jit(solution)/shard_map/pallas_call | solution.py:565
  41.1 11.2 %collective-permute-done.3.far_d_ref = f32[512,128]{1,0:T(8,128)} collective-permute-done((f32[512,128]{1,0:T(8,128)}, f32[512,128]{1,0:T(8,128)}, u32[]{:S(2)}, u32[]{:S(2)}) %collective-permute-start.3) | collective-permute-done | bytes 262176 | tf_op jit(solution)/shard_map/ppermute | solution.py:516
  52.3 5.1 %collective-permute-done.4.far_e_ref = f32[512,128]{1,0:T(8,128)} collective-permute-done((f32[512,128]{1,0:T(8,128)}, f32[512,128]{1,0:T(8,128)}, u32[]{:S(2)}, u32[]{:S(2)}) %collective-permute-start.4) | collective-permute-done | bytes 262176 | tf_op jit(solution)/shard_map/ppermute | solution.py:516
  58.1 4.4 %shard_map.110 = (f32[4,6,5,16,128]{4,3,2,1,0:T(8,128)}, f32[2,5,16,128]{3,2,1,0:T(8,128)S(1)}, f32[2,5,16,128]{3,2,1,0:T(8,128)S(1)}, f32[2,5,16,128]{3,2,1,0:T(8,128)S(1)}, f32[2,5,16,128]{3,2,1,0:T(8,128)S(1)}) custom-call(f32[4,16,128]{2,1,0:T(8,128)S(1)} %get-tuple-element.50.meta_ref, f32[512,128]{1,0:T(8,128)S(1)} %get-tuple-element.51.d_ref, ...), custom_call_target="tpu_custom_call" | custom-call | flops 1 | bytes 1 | tf_op jit(solution)/shard_map/pallas_call | solution.py:575
  62.5 3.5 %all-to-all-start.1 = ((f32[4,6,5,16,128]{4,3,2,1,0:T(8,128)}), f32[4,6,5,16,128]{4,3,2,1,0:T(8,128)S(1)}, u32[]{:S(2)}, u32[]{:S(2)}) async-start(f32[4,6,5,16,128]{4,3,2,1,0:T(8,128)} %get-tuple-element.59), calls=%async_computation.1 | async-start | bytes 1966080 | tf_op jit(solution)/shard_map/all_to_all | solution.py:583
  66.0 2.8 %collective-permute-start.8 = (f32[2,5,16,128]{3,2,1,0:T(8,128)S(1)}, f32[2,5,16,128]{3,2,1,0:T(8,128)S(1)}, u32[]{:S(2)}, u32[]{:S(2)}) collective-permute-start(f32[2,5,16,128]{3,2,1,0:T(8,128)S(1)} %get-tuple-element.60), channel_id=1, source_target_pairs={{0,4},{1,5},{2,6},{3,7},{4,0},{5,1},{6,2},{7,3},{8,12},{9,13},{10,... | collective-permute-start | bytes 245768 | tf_op jit(solution)/shard_map/ppermute | solution.py:520
  68.8 3.7 %collective-permute-start.10 = (f32[2,5,16,128]{3,2,1,0:T(8,128)S(1)}, f32[2,5,16,128]{3,2,1,0:T(8,128)S(1)}, u32[]{:S(2)}, u32[]{:S(2)}) collective-permute-start(f32[2,5,16,128]{3,2,1,0:T(8,128)S(1)} %get-tuple-element.62), channel_id=1, source_target_pairs={{0,20},{1,21},{2,22},{3,23},{4,16},{5,17},{6,18},{7,19},{8,28},{9,... | collective-permute-start | bytes 245768 | tf_op jit(solution)/shard_map/ppermute | solution.py:520
  72.8 8.2 %collective-permute-done.9.rest_1_ = f32[2,5,16,128]{3,2,1,0:T(8,128)S(1)} collective-permute-done((f32[2,5,16,128]{3,2,1,0:T(8,128)S(1)}, f32[2,5,16,128]{3,2,1,0:T(8,128)S(1)}, u32[]{:S(2)}, u32[]{:S(2)}) %collective-permute-start.9) | collective-permute-done | bytes 81952 | tf_op jit(solution)/shard_map/ppermute | solution.py:520
  81.0 2.9 %collective-permute-done.10.rest_2_ = f32[2,5,16,128]{3,2,1,0:T(8,128)S(1)} collective-permute-done((f32[2,5,16,128]{3,2,1,0:T(8,128)S(1)}, f32[2,5,16,128]{3,2,1,0:T(8,128)S(1)}, u32[]{:S(2)}, u32[]{:S(2)}) %collective-permute-start.10) | collective-permute-done | bytes 81952 | tf_op jit(solution)/shard_map/ppermute | solution.py:520
  83.9 1.8 %collective-permute-done.11.rest_3_ = f32[2,5,16,128]{3,2,1,0:T(8,128)S(1)} collective-permute-done((f32[2,5,16,128]{3,2,1,0:T(8,128)S(1)}, f32[2,5,16,128]{3,2,1,0:T(8,128)S(1)}, u32[]{:S(2)}, u32[]{:S(2)}) %collective-permute-start.11) | collective-permute-done | bytes 81952 | tf_op jit(solution)/shard_map/ppermute | solution.py:520
  85.7 12.7 %shard_map.112 = (f32[2,64,512]{2,1,0:T(8,128)S(1)}, f32[2,64,512]{2,1,0:T(8,128)S(1)}, f32[2,5,64,128]{3,2,1,0:T(8,128)S(1)}, f32[32,1,128]{2,1,0:T(1,128)}) custom-call(f32[2,5,64,128]{3,2,1,0:T(8,128)S(1)} %copy-done.5, f32[5,64,128]{2,1,0:T(8,128)S(1)} %get-tuple-element.38.cx_ref, f32[5,64,128]{2,1,0:T(8,128)S(1)} %get-tuple-element.39.cy_ref, ...), custom_call_target="tpu_custom_call" | custom-call | flops 1 | bytes 1 | tf_op jit(solution)/shard_map/pallas_call | solution.py:585
  98.3 3.5 %all-to-all-start.2 = ((f32[32,1,128]{2,1,0:T(1,128)}), f32[32,1,128]{2,1,0:T(1,128)S(1)}, u32[]{:S(2)}, u32[]{:S(2)}) async-start(f32[32,1,128]{2,1,0:T(1,128)} %get-tuple-element.64), calls=%async_computation.2 | async-start | bytes 32768 | tf_op jit(solution)/shard_map/all_to_all | solution.py:590
  101.8 2.8 %shard_map.113.qq_ref = f32[2,64,512]{2,1,0:T(8,128)S(1)} custom-call(f32[2,5,64,128]{3,2,1,0:T(8,128)S(1)} %get-tuple-element.67.h_ref, f32[2,64,512]{2,1,0:T(8,128)S(1)} %get-tuple-element.66.q_ref, f32[5,64,128]{2,1,0:T(8,128)S(1)} %get-tuple-element.38.cx_ref, f32[5,64,128]{2,1,0:T(8,128)S(1)} %get-tuple-element.39.cy_ref), custom_call_target="tpu_custom_call" | custom-call | flops 1 | bytes 1 | tf_op jit(solution)/shard_map/pallas_call | solution.py:591
  104.6 4.3 %all-to-all-done.2.dots_ref = f32[32,1,128]{2,1,0:T(1,128)S(1)} async-done(((f32[32,1,128]{2,1,0:T(1,128)}), f32[32,1,128]{2,1,0:T(1,128)S(1)}, u32[]{:S(2)}, u32[]{:S(2)}) %all-to-all-start.2) | async-done | bytes 16416 | tf_op jit(solution)/shard_map/all_to_all | solution.py:590
  (33 shorter events, 6.4 us)
Async XLA Ops:
  7.5 17.4 %collective-permute-start = (f32[784,128]{1,0:T(8,128)}, f32[784,128]{1,0:T(8,128)S(1)}, u32[]{:S(2)}, u32[]{:S(2)}) collective-permute-start(f32[784,128]{1,0:T(8,128)} %get-tuple-element.42), channel_id=1, source_target_pairs={{0,1},{1,0},{2,3},{3,2},{4,5},{5,4},{6,7},{7,6},{8,9},{9,8},{10,11... | collective-permute-start | bytes 1204232 | tf_op jit(solution)/shard_map/ppermute | solution.py:516
  10.6 17.9 %collective-permute-start.1 = (f32[784,128]{1,0:T(8,128)}, f32[784,128]{1,0:T(8,128)S(1)}, u32[]{:S(2)}, u32[]{:S(2)}) collective-permute-start(f32[784,128]{1,0:T(8,128)} %get-tuple-element.47), channel_id=1, source_target_pairs={{0,2},{1,3},{2,0},{3,1},{4,6},{5,7},{6,4},{7,5},{8,10},{9,11},{10,... | collective-permute-start | bytes 1204232 | tf_op jit(solution)/shard_map/ppermute | solution.py:516
  12.1 17.9 %collective-permute-start.2 = (f32[784,128]{1,0:T(8,128)}, f32[784,128]{1,0:T(8,128)S(1)}, u32[]{:S(2)}, u32[]{:S(2)}) collective-permute-start(f32[784,128]{1,0:T(8,128)} %get-tuple-element.48), channel_id=1, source_target_pairs={{0,3},{1,2},{2,1},{3,0},{4,7},{5,6},{6,5},{7,4},{8,11},{9,10},{10,... | collective-permute-start | bytes 1204232 | tf_op jit(solution)/shard_map/ppermute | solution.py:516
  14.7 21.0 %all-to-all-start = ((f32[4,272,128]{2,1,0:T(8,128)}), f32[4,272,128]{2,1,0:T(8,128)S(1)}, u32[]{:S(2)}, u32[]{:S(2)}) async-start(f32[4,272,128]{2,1,0:T(8,128)} %shard_map.105), calls=%async_computation | async-start | bytes 1114112 | tf_op jit(solution)/shard_map/all_to_all | solution.py:556
  18.2 11.9 %copy-start = (f32[784,128]{1,0:T(8,128)S(1)}, f32[784,128]{1,0:T(8,128)}, u32[]{:S(2)}) copy-start(f32[784,128]{1,0:T(8,128)} %get-tuple-element.41.rest_0_.rest_4_) | copy-start | bytes 1204228
  24.9 32.5 %collective-permute-start.5 = (f32[768,128]{1,0:T(8,128)}, f32[768,128]{1,0:T(8,128)S(1)}, u32[]{:S(2)}, u32[]{:S(2)}) collective-permute-start(f32[768,128]{1,0:T(8,128)} %get-tuple-element.56), channel_id=1, source_target_pairs={{0,1},{1,0},{2,3},{3,2},{4,5},{5,4},{6,7},{7,6},{8,9},{9,8},{10,11... | collective-permute-start | bytes 1179656 | tf_op jit(solution)/shard_map/ppermute | solution.py:516
  26.9 30.5 %collective-permute-start.6 = (f32[768,128]{1,0:T(8,128)}, f32[768,128]{1,0:T(8,128)}, u32[]{:S(2)}, u32[]{:S(2)}) collective-permute-start(f32[768,128]{1,0:T(8,128)} %get-tuple-element.57), channel_id=1, source_target_pairs={{0,2},{1,3},{2,0},{3,1},{4,6},{5,7},{6,4},{7,5},{8,10},{9,11},{10,... | collective-permute-start | bytes 1179656 | tf_op jit(solution)/shard_map/ppermute | solution.py:516
  28.5 29.6 %collective-permute-start.7 = (f32[768,128]{1,0:T(8,128)}, f32[768,128]{1,0:T(8,128)}, u32[]{:S(2)}, u32[]{:S(2)}) collective-permute-start(f32[768,128]{1,0:T(8,128)} %get-tuple-element.58), channel_id=1, source_target_pairs={{0,3},{1,2},{2,1},{3,0},{4,7},{5,6},{6,5},{7,4},{8,11},{9,10},{10,... | collective-permute-start | bytes 1179656 | tf_op jit(solution)/shard_map/ppermute | solution.py:516
  30.1 5.6 %copy-start.1 = (f32[2,1,64,512]{3,2,1,0:T(8,128)S(1)}, f32[2,1,64,512]{3,2,1,0:T(8,128)}, u32[]{:S(2)}) copy-start(f32[2,1,64,512]{3,2,1,0:T(8,128)} %param.9) | copy-start | bytes 786436
  30.1 5.6 %copy-start.2 = (f32[1,64,512]{2,1,0:T(8,128)S(1)}, f32[1,64,512]{2,1,0:T(8,128)}, u32[]{:S(2)}) copy-start(f32[1,64,512]{2,1,0:T(8,128)} %param.10) | copy-start | bytes 393220
  32.8 19.6 %collective-permute-start.3 = (f32[512,128]{1,0:T(8,128)}, f32[512,128]{1,0:T(8,128)}, u32[]{:S(2)}, u32[]{:S(2)}) collective-permute-start(f32[512,128]{1,0:T(8,128)} %get-tuple-element.53), channel_id=1, source_target_pairs={{0,4},{1,5},{2,6},{3,7},{4,0},{5,1},{6,2},{7,3},{8,12},{9,13},{10,... | collective-permute-start | bytes 786440 | tf_op jit(solution)/shard_map/ppermute | solution.py:516
  35.5 21.9 %collective-permute-start.4 = (f32[512,128]{1,0:T(8,128)}, f32[512,128]{1,0:T(8,128)}, u32[]{:S(2)}, u32[]{:S(2)}) collective-permute-start(f32[512,128]{1,0:T(8,128)} %get-tuple-element.54), channel_id=1, source_target_pairs={{0,4},{1,5},{2,6},{3,7},{4,0},{5,1},{6,2},{7,3},{8,12},{9,13},{10,... | collective-permute-start | bytes 786440 | tf_op jit(solution)/shard_map/ppermute | solution.py:516
  38.5 0.7 copy-start.6
  39.2 1.9 %copy-start.4 = (f32[2,5,64,128]{3,2,1,0:T(8,128)}, f32[2,5,64,128]{3,2,1,0:T(8,128)S(1)}, u32[]{:S(2)}) copy-start(f32[2,5,64,128]{3,2,1,0:T(8,128)S(1)} %get-tuple-element.37.c0_ref) | copy-start | bytes 983044
  39.2 18.9 %copy-start.3 = (f32[768,128]{1,0:T(8,128)S(1)}, f32[768,128]{1,0:T(8,128)}, u32[]{:S(2)}) copy-start(f32[768,128]{1,0:T(8,128)} %get-tuple-element.55.rest_0_) | copy-start | bytes 1179652
  62.5 23.2 %all-to-all-start.1 = ((f32[4,6,5,16,128]{4,3,2,1,0:T(8,128)}), f32[4,6,5,16,128]{4,3,2,1,0:T(8,128)S(1)}, u32[]{:S(2)}, u32[]{:S(2)}) async-start(f32[4,6,5,16,128]{4,3,2,1,0:T(8,128)} %get-tuple-element.59), calls=%async_computation.1 | async-start | bytes 1966080 | tf_op jit(solution)/shard_map/all_to_all | solution.py:583
  66.0 6.8 %collective-permute-start.8 = (f32[2,5,16,128]{3,2,1,0:T(8,128)S(1)}, f32[2,5,16,128]{3,2,1,0:T(8,128)S(1)}, u32[]{:S(2)}, u32[]{:S(2)}) collective-permute-start(f32[2,5,16,128]{3,2,1,0:T(8,128)S(1)} %get-tuple-element.60), channel_id=1, source_target_pairs={{0,4},{1,5},{2,6},{3,7},{4,0},{5,1},{6,2},{7,3},{8,12},{9,13},{10,... | collective-permute-start | bytes 245768 | tf_op jit(solution)/shard_map/ppermute | solution.py:520
  68.8 12.2 %collective-permute-start.9 = (f32[2,5,16,128]{3,2,1,0:T(8,128)S(1)}, f32[2,5,16,128]{3,2,1,0:T(8,128)S(1)}, u32[]{:S(2)}, u32[]{:S(2)}) collective-permute-start(f32[2,5,16,128]{3,2,1,0:T(8,128)S(1)} %get-tuple-element.61), channel_id=1, source_target_pairs={{0,12},{1,13},{2,14},{3,15},{4,8},{5,9},{6,10},{7,11},{8,4},{9,5},... | collective-permute-start | bytes 245768 | tf_op jit(solution)/shard_map/ppermute | solution.py:520
  68.8 15.0 %collective-permute-start.10 = (f32[2,5,16,128]{3,2,1,0:T(8,128)S(1)}, f32[2,5,16,128]{3,2,1,0:T(8,128)S(1)}, u32[]{:S(2)}, u32[]{:S(2)}) collective-permute-start(f32[2,5,16,128]{3,2,1,0:T(8,128)S(1)} %get-tuple-element.62), channel_id=1, source_target_pairs={{0,20},{1,21},{2,22},{3,23},{4,16},{5,17},{6,18},{7,19},{8,28},{9,... | collective-permute-start | bytes 245768 | tf_op jit(solution)/shard_map/ppermute | solution.py:520
  72.5 13.1 %copy-start.5 = (f32[2,5,64,128]{3,2,1,0:T(8,128)S(1)}, f32[2,5,64,128]{3,2,1,0:T(8,128)}, u32[]{:S(2)}) copy-start(f32[2,5,64,128]{3,2,1,0:T(8,128)} %copy-done.4) | copy-start | bytes 983044
  72.5 13.1 %copy-start.7 = (f32[2,5,64,128]{3,2,1,0:T(8,128)S(1)}, f32[2,5,64,128]{3,2,1,0:T(8,128)}, u32[]{:S(2)}) copy-start(f32[2,5,64,128]{3,2,1,0:T(8,128)} %copy-done.6) | copy-start | bytes 983044
  72.5 13.1 %collective-permute-start.11 = (f32[2,5,16,128]{3,2,1,0:T(8,128)S(1)}, f32[2,5,16,128]{3,2,1,0:T(8,128)S(1)}, u32[]{:S(2)}, u32[]{:S(2)}) collective-permute-start(f32[2,5,16,128]{3,2,1,0:T(8,128)S(1)} %get-tuple-element.63), channel_id=1, source_target_pairs={{0,28},{1,29},{2,30},{3,31},{4,24},{5,25},{6,26},{7,27},{8,20},{9,... | collective-permute-start | bytes 245768 | tf_op jit(solution)/shard_map/ppermute | solution.py:520
  98.3 10.5 %all-to-all-start.2 = ((f32[32,1,128]{2,1,0:T(1,128)}), f32[32,1,128]{2,1,0:T(1,128)S(1)}, u32[]{:S(2)}, u32[]{:S(2)}) async-start(f32[32,1,128]{2,1,0:T(1,128)} %get-tuple-element.64), calls=%async_computation.2 | async-start | bytes 32768 | tf_op jit(solution)/shard_map/all_to_all | solution.py:590

commit v13 on v11

--- a/solution.py
+++ b/solution.py
@@ -15,8 +15,7 @@
 ROWS = F * NB * LX
 HALF = SEG // 2
 SPLIT = 16
-X_TILES = 2
-Y_LINES = 16
+REACH = M
 VMEM_BYTES = 32 * 1024 * 1024
 PACK_BYTES = 60 * 1024 * 1024
 FIRST = 100_000_000
@@ -276,55 +275,98 @@
     return [pl.ds(i, 8, stride=nx // 8) for i in range(nx // 8)]
 
 
-def sweep_x_into(to_refs, from_refs, cx_ref, plus_refs=None, sign=1.0):
+def shift_x(lines, distance):
+    size = len(lines)
+    moved = []
+    for i in range(size):
+        j = i + distance
+        line = lines[j % size]
+        moved.append(line if 0 <= j < size else pltpu.roll(line, 7 if j >= size else 1, 0))
+    return moved
+
+
+def shift_y(tiles, distance):
+    if distance == 0:
+        return tiles
+    lane = iota(tiles[0].shape, 1)
+    moved = [pltpu.roll(tile, -distance % SEG, 1) for tile in tiles]
+    if distance > 0:
+        return [jnp.where(lane >= SEG - distance, b, a) for a, b in zip(moved, moved[1:] + moved[:1])]
+    return [jnp.where(lane < -distance, a, b) for a, b in zip(moved[-1:] + moved[:-1], moved)]
+
+
+def sweep_diagonals(coeffs, shift):
+    def each(function, *lists):
+        return [function(*items) for items in zip(*lists)]
+
+    back = functools.partial(shift, coeffs)
+    main = each(lambda c, d: 1.0 - c - d, coeffs, back(-1))
+    q0 = each(lambda a, c, d: a * a + c * c + d * d, main, coeffs, back(-1))
+    q1 = each(lambda a, b, c: c * (a + b), main, shift(main, 1), coeffs)
+    q2 = each(lambda c, d: c * d, coeffs, back(1))
+    up0, up1, up2 = shift(q0, 1), shift(q1, 1), shift(q2, 1)
+    low1, low2 = shift(q1, -1), shift(q2, -1)
+    r0 = each(lambda a, b, c, d, e: a * a + b * b + c * c + d * d + e * e,
+              q0, q1, low1, q2, shift(q2, -2))
+    r1 = each(lambda a, b, c, d, e, f, g: a * b + c * (d + e) + f * g,
+              low1, low2, q1, q0, up0, q2, up1)
+    r2 = each(lambda a, b, c, d, e: a * (b + c) + d * e, q2, q0, shift(q0, 2), q1, up1)
+    r3 = each(lambda a, b, c, d: a * b + c * d, q1, up2, q2, shift(q1, 2))
+    r4 = each(lambda a, b: a * b, q2, shift(q2, 2))
+    upper = [r0, r1, r2, r3, r4]
+    return [shift(upper[d], -d) for d in range(REACH, 0, -1)] + upper
+
+
+def make_x_diagonals(out, cx_ref):
     tiles, nx, _ = cx_ref.shape
     picks = x_lines(nx)
-    for start in range(0, tiles, X_TILES):
-        group = range(start, min(start + X_TILES, tiles))
-        chains = [(i, t) for t in group for i in range(len(from_refs))]
-        coeffs = {t: [cx_ref[t, pick, :] for pick in picks] for t in group}
-        wrapped = {t: pltpu.roll(coeffs[t][-1], 1, 0) for t in group}
-        fields = {(i, t): [from_refs[i][t, pick, :] for pick in picks] for i, t in chains}
-        for _ in range(M):
-            for i, t in chains:
-                values = fields[i, t]
-                after = values[1:] + [pltpu.roll(values[0], 7, 0)]
-                low = wrapped[t] * (values[0] - pltpu.roll(values[-1], 1, 0))
-                flux = [c * (b - a) for c, a, b in zip(coeffs[t], values, after)]
-                fields[i, t] = [a + f - g for a, f, g in zip(values, flux, [low] + flux[:-1])]
-        for i, t in chains:
-            for pick, value in zip(picks, fields[i, t]):
+    for t in range(tiles):
+        coeffs = [cx_ref[t, pick, :] for pick in picks]
+        for d, lines in enumerate(sweep_diagonals(coeffs, shift_x)):
+            for pick, line in zip(picks, lines):
+                out[d, t, pick, :] = line
+
+
+def make_y_diagonals(out, cy_ref):
+    tiles, nx, _ = cy_ref.shape
+    for low in range(0, nx, 8):
+        rows = slice(low, low + 8)
+        coeffs = [cy_ref[t, rows, :] for t in range(tiles)]
+        for d, parts in enumerate(sweep_diagonals(coeffs, shift_y)):
+            for t, part in enumerate(parts):
+                out[d, t, rows, :] = part
+
+
+def banded(diagonals, values, shift):
+    total = None
+    for d, diagonal in enumerate(diagonals):
+        terms = [c * v for c, v in zip(diagonal, shift(values, d - REACH))]
+        total = terms if total is None else [a + b for a, b in zip(total, terms)]
+    return total
+
+
+def sweep_x_into(to_refs, from_refs, x_ref, plus_refs=None, sign=1.0):
+    count, tiles, nx, _ = x_ref.shape
+    picks = x_lines(nx)
+    for t in range(tiles):
+        diagonals = [[x_ref[d, t, pick, :] for pick in picks] for d in range(count)]
+        for i, from_ref in enumerate(from_refs):
+            values = [from_ref[t, pick, :] for pick in picks]
+            for pick, value in zip(picks, banded(diagonals, values, shift_x)):
                 if plus_refs is not None:
                     value = value + sign * plus_refs[i][t, pick, :]
                 to_refs[i][t, pick, :] = value
 
 
-def sweep_y_into(to_refs, from_refs, cy_ref):
-    tiles, nx, _ = cy_ref.shape
-    lane = iota((Y_LINES, SEG), 1)
-
-    def next_cells(values):
-        moved = [pltpu.roll(value, SEG - 1, 1) for value in values]
-        return [jnp.where(lane == SEG - 1, b, a) for a, b in zip(moved, moved[1:] + moved[:1])]
-
-    def previous_cells(values):
-        moved = [pltpu.roll(value, 1, 1) for value in values]
-        return [jnp.where(lane == 0, a, b) for a, b in zip(moved[-1:] + moved[:-1], moved)]
-
-    for low in range(0, nx, Y_LINES):
-        lines = slice(low, low + Y_LINES)
-        coeffs = [cy_ref[t, lines, :] for t in range(tiles)]
-        coeffs_low = previous_cells(coeffs)
-        fields = [[ref[t, lines, :] for t in range(tiles)] for ref in from_refs]
-        for _ in range(M):
-            for i, values in enumerate(fields):
-                after, before = next_cells(values), previous_cells(values)
-                fields[i] = [
-                    a + c * (b - a) - d * (a - e)
-                    for a, b, c, d, e in zip(values, after, coeffs, coeffs_low, before)]
-        for to_ref, values in zip(to_refs, fields):
-            for t, value in enumerate(values):
-                to_ref[t, lines, :] = value
+def sweep_y_into(to_refs, from_refs, y_ref):
+    count, tiles, nx, _ = y_ref.shape
+    for low in range(0, nx, 8):
+        rows = slice(low, low + 8)
+        diagonals = [[y_ref[d, t, rows, :] for t in range(tiles)] for d in range(count)]
+        for to_ref, from_ref in zip(to_refs, from_refs):
+            values = [from_ref[t, rows, :] for t in range(tiles)]
+            for t, value in enumerate(banded(diagonals, values, shift_y)):
+                to_ref[t, rows, :] = value
 
 
 def normal_into(to_refs, from_refs, diagonal_refs, side_refs, base_refs=None):
@@ -349,7 +391,8 @@
     return [ref.at[start + f] for f in range(F)]
 
 
-def start_kernel(c0_ref, cx_ref, swap_ref, c0_out, cx_out, cy_out, u_out, token_out, work):
+def start_kernel(c0_ref, cx_ref, swap_ref, c0_out, x_out, y_out, u_out, token_out, cx_out, cy_out,
+                 work):
     token_out[...] = jnp.zeros_like(token_out)
     nx = cx_ref.shape[0]
     spans, count = swap_ref.shape[0], cy_out.shape[0]
@@ -373,8 +416,10 @@
     cx_out[:, nx - 1:, :] = jnp.zeros((count, 1, SEG), jnp.float32)
     for f in range(F):
         c0_out[f, count - 1] = beside(f)
-    sweep_x_into(of_fields(work), of_fields(c0_out), cx_out)
-    sweep_y_into(of_fields(u_out), of_fields(work), cy_out)
+    make_x_diagonals(x_out, cx_out)
+    make_y_diagonals(y_out, cy_out)
+    sweep_x_into(of_fields(work), of_fields(c0_out), x_out)
+    sweep_y_into(of_fields(u_out), of_fields(work), y_out)
 
 
 def join_kernel(spans, *rest):
@@ -387,7 +432,7 @@
                 out[f, t, rows, :] = part[f, t]
 
 
-def solve_kernel(c0_ref, cx_ref, cy_ref, u_ref, obs_ref, far_ref, r_out, q_out, h_out, dots_out,
+def solve_kernel(c0_ref, x_ref, y_ref, u_ref, obs_ref, far_ref, r_out, q_out, h_out, dots_out,
                  vec, coef, work):
     for p in range(obs_ref.shape[0]):
         rows = slice(p * LX, (p + 1) * LX)
@@ -400,15 +445,15 @@
     one, two, r, q, s, h = (of_fields(ref) for ref in (
         work.at[0], work.at[1], vec.at[0], vec.at[1], vec.at[2], h_out))
     normal_into(one, of_fields(u_ref), *sides, of_fields(coef, 2 * F))
-    sweep_y_into(two, one, cy_ref)
-    sweep_x_into(r, two, cx_ref, of_fields(c0_ref), -1.0)
-    sweep_x_into(one, r, cx_ref)
-    sweep_y_into(two, one, cy_ref)
+    sweep_y_into(two, one, y_ref)
+    sweep_x_into(r, two, x_ref, of_fields(c0_ref), -1.0)
+    sweep_x_into(one, r, x_ref)
+    sweep_y_into(two, one, y_ref)
     normal_into(one, two, *sides)
-    sweep_y_into(two, one, cy_ref)
-    sweep_x_into(q, two, cx_ref, r)
-    sweep_x_into(one, q, cx_ref)
-    sweep_y_into(s, one, cy_ref)
+    sweep_y_into(two, one, y_ref)
+    sweep_x_into(q, two, x_ref, r)
+    sweep_x_into(one, q, x_ref)
+    sweep_y_into(s, one, y_ref)
     normal_into(h, s, *sides)
 
     tiles, nx = vec.shape[2] - 1, vec.shape[3]
@@ -431,9 +476,9 @@
     dots_out[...] = jnp.broadcast_to(dots, dots_out.shape)
 
 
-def last_kernel(h_ref, q_ref, cx_ref, cy_ref, qq_out, work):
-    sweep_y_into(of_fields(work.at[0]), of_fields(h_ref), cy_ref)
-    sweep_x_into(of_fields(work.at[1]), of_fields(work.at[0]), cx_ref)
+def last_kernel(h_ref, q_ref, x_ref, y_ref, qq_out, work):
+    sweep_y_into(of_fields(work.at[0]), of_fields(h_ref), y_ref)
+    sweep_x_into(of_fields(work.at[1]), of_fields(work.at[0]), x_ref)
     for f in range(F):
         for t in range(work.shape[2] - 1):
             tile = slice(t * SEG, (t + 1) * SEG)
@@ -544,11 +589,11 @@
         limit=PACK_BYTES,
     )(slots, coef_y[0], c0, cx)
     swap = lax.all_to_all(swap, "px", split_axis=0, concat_axis=0, tiled=True)
-    c0_ext, cx_ext, cy_ext, u_ext, token = call(
+    c0_ext, x_sweep, y_sweep, u_ext, token = call(
         start_kernel,
-        (f32(F, tiles, nx, SEG), f32(tiles, nx, SEG), f32(tiles, nx, SEG), f32(F, tiles, nx, SEG),
-         f32(8, SEG)),
-        [vmem(F, tiles, nx, SEG)],
+        (f32(F, tiles, nx, SEG), f32(2 * REACH + 1, tiles, nx, SEG),
+         f32(2 * REACH + 1, tiles, nx, SEG), f32(F, tiles, nx, SEG), f32(8, SEG)),
+        [vmem(tiles, nx, SEG), vmem(tiles, nx, SEG), vmem(F, tiles, nx, SEG)],
     )(c0, cx, swap)
 
     def sum_weights(side, token, weight):
@@ -576,10 +621,10 @@
         solve_kernel,
         (f32(F, nx, width),) * 2 + (f32(F, tiles, nx, SEG), f32(groups * spans, 1, SEG)),
         [vmem(3, F, tiles, nx, SEG), vmem(3 * F, tiles, nx, SEG), vmem(2, F, tiles, nx, SEG)],
-    )(c0_ext, cx_ext, cy_ext, u_ext, parts, far_sums)
+    )(c0_ext, x_sweep, y_sweep, u_ext, parts, far_sums)
     dots = lax.all_to_all(dots, ("px", "py"), split_axis=0, concat_axis=0, tiled=True)
     qq = call(last_kernel, f32(F, nx, width), [vmem(2, F, tiles, nx, SEG)])(
-        h, q, cx_ext, cy_ext)
+        h, q, x_sweep, y_sweep)
     control, residual = call(finish_kernel, (f32(F, nx, width),) * 2)(dots, c0, r, q, qq)
     return control[:, None], residual[:, None]
 

time: 105 us -> 113 us (1.076); the launches traced: 105 us -> 112 us
  local copies, waits for them, and re-layouts: 0.76 us -> 16.1 us
  waiting for transfers between devices: 38 us -> 28.8 us
    unnamed x16 -> x48, local copies, waits for them, and re-layouts: 0.76 us -> 16.1 us
    ppermute x8, waiting for transfers between devices: 19.8 us -> 11.7 us  [to_half(): return lax.ppermute(block, 'py', [(i, i ^ k) for i in range(groups)])]
    pallas_call x1, Pallas kernels: 1.53 us -> 3.02 us  [shards(): call(start_kernel, (f32(F, tiles, nx, SEG), f32(2 * REACH + 1, tiles, nx,...]
    all_to_all x1, waiting for transfers between devices: 5.46 us -> 4.28 us  [shards(): lax.all_to_all(dots, ('px', 'py'), split_axis=0, concat_axis=0, tiled=True)]
where the time goes in v13:
time: 113 us; the launch traced here: 112 us
  Pallas kernels  37 us (33%)
  starting transfers between devices  29 us (26%)
  waiting for transfers between devices  28.8 us (25%)
  local copies, waits for them, and re-layouts  16.1 us (14%)
    unnamed x48, local copies, waits for them, and re-layouts  16.1 us
    ppermute x4, waiting for transfers between devices, across(): lax.ppermute(parts[k], ('px', 'py'), [(i * groups + j, (i ^ k) * groups +...  12.8 us
    ppermute x8, waiting for transfers between devices, to_half(): return lax.ppermute(block, 'py', [(i, i ^ k) for i in range(groups)])  11.7 us
    ppermute x8, starting transfers between devices, to_half(): return lax.ppermute(block, 'py', [(i, i ^ k) for i in range(groups)])  11.1 us
    pallas_call x1, Pallas kernels, shards(): call(solve_kernel, (f32(F, nx, width),) * 2 + (f32(F, tiles, nx, SEG), f3...  7.23 us
    pallas_call x1, Pallas kernels, shards(): call(functools.partial(pack_weights_kernel, groups, cap, blk, block_rows)...  6.9 us
    pallas_call x1, Pallas kernels, shards(): call(functools.partial(pack_products_kernel, groups, cap), (f32(2 * cap,...  6.76 us
    ppermute x4, starting transfers between devices, across(): lax.ppermute(parts[k], ('px', 'py'), [(i * groups + j, (i ^ k) * groups +...  6.6 us
  transfers between devices with their start and end apart: 15, of which 8 were waited for; matrix products, arithmetic and copies ran while one was open for 0% of the time, Pallas kernels for 16%

profile of v13, /device:TPU:0, one launch (start us, length us, event | category | flops | bytes accessed | tf_op | source)
XLA Modules:
  0.0 111.8 jit_solution(17519844848927186855)
XLA Ops:
  0.6 6.9 %shard_map.104 = (f32[784,128]{1,0:T(8,128)}, f32[784,128]{1,0:T(8,128)}, f32[784,128]{1,0:T(8,128)}, f32[784,128]{1,0:T(8,128)}, s32[8,128]{1,0:T(8,128)}) custom-call(s32[8,128]{1,0:T(8,128)} %bitcast.19, s32[8,128]{1,0:T(8,128)} %bitcast.20, s32[8,128]{1,0:T(8,128)} %bitcast.21, f32[8,128]{1,0:T(8,128)} %bitcast.22, f32[1024,128]{1,0:T(8,128)} %w_hbm.3), custom_call_target="tpu_custom_call" | custom-call | flops 1 | bytes 1 | tf_op jit(solution)/shard_map/pallas_call | solution.py:560
  7.5 3.0 %collective-permute-start = (f32[784,128]{1,0:T(8,128)}, f32[784,128]{1,0:T(8,128)S(1)}, u32[]{:S(2)}, u32[]{:S(2)}) collective-permute-start(f32[784,128]{1,0:T(8,128)} %get-tuple-element.42), channel_id=1, source_target_pairs={{0,1},{1,0},{2,3},{3,2},{4,5},{5,4},{6,7},{7,6},{8,9},{9,8},{10,11... | collective-permute-start | bytes 1204232 | tf_op jit(solution)/shard_map/ppermute | solution.py:551
  10.5 1.6 %collective-permute-start.1 = (f32[784,128]{1,0:T(8,128)}, f32[784,128]{1,0:T(8,128)S(1)}, u32[]{:S(2)}, u32[]{:S(2)}) collective-permute-start(f32[784,128]{1,0:T(8,128)} %get-tuple-element.47), channel_id=1, source_target_pairs={{0,2},{1,3},{2,0},{3,1},{4,6},{5,7},{6,4},{7,5},{8,10},{9,11},{10,... | collective-permute-start | bytes 1204232 | tf_op jit(solution)/shard_map/ppermute | solution.py:551
  12.1 2.6 %shard_map.105 = f32[4,272,128]{2,1,0:T(8,128)} custom-call(s32[8,128]{1,0:T(8,128)} %get-tuple-element.36._.slot_ref, f32[16,2048]{1,0:T(8,128)} %bitcast.18, f32[2,64,512]{2,1,0:T(8,128)} %bitcast.13, f32[64,512]{1,0:T(8,128)} %bitcast.16), custom_call_target="tpu_custom_call" | custom-call | flops 1 | bytes 1 | tf_op jit(solution)/shard_map/pallas_call | solution.py:584
  14.7 3.5 %all-to-all-start = ((f32[4,272,128]{2,1,0:T(8,128)}), f32[4,272,128]{2,1,0:T(8,128)S(1)}, u32[]{:S(2)}, u32[]{:S(2)}) async-start(f32[4,272,128]{2,1,0:T(8,128)} %shard_map.105), calls=%async_computation | async-start | bytes 1114112 | tf_op jit(solution)/shard_map/all_to_all | solution.py:591
  18.2 6.8 %shard_map.107 = (f32[768,128]{1,0:T(8,128)}, f32[768,128]{1,0:T(8,128)}, f32[768,128]{1,0:T(8,128)}, f32[768,128]{1,0:T(8,128)}) custom-call(s32[8,128]{1,0:T(8,128)} %get-tuple-element.36._.slot_ref, f32[1024,128]{1,0:T(8,128)} %w_hbm.3, f32[1024,128]{1,0:T(8,128)} %d_hbm.1), custom_call_target="tpu_custom_call" | custom-call | flops 1 | bytes 1 | tf_op jit(solution)/shard_map/pallas_call | solution.py:572
  25.0 2.0 %collective-permute-start.5 = (f32[768,128]{1,0:T(8,128)}, f32[768,128]{1,0:T(8,128)}, u32[]{:S(2)}, u32[]{:S(2)}) collective-permute-start(f32[768,128]{1,0:T(8,128)} %get-tuple-element.56), channel_id=1, source_target_pairs={{0,1},{1,0},{2,3},{3,2},{4,5},{5,4},{6,7},{7,6},{8,9},{9,8},{10,11... | collective-permute-start | bytes 1179656 | tf_op jit(solution)/shard_map/ppermute | solution.py:551
  27.0 1.6 %collective-permute-start.6 = (f32[768,128]{1,0:T(8,128)}, f32[768,128]{1,0:T(8,128)}, u32[]{:S(2)}, u32[]{:S(2)}) collective-permute-start(f32[768,128]{1,0:T(8,128)} %get-tuple-element.57), channel_id=1, source_target_pairs={{0,2},{1,3},{2,0},{3,1},{4,6},{5,7},{6,4},{7,5},{8,10},{9,11},{10,... | collective-permute-start | bytes 1179656 | tf_op jit(solution)/shard_map/ppermute | solution.py:551
  30.0 2.7 %shard_map.109 = (f32[4,16,128]{2,1,0:T(8,128)}, f32[512,128]{1,0:T(8,128)}, f32[512,128]{1,0:T(8,128)}) custom-call(f32[784,128]{1,0:T(8,128)S(1)} %copy-done, f32[784,128]{1,0:T(8,128)S(1)} %collective-permute-done.rest_1_, f32[784,128]{1,0:T(8,128)S(1)} %collective-permute-done.1.rest_2_, f32[784,128]{1,0:T(8,128)S(1)} %collective-permute-done.2.rest_3_, ...), custom_call_target="tpu_custom_call" | custom-call | flops 100000000 | bytes 100000000 | tf_op jit(solution)/shard_map/pallas_call | solution.py:600
  32.7 2.8 %collective-permute-start.3 = (f32[512,128]{1,0:T(8,128)}, f32[512,128]{1,0:T(8,128)}, u32[]{:S(2)}, u32[]{:S(2)}) collective-permute-start(f32[512,128]{1,0:T(8,128)} %get-tuple-element.53), channel_id=1, source_target_pairs={{0,4},{1,5},{2,6},{3,7},{4,0},{5,1},{6,2},{7,3},{8,12},{9,13},{10,... | collective-permute-start | bytes 786440 | tf_op jit(solution)/shard_map/ppermute | solution.py:551
  38.5 3.0 %shard_map.106 = (f32[2,5,64,128]{3,2,1,0:T(8,128)S(1)}, f32[9,5,64,128]{3,2,1,0:T(8,128)S(1)}, f32[9,5,64,128]{3,2,1,0:T(8,128)S(1)}, f32[2,5,64,128]{3,2,1,0:T(8,128)S(1)}, f32[8,128]{1,0:T(8,128)S(1)}) custom-call(f32[2,64,512]{2,1,0:T(8,128)S(1)} %bitcast.14, f32[64,512]{1,0:T(8,128)S(1)} %bitcast.17, f32[4,272,128]{2,1,0:T(8,128)S(1)} %copy-done.4), custom_call_target="tpu_custom_call" | custom-call | flops 1 | bytes 1 | tf_op jit(solution)/shard_map/pallas_call | solution.py:592
  45.9 1.9 %shard_map.108 = (f32[4,16,128]{2,1,0:T(8,128)S(1)}, f32[512,128]{1,0:T(8,128)S(1)}, f32[512,128]{1,0:T(8,128)S(1)}) custom-call(f32[784,128]{1,0:T(8,128)S(1)} %copy-done, f32[784,128]{1,0:T(8,128)S(1)} %copy-done.6, f32[784,128]{1,0:T(8,128)S(1)} %copy-done.8, f32[784,128]{1,0:T(8,128)S(1)} %copy-done.10, f32[8,128]{1,0:T(8,128)S(1)} %get-tuple-element.49.rest_4_), custom_call_target="tpu_custom_call" | custom-call | flops 1 | bytes 1 | tf_op jit(solution)/shard_map/pallas_call | solution.py:600
  47.8 4.5 %collective-permute-done.3.far_d_ref = f32[512,128]{1,0:T(8,128)} collective-permute-done((f32[512,128]{1,0:T(8,128)}, f32[512,128]{1,0:T(8,128)}, u32[]{:S(2)}, u32[]{:S(2)}) %collective-permute-start.3) | collective-permute-done | bytes 262176 | tf_op jit(solution)/shard_map/ppermute | solution.py:551
  52.4 5.0 %collective-permute-done.4.far_e_ref = f32[512,128]{1,0:T(8,128)} collective-permute-done((f32[512,128]{1,0:T(8,128)}, f32[512,128]{1,0:T(8,128)}, u32[]{:S(2)}, u32[]{:S(2)}) %collective-permute-start.4) | collective-permute-done | bytes 262176 | tf_op jit(solution)/shard_map/ppermute | solution.py:551
  59.1 3.6 %shard_map.110 = (f32[4,6,5,16,128]{4,3,2,1,0:T(8,128)S(1)}, f32[2,5,16,128]{3,2,1,0:T(8,128)S(1)}, f32[2,5,16,128]{3,2,1,0:T(8,128)S(1)}, f32[2,5,16,128]{3,2,1,0:T(8,128)S(1)}, f32[2,5,16,128]{3,2,1,0:T(8,128)S(1)}) custom-call(f32[4,16,128]{2,1,0:T(8,128)S(1)} %get-tuple-element.50.meta_ref, f32[512,128]{1,0:T(8,128)S(1)} %get-tuple-element.51.d_ref, ...), custom_call_target="tpu_custom_call" | custom-call | flops 1 | bytes 1 | tf_op jit(solution)/shard_map/pallas_call | solution.py:610
  63.6 4.4 %all-to-all-start.1 = ((f32[4,6,5,16,128]{4,3,2,1,0:T(8,128)}), f32[4,6,5,16,128]{4,3,2,1,0:T(8,128)}, u32[]{:S(2)}, u32[]{:S(2)}) async-start(f32[4,6,5,16,128]{4,3,2,1,0:T(8,128)} %copy-done.13), calls=%async_computation.1 | async-start | bytes 1966080 | tf_op jit(solution)/shard_map/all_to_all | solution.py:618
  68.0 2.8 %collective-permute-start.8 = (f32[2,5,16,128]{3,2,1,0:T(8,128)S(1)}, f32[2,5,16,128]{3,2,1,0:T(8,128)S(1)}, u32[]{:S(2)}, u32[]{:S(2)}) collective-permute-start(f32[2,5,16,128]{3,2,1,0:T(8,128)S(1)} %get-tuple-element.60), channel_id=1, source_target_pairs={{0,4},{1,5},{2,6},{3,7},{4,0},{5,1},{6,2},{7,3},{8,12},{9,13},{10,... | collective-permute-start | bytes 245768 | tf_op jit(solution)/shard_map/ppermute | solution.py:555
  70.8 3.6 %collective-permute-start.10 = (f32[2,5,16,128]{3,2,1,0:T(8,128)S(1)}, f32[2,5,16,128]{3,2,1,0:T(8,128)S(1)}, u32[]{:S(2)}, u32[]{:S(2)}) collective-permute-start(f32[2,5,16,128]{3,2,1,0:T(8,128)S(1)} %get-tuple-element.62), channel_id=1, source_target_pairs={{0,20},{1,21},{2,22},{3,23},{4,16},{5,17},{6,18},{7,19},{8,28},{9,... | collective-permute-start | bytes 245768 | tf_op jit(solution)/shard_map/ppermute | solution.py:555
  74.6 8.2 %collective-permute-done.9.rest_1_ = f32[2,5,16,128]{3,2,1,0:T(8,128)S(1)} collective-permute-done((f32[2,5,16,128]{3,2,1,0:T(8,128)S(1)}, f32[2,5,16,128]{3,2,1,0:T(8,128)S(1)}, u32[]{:S(2)}, u32[]{:S(2)}) %collective-permute-start.9) | collective-permute-done | bytes 81952 | tf_op jit(solution)/shard_map/ppermute | solution.py:555
  82.8 2.9 %collective-permute-done.10.rest_2_ = f32[2,5,16,128]{3,2,1,0:T(8,128)S(1)} collective-permute-done((f32[2,5,16,128]{3,2,1,0:T(8,128)S(1)}, f32[2,5,16,128]{3,2,1,0:T(8,128)S(1)}, u32[]{:S(2)}, u32[]{:S(2)}) %collective-permute-start.10) | collective-permute-done | bytes 81952 | tf_op jit(solution)/shard_map/ppermute | solution.py:555
  85.7 1.8 %collective-permute-done.11.rest_3_ = f32[2,5,16,128]{3,2,1,0:T(8,128)S(1)} collective-permute-done((f32[2,5,16,128]{3,2,1,0:T(8,128)S(1)}, f32[2,5,16,128]{3,2,1,0:T(8,128)S(1)}, u32[]{:S(2)}, u32[]{:S(2)}) %collective-permute-start.11) | collective-permute-done | bytes 81952 | tf_op jit(solution)/shard_map/ppermute | solution.py:555
  89.4 7.2 %shard_map.112 = (f32[2,64,512]{2,1,0:T(8,128)S(1)}, f32[2,64,512]{2,1,0:T(8,128)S(1)}, f32[2,5,64,128]{3,2,1,0:T(8,128)S(1)}, f32[32,1,128]{2,1,0:T(1,128)}) custom-call(f32[2,5,64,128]{3,2,1,0:T(8,128)S(1)} %copy-done.17, f32[9,5,64,128]{3,2,1,0:T(8,128)S(1)} %get-tuple-element.38.x_ref, f32[9,5,64,128]{3,2,1,0:T(8,128)S(1)} %get-tuple-element.39.y_ref, ...), custom_call_target="tpu_custom_call" | custom-call | flops 1 | bytes 1 | tf_op jit(solution)/shard_map/pallas_call | solution.py:620
  98.1 3.5 %all-to-all-start.2 = ((f32[32,1,128]{2,1,0:T(1,128)}), f32[32,1,128]{2,1,0:T(1,128)S(1)}, u32[]{:S(2)}, u32[]{:S(2)}) async-start(f32[32,1,128]{2,1,0:T(1,128)} %get-tuple-element.64), calls=%async_computation.2 | async-start | bytes 32768 | tf_op jit(solution)/shard_map/all_to_all | solution.py:625
  104.4 4.3 %all-to-all-done.2.dots_ref = f32[32,1,128]{2,1,0:T(1,128)S(1)} async-done(((f32[32,1,128]{2,1,0:T(1,128)}), f32[32,1,128]{2,1,0:T(1,128)S(1)}, u32[]{:S(2)}, u32[]{:S(2)}) %all-to-all-start.2) | async-done | bytes 16416 | tf_op jit(solution)/shard_map/all_to_all | solution.py:625
  (65 shorter events, 21.2 us)
Async XLA Ops:
  7.5 17.4 %collective-permute-start = (f32[784,128]{1,0:T(8,128)}, f32[784,128]{1,0:T(8,128)S(1)}, u32[]{:S(2)}, u32[]{:S(2)}) collective-permute-start(f32[784,128]{1,0:T(8,128)} %get-tuple-element.42), channel_id=1, source_target_pairs={{0,1},{1,0},{2,3},{3,2},{4,5},{5,4},{6,7},{7,6},{8,9},{9,8},{10,11... | collective-permute-start | bytes 1204232 | tf_op jit(solution)/shard_map/ppermute | solution.py:551
  10.5 18.0 %collective-permute-start.1 = (f32[784,128]{1,0:T(8,128)}, f32[784,128]{1,0:T(8,128)S(1)}, u32[]{:S(2)}, u32[]{:S(2)}) collective-permute-start(f32[784,128]{1,0:T(8,128)} %get-tuple-element.47), channel_id=1, source_target_pairs={{0,2},{1,3},{2,0},{3,1},{4,6},{5,7},{6,4},{7,5},{8,10},{9,11},{10,... | collective-permute-start | bytes 1204232 | tf_op jit(solution)/shard_map/ppermute | solution.py:551
  12.1 17.9 %collective-permute-start.2 = (f32[784,128]{1,0:T(8,128)}, f32[784,128]{1,0:T(8,128)S(1)}, u32[]{:S(2)}, u32[]{:S(2)}) collective-permute-start(f32[784,128]{1,0:T(8,128)} %get-tuple-element.48), channel_id=1, source_target_pairs={{0,3},{1,2},{2,1},{3,0},{4,7},{5,6},{6,5},{7,4},{8,11},{9,10},{10,... | collective-permute-start | bytes 1204232 | tf_op jit(solution)/shard_map/ppermute | solution.py:551
  12.1 17.9 %copy-start = (f32[784,128]{1,0:T(8,128)S(1)}, f32[784,128]{1,0:T(8,128)}, u32[]{:S(2)}) copy-start(f32[784,128]{1,0:T(8,128)} %get-tuple-element.41.rest_0_.rest_4_) | copy-start | bytes 1204228
  14.7 20.9 %all-to-all-start = ((f32[4,272,128]{2,1,0:T(8,128)}), f32[4,272,128]{2,1,0:T(8,128)S(1)}, u32[]{:S(2)}, u32[]{:S(2)}) async-start(f32[4,272,128]{2,1,0:T(8,128)} %shard_map.105), calls=%async_computation | async-start | bytes 1114112 | tf_op jit(solution)/shard_map/all_to_all | solution.py:591
  18.2 18.2 %copy-start.14 = (f32[1,64,512]{2,1,0:T(8,128)S(1)}, f32[1,64,512]{2,1,0:T(8,128)}, u32[]{:S(2)}) copy-start(f32[1,64,512]{2,1,0:T(8,128)} %param.10) | copy-start | bytes 393220
  25.0 10.6 %copy-start.5 = (f32[784,128]{1,0:T(8,128)}, f32[784,128]{1,0:T(8,128)S(1)}, u32[]{:S(2)}) copy-start(f32[784,128]{1,0:T(8,128)S(1)} %collective-permute-done.rest_1_) | copy-start | bytes 1204228
  25.0 32.4 %collective-permute-start.5 = (f32[768,128]{1,0:T(8,128)}, f32[768,128]{1,0:T(8,128)}, u32[]{:S(2)}, u32[]{:S(2)}) collective-permute-start(f32[768,128]{1,0:T(8,128)} %get-tuple-element.56), channel_id=1, source_target_pairs={{0,1},{1,0},{2,3},{3,2},{4,5},{5,4},{6,7},{7,6},{8,9},{9,8},{10,11... | collective-permute-start | bytes 1179656 | tf_op jit(solution)/shard_map/ppermute | solution.py:551
  27.0 30.4 %collective-permute-start.6 = (f32[768,128]{1,0:T(8,128)}, f32[768,128]{1,0:T(8,128)}, u32[]{:S(2)}, u32[]{:S(2)}) collective-permute-start(f32[768,128]{1,0:T(8,128)} %get-tuple-element.57), channel_id=1, source_target_pairs={{0,2},{1,3},{2,0},{3,1},{4,6},{5,7},{6,4},{7,5},{8,10},{9,11},{10,... | collective-permute-start | bytes 1179656 | tf_op jit(solution)/shard_map/ppermute | solution.py:551
  28.5 29.6 %collective-permute-start.7 = (f32[768,128]{1,0:T(8,128)}, f32[768,128]{1,0:T(8,128)}, u32[]{:S(2)}, u32[]{:S(2)}) collective-permute-start(f32[768,128]{1,0:T(8,128)} %get-tuple-element.58), channel_id=1, source_target_pairs={{0,3},{1,2},{2,1},{3,0},{4,7},{5,6},{6,5},{7,4},{8,11},{9,10},{10,... | collective-permute-start | bytes 1179656 | tf_op jit(solution)/shard_map/ppermute | solution.py:551
  28.6 7.1 %copy-start.7 = (f32[784,128]{1,0:T(8,128)}, f32[784,128]{1,0:T(8,128)S(1)}, u32[]{:S(2)}) copy-start(f32[784,128]{1,0:T(8,128)S(1)} %collective-permute-done.1.rest_2_) | copy-start | bytes 1204228
  30.0 5.6 %copy-start.9 = (f32[784,128]{1,0:T(8,128)}, f32[784,128]{1,0:T(8,128)S(1)}, u32[]{:S(2)}) copy-start(f32[784,128]{1,0:T(8,128)S(1)} %collective-permute-done.2.rest_3_) | copy-start | bytes 1204228
  32.7 19.7 %collective-permute-start.3 = (f32[512,128]{1,0:T(8,128)}, f32[512,128]{1,0:T(8,128)}, u32[]{:S(2)}, u32[]{:S(2)}) collective-permute-start(f32[512,128]{1,0:T(8,128)} %get-tuple-element.53), channel_id=1, source_target_pairs={{0,4},{1,5},{2,6},{3,7},{4,0},{5,1},{6,2},{7,3},{8,12},{9,13},{10,... | collective-permute-start | bytes 786440 | tf_op jit(solution)/shard_map/ppermute | solution.py:551
  35.5 21.9 %collective-permute-start.4 = (f32[512,128]{1,0:T(8,128)}, f32[512,128]{1,0:T(8,128)}, u32[]{:S(2)}, u32[]{:S(2)}) collective-permute-start(f32[512,128]{1,0:T(8,128)} %get-tuple-element.54), channel_id=1, source_target_pairs={{0,4},{1,5},{2,6},{3,7},{4,0},{5,1},{6,2},{7,3},{8,12},{9,13},{10,... | collective-permute-start | bytes 786440 | tf_op jit(solution)/shard_map/ppermute | solution.py:551
  37.4 1.1 copy-start.4
  42.9 1.0 copy-start.6
  43.9 1.0 copy-start.8
  63.6 23.9 %all-to-all-start.1 = ((f32[4,6,5,16,128]{4,3,2,1,0:T(8,128)}), f32[4,6,5,16,128]{4,3,2,1,0:T(8,128)}, u32[]{:S(2)}, u32[]{:S(2)}) async-start(f32[4,6,5,16,128]{4,3,2,1,0:T(8,128)} %copy-done.13), calls=%async_computation.1 | async-start | bytes 1966080 | tf_op jit(solution)/shard_map/all_to_all | solution.py:618
  68.0 6.6 %collective-permute-start.8 = (f32[2,5,16,128]{3,2,1,0:T(8,128)S(1)}, f32[2,5,16,128]{3,2,1,0:T(8,128)S(1)}, u32[]{:S(2)}, u32[]{:S(2)}) collective-permute-start(f32[2,5,16,128]{3,2,1,0:T(8,128)S(1)} %get-tuple-element.60), channel_id=1, source_target_pairs={{0,4},{1,5},{2,6},{3,7},{4,0},{5,1},{6,2},{7,3},{8,12},{9,13},{10,... | collective-permute-start | bytes 245768 | tf_op jit(solution)/shard_map/ppermute | solution.py:555
  70.8 12.0 %collective-permute-start.9 = (f32[2,5,16,128]{3,2,1,0:T(8,128)S(1)}, f32[2,5,16,128]{3,2,1,0:T(8,128)S(1)}, u32[]{:S(2)}, u32[]{:S(2)}) collective-permute-start(f32[2,5,16,128]{3,2,1,0:T(8,128)S(1)} %get-tuple-element.61), channel_id=1, source_target_pairs={{0,12},{1,13},{2,14},{3,15},{4,8},{5,9},{6,10},{7,11},{8,4},{9,5},... | collective-permute-start | bytes 245768 | tf_op jit(solution)/shard_map/ppermute | solution.py:555
  70.8 14.9 %collective-permute-start.10 = (f32[2,5,16,128]{3,2,1,0:T(8,128)S(1)}, f32[2,5,16,128]{3,2,1,0:T(8,128)S(1)}, u32[]{:S(2)}, u32[]{:S(2)}) collective-permute-start(f32[2,5,16,128]{3,2,1,0:T(8,128)S(1)} %get-tuple-element.62), channel_id=1, source_target_pairs={{0,20},{1,21},{2,22},{3,23},{4,16},{5,17},{6,18},{7,19},{8,28},{9,... | collective-permute-start | bytes 245768 | tf_op jit(solution)/shard_map/ppermute | solution.py:555
  74.4 13.1 %collective-permute-start.11 = (f32[2,5,16,128]{3,2,1,0:T(8,128)S(1)}, f32[2,5,16,128]{3,2,1,0:T(8,128)S(1)}, u32[]{:S(2)}, u32[]{:S(2)}) collective-permute-start(f32[2,5,16,128]{3,2,1,0:T(8,128)S(1)} %get-tuple-element.63), channel_id=1, source_target_pairs={{0,28},{1,29},{2,30},{3,31},{4,24},{5,25},{6,26},{7,27},{8,20},{9,... | collective-permute-start | bytes 245768 | tf_op jit(solution)/shard_map/ppermute | solution.py:555
  98.1 10.6 %all-to-all-start.2 = ((f32[32,1,128]{2,1,0:T(1,128)}), f32[32,1,128]{2,1,0:T(1,128)S(1)}, u32[]{:S(2)}, u32[]{:S(2)}) async-start(f32[32,1,128]{2,1,0:T(1,128)} %get-tuple-element.64), calls=%async_computation.2 | async-start | bytes 32768 | tf_op jit(solution)/shard_map/all_to_all | solution.py:625
  102.5 6.1 %copy-start.2 = (f32[2,1,64,512]{3,2,1,0:T(8,128)S(1)}, f32[2,1,64,512]{3,2,1,0:T(8,128)}, u32[]{:S(2)}) copy-start(f32[2,1,64,512]{3,2,1,0:T(8,128)} %param.9) | copy-start | bytes 786436
  (15 other events, 13.1 us)

commit v14 on v13

--- a/solution.py
+++ b/solution.py
@@ -16,7 +16,7 @@
 HALF = SEG // 2
 SPLIT = 16
 REACH = M
-VMEM_BYTES = 32 * 1024 * 1024
+VMEM_BYTES = 16 * 1024 * 1024
 PACK_BYTES = 60 * 1024 * 1024
 FIRST = 100_000_000
 JOIN = 100_000_000
@@ -313,8 +313,7 @@
     r2 = each(lambda a, b, c, d, e: a * (b + c) + d * e, q2, q0, shift(q0, 2), q1, up1)
     r3 = each(lambda a, b, c, d: a * b + c * d, q1, up2, q2, shift(q1, 2))
     r4 = each(lambda a, b: a * b, q2, shift(q2, 2))
-    upper = [r0, r1, r2, r3, r4]
-    return [shift(upper[d], -d) for d in range(REACH, 0, -1)] + upper
+    return [r0, r1, r2, r3, r4]
 
 
 def make_x_diagonals(out, cx_ref):
@@ -338,10 +337,11 @@
 
 
 def banded(diagonals, values, shift):
-    total = None
-    for d, diagonal in enumerate(diagonals):
-        terms = [c * v for c, v in zip(diagonal, shift(values, d - REACH))]
-        total = terms if total is None else [a + b for a, b in zip(total, terms)]
+    total = [c * v for c, v in zip(diagonals[0], values)]
+    for d in range(1, REACH + 1):
+        above = [c * v for c, v in zip(diagonals[d], shift(values, d))]
+        below = shift([c * v for c, v in zip(diagonals[d], values)], -d)
+        total = [a + (b + c) for a, b, c in zip(total, above, below)]
     return total
 
 
@@ -591,8 +591,8 @@
     swap = lax.all_to_all(swap, "px", split_axis=0, concat_axis=0, tiled=True)
     c0_ext, x_sweep, y_sweep, u_ext, token = call(
         start_kernel,
-        (f32(F, tiles, nx, SEG), f32(2 * REACH + 1, tiles, nx, SEG),
-         f32(2 * REACH + 1, tiles, nx, SEG), f32(F, tiles, nx, SEG), f32(8, SEG)),
+        (f32(F, tiles, nx, SEG), f32(REACH + 1, tiles, nx, SEG),
+         f32(REACH + 1, tiles, nx, SEG), f32(F, tiles, nx, SEG), f32(8, SEG)),
         [vmem(tiles, nx, SEG), vmem(tiles, nx, SEG), vmem(F, tiles, nx, SEG)],
     )(c0, cx, swap)
 

time: 113 us -> 107 us (0.947)
  local copies, waits for them, and re-layouts: 16.1 us -> 8.78 us
  waiting for transfers between devices: 28.8 us -> 34.1 us
  Pallas kernels: 37 us -> 34.6 us
    unnamed x48 -> x34, local copies, waits for them, and re-layouts: 16.1 us -> 8.78 us
    ppermute x8, waiting for transfers between devices: 11.7 us -> 16.4 us  [to_half(): return lax.ppermute(block, 'py', [(i, i ^ k) for i in range(groups)])]
    pallas_call x1, Pallas kernels: 7.23 us -> 5.72 us  [shards(): call(solve_kernel, (f32(F, nx, width),) * 2 + (f32(F, tiles, nx, SEG), f3...]
where the time goes in v14:
time: 107 us
  Pallas kernels  34.6 us (32%)
  waiting for transfers between devices  34.1 us (32%)
  starting transfers between devices  28.3 us (26%)
  local copies, waits for them, and re-layouts  8.78 us (8%)
    ppermute x8, waiting for transfers between devices, to_half(): return lax.ppermute(block, 'py', [(i, i ^ k) for i in range(groups)])  16.4 us
    ppermute x4, waiting for transfers between devices, across(): lax.ppermute(parts[k], ('px', 'py'), [(i * groups + j, (i ^ k) * groups +...  12.8 us
    ppermute x8, starting transfers between devices, to_half(): return lax.ppermute(block, 'py', [(i, i ^ k) for i in range(groups)])  11.1 us
    unnamed x34, local copies, waits for them, and re-layouts  8.78 us
    pallas_call x1, Pallas kernels, shards(): call(functools.partial(pack_weights_kernel, groups, cap, blk, block_rows)...  6.93 us
    pallas_call x1, Pallas kernels, shards(): call(functools.partial(pack_products_kernel, groups, cap), (f32(2 * cap,...  6.75 us
    ppermute x4, starting transfers between devices, across(): lax.ppermute(parts[k], ('px', 'py'), [(i * groups + j, (i ^ k) * groups +...  6.64 us
    pallas_call x1, Pallas kernels, shards(): call(solve_kernel, (f32(F, nx, width),) * 2 + (f32(F, tiles, nx, SEG), f3...  5.72 us
  transfers between devices with their start and end apart: 15, of which 8 were waited for; matrix products, arithmetic and copies ran while one was open for 0% of the time, Pallas kernels for 16%

profile of v14, /device:TPU:0, one launch (start us, length us, event | category | flops | bytes accessed | tf_op | source)
XLA Modules:
  0.0 106.7 jit_solution(15776521185795013887)
XLA Ops:
  0.6 6.9 %shard_map.104 = (f32[784,128]{1,0:T(8,128)}, f32[784,128]{1,0:T(8,128)}, f32[784,128]{1,0:T(8,128)}, f32[784,128]{1,0:T(8,128)}, s32[8,128]{1,0:T(8,128)}) custom-call(s32[8,128]{1,0:T(8,128)} %bitcast.19, s32[8,128]{1,0:T(8,128)} %bitcast.20, s32[8,128]{1,0:T(8,128)} %bitcast.21, f32[8,128]{1,0:T(8,128)} %bitcast.22, f32[1024,128]{1,0:T(8,128)} %w_hbm.3), custom_call_target="tpu_custom_call" | custom-call | flops 1 | bytes 1 | tf_op jit(solution)/shard_map/pallas_call | solution.py:560
  7.6 3.0 %collective-permute-start = (f32[784,128]{1,0:T(8,128)}, f32[784,128]{1,0:T(8,128)S(1)}, u32[]{:S(2)}, u32[]{:S(2)}) collective-permute-start(f32[784,128]{1,0:T(8,128)} %get-tuple-element.42), channel_id=1, source_target_pairs={{0,1},{1,0},{2,3},{3,2},{4,5},{5,4},{6,7},{7,6},{8,9},{9,8},{10,11... | collective-permute-start | bytes 1204232 | tf_op jit(solution)/shard_map/ppermute | solution.py:551
  10.6 1.6 %collective-permute-start.1 = (f32[784,128]{1,0:T(8,128)}, f32[784,128]{1,0:T(8,128)S(1)}, u32[]{:S(2)}, u32[]{:S(2)}) collective-permute-start(f32[784,128]{1,0:T(8,128)} %get-tuple-element.47), channel_id=1, source_target_pairs={{0,2},{1,3},{2,0},{3,1},{4,6},{5,7},{6,4},{7,5},{8,10},{9,11},{10,... | collective-permute-start | bytes 1204232 | tf_op jit(solution)/shard_map/ppermute | solution.py:551
  12.2 2.5 %shard_map.105 = f32[4,272,128]{2,1,0:T(8,128)} custom-call(s32[8,128]{1,0:T(8,128)} %get-tuple-element.36._.slot_ref, f32[16,2048]{1,0:T(8,128)} %bitcast.18, f32[2,64,512]{2,1,0:T(8,128)} %bitcast.13, f32[64,512]{1,0:T(8,128)} %bitcast.16), custom_call_target="tpu_custom_call" | custom-call | flops 1 | bytes 1 | tf_op jit(solution)/shard_map/pallas_call | solution.py:584
  14.7 3.5 %all-to-all-start = ((f32[4,272,128]{2,1,0:T(8,128)}), f32[4,272,128]{2,1,0:T(8,128)S(1)}, u32[]{:S(2)}, u32[]{:S(2)}) async-start(f32[4,272,128]{2,1,0:T(8,128)} %shard_map.105), calls=%async_computation | async-start | bytes 1114112 | tf_op jit(solution)/shard_map/all_to_all | solution.py:591
  18.2 6.7 %shard_map.107 = (f32[768,128]{1,0:T(8,128)}, f32[768,128]{1,0:T(8,128)}, f32[768,128]{1,0:T(8,128)}, f32[768,128]{1,0:T(8,128)}) custom-call(s32[8,128]{1,0:T(8,128)} %get-tuple-element.36._.slot_ref, f32[1024,128]{1,0:T(8,128)} %w_hbm.3, f32[1024,128]{1,0:T(8,128)} %d_hbm.1), custom_call_target="tpu_custom_call" | custom-call | flops 1 | bytes 1 | tf_op jit(solution)/shard_map/pallas_call | solution.py:572
  24.9 2.0 %collective-permute-start.5 = (f32[768,128]{1,0:T(8,128)}, f32[768,128]{1,0:T(8,128)}, u32[]{:S(2)}, u32[]{:S(2)}) collective-permute-start(f32[768,128]{1,0:T(8,128)} %get-tuple-element.56), channel_id=1, source_target_pairs={{0,1},{1,0},{2,3},{3,2},{4,5},{5,4},{6,7},{7,6},{8,9},{9,8},{10,11... | collective-permute-start | bytes 1179656 | tf_op jit(solution)/shard_map/ppermute | solution.py:551
  28.5 1.6 %collective-permute-done.2.rest_3_ = f32[784,128]{1,0:T(8,128)S(1)} collective-permute-done((f32[784,128]{1,0:T(8,128)}, f32[784,128]{1,0:T(8,128)S(1)}, u32[]{:S(2)}, u32[]{:S(2)}) %collective-permute-start.2) | collective-permute-done | bytes 401440 | tf_op jit(solution)/shard_map/ppermute | solution.py:551
  30.1 2.7 %shard_map.109 = (f32[4,16,128]{2,1,0:T(8,128)}, f32[512,128]{1,0:T(8,128)}, f32[512,128]{1,0:T(8,128)}) custom-call(f32[784,128]{1,0:T(8,128)S(1)} %copy-done, f32[784,128]{1,0:T(8,128)S(1)} %collective-permute-done.rest_1_, f32[784,128]{1,0:T(8,128)S(1)} %collective-permute-done.1.rest_2_, f32[784,128]{1,0:T(8,128)S(1)} %collective-permute-done.2.rest_3_, ...), custom_call_target="tpu_custom_call" | custom-call | flops 100000000 | bytes 100000000 | tf_op jit(solution)/shard_map/pallas_call | solution.py:600
  32.8 2.8 %collective-permute-start.3 = (f32[512,128]{1,0:T(8,128)}, f32[512,128]{1,0:T(8,128)}, u32[]{:S(2)}, u32[]{:S(2)}) collective-permute-start(f32[512,128]{1,0:T(8,128)} %get-tuple-element.53), channel_id=1, source_target_pairs={{0,4},{1,5},{2,6},{3,7},{4,0},{5,1},{6,2},{7,3},{8,12},{9,13},{10,... | collective-permute-start | bytes 786440 | tf_op jit(solution)/shard_map/ppermute | solution.py:551
  35.7 2.2 %shard_map.106 = (f32[2,5,64,128]{3,2,1,0:T(8,128)S(1)}, f32[5,5,64,128]{3,2,1,0:T(8,128)S(1)}, f32[5,5,64,128]{3,2,1,0:T(8,128)S(1)}, f32[2,5,64,128]{3,2,1,0:T(8,128)S(1)}, f32[8,128]{1,0:T(8,128)S(1)}) custom-call(f32[2,64,512]{2,1,0:T(8,128)S(1)} %bitcast.14, f32[64,512]{1,0:T(8,128)S(1)} %bitcast.17, f32[4,272,128]{2,1,0:T(8,128)S(1)} %all-to-all-done.swap_ref), custom_call_target="tpu_custom_call" | custom-call | flops 1 | bytes 1 | tf_op jit(solution)/shard_map/pallas_call | solution.py:592
  41.5 1.9 %shard_map.108 = (f32[4,16,128]{2,1,0:T(8,128)S(1)}, f32[512,128]{1,0:T(8,128)S(1)}, f32[512,128]{1,0:T(8,128)S(1)}) custom-call(f32[784,128]{1,0:T(8,128)S(1)} %copy-done, f32[784,128]{1,0:T(8,128)S(1)} %collective-permute-done.rest_1_, f32[784,128]{1,0:T(8,128)S(1)} %copy-done.3, f32[784,128]{1,0:T(8,128)S(1)} %copy-done.5, ...), custom_call_target="tpu_custom_call" | custom-call | flops 1 | bytes 1 | tf_op jit(solution)/shard_map/pallas_call | solution.py:600
  43.4 9.0 %collective-permute-done.3.far_d_ref = f32[512,128]{1,0:T(8,128)} collective-permute-done((f32[512,128]{1,0:T(8,128)}, f32[512,128]{1,0:T(8,128)}, u32[]{:S(2)}, u32[]{:S(2)}) %collective-permute-start.3) | collective-permute-done | bytes 262176 | tf_op jit(solution)/shard_map/ppermute | solution.py:551
  52.3 5.1 %collective-permute-done.4.far_e_ref = f32[512,128]{1,0:T(8,128)} collective-permute-done((f32[512,128]{1,0:T(8,128)}, f32[512,128]{1,0:T(8,128)}, u32[]{:S(2)}, u32[]{:S(2)}) %collective-permute-start.4) | collective-permute-done | bytes 262176 | tf_op jit(solution)/shard_map/ppermute | solution.py:551
  58.1 3.6 %shard_map.110 = (f32[4,6,5,16,128]{4,3,2,1,0:T(8,128)S(1)}, f32[2,5,16,128]{3,2,1,0:T(8,128)S(1)}, f32[2,5,16,128]{3,2,1,0:T(8,128)S(1)}, f32[2,5,16,128]{3,2,1,0:T(8,128)S(1)}, f32[2,5,16,128]{3,2,1,0:T(8,128)S(1)}) custom-call(f32[4,16,128]{2,1,0:T(8,128)S(1)} %get-tuple-element.50.meta_ref, f32[512,128]{1,0:T(8,128)S(1)} %get-tuple-element.51.d_ref, ...), custom_call_target="tpu_custom_call" | custom-call | flops 1 | bytes 1 | tf_op jit(solution)/shard_map/pallas_call | solution.py:610
  62.6 3.7 %all-to-all-start.1 = ((f32[4,6,5,16,128]{4,3,2,1,0:T(8,128)}), f32[4,6,5,16,128]{4,3,2,1,0:T(8,128)S(1)}, u32[]{:S(2)}, u32[]{:S(2)}) async-start(f32[4,6,5,16,128]{4,3,2,1,0:T(8,128)} %copy-done.6), calls=%async_computation.1 | async-start | bytes 1966080 | tf_op jit(solution)/shard_map/all_to_all | solution.py:618
  66.3 2.8 %collective-permute-start.8 = (f32[2,5,16,128]{3,2,1,0:T(8,128)S(1)}, f32[2,5,16,128]{3,2,1,0:T(8,128)S(1)}, u32[]{:S(2)}, u32[]{:S(2)}) collective-permute-start(f32[2,5,16,128]{3,2,1,0:T(8,128)S(1)} %get-tuple-element.60), channel_id=1, source_target_pairs={{0,4},{1,5},{2,6},{3,7},{4,0},{5,1},{6,2},{7,3},{8,12},{9,13},{10,... | collective-permute-start | bytes 245768 | tf_op jit(solution)/shard_map/ppermute | solution.py:555
  69.1 3.6 %collective-permute-start.10 = (f32[2,5,16,128]{3,2,1,0:T(8,128)S(1)}, f32[2,5,16,128]{3,2,1,0:T(8,128)S(1)}, u32[]{:S(2)}, u32[]{:S(2)}) collective-permute-start(f32[2,5,16,128]{3,2,1,0:T(8,128)S(1)} %get-tuple-element.62), channel_id=1, source_target_pairs={{0,20},{1,21},{2,22},{3,23},{4,16},{5,17},{6,18},{7,19},{8,28},{9,... | collective-permute-start | bytes 245768 | tf_op jit(solution)/shard_map/ppermute | solution.py:555
  73.0 8.2 %collective-permute-done.9.rest_1_ = f32[2,5,16,128]{3,2,1,0:T(8,128)S(1)} collective-permute-done((f32[2,5,16,128]{3,2,1,0:T(8,128)S(1)}, f32[2,5,16,128]{3,2,1,0:T(8,128)S(1)}, u32[]{:S(2)}, u32[]{:S(2)}) %collective-permute-start.9) | collective-permute-done | bytes 81952 | tf_op jit(solution)/shard_map/ppermute | solution.py:555
  81.1 2.9 %collective-permute-done.10.rest_2_ = f32[2,5,16,128]{3,2,1,0:T(8,128)S(1)} collective-permute-done((f32[2,5,16,128]{3,2,1,0:T(8,128)S(1)}, f32[2,5,16,128]{3,2,1,0:T(8,128)S(1)}, u32[]{:S(2)}, u32[]{:S(2)}) %collective-permute-start.10) | collective-permute-done | bytes 81952 | tf_op jit(solution)/shard_map/ppermute | solution.py:555
  84.0 1.8 %collective-permute-done.11.rest_3_ = f32[2,5,16,128]{3,2,1,0:T(8,128)S(1)} collective-permute-done((f32[2,5,16,128]{3,2,1,0:T(8,128)S(1)}, f32[2,5,16,128]{3,2,1,0:T(8,128)S(1)}, u32[]{:S(2)}, u32[]{:S(2)}) %collective-permute-start.11) | collective-permute-done | bytes 81952 | tf_op jit(solution)/shard_map/ppermute | solution.py:555
  87.8 5.7 %shard_map.112 = (f32[2,64,512]{2,1,0:T(8,128)S(1)}, f32[2,64,512]{2,1,0:T(8,128)S(1)}, f32[2,5,64,128]{3,2,1,0:T(8,128)S(1)}, f32[32,1,128]{2,1,0:T(1,128)}) custom-call(f32[2,5,64,128]{3,2,1,0:T(8,128)S(1)} %copy-done.10, f32[5,5,64,128]{3,2,1,0:T(8,128)S(1)} %get-tuple-element.38.x_ref, f32[5,5,64,128]{3,2,1,0:T(8,128)S(1)} %get-tuple-element.39.y_ref, ...), custom_call_target="tpu_custom_call" | custom-call | flops 1 | bytes 1 | tf_op jit(solution)/shard_map/pallas_call | solution.py:620
  94.9 3.5 %all-to-all-start.2 = ((f32[32,1,128]{2,1,0:T(1,128)}), f32[32,1,128]{2,1,0:T(1,128)S(1)}, u32[]{:S(2)}, u32[]{:S(2)}) async-start(f32[32,1,128]{2,1,0:T(1,128)} %get-tuple-element.64), calls=%async_computation.2 | async-start | bytes 32768 | tf_op jit(solution)/shard_map/all_to_all | solution.py:625
  100.4 5.0 %all-to-all-done.2.dots_ref = f32[32,1,128]{2,1,0:T(1,128)S(1)} async-done(((f32[32,1,128]{2,1,0:T(1,128)}), f32[32,1,128]{2,1,0:T(1,128)S(1)}, u32[]{:S(2)}, u32[]{:S(2)}) %all-to-all-start.2) | async-done | bytes 16416 | tf_op jit(solution)/shard_map/all_to_all | solution.py:625
  (51 shorter events, 13.9 us)
Async XLA Ops:
  7.6 17.4 %collective-permute-start = (f32[784,128]{1,0:T(8,128)}, f32[784,128]{1,0:T(8,128)S(1)}, u32[]{:S(2)}, u32[]{:S(2)}) collective-permute-start(f32[784,128]{1,0:T(8,128)} %get-tuple-element.42), channel_id=1, source_target_pairs={{0,1},{1,0},{2,3},{3,2},{4,5},{5,4},{6,7},{7,6},{8,9},{9,8},{10,11... | collective-permute-start | bytes 1204232 | tf_op jit(solution)/shard_map/ppermute | solution.py:551
  10.6 17.9 %collective-permute-start.1 = (f32[784,128]{1,0:T(8,128)}, f32[784,128]{1,0:T(8,128)S(1)}, u32[]{:S(2)}, u32[]{:S(2)}) collective-permute-start(f32[784,128]{1,0:T(8,128)} %get-tuple-element.47), channel_id=1, source_target_pairs={{0,2},{1,3},{2,0},{3,1},{4,6},{5,7},{6,4},{7,5},{8,10},{9,11},{10,... | collective-permute-start | bytes 1204232 | tf_op jit(solution)/shard_map/ppermute | solution.py:551
  12.2 17.9 %collective-permute-start.2 = (f32[784,128]{1,0:T(8,128)}, f32[784,128]{1,0:T(8,128)S(1)}, u32[]{:S(2)}, u32[]{:S(2)}) collective-permute-start(f32[784,128]{1,0:T(8,128)} %get-tuple-element.48), channel_id=1, source_target_pairs={{0,3},{1,2},{2,1},{3,0},{4,7},{5,6},{6,5},{7,4},{8,11},{9,10},{10,... | collective-permute-start | bytes 1204232 | tf_op jit(solution)/shard_map/ppermute | solution.py:551
  14.7 21.1 %all-to-all-start = ((f32[4,272,128]{2,1,0:T(8,128)}), f32[4,272,128]{2,1,0:T(8,128)S(1)}, u32[]{:S(2)}, u32[]{:S(2)}) async-start(f32[4,272,128]{2,1,0:T(8,128)} %shard_map.105), calls=%async_computation | async-start | bytes 1114112 | tf_op jit(solution)/shard_map/all_to_all | solution.py:591
  18.2 11.9 %copy-start = (f32[784,128]{1,0:T(8,128)S(1)}, f32[784,128]{1,0:T(8,128)}, u32[]{:S(2)}) copy-start(f32[784,128]{1,0:T(8,128)} %get-tuple-element.41.rest_0_.rest_4_) | copy-start | bytes 1204228
  24.9 32.5 %collective-permute-start.5 = (f32[768,128]{1,0:T(8,128)}, f32[768,128]{1,0:T(8,128)}, u32[]{:S(2)}, u32[]{:S(2)}) collective-permute-start(f32[768,128]{1,0:T(8,128)} %get-tuple-element.56), channel_id=1, source_target_pairs={{0,1},{1,0},{2,3},{3,2},{4,5},{5,4},{6,7},{7,6},{8,9},{9,8},{10,11... | collective-permute-start | bytes 1179656 | tf_op jit(solution)/shard_map/ppermute | solution.py:551
  26.9 30.5 %collective-permute-start.6 = (f32[768,128]{1,0:T(8,128)}, f32[768,128]{1,0:T(8,128)}, u32[]{:S(2)}, u32[]{:S(2)}) collective-permute-start(f32[768,128]{1,0:T(8,128)} %get-tuple-element.57), channel_id=1, source_target_pairs={{0,2},{1,3},{2,0},{3,1},{4,6},{5,7},{6,4},{7,5},{8,10},{9,11},{10,... | collective-permute-start | bytes 1179656 | tf_op jit(solution)/shard_map/ppermute | solution.py:551
  28.5 29.6 %collective-permute-start.7 = (f32[768,128]{1,0:T(8,128)}, f32[768,128]{1,0:T(8,128)}, u32[]{:S(2)}, u32[]{:S(2)}) collective-permute-start(f32[768,128]{1,0:T(8,128)} %get-tuple-element.58), channel_id=1, source_target_pairs={{0,3},{1,2},{2,1},{3,0},{4,7},{5,6},{6,5},{7,4},{8,11},{9,10},{10,... | collective-permute-start | bytes 1179656 | tf_op jit(solution)/shard_map/ppermute | solution.py:551
  28.5 4.3 %copy-start.2 = (f32[784,128]{1,0:T(8,128)}, f32[784,128]{1,0:T(8,128)S(1)}, u32[]{:S(2)}) copy-start(f32[784,128]{1,0:T(8,128)S(1)} %collective-permute-done.1.rest_2_) | copy-start | bytes 1204228
  30.1 2.7 %copy-start.4 = (f32[784,128]{1,0:T(8,128)}, f32[784,128]{1,0:T(8,128)S(1)}, u32[]{:S(2)}) copy-start(f32[784,128]{1,0:T(8,128)S(1)} %collective-permute-done.2.rest_3_) | copy-start | bytes 1204228
  30.1 5.6 %copy-start.1 = (f32[2,1,64,512]{3,2,1,0:T(8,128)S(1)}, f32[2,1,64,512]{3,2,1,0:T(8,128)}, u32[]{:S(2)}) copy-start(f32[2,1,64,512]{3,2,1,0:T(8,128)} %param.9) | copy-start | bytes 786436
  30.1 5.6 %copy-start.7 = (f32[1,64,512]{2,1,0:T(8,128)S(1)}, f32[1,64,512]{2,1,0:T(8,128)}, u32[]{:S(2)}) copy-start(f32[1,64,512]{2,1,0:T(8,128)} %param.10) | copy-start | bytes 393220
  32.8 19.5 %collective-permute-start.3 = (f32[512,128]{1,0:T(8,128)}, f32[512,128]{1,0:T(8,128)}, u32[]{:S(2)}, u32[]{:S(2)}) collective-permute-start(f32[512,128]{1,0:T(8,128)} %get-tuple-element.53), channel_id=1, source_target_pairs={{0,4},{1,5},{2,6},{3,7},{4,0},{5,1},{6,2},{7,3},{8,12},{9,13},{10,... | collective-permute-start | bytes 786440 | tf_op jit(solution)/shard_map/ppermute | solution.py:551
  35.6 21.9 %collective-permute-start.4 = (f32[512,128]{1,0:T(8,128)}, f32[512,128]{1,0:T(8,128)}, u32[]{:S(2)}, u32[]{:S(2)}) collective-permute-start(f32[512,128]{1,0:T(8,128)} %get-tuple-element.54), channel_id=1, source_target_pairs={{0,4},{1,5},{2,6},{3,7},{4,0},{5,1},{6,2},{7,3},{8,12},{9,13},{10,... | collective-permute-start | bytes 786440 | tf_op jit(solution)/shard_map/ppermute | solution.py:551
  39.5 1.0 copy-start.3
  40.5 1.0 copy-start.5
  41.5 16.7 %copy-start.8 = (f32[768,128]{1,0:T(8,128)S(1)}, f32[768,128]{1,0:T(8,128)}, u32[]{:S(2)}) copy-start(f32[768,128]{1,0:T(8,128)} %get-tuple-element.55.rest_0_) | copy-start | bytes 1179652
  62.6 23.2 %all-to-all-start.1 = ((f32[4,6,5,16,128]{4,3,2,1,0:T(8,128)}), f32[4,6,5,16,128]{4,3,2,1,0:T(8,128)S(1)}, u32[]{:S(2)}, u32[]{:S(2)}) async-start(f32[4,6,5,16,128]{4,3,2,1,0:T(8,128)} %copy-done.6), calls=%async_computation.1 | async-start | bytes 1966080 | tf_op jit(solution)/shard_map/all_to_all | solution.py:618
  66.3 6.6 %collective-permute-start.8 = (f32[2,5,16,128]{3,2,1,0:T(8,128)S(1)}, f32[2,5,16,128]{3,2,1,0:T(8,128)S(1)}, u32[]{:S(2)}, u32[]{:S(2)}) collective-permute-start(f32[2,5,16,128]{3,2,1,0:T(8,128)S(1)} %get-tuple-element.60), channel_id=1, source_target_pairs={{0,4},{1,5},{2,6},{3,7},{4,0},{5,1},{6,2},{7,3},{8,12},{9,13},{10,... | collective-permute-start | bytes 245768 | tf_op jit(solution)/shard_map/ppermute | solution.py:555
  69.1 12.0 %collective-permute-start.9 = (f32[2,5,16,128]{3,2,1,0:T(8,128)S(1)}, f32[2,5,16,128]{3,2,1,0:T(8,128)S(1)}, u32[]{:S(2)}, u32[]{:S(2)}) collective-permute-start(f32[2,5,16,128]{3,2,1,0:T(8,128)S(1)} %get-tuple-element.61), channel_id=1, source_target_pairs={{0,12},{1,13},{2,14},{3,15},{4,8},{5,9},{6,10},{7,11},{8,4},{9,5},... | collective-permute-start | bytes 245768 | tf_op jit(solution)/shard_map/ppermute | solution.py:555
  69.1 14.9 %collective-permute-start.10 = (f32[2,5,16,128]{3,2,1,0:T(8,128)S(1)}, f32[2,5,16,128]{3,2,1,0:T(8,128)S(1)}, u32[]{:S(2)}, u32[]{:S(2)}) collective-permute-start(f32[2,5,16,128]{3,2,1,0:T(8,128)S(1)} %get-tuple-element.62), channel_id=1, source_target_pairs={{0,20},{1,21},{2,22},{3,23},{4,16},{5,17},{6,18},{7,19},{8,28},{9,... | collective-permute-start | bytes 245768 | tf_op jit(solution)/shard_map/ppermute | solution.py:555
  72.7 13.1 %collective-permute-start.11 = (f32[2,5,16,128]{3,2,1,0:T(8,128)S(1)}, f32[2,5,16,128]{3,2,1,0:T(8,128)S(1)}, u32[]{:S(2)}, u32[]{:S(2)}) collective-permute-start(f32[2,5,16,128]{3,2,1,0:T(8,128)S(1)} %get-tuple-element.63), channel_id=1, source_target_pairs={{0,28},{1,29},{2,30},{3,31},{4,24},{5,25},{6,26},{7,27},{8,20},{9,... | collective-permute-start | bytes 245768 | tf_op jit(solution)/shard_map/ppermute | solution.py:555
  94.9 10.5 %all-to-all-start.2 = ((f32[32,1,128]{2,1,0:T(1,128)}), f32[32,1,128]{2,1,0:T(1,128)S(1)}, u32[]{:S(2)}, u32[]{:S(2)}) async-start(f32[32,1,128]{2,1,0:T(1,128)} %get-tuple-element.64), calls=%async_computation.2 | async-start | bytes 32768 | tf_op jit(solution)/shard_map/all_to_all | solution.py:625
  99.4 6.1 %copy-start.16 = (f32[2,64,512]{2,1,0:T(8,128)S(1)}, f32[2,64,512]{2,1,0:T(8,128)}, u32[]{:S(2)}) copy-start(f32[2,64,512]{2,1,0:T(8,128)} %copy-done.15) | copy-start | bytes 786436
  (8 other events, 6.8 us)

commit v15 on v14

--- a/solution.py
+++ b/solution.py
@@ -255,7 +255,9 @@
 
 
 def products_kernel(half, cap, blk, meta_ref, d_ref, e_ref, far_d_ref, far_e_ref, *rest):
-    v_refs, (out, *far_outs, acc_ref, sums_ref, far_ref, side) = rest[:half], rest[half:]
+    v_refs, (out, token_out, *far_outs, acc_ref, sums_ref, far_ref, side) = (
+        rest[:half], rest[half:])
+    token_out[...] = jnp.zeros_like(token_out)
     spans = out.shape[0]
     sum_products(half, cap, blk, 1, meta_ref, v_refs, acc_ref, far_ref)
     me = lax.axis_index("px")
@@ -391,7 +393,7 @@
     return [ref.at[start + f] for f in range(F)]
 
 
-def start_kernel(c0_ref, cx_ref, swap_ref, c0_out, x_out, y_out, u_out, token_out, cx_out, cy_out,
+def start_kernel(c0_ref, cx_ref, swap_ref, c0_out, cx_out, cy_out, u_out, token_out, x_ref, y_ref,
                  work):
     token_out[...] = jnp.zeros_like(token_out)
     nx = cx_ref.shape[0]
@@ -416,10 +418,15 @@
     cx_out[:, nx - 1:, :] = jnp.zeros((count, 1, SEG), jnp.float32)
     for f in range(F):
         c0_out[f, count - 1] = beside(f)
-    make_x_diagonals(x_out, cx_out)
-    make_y_diagonals(y_out, cy_out)
-    sweep_x_into(of_fields(work), of_fields(c0_out), x_out)
-    sweep_y_into(of_fields(u_out), of_fields(work), y_out)
+    make_x_diagonals(x_ref, cx_out)
+    make_y_diagonals(y_ref, cy_out)
+    sweep_x_into(of_fields(work), of_fields(c0_out), x_ref)
+    sweep_y_into(of_fields(u_out), of_fields(work), y_ref)
+
+
+def diagonals_kernel(_, cx_ref, cy_ref, x_out, y_out):
+    make_x_diagonals(x_out, cx_ref)
+    make_y_diagonals(y_out, cy_ref)
 
 
 def join_kernel(spans, *rest):
@@ -589,11 +596,12 @@
         limit=PACK_BYTES,
     )(slots, coef_y[0], c0, cx)
     swap = lax.all_to_all(swap, "px", split_axis=0, concat_axis=0, tiled=True)
-    c0_ext, x_sweep, y_sweep, u_ext, token = call(
+    c0_ext, cx_ext, cy_ext, u_ext, token = call(
         start_kernel,
-        (f32(F, tiles, nx, SEG), f32(REACH + 1, tiles, nx, SEG),
-         f32(REACH + 1, tiles, nx, SEG), f32(F, tiles, nx, SEG), f32(8, SEG)),
-        [vmem(tiles, nx, SEG), vmem(tiles, nx, SEG), vmem(F, tiles, nx, SEG)],
+        (f32(F, tiles, nx, SEG), f32(tiles, nx, SEG), f32(tiles, nx, SEG), f32(F, tiles, nx, SEG),
+         f32(8, SEG)),
+        [vmem(REACH + 1, tiles, nx, SEG), vmem(REACH + 1, tiles, nx, SEG),
+         vmem(F, tiles, nx, SEG)],
     )(c0, cx, swap)
 
     def sum_weights(side, token, weight):
@@ -607,14 +615,16 @@
     meta, *side_across = sum_weights(1, w_blocks[0], FIRST)
     side_across = [to_half(values, half) for values in side_across]
     meta, *side = sum_weights(0, token, 1)
-    parts, *sums_across = call(
+    parts, token, *sums_across = call(
         functools.partial(products_kernel, half, cap, blk),
-        (f32(spans, 3 * F, tiles, LX, SEG),) + (f32(F, tiles, LX, SEG),) * spans,
+        (f32(spans, 3 * F, tiles, LX, SEG), f32(8, SEG)) + (f32(F, tiles, LX, SEG),) * spans,
         [vmem(ROWS, 2 * SEG), vmem(ROWS, SEG), vmem(ROWS, SEG), vmem(2, ROWS, SEG)],
     )(meta, *side, *side_across, *v_blocks)
     far_sums = call(
         functools.partial(join_kernel, spans), f32(F, tiles, nx, SEG), weight=JOIN,
     )(*across(sums_across))
+    x_sweep, y_sweep = call(
+        diagonals_kernel, (f32(REACH + 1, tiles, nx, SEG),) * 2)(token, cx_ext, cy_ext)
     parts = lax.all_to_all(parts, "px", split_axis=0, concat_axis=0, tiled=True)
 
     r, q, h, dots = call(

time: 107 us -> 107 us (level)
  local copies, waits for them, and re-layouts: 8.78 us -> 6.45 us
  Pallas kernels: 34.6 us -> 36.8 us
    unnamed x34 -> x32, local copies, waits for them, and re-layouts: 8.78 us -> 6.45 us
    pallas_call x1 -> x2, Pallas kernels: 2.24 us -> 3.75 us  [the longest x1 2.31 us: shards(): call(start_kernel, (f32(F, tiles, nx, SEG), f32(tiles, nx, SEG), f32(tile...]
    ppermute x8, waiting for transfers between devices: 16.4 us -> 17.7 us  [to_half(): return lax.ppermute(block, 'py', [(i, i ^ k) for i in range(groups)])]
    ppermute x4, waiting for transfers between devices: 12.8 us -> 11.5 us  [across(): lax.ppermute(parts[k], ('px', 'py'), [(i * groups + j, (i ^ k) * groups +...]
  transfers between devices with their start and end apart: 15 -> 15, of which waited for: 8 -> 8; matrix products, arithmetic and copies ran while one was open for 0% -> 0% of each run, Pallas kernels for 16% -> 17%
where the time goes in v15:
time: 107 us
  Pallas kernels  36.8 us (34%)
  waiting for transfers between devices  34.3 us (32%)
  starting transfers between devices  28.5 us (27%)
  local copies, waits for them, and re-layouts  6.45 us (6%)
    ppermute x8, waiting for transfers between devices, to_half(): return lax.ppermute(block, 'py', [(i, i ^ k) for i in range(groups)])  17.7 us
    ppermute x4, waiting for transfers between devices, across(): lax.ppermute(parts[k], ('px', 'py'), [(i * groups + j, (i ^ k) * groups +...  11.5 us
    ppermute x8, starting transfers between devices, to_half(): return lax.ppermute(block, 'py', [(i, i ^ k) for i in range(groups)])  11.1 us
    pallas_call x1, Pallas kernels, shards(): call(functools.partial(pack_weights_kernel, groups, cap, blk, block_rows)...  6.87 us
    pallas_call x1, Pallas kernels, shards(): call(functools.partial(pack_products_kernel, groups, cap), (f32(2 * cap,...  6.71 us
    ppermute x4, starting transfers between devices, across(): lax.ppermute(parts[k], ('px', 'py'), [(i * groups + j, (i ^ k) * groups +...  6.64 us
    unnamed x32, local copies, waits for them, and re-layouts  6.45 us
    pallas_call x1, Pallas kernels, shards(): call(solve_kernel, (f32(F, nx, width),) * 2 + (f32(F, tiles, nx, SEG), f3...  5.72 us
  transfers between devices with their start and end apart: 15, of which 8 were waited for; matrix products, arithmetic and copies ran while one was open for 0% of the time, Pallas kernels for 17%

profile of v15, /device:TPU:0, one launch (start us, length us, event | category | flops | bytes accessed | tf_op | source)
XLA Modules:
  0.0 106.8 jit_solution(355140797573673268)
XLA Ops:
  0.6 6.9 %shard_map.104 = (f32[784,128]{1,0:T(8,128)}, f32[784,128]{1,0:T(8,128)}, f32[784,128]{1,0:T(8,128)}, f32[784,128]{1,0:T(8,128)}, s32[8,128]{1,0:T(8,128)}) custom-call(s32[8,128]{1,0:T(8,128)} %bitcast.19, s32[8,128]{1,0:T(8,128)} %bitcast.20, s32[8,128]{1,0:T(8,128)} %bitcast.21, f32[8,128]{1,0:T(8,128)} %bitcast.22, f32[1024,128]{1,0:T(8,128)} %w_hbm.3), custom_call_target="tpu_custom_call" | custom-call | flops 1 | bytes 1 | tf_op jit(solution)/shard_map/pallas_call | solution.py:567
  7.5 3.0 %collective-permute-start = (f32[784,128]{1,0:T(8,128)}, f32[784,128]{1,0:T(8,128)S(1)}, u32[]{:S(2)}, u32[]{:S(2)}) collective-permute-start(f32[784,128]{1,0:T(8,128)} %get-tuple-element.42), channel_id=1, source_target_pairs={{0,1},{1,0},{2,3},{3,2},{4,5},{5,4},{6,7},{7,6},{8,9},{9,8},{10,11... | collective-permute-start | bytes 1204232 | tf_op jit(solution)/shard_map/ppermute | solution.py:558
  10.5 1.6 %collective-permute-start.1 = (f32[784,128]{1,0:T(8,128)}, f32[784,128]{1,0:T(8,128)S(1)}, u32[]{:S(2)}, u32[]{:S(2)}) collective-permute-start(f32[784,128]{1,0:T(8,128)} %get-tuple-element.47), channel_id=1, source_target_pairs={{0,2},{1,3},{2,0},{3,1},{4,6},{5,7},{6,4},{7,5},{8,10},{9,11},{10,... | collective-permute-start | bytes 1204232 | tf_op jit(solution)/shard_map/ppermute | solution.py:558
  12.1 2.5 %shard_map.105 = f32[4,272,128]{2,1,0:T(8,128)} custom-call(s32[8,128]{1,0:T(8,128)} %get-tuple-element.39._.slot_ref, f32[16,2048]{1,0:T(8,128)} %bitcast.18, f32[2,64,512]{2,1,0:T(8,128)} %bitcast.13, f32[64,512]{1,0:T(8,128)} %bitcast.16), custom_call_target="tpu_custom_call" | custom-call | flops 1 | bytes 1 | tf_op jit(solution)/shard_map/pallas_call | solution.py:591
  14.6 3.5 %all-to-all-start = ((f32[4,272,128]{2,1,0:T(8,128)}), f32[4,272,128]{2,1,0:T(8,128)S(1)}, u32[]{:S(2)}, u32[]{:S(2)}) async-start(f32[4,272,128]{2,1,0:T(8,128)} %shard_map.105), calls=%async_computation | async-start | bytes 1114112 | tf_op jit(solution)/shard_map/all_to_all | solution.py:598
  18.1 6.7 %shard_map.107 = (f32[768,128]{1,0:T(8,128)}, f32[768,128]{1,0:T(8,128)}, f32[768,128]{1,0:T(8,128)}, f32[768,128]{1,0:T(8,128)}) custom-call(s32[8,128]{1,0:T(8,128)} %get-tuple-element.39._.slot_ref, f32[1024,128]{1,0:T(8,128)} %w_hbm.3, f32[1024,128]{1,0:T(8,128)} %d_hbm.1), custom_call_target="tpu_custom_call" | custom-call | flops 1 | bytes 1 | tf_op jit(solution)/shard_map/pallas_call | solution.py:579
  24.8 2.0 %collective-permute-start.5 = (f32[768,128]{1,0:T(8,128)}, f32[768,128]{1,0:T(8,128)S(1)}, u32[]{:S(2)}, u32[]{:S(2)}) collective-permute-start(f32[768,128]{1,0:T(8,128)} %get-tuple-element.56), channel_id=1, source_target_pairs={{0,1},{1,0},{2,3},{3,2},{4,5},{5,4},{6,7},{7,6},{8,9},{9,8},{10,11... | collective-permute-start | bytes 1179656 | tf_op jit(solution)/shard_map/ppermute | solution.py:558
  28.4 1.7 %collective-permute-done.2.rest_3_ = f32[784,128]{1,0:T(8,128)S(1)} collective-permute-done((f32[784,128]{1,0:T(8,128)}, f32[784,128]{1,0:T(8,128)S(1)}, u32[]{:S(2)}, u32[]{:S(2)}) %collective-permute-start.2) | collective-permute-done | bytes 401440 | tf_op jit(solution)/shard_map/ppermute | solution.py:558
  30.1 2.7 %shard_map.109 = (f32[4,16,128]{2,1,0:T(8,128)}, f32[512,128]{1,0:T(8,128)}, f32[512,128]{1,0:T(8,128)}) custom-call(f32[784,128]{1,0:T(8,128)S(1)} %copy-done, f32[784,128]{1,0:T(8,128)S(1)} %collective-permute-done.rest_1_, f32[784,128]{1,0:T(8,128)S(1)} %collective-permute-done.1.rest_2_, f32[784,128]{1,0:T(8,128)S(1)} %collective-permute-done.2.rest_3_, ...), custom_call_target="tpu_custom_call" | custom-call | flops 100000000 | bytes 100000000 | tf_op jit(solution)/shard_map/pallas_call | solution.py:608
  32.8 2.8 %collective-permute-start.3 = (f32[512,128]{1,0:T(8,128)}, f32[512,128]{1,0:T(8,128)S(1)}, u32[]{:S(2)}, u32[]{:S(2)}) collective-permute-start(f32[512,128]{1,0:T(8,128)} %get-tuple-element.53), channel_id=1, source_target_pairs={{0,4},{1,5},{2,6},{3,7},{4,0},{5,1},{6,2},{7,3},{8,12},{9,13},{10,... | collective-permute-start | bytes 786440 | tf_op jit(solution)/shard_map/ppermute | solution.py:558
  35.7 2.3 %shard_map.106 = (f32[2,5,64,128]{3,2,1,0:T(8,128)S(1)}, f32[5,64,128]{2,1,0:T(8,128)S(1)}, f32[5,64,128]{2,1,0:T(8,128)S(1)}, f32[2,5,64,128]{3,2,1,0:T(8,128)S(1)}, f32[8,128]{1,0:T(8,128)S(1)}) custom-call(f32[2,64,512]{2,1,0:T(8,128)S(1)} %bitcast.14, f32[64,512]{1,0:T(8,128)S(1)} %bitcast.17, f32[4,272,128]{2,1,0:T(8,128)S(1)} %all-to-all-done.swap_ref), custom_call_target="tpu_custom_call" | custom-call | flops 1 | bytes 1 | tf_op jit(solution)/shard_map/pallas_call | solution.py:599
  40.1 1.9 %shard_map.108 = (f32[4,16,128]{2,1,0:T(8,128)S(1)}, f32[512,128]{1,0:T(8,128)S(1)}, f32[512,128]{1,0:T(8,128)S(1)}) custom-call(f32[784,128]{1,0:T(8,128)S(1)} %copy-done, f32[784,128]{1,0:T(8,128)S(1)} %collective-permute-done.rest_1_, f32[784,128]{1,0:T(8,128)S(1)} %collective-permute-done.1.rest_2_, f32[784,128]{1,0:T(8,128)S(1)} %collective-permute-done.2.rest_3_, ...), custom_call_target="tpu_custom_call" | custom-call | flops 1 | bytes 1 | tf_op jit(solution)/shard_map/pallas_call | solution.py:608
  42.0 10.2 %collective-permute-done.3.far_d_ref = f32[512,128]{1,0:T(8,128)S(1)} collective-permute-done((f32[512,128]{1,0:T(8,128)}, f32[512,128]{1,0:T(8,128)S(1)}, u32[]{:S(2)}, u32[]{:S(2)}) %collective-permute-start.3) | collective-permute-done | bytes 262176 | tf_op jit(solution)/shard_map/ppermute | solution.py:558
  52.2 5.1 %collective-permute-done.4.far_e_ref = f32[512,128]{1,0:T(8,128)} collective-permute-done((f32[512,128]{1,0:T(8,128)}, f32[512,128]{1,0:T(8,128)}, u32[]{:S(2)}, u32[]{:S(2)}) %collective-permute-start.4) | collective-permute-done | bytes 262176 | tf_op jit(solution)/shard_map/ppermute | solution.py:558
  58.1 4.3 %shard_map.110 = (f32[4,6,5,16,128]{4,3,2,1,0:T(8,128)}, f32[8,128]{1,0:T(8,128)S(1)}, f32[2,5,16,128]{3,2,1,0:T(8,128)}, f32[2,5,16,128]{3,2,1,0:T(8,128)}, f32...) custom-call(f32[4,16,128]{2,1,0:T(8,128)S(1)} %get-tuple-element.50.meta_ref, f32[512,128]{1,0:T(8,128)S(1)} %get-tuple-element.51.d_ref, ...), custom_call_target="tpu_custom_call" | custom-call | flops 1 | bytes 1 | tf_op jit(solution)/shard_map/pallas_call | solution.py:618
  62.4 3.8 %all-to-all-start.1 = ((f32[4,6,5,16,128]{4,3,2,1,0:T(8,128)}), f32[4,6,5,16,128]{4,3,2,1,0:T(8,128)S(1)}, u32[]{:S(2)}, u32[]{:S(2)}) async-start(f32[4,6,5,16,128]{4,3,2,1,0:T(8,128)} %get-tuple-element.65), calls=%async_computation.1 | async-start | bytes 1966080 | tf_op jit(solution)/shard_map/all_to_all | solution.py:628
  66.2 2.8 %collective-permute-start.8 = (f32[2,5,16,128]{3,2,1,0:T(8,128)}, f32[2,5,16,128]{3,2,1,0:T(8,128)S(1)}, u32[]{:S(2)}, u32[]{:S(2)}) collective-permute-start(f32[2,5,16,128]{3,2,1,0:T(8,128)} %get-tuple-element.66), channel_id=1, source_target_pairs={{0,4},{1,5},{2,6},{3,7},{4,0},{5,1},{6,2},{7,3},{8,12},{9,13},{10,... | collective-permute-start | bytes 245768 | tf_op jit(solution)/shard_map/ppermute | solution.py:562
  69.0 3.6 %collective-permute-start.10 = (f32[2,5,16,128]{3,2,1,0:T(8,128)}, f32[2,5,16,128]{3,2,1,0:T(8,128)S(1)}, u32[]{:S(2)}, u32[]{:S(2)}) collective-permute-start(f32[2,5,16,128]{3,2,1,0:T(8,128)} %get-tuple-element.68), channel_id=1, source_target_pairs={{0,20},{1,21},{2,22},{3,23},{4,16},{5,17},{6,18},{7,19},{8,28},{9,... | collective-permute-start | bytes 245768 | tf_op jit(solution)/shard_map/ppermute | solution.py:562
  74.3 6.9 %collective-permute-done.9.rest_1_ = f32[2,5,16,128]{3,2,1,0:T(8,128)S(1)} collective-permute-done((f32[2,5,16,128]{3,2,1,0:T(8,128)}, f32[2,5,16,128]{3,2,1,0:T(8,128)S(1)}, u32[]{:S(2)}, u32[]{:S(2)}) %collective-permute-start.9) | collective-permute-done | bytes 81952 | tf_op jit(solution)/shard_map/ppermute | solution.py:562
  81.2 2.9 %collective-permute-done.10.rest_2_ = f32[2,5,16,128]{3,2,1,0:T(8,128)S(1)} collective-permute-done((f32[2,5,16,128]{3,2,1,0:T(8,128)}, f32[2,5,16,128]{3,2,1,0:T(8,128)S(1)}, u32[]{:S(2)}, u32[]{:S(2)}) %collective-permute-start.10) | collective-permute-done | bytes 81952 | tf_op jit(solution)/shard_map/ppermute | solution.py:562
  84.1 1.8 %collective-permute-done.11.rest_3_ = f32[2,5,16,128]{3,2,1,0:T(8,128)S(1)} collective-permute-done((f32[2,5,16,128]{3,2,1,0:T(8,128)}, f32[2,5,16,128]{3,2,1,0:T(8,128)S(1)}, u32[]{:S(2)}, u32[]{:S(2)}) %collective-permute-start.11) | collective-permute-done | bytes 81952 | tf_op jit(solution)/shard_map/ppermute | solution.py:562
  87.9 5.7 %shard_map.113 = (f32[2,64,512]{2,1,0:T(8,128)S(1)}, f32[2,64,512]{2,1,0:T(8,128)S(1)}, f32[2,5,64,128]{3,2,1,0:T(8,128)S(1)}, f32[32,1,128]{2,1,0:T(1,128)}) custom-call(f32[2,5,64,128]{3,2,1,0:T(8,128)S(1)} %copy-done.5, f32[5,5,64,128]{3,2,1,0:T(8,128)S(1)} %get-tuple-element.62.x_ref, f32[5,5,64,128]{3,2,1,0:T(8,128)S(1)} %get-tuple-element.63.y_ref, ...), custom_call_target="tpu_custom_call" | custom-call | flops 1 | bytes 1 | tf_op jit(solution)/shard_map/pallas_call | solution.py:630
  95.0 3.5 %all-to-all-start.2 = ((f32[32,1,128]{2,1,0:T(1,128)}), f32[32,1,128]{2,1,0:T(1,128)S(1)}, u32[]{:S(2)}, u32[]{:S(2)}) async-start(f32[32,1,128]{2,1,0:T(1,128)} %get-tuple-element.70), calls=%async_computation.2 | async-start | bytes 32768 | tf_op jit(solution)/shard_map/all_to_all | solution.py:635
  100.5 5.0 %all-to-all-done.2.dots_ref = f32[32,1,128]{2,1,0:T(1,128)S(1)} async-done(((f32[32,1,128]{2,1,0:T(1,128)}), f32[32,1,128]{2,1,0:T(1,128)S(1)}, u32[]{:S(2)}, u32[]{:S(2)}) %all-to-all-start.2) | async-done | bytes 16416 | tf_op jit(solution)/shard_map/all_to_all | solution.py:635
  (50 shorter events, 13.0 us)
Async XLA Ops:
  7.5 17.3 %collective-permute-start = (f32[784,128]{1,0:T(8,128)}, f32[784,128]{1,0:T(8,128)S(1)}, u32[]{:S(2)}, u32[]{:S(2)}) collective-permute-start(f32[784,128]{1,0:T(8,128)} %get-tuple-element.42), channel_id=1, source_target_pairs={{0,1},{1,0},{2,3},{3,2},{4,5},{5,4},{6,7},{7,6},{8,9},{9,8},{10,11... | collective-permute-start | bytes 1204232 | tf_op jit(solution)/shard_map/ppermute | solution.py:558
  10.5 17.9 %collective-permute-start.1 = (f32[784,128]{1,0:T(8,128)}, f32[784,128]{1,0:T(8,128)S(1)}, u32[]{:S(2)}, u32[]{:S(2)}) collective-permute-start(f32[784,128]{1,0:T(8,128)} %get-tuple-element.47), channel_id=1, source_target_pairs={{0,2},{1,3},{2,0},{3,1},{4,6},{5,7},{6,4},{7,5},{8,10},{9,11},{10,... | collective-permute-start | bytes 1204232 | tf_op jit(solution)/shard_map/ppermute | solution.py:558
  12.1 18.0 %collective-permute-start.2 = (f32[784,128]{1,0:T(8,128)}, f32[784,128]{1,0:T(8,128)S(1)}, u32[]{:S(2)}, u32[]{:S(2)}) collective-permute-start(f32[784,128]{1,0:T(8,128)} %get-tuple-element.48), channel_id=1, source_target_pairs={{0,3},{1,2},{2,1},{3,0},{4,7},{5,6},{6,5},{7,4},{8,11},{9,10},{10,... | collective-permute-start | bytes 1204232 | tf_op jit(solution)/shard_map/ppermute | solution.py:558
  14.6 21.1 %all-to-all-start = ((f32[4,272,128]{2,1,0:T(8,128)}), f32[4,272,128]{2,1,0:T(8,128)S(1)}, u32[]{:S(2)}, u32[]{:S(2)}) async-start(f32[4,272,128]{2,1,0:T(8,128)} %shard_map.105), calls=%async_computation | async-start | bytes 1114112 | tf_op jit(solution)/shard_map/all_to_all | solution.py:598
  18.1 12.0 %copy-start = (f32[784,128]{1,0:T(8,128)S(1)}, f32[784,128]{1,0:T(8,128)}, u32[]{:S(2)}) copy-start(f32[784,128]{1,0:T(8,128)} %get-tuple-element.41.rest_0_.rest_4_) | copy-start | bytes 1204228
  24.8 32.5 %collective-permute-start.5 = (f32[768,128]{1,0:T(8,128)}, f32[768,128]{1,0:T(8,128)S(1)}, u32[]{:S(2)}, u32[]{:S(2)}) collective-permute-start(f32[768,128]{1,0:T(8,128)} %get-tuple-element.56), channel_id=1, source_target_pairs={{0,1},{1,0},{2,3},{3,2},{4,5},{5,4},{6,7},{7,6},{8,9},{9,8},{10,11... | collective-permute-start | bytes 1179656 | tf_op jit(solution)/shard_map/ppermute | solution.py:558
  26.8 30.5 %collective-permute-start.6 = (f32[768,128]{1,0:T(8,128)}, f32[768,128]{1,0:T(8,128)}, u32[]{:S(2)}, u32[]{:S(2)}) collective-permute-start(f32[768,128]{1,0:T(8,128)} %get-tuple-element.57), channel_id=1, source_target_pairs={{0,2},{1,3},{2,0},{3,1},{4,6},{5,7},{6,4},{7,5},{8,10},{9,11},{10,... | collective-permute-start | bytes 1179656 | tf_op jit(solution)/shard_map/ppermute | solution.py:558
  28.4 29.7 %collective-permute-start.7 = (f32[768,128]{1,0:T(8,128)}, f32[768,128]{1,0:T(8,128)}, u32[]{:S(2)}, u32[]{:S(2)}) collective-permute-start(f32[768,128]{1,0:T(8,128)} %get-tuple-element.58), channel_id=1, source_target_pairs={{0,3},{1,2},{2,1},{3,0},{4,7},{5,6},{6,5},{7,4},{8,11},{9,10},{10,... | collective-permute-start | bytes 1179656 | tf_op jit(solution)/shard_map/ppermute | solution.py:558
  30.1 5.6 %copy-start.1 = (f32[2,1,64,512]{3,2,1,0:T(8,128)S(1)}, f32[2,1,64,512]{3,2,1,0:T(8,128)}, u32[]{:S(2)}) copy-start(f32[2,1,64,512]{3,2,1,0:T(8,128)} %param.9) | copy-start | bytes 786436
  30.1 5.6 %copy-start.2 = (f32[1,64,512]{2,1,0:T(8,128)S(1)}, f32[1,64,512]{2,1,0:T(8,128)}, u32[]{:S(2)}) copy-start(f32[1,64,512]{2,1,0:T(8,128)} %param.10) | copy-start | bytes 393220
  32.8 19.5 %collective-permute-start.3 = (f32[512,128]{1,0:T(8,128)}, f32[512,128]{1,0:T(8,128)S(1)}, u32[]{:S(2)}, u32[]{:S(2)}) collective-permute-start(f32[512,128]{1,0:T(8,128)} %get-tuple-element.53), channel_id=1, source_target_pairs={{0,4},{1,5},{2,6},{3,7},{4,0},{5,1},{6,2},{7,3},{8,12},{9,13},{10,... | collective-permute-start | bytes 786440 | tf_op jit(solution)/shard_map/ppermute | solution.py:558
  35.5 21.8 %collective-permute-start.4 = (f32[512,128]{1,0:T(8,128)}, f32[512,128]{1,0:T(8,128)}, u32[]{:S(2)}, u32[]{:S(2)}) collective-permute-start(f32[512,128]{1,0:T(8,128)} %get-tuple-element.54), channel_id=1, source_target_pairs={{0,4},{1,5},{2,6},{3,7},{4,0},{5,1},{6,2},{7,3},{8,12},{9,13},{10,... | collective-permute-start | bytes 786440 | tf_op jit(solution)/shard_map/ppermute | solution.py:558
  40.1 1.9 %copy-start.4 = (f32[2,5,64,128]{3,2,1,0:T(8,128)}, f32[2,5,64,128]{3,2,1,0:T(8,128)S(1)}, u32[]{:S(2)}) copy-start(f32[2,5,64,128]{3,2,1,0:T(8,128)S(1)} %get-tuple-element.40.c0_ref) | copy-start | bytes 983044
  40.1 18.0 %copy-start.3 = (f32[768,128]{1,0:T(8,128)S(1)}, f32[768,128]{1,0:T(8,128)}, u32[]{:S(2)}) copy-start(f32[768,128]{1,0:T(8,128)} %get-tuple-element.55.rest_0_) | copy-start | bytes 1179652
  62.4 10.5 %copy-start.13 = (f32[5,64,128]{2,1,0:T(8,128)S(1)}, f32[5,64,128]{2,1,0:T(8,128)}, u32[]{:S(2)}) copy-start(f32[5,64,128]{2,1,0:T(8,128)} %copy-done.12) | copy-start | bytes 491524
  62.4 10.5 %copy-start.15 = (f32[5,64,128]{2,1,0:T(8,128)S(1)}, f32[5,64,128]{2,1,0:T(8,128)}, u32[]{:S(2)}) copy-start(f32[5,64,128]{2,1,0:T(8,128)} %copy-done.14) | copy-start | bytes 491524
  62.4 23.5 %all-to-all-start.1 = ((f32[4,6,5,16,128]{4,3,2,1,0:T(8,128)}), f32[4,6,5,16,128]{4,3,2,1,0:T(8,128)S(1)}, u32[]{:S(2)}, u32[]{:S(2)}) async-start(f32[4,6,5,16,128]{4,3,2,1,0:T(8,128)} %get-tuple-element.65), calls=%async_computation.1 | async-start | bytes 1966080 | tf_op jit(solution)/shard_map/all_to_all | solution.py:628
  66.2 8.1 %collective-permute-start.8 = (f32[2,5,16,128]{3,2,1,0:T(8,128)}, f32[2,5,16,128]{3,2,1,0:T(8,128)S(1)}, u32[]{:S(2)}, u32[]{:S(2)}) collective-permute-start(f32[2,5,16,128]{3,2,1,0:T(8,128)} %get-tuple-element.66), channel_id=1, source_target_pairs={{0,4},{1,5},{2,6},{3,7},{4,0},{5,1},{6,2},{7,3},{8,12},{9,13},{10,... | collective-permute-start | bytes 245768 | tf_op jit(solution)/shard_map/ppermute | solution.py:562
  69.0 12.2 %collective-permute-start.9 = (f32[2,5,16,128]{3,2,1,0:T(8,128)}, f32[2,5,16,128]{3,2,1,0:T(8,128)S(1)}, u32[]{:S(2)}, u32[]{:S(2)}) collective-permute-start(f32[2,5,16,128]{3,2,1,0:T(8,128)} %get-tuple-element.67), channel_id=1, source_target_pairs={{0,12},{1,13},{2,14},{3,15},{4,8},{5,9},{6,10},{7,11},{8,4},{9,5},... | collective-permute-start | bytes 245768 | tf_op jit(solution)/shard_map/ppermute | solution.py:562
  69.0 15.1 %collective-permute-start.10 = (f32[2,5,16,128]{3,2,1,0:T(8,128)}, f32[2,5,16,128]{3,2,1,0:T(8,128)S(1)}, u32[]{:S(2)}, u32[]{:S(2)}) collective-permute-start(f32[2,5,16,128]{3,2,1,0:T(8,128)} %get-tuple-element.68), channel_id=1, source_target_pairs={{0,20},{1,21},{2,22},{3,23},{4,16},{5,17},{6,18},{7,19},{8,28},{9,... | collective-permute-start | bytes 245768 | tf_op jit(solution)/shard_map/ppermute | solution.py:562
  72.6 13.3 %collective-permute-start.11 = (f32[2,5,16,128]{3,2,1,0:T(8,128)}, f32[2,5,16,128]{3,2,1,0:T(8,128)S(1)}, u32[]{:S(2)}, u32[]{:S(2)}) collective-permute-start(f32[2,5,16,128]{3,2,1,0:T(8,128)} %get-tuple-element.69), channel_id=1, source_target_pairs={{0,28},{1,29},{2,30},{3,31},{4,24},{5,25},{6,26},{7,27},{8,20},{9,... | collective-permute-start | bytes 245768 | tf_op jit(solution)/shard_map/ppermute | solution.py:562
  85.9 1.0 copy-start.5
  95.0 10.5 %all-to-all-start.2 = ((f32[32,1,128]{2,1,0:T(1,128)}), f32[32,1,128]{2,1,0:T(1,128)S(1)}, u32[]{:S(2)}, u32[]{:S(2)}) async-start(f32[32,1,128]{2,1,0:T(1,128)} %get-tuple-element.70), calls=%async_computation.2 | async-start | bytes 32768 | tf_op jit(solution)/shard_map/all_to_all | solution.py:635
  99.5 6.1 %copy-start.11 = (f32[2,64,512]{2,1,0:T(8,128)S(1)}, f32[2,64,512]{2,1,0:T(8,128)}, u32[]{:S(2)}) copy-start(f32[2,64,512]{2,1,0:T(8,128)} %copy-done.10) | copy-start | bytes 786436
  (7 other events, 5.5 us)

commit v16 on v15

--- a/solution.py
+++ b/solution.py
@@ -17,7 +17,7 @@
 SPLIT = 16
 REACH = M
 VMEM_BYTES = 16 * 1024 * 1024
-PACK_BYTES = 60 * 1024 * 1024
+PACK_BYTES = 57 * 1024 * 1024
 FIRST = 100_000_000
 JOIN = 100_000_000
 

time: 107 us -> 107 us (level)
  no operation moved by 1% of the time
where the time goes in v16:
time: 107 us
  Pallas kernels  36.8 us (34%)
  waiting for transfers between devices  34.3 us (32%)
  starting transfers between devices  28.5 us (27%)
  local copies, waits for them, and re-layouts  6.45 us (6%)
    ppermute x8, waiting for transfers between devices, to_half(): return lax.ppermute(block, 'py', [(i, i ^ k) for i in range(groups)])  17.7 us
    ppermute x4, waiting for transfers between devices, across(): lax.ppermute(parts[k], ('px', 'py'), [(i * groups + j, (i ^ k) * groups +...  11.5 us
    ppermute x8, starting transfers between devices, to_half(): return lax.ppermute(block, 'py', [(i, i ^ k) for i in range(groups)])  11.1 us
    pallas_call x1, Pallas kernels, shards(): call(functools.partial(pack_weights_kernel, groups, cap, blk, block_rows)...  6.87 us
    pallas_call x1, Pallas kernels, shards(): call(functools.partial(pack_products_kernel, groups, cap), (f32(2 * cap,...  6.71 us
    ppermute x4, starting transfers between devices, across(): lax.ppermute(parts[k], ('px', 'py'), [(i * groups + j, (i ^ k) * groups +...  6.64 us
    unnamed x32, local copies, waits for them, and re-layouts  6.45 us
    pallas_call x1, Pallas kernels, shards(): call(solve_kernel, (f32(F, nx, width),) * 2 + (f32(F, tiles, nx, SEG), f3...  5.72 us
  transfers between devices with their start and end apart: 15, of which 8 were waited for; matrix products, arithmetic and copies ran while one was open for 0% of the time, Pallas kernels for 17%

profile of v16, /device:TPU:0, one launch (start us, length us, event | category | flops | bytes accessed | tf_op | source)
XLA Modules:
  0.0 106.8 jit_solution(355140797573673268)
XLA Ops:
  0.6 6.9 %shard_map.104 = (f32[784,128]{1,0:T(8,128)}, f32[784,128]{1,0:T(8,128)}, f32[784,128]{1,0:T(8,128)}, f32[784,128]{1,0:T(8,128)}, s32[8,128]{1,0:T(8,128)}) custom-call(s32[8,128]{1,0:T(8,128)} %bitcast.19, s32[8,128]{1,0:T(8,128)} %bitcast.20, s32[8,128]{1,0:T(8,128)} %bitcast.21, f32[8,128]{1,0:T(8,128)} %bitcast.22, f32[1024,128]{1,0:T(8,128)} %w_hbm.3), custom_call_target="tpu_custom_call" | custom-call | flops 1 | bytes 1 | tf_op jit(solution)/shard_map/pallas_call | solution.py:567
  7.5 3.0 %collective-permute-start = (f32[784,128]{1,0:T(8,128)}, f32[784,128]{1,0:T(8,128)S(1)}, u32[]{:S(2)}, u32[]{:S(2)}) collective-permute-start(f32[784,128]{1,0:T(8,128)} %get-tuple-element.42), channel_id=1, source_target_pairs={{0,1},{1,0},{2,3},{3,2},{4,5},{5,4},{6,7},{7,6},{8,9},{9,8},{10,11... | collective-permute-start | bytes 1204232 | tf_op jit(solution)/shard_map/ppermute | solution.py:558
  10.5 1.6 %collective-permute-start.1 = (f32[784,128]{1,0:T(8,128)}, f32[784,128]{1,0:T(8,128)S(1)}, u32[]{:S(2)}, u32[]{:S(2)}) collective-permute-start(f32[784,128]{1,0:T(8,128)} %get-tuple-element.47), channel_id=1, source_target_pairs={{0,2},{1,3},{2,0},{3,1},{4,6},{5,7},{6,4},{7,5},{8,10},{9,11},{10,... | collective-permute-start | bytes 1204232 | tf_op jit(solution)/shard_map/ppermute | solution.py:558
  12.1 2.5 %shard_map.105 = f32[4,272,128]{2,1,0:T(8,128)} custom-call(s32[8,128]{1,0:T(8,128)} %get-tuple-element.39._.slot_ref, f32[16,2048]{1,0:T(8,128)} %bitcast.18, f32[2,64,512]{2,1,0:T(8,128)} %bitcast.13, f32[64,512]{1,0:T(8,128)} %bitcast.16), custom_call_target="tpu_custom_call" | custom-call | flops 1 | bytes 1 | tf_op jit(solution)/shard_map/pallas_call | solution.py:591
  14.6 3.5 %all-to-all-start = ((f32[4,272,128]{2,1,0:T(8,128)}), f32[4,272,128]{2,1,0:T(8,128)S(1)}, u32[]{:S(2)}, u32[]{:S(2)}) async-start(f32[4,272,128]{2,1,0:T(8,128)} %shard_map.105), calls=%async_computation | async-start | bytes 1114112 | tf_op jit(solution)/shard_map/all_to_all | solution.py:598
  18.1 6.7 %shard_map.107 = (f32[768,128]{1,0:T(8,128)}, f32[768,128]{1,0:T(8,128)}, f32[768,128]{1,0:T(8,128)}, f32[768,128]{1,0:T(8,128)}) custom-call(s32[8,128]{1,0:T(8,128)} %get-tuple-element.39._.slot_ref, f32[1024,128]{1,0:T(8,128)} %w_hbm.3, f32[1024,128]{1,0:T(8,128)} %d_hbm.1), custom_call_target="tpu_custom_call" | custom-call | flops 1 | bytes 1 | tf_op jit(solution)/shard_map/pallas_call | solution.py:579
  24.8 2.0 %collective-permute-start.5 = (f32[768,128]{1,0:T(8,128)}, f32[768,128]{1,0:T(8,128)S(1)}, u32[]{:S(2)}, u32[]{:S(2)}) collective-permute-start(f32[768,128]{1,0:T(8,128)} %get-tuple-element.56), channel_id=1, source_target_pairs={{0,1},{1,0},{2,3},{3,2},{4,5},{5,4},{6,7},{7,6},{8,9},{9,8},{10,11... | collective-permute-start | bytes 1179656 | tf_op jit(solution)/shard_map/ppermute | solution.py:558
  28.4 1.7 %collective-permute-done.2.rest_3_ = f32[784,128]{1,0:T(8,128)S(1)} collective-permute-done((f32[784,128]{1,0:T(8,128)}, f32[784,128]{1,0:T(8,128)S(1)}, u32[]{:S(2)}, u32[]{:S(2)}) %collective-permute-start.2) | collective-permute-done | bytes 401440 | tf_op jit(solution)/shard_map/ppermute | solution.py:558
  30.1 2.7 %shard_map.109 = (f32[4,16,128]{2,1,0:T(8,128)}, f32[512,128]{1,0:T(8,128)}, f32[512,128]{1,0:T(8,128)}) custom-call(f32[784,128]{1,0:T(8,128)S(1)} %copy-done, f32[784,128]{1,0:T(8,128)S(1)} %collective-permute-done.rest_1_, f32[784,128]{1,0:T(8,128)S(1)} %collective-permute-done.1.rest_2_, f32[784,128]{1,0:T(8,128)S(1)} %collective-permute-done.2.rest_3_, ...), custom_call_target="tpu_custom_call" | custom-call | flops 100000000 | bytes 100000000 | tf_op jit(solution)/shard_map/pallas_call | solution.py:608
  32.8 2.8 %collective-permute-start.3 = (f32[512,128]{1,0:T(8,128)}, f32[512,128]{1,0:T(8,128)S(1)}, u32[]{:S(2)}, u32[]{:S(2)}) collective-permute-start(f32[512,128]{1,0:T(8,128)} %get-tuple-element.53), channel_id=1, source_target_pairs={{0,4},{1,5},{2,6},{3,7},{4,0},{5,1},{6,2},{7,3},{8,12},{9,13},{10,... | collective-permute-start | bytes 786440 | tf_op jit(solution)/shard_map/ppermute | solution.py:558
  35.7 2.3 %shard_map.106 = (f32[2,5,64,128]{3,2,1,0:T(8,128)S(1)}, f32[5,64,128]{2,1,0:T(8,128)S(1)}, f32[5,64,128]{2,1,0:T(8,128)S(1)}, f32[2,5,64,128]{3,2,1,0:T(8,128)S(1)}, f32[8,128]{1,0:T(8,128)S(1)}) custom-call(f32[2,64,512]{2,1,0:T(8,128)S(1)} %bitcast.14, f32[64,512]{1,0:T(8,128)S(1)} %bitcast.17, f32[4,272,128]{2,1,0:T(8,128)S(1)} %all-to-all-done.swap_ref), custom_call_target="tpu_custom_call" | custom-call | flops 1 | bytes 1 | tf_op jit(solution)/shard_map/pallas_call | solution.py:599
  40.1 1.9 %shard_map.108 = (f32[4,16,128]{2,1,0:T(8,128)S(1)}, f32[512,128]{1,0:T(8,128)S(1)}, f32[512,128]{1,0:T(8,128)S(1)}) custom-call(f32[784,128]{1,0:T(8,128)S(1)} %copy-done, f32[784,128]{1,0:T(8,128)S(1)} %collective-permute-done.rest_1_, f32[784,128]{1,0:T(8,128)S(1)} %collective-permute-done.1.rest_2_, f32[784,128]{1,0:T(8,128)S(1)} %collective-permute-done.2.rest_3_, ...), custom_call_target="tpu_custom_call" | custom-call | flops 1 | bytes 1 | tf_op jit(solution)/shard_map/pallas_call | solution.py:608
  42.0 10.2 %collective-permute-done.3.far_d_ref = f32[512,128]{1,0:T(8,128)S(1)} collective-permute-done((f32[512,128]{1,0:T(8,128)}, f32[512,128]{1,0:T(8,128)S(1)}, u32[]{:S(2)}, u32[]{:S(2)}) %collective-permute-start.3) | collective-permute-done | bytes 262176 | tf_op jit(solution)/shard_map/ppermute | solution.py:558
  52.2 5.1 %collective-permute-done.4.far_e_ref = f32[512,128]{1,0:T(8,128)} collective-permute-done((f32[512,128]{1,0:T(8,128)}, f32[512,128]{1,0:T(8,128)}, u32[]{:S(2)}, u32[]{:S(2)}) %collective-permute-start.4) | collective-permute-done | bytes 262176 | tf_op jit(solution)/shard_map/ppermute | solution.py:558
  58.1 4.3 %shard_map.110 = (f32[4,6,5,16,128]{4,3,2,1,0:T(8,128)}, f32[8,128]{1,0:T(8,128)S(1)}, f32[2,5,16,128]{3,2,1,0:T(8,128)}, f32[2,5,16,128]{3,2,1,0:T(8,128)}, f32...) custom-call(f32[4,16,128]{2,1,0:T(8,128)S(1)} %get-tuple-element.50.meta_ref, f32[512,128]{1,0:T(8,128)S(1)} %get-tuple-element.51.d_ref, ...), custom_call_target="tpu_custom_call" | custom-call | flops 1 | bytes 1 | tf_op jit(solution)/shard_map/pallas_call | solution.py:618
  62.4 3.8 %all-to-all-start.1 = ((f32[4,6,5,16,128]{4,3,2,1,0:T(8,128)}), f32[4,6,5,16,128]{4,3,2,1,0:T(8,128)S(1)}, u32[]{:S(2)}, u32[]{:S(2)}) async-start(f32[4,6,5,16,128]{4,3,2,1,0:T(8,128)} %get-tuple-element.65), calls=%async_computation.1 | async-start | bytes 1966080 | tf_op jit(solution)/shard_map/all_to_all | solution.py:628
  66.2 2.8 %collective-permute-start.8 = (f32[2,5,16,128]{3,2,1,0:T(8,128)}, f32[2,5,16,128]{3,2,1,0:T(8,128)S(1)}, u32[]{:S(2)}, u32[]{:S(2)}) collective-permute-start(f32[2,5,16,128]{3,2,1,0:T(8,128)} %get-tuple-element.66), channel_id=1, source_target_pairs={{0,4},{1,5},{2,6},{3,7},{4,0},{5,1},{6,2},{7,3},{8,12},{9,13},{10,... | collective-permute-start | bytes 245768 | tf_op jit(solution)/shard_map/ppermute | solution.py:562
  69.0 3.6 %collective-permute-start.10 = (f32[2,5,16,128]{3,2,1,0:T(8,128)}, f32[2,5,16,128]{3,2,1,0:T(8,128)S(1)}, u32[]{:S(2)}, u32[]{:S(2)}) collective-permute-start(f32[2,5,16,128]{3,2,1,0:T(8,128)} %get-tuple-element.68), channel_id=1, source_target_pairs={{0,20},{1,21},{2,22},{3,23},{4,16},{5,17},{6,18},{7,19},{8,28},{9,... | collective-permute-start | bytes 245768 | tf_op jit(solution)/shard_map/ppermute | solution.py:562
  74.3 6.9 %collective-permute-done.9.rest_1_ = f32[2,5,16,128]{3,2,1,0:T(8,128)S(1)} collective-permute-done((f32[2,5,16,128]{3,2,1,0:T(8,128)}, f32[2,5,16,128]{3,2,1,0:T(8,128)S(1)}, u32[]{:S(2)}, u32[]{:S(2)}) %collective-permute-start.9) | collective-permute-done | bytes 81952 | tf_op jit(solution)/shard_map/ppermute | solution.py:562
  81.2 2.9 %collective-permute-done.10.rest_2_ = f32[2,5,16,128]{3,2,1,0:T(8,128)S(1)} collective-permute-done((f32[2,5,16,128]{3,2,1,0:T(8,128)}, f32[2,5,16,128]{3,2,1,0:T(8,128)S(1)}, u32[]{:S(2)}, u32[]{:S(2)}) %collective-permute-start.10) | collective-permute-done | bytes 81952 | tf_op jit(solution)/shard_map/ppermute | solution.py:562
  84.1 1.8 %collective-permute-done.11.rest_3_ = f32[2,5,16,128]{3,2,1,0:T(8,128)S(1)} collective-permute-done((f32[2,5,16,128]{3,2,1,0:T(8,128)}, f32[2,5,16,128]{3,2,1,0:T(8,128)S(1)}, u32[]{:S(2)}, u32[]{:S(2)}) %collective-permute-start.11) | collective-permute-done | bytes 81952 | tf_op jit(solution)/shard_map/ppermute | solution.py:562
  87.9 5.7 %shard_map.113 = (f32[2,64,512]{2,1,0:T(8,128)S(1)}, f32[2,64,512]{2,1,0:T(8,128)S(1)}, f32[2,5,64,128]{3,2,1,0:T(8,128)S(1)}, f32[32,1,128]{2,1,0:T(1,128)}) custom-call(f32[2,5,64,128]{3,2,1,0:T(8,128)S(1)} %copy-done.5, f32[5,5,64,128]{3,2,1,0:T(8,128)S(1)} %get-tuple-element.62.x_ref, f32[5,5,64,128]{3,2,1,0:T(8,128)S(1)} %get-tuple-element.63.y_ref, ...), custom_call_target="tpu_custom_call" | custom-call | flops 1 | bytes 1 | tf_op jit(solution)/shard_map/pallas_call | solution.py:630
  95.0 3.5 %all-to-all-start.2 = ((f32[32,1,128]{2,1,0:T(1,128)}), f32[32,1,128]{2,1,0:T(1,128)S(1)}, u32[]{:S(2)}, u32[]{:S(2)}) async-start(f32[32,1,128]{2,1,0:T(1,128)} %get-tuple-element.70), calls=%async_computation.2 | async-start | bytes 32768 | tf_op jit(solution)/shard_map/all_to_all | solution.py:635
  100.5 5.0 %all-to-all-done.2.dots_ref = f32[32,1,128]{2,1,0:T(1,128)S(1)} async-done(((f32[32,1,128]{2,1,0:T(1,128)}), f32[32,1,128]{2,1,0:T(1,128)S(1)}, u32[]{:S(2)}, u32[]{:S(2)}) %all-to-all-start.2) | async-done | bytes 16416 | tf_op jit(solution)/shard_map/all_to_all | solution.py:635
  (50 shorter events, 13.0 us)
Async XLA Ops:
  7.5 17.3 %collective-permute-start = (f32[784,128]{1,0:T(8,128)}, f32[784,128]{1,0:T(8,128)S(1)}, u32[]{:S(2)}, u32[]{:S(2)}) collective-permute-start(f32[784,128]{1,0:T(8,128)} %get-tuple-element.42), channel_id=1, source_target_pairs={{0,1},{1,0},{2,3},{3,2},{4,5},{5,4},{6,7},{7,6},{8,9},{9,8},{10,11... | collective-permute-start | bytes 1204232 | tf_op jit(solution)/shard_map/ppermute | solution.py:558
  10.5 17.9 %collective-permute-start.1 = (f32[784,128]{1,0:T(8,128)}, f32[784,128]{1,0:T(8,128)S(1)}, u32[]{:S(2)}, u32[]{:S(2)}) collective-permute-start(f32[784,128]{1,0:T(8,128)} %get-tuple-element.47), channel_id=1, source_target_pairs={{0,2},{1,3},{2,0},{3,1},{4,6},{5,7},{6,4},{7,5},{8,10},{9,11},{10,... | collective-permute-start | bytes 1204232 | tf_op jit(solution)/shard_map/ppermute | solution.py:558
  12.1 18.0 %collective-permute-start.2 = (f32[784,128]{1,0:T(8,128)}, f32[784,128]{1,0:T(8,128)S(1)}, u32[]{:S(2)}, u32[]{:S(2)}) collective-permute-start(f32[784,128]{1,0:T(8,128)} %get-tuple-element.48), channel_id=1, source_target_pairs={{0,3},{1,2},{2,1},{3,0},{4,7},{5,6},{6,5},{7,4},{8,11},{9,10},{10,... | collective-permute-start | bytes 1204232 | tf_op jit(solution)/shard_map/ppermute | solution.py:558
  14.6 21.1 %all-to-all-start = ((f32[4,272,128]{2,1,0:T(8,128)}), f32[4,272,128]{2,1,0:T(8,128)S(1)}, u32[]{:S(2)}, u32[]{:S(2)}) async-start(f32[4,272,128]{2,1,0:T(8,128)} %shard_map.105), calls=%async_computation | async-start | bytes 1114112 | tf_op jit(solution)/shard_map/all_to_all | solution.py:598
  18.1 12.0 %copy-start = (f32[784,128]{1,0:T(8,128)S(1)}, f32[784,128]{1,0:T(8,128)}, u32[]{:S(2)}) copy-start(f32[784,128]{1,0:T(8,128)} %get-tuple-element.41.rest_0_.rest_4_) | copy-start | bytes 1204228
  24.8 32.5 %collective-permute-start.5 = (f32[768,128]{1,0:T(8,128)}, f32[768,128]{1,0:T(8,128)S(1)}, u32[]{:S(2)}, u32[]{:S(2)}) collective-permute-start(f32[768,128]{1,0:T(8,128)} %get-tuple-element.56), channel_id=1, source_target_pairs={{0,1},{1,0},{2,3},{3,2},{4,5},{5,4},{6,7},{7,6},{8,9},{9,8},{10,11... | collective-permute-start | bytes 1179656 | tf_op jit(solution)/shard_map/ppermute | solution.py:558
  26.8 30.5 %collective-permute-start.6 = (f32[768,128]{1,0:T(8,128)}, f32[768,128]{1,0:T(8,128)}, u32[]{:S(2)}, u32[]{:S(2)}) collective-permute-start(f32[768,128]{1,0:T(8,128)} %get-tuple-element.57), channel_id=1, source_target_pairs={{0,2},{1,3},{2,0},{3,1},{4,6},{5,7},{6,4},{7,5},{8,10},{9,11},{10,... | collective-permute-start | bytes 1179656 | tf_op jit(solution)/shard_map/ppermute | solution.py:558
  28.4 29.7 %collective-permute-start.7 = (f32[768,128]{1,0:T(8,128)}, f32[768,128]{1,0:T(8,128)}, u32[]{:S(2)}, u32[]{:S(2)}) collective-permute-start(f32[768,128]{1,0:T(8,128)} %get-tuple-element.58), channel_id=1, source_target_pairs={{0,3},{1,2},{2,1},{3,0},{4,7},{5,6},{6,5},{7,4},{8,11},{9,10},{10,... | collective-permute-start | bytes 1179656 | tf_op jit(solution)/shard_map/ppermute | solution.py:558
  30.1 5.6 %copy-start.1 = (f32[2,1,64,512]{3,2,1,0:T(8,128)S(1)}, f32[2,1,64,512]{3,2,1,0:T(8,128)}, u32[]{:S(2)}) copy-start(f32[2,1,64,512]{3,2,1,0:T(8,128)} %param.9) | copy-start | bytes 786436
  30.1 5.6 %copy-start.2 = (f32[1,64,512]{2,1,0:T(8,128)S(1)}, f32[1,64,512]{2,1,0:T(8,128)}, u32[]{:S(2)}) copy-start(f32[1,64,512]{2,1,0:T(8,128)} %param.10) | copy-start | bytes 393220
  32.8 19.5 %collective-permute-start.3 = (f32[512,128]{1,0:T(8,128)}, f32[512,128]{1,0:T(8,128)S(1)}, u32[]{:S(2)}, u32[]{:S(2)}) collective-permute-start(f32[512,128]{1,0:T(8,128)} %get-tuple-element.53), channel_id=1, source_target_pairs={{0,4},{1,5},{2,6},{3,7},{4,0},{5,1},{6,2},{7,3},{8,12},{9,13},{10,... | collective-permute-start | bytes 786440 | tf_op jit(solution)/shard_map/ppermute | solution.py:558
  35.5 21.8 %collective-permute-start.4 = (f32[512,128]{1,0:T(8,128)}, f32[512,128]{1,0:T(8,128)}, u32[]{:S(2)}, u32[]{:S(2)}) collective-permute-start(f32[512,128]{1,0:T(8,128)} %get-tuple-element.54), channel_id=1, source_target_pairs={{0,4},{1,5},{2,6},{3,7},{4,0},{5,1},{6,2},{7,3},{8,12},{9,13},{10,... | collective-permute-start | bytes 786440 | tf_op jit(solution)/shard_map/ppermute | solution.py:558
  40.1 1.9 %copy-start.4 = (f32[2,5,64,128]{3,2,1,0:T(8,128)}, f32[2,5,64,128]{3,2,1,0:T(8,128)S(1)}, u32[]{:S(2)}) copy-start(f32[2,5,64,128]{3,2,1,0:T(8,128)S(1)} %get-tuple-element.40.c0_ref) | copy-start | bytes 983044
  40.1 18.0 %copy-start.3 = (f32[768,128]{1,0:T(8,128)S(1)}, f32[768,128]{1,0:T(8,128)}, u32[]{:S(2)}) copy-start(f32[768,128]{1,0:T(8,128)} %get-tuple-element.55.rest_0_) | copy-start | bytes 1179652
  62.4 10.5 %copy-start.13 = (f32[5,64,128]{2,1,0:T(8,128)S(1)}, f32[5,64,128]{2,1,0:T(8,128)}, u32[]{:S(2)}) copy-start(f32[5,64,128]{2,1,0:T(8,128)} %copy-done.12) | copy-start | bytes 491524
  62.4 10.5 %copy-start.15 = (f32[5,64,128]{2,1,0:T(8,128)S(1)}, f32[5,64,128]{2,1,0:T(8,128)}, u32[]{:S(2)}) copy-start(f32[5,64,128]{2,1,0:T(8,128)} %copy-done.14) | copy-start | bytes 491524
  62.4 23.5 %all-to-all-start.1 = ((f32[4,6,5,16,128]{4,3,2,1,0:T(8,128)}), f32[4,6,5,16,128]{4,3,2,1,0:T(8,128)S(1)}, u32[]{:S(2)}, u32[]{:S(2)}) async-start(f32[4,6,5,16,128]{4,3,2,1,0:T(8,128)} %get-tuple-element.65), calls=%async_computation.1 | async-start | bytes 1966080 | tf_op jit(solution)/shard_map/all_to_all | solution.py:628
  66.2 8.1 %collective-permute-start.8 = (f32[2,5,16,128]{3,2,1,0:T(8,128)}, f32[2,5,16,128]{3,2,1,0:T(8,128)S(1)}, u32[]{:S(2)}, u32[]{:S(2)}) collective-permute-start(f32[2,5,16,128]{3,2,1,0:T(8,128)} %get-tuple-element.66), channel_id=1, source_target_pairs={{0,4},{1,5},{2,6},{3,7},{4,0},{5,1},{6,2},{7,3},{8,12},{9,13},{10,... | collective-permute-start | bytes 245768 | tf_op jit(solution)/shard_map/ppermute | solution.py:562
  69.0 12.2 %collective-permute-start.9 = (f32[2,5,16,128]{3,2,1,0:T(8,128)}, f32[2,5,16,128]{3,2,1,0:T(8,128)S(1)}, u32[]{:S(2)}, u32[]{:S(2)}) collective-permute-start(f32[2,5,16,128]{3,2,1,0:T(8,128)} %get-tuple-element.67), channel_id=1, source_target_pairs={{0,12},{1,13},{2,14},{3,15},{4,8},{5,9},{6,10},{7,11},{8,4},{9,5},... | collective-permute-start | bytes 245768 | tf_op jit(solution)/shard_map/ppermute | solution.py:562
  69.0 15.1 %collective-permute-start.10 = (f32[2,5,16,128]{3,2,1,0:T(8,128)}, f32[2,5,16,128]{3,2,1,0:T(8,128)S(1)}, u32[]{:S(2)}, u32[]{:S(2)}) collective-permute-start(f32[2,5,16,128]{3,2,1,0:T(8,128)} %get-tuple-element.68), channel_id=1, source_target_pairs={{0,20},{1,21},{2,22},{3,23},{4,16},{5,17},{6,18},{7,19},{8,28},{9,... | collective-permute-start | bytes 245768 | tf_op jit(solution)/shard_map/ppermute | solution.py:562
  72.6 13.3 %collective-permute-start.11 = (f32[2,5,16,128]{3,2,1,0:T(8,128)}, f32[2,5,16,128]{3,2,1,0:T(8,128)S(1)}, u32[]{:S(2)}, u32[]{:S(2)}) collective-permute-start(f32[2,5,16,128]{3,2,1,0:T(8,128)} %get-tuple-element.69), channel_id=1, source_target_pairs={{0,28},{1,29},{2,30},{3,31},{4,24},{5,25},{6,26},{7,27},{8,20},{9,... | collective-permute-start | bytes 245768 | tf_op jit(solution)/shard_map/ppermute | solution.py:562
  85.9 1.0 copy-start.5
  95.0 10.5 %all-to-all-start.2 = ((f32[32,1,128]{2,1,0:T(1,128)}), f32[32,1,128]{2,1,0:T(1,128)S(1)}, u32[]{:S(2)}, u32[]{:S(2)}) async-start(f32[32,1,128]{2,1,0:T(1,128)} %get-tuple-element.70), calls=%async_computation.2 | async-start | bytes 32768 | tf_op jit(solution)/shard_map/all_to_all | solution.py:635
  99.5 6.1 %copy-start.11 = (f32[2,64,512]{2,1,0:T(8,128)S(1)}, f32[2,64,512]{2,1,0:T(8,128)}, u32[]{:S(2)}) copy-start(f32[2,64,512]{2,1,0:T(8,128)} %copy-done.10) | copy-start | bytes 786436
  (7 other events, 5.5 us)

commit v17 on v11

--- a/solution.py
+++ b/solution.py
@@ -533,7 +533,8 @@
         limit=PACK_BYTES,
     )(slots, obs_weight, innovation))
     w_blocks[1:] = [to_half(w_blocks[k], k) for k in range(1, half)]
-    w_blocks[1], *v_blocks[1:] = lax.optimization_barrier((w_blocks[1], *v_blocks[1:]))
+    lead = half // 2
+    w_blocks[lead], *v_blocks[1:] = lax.optimization_barrier((w_blocks[lead], *v_blocks[1:]))
     v_blocks[1:] = [to_half(v_blocks[k], k) for k in range(1, half)]
 
     swap = call(

time: 105 us -> 105 us (level)
  no operation moved by 1% of the time
where the time goes in v17:
time: 105 us
  waiting for transfers between devices  38 us (36%)
  Pallas kernels  37 us (35%)
  starting transfers between devices  28.2 us (27%)
    ppermute x8, waiting for transfers between devices, to_half(): return lax.ppermute(block, 'py', [(i, i ^ k) for i in range(groups)])  19.7 us
    ppermute x4, waiting for transfers between devices, across(): lax.ppermute(parts[k], ('px', 'py'), [(i * groups + j, (i ^ k) * groups +...  12.8 us
    ppermute x8, starting transfers between devices, to_half(): return lax.ppermute(block, 'py', [(i, i ^ k) for i in range(groups)])  11.1 us
    pallas_call x1, Pallas kernels, shards(): call(solve_kernel, (f32(F, nx, width),) * 2 + (f32(F, tiles, nx, SEG), f3...  7.52 us
    pallas_call x1, Pallas kernels, shards(): call(functools.partial(pack_weights_kernel, groups, cap, blk, block_rows)...  6.91 us
    pallas_call x1, Pallas kernels, shards(): call(functools.partial(pack_products_kernel, groups, cap), (f32(2 * cap,...  6.76 us
    ppermute x4, starting transfers between devices, across(): lax.ppermute(parts[k], ('px', 'py'), [(i * groups + j, (i ^ k) * groups +...  6.46 us
    all_to_all x1, waiting for transfers between devices, shards(): lax.all_to_all(dots, ('px', 'py'), split_axis=0, concat_axis=0, tiled=True)  5.46 us
  transfers between devices with their start and end apart: 15, of which 8 were waited for; matrix products, arithmetic and copies ran while one was open for 0% of the time, Pallas kernels for 16%

profile of v17, /device:TPU:0, one launch (start us, length us, event | category | flops | bytes accessed | tf_op | source)
XLA Modules:
  0.0 104.7 jit_solution(4446937773584705281)
XLA Ops:
  0.6 6.9 %shard_map.104 = (f32[784,128]{1,0:T(8,128)}, f32[784,128]{1,0:T(8,128)}, f32[784,128]{1,0:T(8,128)}, f32[784,128]{1,0:T(8,128)}, s32[8,128]{1,0:T(8,128)}) custom-call(s32[8,128]{1,0:T(8,128)} %bitcast.19, s32[8,128]{1,0:T(8,128)} %bitcast.20, s32[8,128]{1,0:T(8,128)} %bitcast.21, f32[8,128]{1,0:T(8,128)} %bitcast.22, f32[1024,128]{1,0:T(8,128)} %w_hbm.3), custom_call_target="tpu_custom_call" | custom-call | flops 1 | bytes 1 | tf_op jit(solution)/shard_map/pallas_call | solution.py:515
  7.5 3.1 %collective-permute-start.1 = (f32[784,128]{1,0:T(8,128)}, f32[784,128]{1,0:T(8,128)S(1)}, u32[]{:S(2)}, u32[]{:S(2)}) collective-permute-start(f32[784,128]{1,0:T(8,128)} %get-tuple-element.43), channel_id=1, source_target_pairs={{0,2},{1,3},{2,0},{3,1},{4,6},{5,7},{6,4},{7,5},{8,10},{9,11},{10,... | collective-permute-start | bytes 1204232 | tf_op jit(solution)/shard_map/ppermute | solution.py:506
  12.2 2.5 %shard_map.105 = f32[4,272,128]{2,1,0:T(8,128)} custom-call(s32[8,128]{1,0:T(8,128)} %get-tuple-element.36._.slot_ref, f32[16,2048]{1,0:T(8,128)} %bitcast.18, f32[2,64,512]{2,1,0:T(8,128)} %bitcast.13, f32[64,512]{1,0:T(8,128)} %bitcast.16), custom_call_target="tpu_custom_call" | custom-call | flops 1 | bytes 1 | tf_op jit(solution)/shard_map/pallas_call | solution.py:540
  14.7 3.5 %all-to-all-start = ((f32[4,272,128]{2,1,0:T(8,128)}), f32[4,272,128]{2,1,0:T(8,128)S(1)}, u32[]{:S(2)}, u32[]{:S(2)}) async-start(f32[4,272,128]{2,1,0:T(8,128)} %shard_map.105), calls=%async_computation | async-start | bytes 1114112 | tf_op jit(solution)/shard_map/all_to_all | solution.py:547
  18.2 6.8 %shard_map.107 = (f32[768,128]{1,0:T(8,128)}, f32[768,128]{1,0:T(8,128)}, f32[768,128]{1,0:T(8,128)}, f32[768,128]{1,0:T(8,128)}) custom-call(s32[8,128]{1,0:T(8,128)} %get-tuple-element.36._.slot_ref, f32[1024,128]{1,0:T(8,128)} %w_hbm.3, f32[1024,128]{1,0:T(8,128)} %d_hbm.1), custom_call_target="tpu_custom_call" | custom-call | flops 1 | bytes 1 | tf_op jit(solution)/shard_map/pallas_call | solution.py:527
  25.0 1.9 %collective-permute-start.5 = (f32[768,128]{1,0:T(8,128)}, f32[768,128]{1,0:T(8,128)S(1)}, u32[]{:S(2)}, u32[]{:S(2)}) collective-permute-start(f32[768,128]{1,0:T(8,128)} %get-tuple-element.56), channel_id=1, source_target_pairs={{0,1},{1,0},{2,3},{3,2},{4,5},{5,4},{6,7},{7,6},{8,9},{9,8},{10,11... | collective-permute-start | bytes 1179656 | tf_op jit(solution)/shard_map/ppermute | solution.py:506
  26.9 1.6 %collective-permute-start.6 = (f32[768,128]{1,0:T(8,128)}, f32[768,128]{1,0:T(8,128)}, u32[]{:S(2)}, u32[]{:S(2)}) collective-permute-start(f32[768,128]{1,0:T(8,128)} %get-tuple-element.57), channel_id=1, source_target_pairs={{0,2},{1,3},{2,0},{3,1},{4,6},{5,7},{6,4},{7,5},{8,10},{9,11},{10,... | collective-permute-start | bytes 1179656 | tf_op jit(solution)/shard_map/ppermute | solution.py:506
  28.6 2.1 %collective-permute-done.rest_1_ = f32[784,128]{1,0:T(8,128)S(1)} collective-permute-done((f32[784,128]{1,0:T(8,128)}, f32[784,128]{1,0:T(8,128)S(1)}, u32[]{:S(2)}, u32[]{:S(2)}) %collective-permute-start) | collective-permute-done | bytes 401440 | tf_op jit(solution)/shard_map/ppermute | solution.py:506
  30.7 2.7 %shard_map.109 = (f32[4,16,128]{2,1,0:T(8,128)}, f32[512,128]{1,0:T(8,128)}, f32[512,128]{1,0:T(8,128)}) custom-call(f32[784,128]{1,0:T(8,128)S(1)} %copy-done, f32[784,128]{1,0:T(8,128)S(1)} %collective-permute-done.rest_1_, f32[784,128]{1,0:T(8,128)S(1)} %collective-permute-done.1.rest_2_, f32[784,128]{1,0:T(8,128)S(1)} %collective-permute-done.2.rest_3_, ...), custom_call_target="tpu_custom_call" | custom-call | flops 100000000 | bytes 100000000 | tf_op jit(solution)/shard_map/pallas_call | solution.py:556
  33.3 2.4 %collective-permute-start.3 = (f32[512,128]{1,0:T(8,128)}, f32[512,128]{1,0:T(8,128)}, u32[]{:S(2)}, u32[]{:S(2)}) collective-permute-start(f32[512,128]{1,0:T(8,128)} %get-tuple-element.53), channel_id=1, source_target_pairs={{0,4},{1,5},{2,6},{3,7},{4,0},{5,1},{6,2},{7,3},{8,12},{9,13},{10,... | collective-permute-start | bytes 786440 | tf_op jit(solution)/shard_map/ppermute | solution.py:506
  38.6 1.9 %shard_map.108 = (f32[4,16,128]{2,1,0:T(8,128)S(1)}, f32[512,128]{1,0:T(8,128)S(1)}, f32[512,128]{1,0:T(8,128)S(1)}) custom-call(f32[784,128]{1,0:T(8,128)S(1)} %copy-done, f32[784,128]{1,0:T(8,128)S(1)} %collective-permute-done.rest_1_, f32[784,128]{1,0:T(8,128)S(1)} %collective-permute-done.1.rest_2_, f32[784,128]{1,0:T(8,128)S(1)} %collective-permute-done.2.rest_3_, ...), custom_call_target="tpu_custom_call" | custom-call | flops 1 | bytes 1 | tf_op jit(solution)/shard_map/pallas_call | solution.py:556
  40.5 11.8 %collective-permute-done.3.far_d_ref = f32[512,128]{1,0:T(8,128)} collective-permute-done((f32[512,128]{1,0:T(8,128)}, f32[512,128]{1,0:T(8,128)}, u32[]{:S(2)}, u32[]{:S(2)}) %collective-permute-start.3) | collective-permute-done | bytes 262176 | tf_op jit(solution)/shard_map/ppermute | solution.py:506
  52.3 4.9 %collective-permute-done.4.far_e_ref = f32[512,128]{1,0:T(8,128)} collective-permute-done((f32[512,128]{1,0:T(8,128)}, f32[512,128]{1,0:T(8,128)}, u32[]{:S(2)}, u32[]{:S(2)}) %collective-permute-start.4) | collective-permute-done | bytes 262176 | tf_op jit(solution)/shard_map/ppermute | solution.py:506
  58.1 4.4 %shard_map.110 = (f32[4,6,5,16,128]{4,3,2,1,0:T(8,128)}, f32[2,5,16,128]{3,2,1,0:T(8,128)S(1)}, f32[2,5,16,128]{3,2,1,0:T(8,128)S(1)}, f32[2,5,16,128]{3,2,1,0:T(8,128)S(1)}, f32[2,5,16,128]{3,2,1,0:T(8,128)S(1)}) custom-call(f32[4,16,128]{2,1,0:T(8,128)S(1)} %get-tuple-element.50.meta_ref, f32[512,128]{1,0:T(8,128)S(1)} %get-tuple-element.51.d_ref, ...), custom_call_target="tpu_custom_call" | custom-call | flops 1 | bytes 1 | tf_op jit(solution)/shard_map/pallas_call | solution.py:566
  62.5 3.7 %all-to-all-start.1 = ((f32[4,6,5,16,128]{4,3,2,1,0:T(8,128)}), f32[4,6,5,16,128]{4,3,2,1,0:T(8,128)S(1)}, u32[]{:S(2)}, u32[]{:S(2)}) async-start(f32[4,6,5,16,128]{4,3,2,1,0:T(8,128)} %get-tuple-element.59), calls=%async_computation.1 | async-start | bytes 1966080 | tf_op jit(solution)/shard_map/all_to_all | solution.py:574
  66.2 2.6 %collective-permute-start.8 = (f32[2,5,16,128]{3,2,1,0:T(8,128)S(1)}, f32[2,5,16,128]{3,2,1,0:T(8,128)S(1)}, u32[]{:S(2)}, u32[]{:S(2)}) collective-permute-start(f32[2,5,16,128]{3,2,1,0:T(8,128)S(1)} %get-tuple-element.60), channel_id=1, source_target_pairs={{0,4},{1,5},{2,6},{3,7},{4,0},{5,1},{6,2},{7,3},{8,12},{9,13},{10,... | collective-permute-start | bytes 245768 | tf_op jit(solution)/shard_map/ppermute | solution.py:510
  68.7 3.6 %collective-permute-start.10 = (f32[2,5,16,128]{3,2,1,0:T(8,128)S(1)}, f32[2,5,16,128]{3,2,1,0:T(8,128)S(1)}, u32[]{:S(2)}, u32[]{:S(2)}) collective-permute-start(f32[2,5,16,128]{3,2,1,0:T(8,128)S(1)} %get-tuple-element.62), channel_id=1, source_target_pairs={{0,20},{1,21},{2,22},{3,23},{4,16},{5,17},{6,18},{7,19},{8,28},{9,... | collective-permute-start | bytes 245768 | tf_op jit(solution)/shard_map/ppermute | solution.py:510
  72.6 8.2 %collective-permute-done.9.rest_1_ = f32[2,5,16,128]{3,2,1,0:T(8,128)S(1)} collective-permute-done((f32[2,5,16,128]{3,2,1,0:T(8,128)S(1)}, f32[2,5,16,128]{3,2,1,0:T(8,128)S(1)}, u32[]{:S(2)}, u32[]{:S(2)}) %collective-permute-start.9) | collective-permute-done | bytes 81952 | tf_op jit(solution)/shard_map/ppermute | solution.py:510
  80.8 2.9 %collective-permute-done.10.rest_2_ = f32[2,5,16,128]{3,2,1,0:T(8,128)S(1)} collective-permute-done((f32[2,5,16,128]{3,2,1,0:T(8,128)S(1)}, f32[2,5,16,128]{3,2,1,0:T(8,128)S(1)}, u32[]{:S(2)}, u32[]{:S(2)}) %collective-permute-start.10) | collective-permute-done | bytes 81952 | tf_op jit(solution)/shard_map/ppermute | solution.py:510
  83.7 1.8 %collective-permute-done.11.rest_3_ = f32[2,5,16,128]{3,2,1,0:T(8,128)S(1)} collective-permute-done((f32[2,5,16,128]{3,2,1,0:T(8,128)S(1)}, f32[2,5,16,128]{3,2,1,0:T(8,128)S(1)}, u32[]{:S(2)}, u32[]{:S(2)}) %collective-permute-start.11) | collective-permute-done | bytes 81952 | tf_op jit(solution)/shard_map/ppermute | solution.py:510
  85.5 7.5 %shard_map.112 = (f32[2,64,512]{2,1,0:T(8,128)S(1)}, f32[2,64,512]{2,1,0:T(8,128)S(1)}, f32[2,5,64,128]{3,2,1,0:T(8,128)S(1)}, f32[32,1,128]{2,1,0:T(1,128)}) custom-call(f32[2,5,64,128]{3,2,1,0:T(8,128)S(1)} %copy-done.5, f32[5,64,128]{2,1,0:T(8,128)S(1)} %get-tuple-element.38.cx_ref, f32[5,64,128]{2,1,0:T(8,128)S(1)} %get-tuple-element.39.cy_ref, ...), custom_call_target="tpu_custom_call" | custom-call | flops 1 | bytes 1 | tf_op jit(solution)/shard_map/pallas_call | solution.py:576
  93.0 3.4 %all-to-all-start.2 = ((f32[32,1,128]{2,1,0:T(1,128)}), f32[32,1,128]{2,1,0:T(1,128)S(1)}, u32[]{:S(2)}, u32[]{:S(2)}) async-start(f32[32,1,128]{2,1,0:T(1,128)} %get-tuple-element.64), calls=%async_computation.2 | async-start | bytes 32768 | tf_op jit(solution)/shard_map/all_to_all | solution.py:581
  96.4 1.6 %shard_map.113.qq_ref = f32[2,64,512]{2,1,0:T(8,128)S(1)} custom-call(f32[2,5,64,128]{3,2,1,0:T(8,128)S(1)} %get-tuple-element.67.h_ref, f32[2,64,512]{2,1,0:T(8,128)S(1)} %get-tuple-element.66.q_ref, f32[5,64,128]{2,1,0:T(8,128)S(1)} %get-tuple-element.38.cx_ref, f32[5,64,128]{2,1,0:T(8,128)S(1)} %get-tuple-element.39.cy_ref), custom_call_target="tpu_custom_call" | custom-call | flops 1 | bytes 1 | tf_op jit(solution)/shard_map/pallas_call | solution.py:582
  98.0 5.5 %all-to-all-done.2.dots_ref = f32[32,1,128]{2,1,0:T(1,128)S(1)} async-done(((f32[32,1,128]{2,1,0:T(1,128)}), f32[32,1,128]{2,1,0:T(1,128)S(1)}, u32[]{:S(2)}, u32[]{:S(2)}) %all-to-all-start.2) | async-done | bytes 16416 | tf_op jit(solution)/shard_map/all_to_all | solution.py:581
  (33 shorter events, 6.9 us)
Async XLA Ops:
  7.5 17.4 %collective-permute-start.1 = (f32[784,128]{1,0:T(8,128)}, f32[784,128]{1,0:T(8,128)S(1)}, u32[]{:S(2)}, u32[]{:S(2)}) collective-permute-start(f32[784,128]{1,0:T(8,128)} %get-tuple-element.43), channel_id=1, source_target_pairs={{0,2},{1,3},{2,0},{3,1},{4,6},{5,7},{6,4},{7,5},{8,10},{9,11},{10,... | collective-permute-start | bytes 1204232 | tf_op jit(solution)/shard_map/ppermute | solution.py:506
  10.6 20.0 %collective-permute-start = (f32[784,128]{1,0:T(8,128)}, f32[784,128]{1,0:T(8,128)S(1)}, u32[]{:S(2)}, u32[]{:S(2)}) collective-permute-start(f32[784,128]{1,0:T(8,128)} %get-tuple-element.42), channel_id=1, source_target_pairs={{0,1},{1,0},{2,3},{3,2},{4,5},{5,4},{6,7},{7,6},{8,9},{9,8},{10,11... | collective-permute-start | bytes 1204232 | tf_op jit(solution)/shard_map/ppermute | solution.py:506
  12.1 18.5 %collective-permute-start.2 = (f32[784,128]{1,0:T(8,128)}, f32[784,128]{1,0:T(8,128)S(1)}, u32[]{:S(2)}, u32[]{:S(2)}) collective-permute-start(f32[784,128]{1,0:T(8,128)} %get-tuple-element.48), channel_id=1, source_target_pairs={{0,3},{1,2},{2,1},{3,0},{4,7},{5,6},{6,5},{7,4},{8,11},{9,10},{10,... | collective-permute-start | bytes 1204232 | tf_op jit(solution)/shard_map/ppermute | solution.py:506
  14.7 21.6 %all-to-all-start = ((f32[4,272,128]{2,1,0:T(8,128)}), f32[4,272,128]{2,1,0:T(8,128)S(1)}, u32[]{:S(2)}, u32[]{:S(2)}) async-start(f32[4,272,128]{2,1,0:T(8,128)} %shard_map.105), calls=%async_computation | async-start | bytes 1114112 | tf_op jit(solution)/shard_map/all_to_all | solution.py:547
  18.2 12.4 %copy-start = (f32[784,128]{1,0:T(8,128)S(1)}, f32[784,128]{1,0:T(8,128)}, u32[]{:S(2)}) copy-start(f32[784,128]{1,0:T(8,128)} %get-tuple-element.41.rest_0_.rest_4_) | copy-start | bytes 1204228
  25.0 32.2 %collective-permute-start.5 = (f32[768,128]{1,0:T(8,128)}, f32[768,128]{1,0:T(8,128)S(1)}, u32[]{:S(2)}, u32[]{:S(2)}) collective-permute-start(f32[768,128]{1,0:T(8,128)} %get-tuple-element.56), channel_id=1, source_target_pairs={{0,1},{1,0},{2,3},{3,2},{4,5},{5,4},{6,7},{7,6},{8,9},{9,8},{10,11... | collective-permute-start | bytes 1179656 | tf_op jit(solution)/shard_map/ppermute | solution.py:506
  26.9 30.3 %collective-permute-start.6 = (f32[768,128]{1,0:T(8,128)}, f32[768,128]{1,0:T(8,128)}, u32[]{:S(2)}, u32[]{:S(2)}) collective-permute-start(f32[768,128]{1,0:T(8,128)} %get-tuple-element.57), channel_id=1, source_target_pairs={{0,2},{1,3},{2,0},{3,1},{4,6},{5,7},{6,4},{7,5},{8,10},{9,11},{10,... | collective-permute-start | bytes 1179656 | tf_op jit(solution)/shard_map/ppermute | solution.py:506
  28.5 29.6 %collective-permute-start.7 = (f32[768,128]{1,0:T(8,128)}, f32[768,128]{1,0:T(8,128)}, u32[]{:S(2)}, u32[]{:S(2)}) collective-permute-start(f32[768,128]{1,0:T(8,128)} %get-tuple-element.58), channel_id=1, source_target_pairs={{0,3},{1,2},{2,1},{3,0},{4,7},{5,6},{6,5},{7,4},{8,11},{9,10},{10,... | collective-permute-start | bytes 1179656 | tf_op jit(solution)/shard_map/ppermute | solution.py:506
  30.6 5.6 %copy-start.1 = (f32[2,1,64,512]{3,2,1,0:T(8,128)S(1)}, f32[2,1,64,512]{3,2,1,0:T(8,128)}, u32[]{:S(2)}) copy-start(f32[2,1,64,512]{3,2,1,0:T(8,128)} %param.9) | copy-start | bytes 786436
  30.6 5.6 %copy-start.2 = (f32[1,64,512]{2,1,0:T(8,128)S(1)}, f32[1,64,512]{2,1,0:T(8,128)}, u32[]{:S(2)}) copy-start(f32[1,64,512]{2,1,0:T(8,128)} %param.10) | copy-start | bytes 393220
  33.3 19.0 %collective-permute-start.3 = (f32[512,128]{1,0:T(8,128)}, f32[512,128]{1,0:T(8,128)}, u32[]{:S(2)}, u32[]{:S(2)}) collective-permute-start(f32[512,128]{1,0:T(8,128)} %get-tuple-element.53), channel_id=1, source_target_pairs={{0,4},{1,5},{2,6},{3,7},{4,0},{5,1},{6,2},{7,3},{8,12},{9,13},{10,... | collective-permute-start | bytes 786440 | tf_op jit(solution)/shard_map/ppermute | solution.py:506
  35.8 21.4 %collective-permute-start.4 = (f32[512,128]{1,0:T(8,128)}, f32[512,128]{1,0:T(8,128)}, u32[]{:S(2)}, u32[]{:S(2)}) collective-permute-start(f32[512,128]{1,0:T(8,128)} %get-tuple-element.54), channel_id=1, source_target_pairs={{0,4},{1,5},{2,6},{3,7},{4,0},{5,1},{6,2},{7,3},{8,12},{9,13},{10,... | collective-permute-start | bytes 786440 | tf_op jit(solution)/shard_map/ppermute | solution.py:506
  37.8 0.7 copy-start.6
  38.6 1.9 %copy-start.4 = (f32[2,5,64,128]{3,2,1,0:T(8,128)}, f32[2,5,64,128]{3,2,1,0:T(8,128)S(1)}, u32[]{:S(2)}) copy-start(f32[2,5,64,128]{3,2,1,0:T(8,128)S(1)} %get-tuple-element.37.c0_ref) | copy-start | bytes 983044
  38.6 19.5 %copy-start.3 = (f32[768,128]{1,0:T(8,128)S(1)}, f32[768,128]{1,0:T(8,128)}, u32[]{:S(2)}) copy-start(f32[768,128]{1,0:T(8,128)} %get-tuple-element.55.rest_0_) | copy-start | bytes 1179652
  62.5 23.0 %all-to-all-start.1 = ((f32[4,6,5,16,128]{4,3,2,1,0:T(8,128)}), f32[4,6,5,16,128]{4,3,2,1,0:T(8,128)S(1)}, u32[]{:S(2)}, u32[]{:S(2)}) async-start(f32[4,6,5,16,128]{4,3,2,1,0:T(8,128)} %get-tuple-element.59), calls=%async_computation.1 | async-start | bytes 1966080 | tf_op jit(solution)/shard_map/all_to_all | solution.py:574
  66.2 6.5 %collective-permute-start.8 = (f32[2,5,16,128]{3,2,1,0:T(8,128)S(1)}, f32[2,5,16,128]{3,2,1,0:T(8,128)S(1)}, u32[]{:S(2)}, u32[]{:S(2)}) collective-permute-start(f32[2,5,16,128]{3,2,1,0:T(8,128)S(1)} %get-tuple-element.60), channel_id=1, source_target_pairs={{0,4},{1,5},{2,6},{3,7},{4,0},{5,1},{6,2},{7,3},{8,12},{9,13},{10,... | collective-permute-start | bytes 245768 | tf_op jit(solution)/shard_map/ppermute | solution.py:510
  68.7 12.1 %collective-permute-start.9 = (f32[2,5,16,128]{3,2,1,0:T(8,128)S(1)}, f32[2,5,16,128]{3,2,1,0:T(8,128)S(1)}, u32[]{:S(2)}, u32[]{:S(2)}) collective-permute-start(f32[2,5,16,128]{3,2,1,0:T(8,128)S(1)} %get-tuple-element.61), channel_id=1, source_target_pairs={{0,12},{1,13},{2,14},{3,15},{4,8},{5,9},{6,10},{7,11},{8,4},{9,5},... | collective-permute-start | bytes 245768 | tf_op jit(solution)/shard_map/ppermute | solution.py:510
  68.7 14.9 %collective-permute-start.10 = (f32[2,5,16,128]{3,2,1,0:T(8,128)S(1)}, f32[2,5,16,128]{3,2,1,0:T(8,128)S(1)}, u32[]{:S(2)}, u32[]{:S(2)}) collective-permute-start(f32[2,5,16,128]{3,2,1,0:T(8,128)S(1)} %get-tuple-element.62), channel_id=1, source_target_pairs={{0,20},{1,21},{2,22},{3,23},{4,16},{5,17},{6,18},{7,19},{8,28},{9,... | collective-permute-start | bytes 245768 | tf_op jit(solution)/shard_map/ppermute | solution.py:510
  72.3 13.2 %copy-start.5 = (f32[2,5,64,128]{3,2,1,0:T(8,128)S(1)}, f32[2,5,64,128]{3,2,1,0:T(8,128)}, u32[]{:S(2)}) copy-start(f32[2,5,64,128]{3,2,1,0:T(8,128)} %copy-done.4) | copy-start | bytes 983044
  72.3 13.2 %copy-start.7 = (f32[2,5,64,128]{3,2,1,0:T(8,128)S(1)}, f32[2,5,64,128]{3,2,1,0:T(8,128)}, u32[]{:S(2)}) copy-start(f32[2,5,64,128]{3,2,1,0:T(8,128)} %copy-done.6) | copy-start | bytes 983044
  72.3 13.1 %collective-permute-start.11 = (f32[2,5,16,128]{3,2,1,0:T(8,128)S(1)}, f32[2,5,16,128]{3,2,1,0:T(8,128)S(1)}, u32[]{:S(2)}, u32[]{:S(2)}) collective-permute-start(f32[2,5,16,128]{3,2,1,0:T(8,128)S(1)} %get-tuple-element.63), channel_id=1, source_target_pairs={{0,28},{1,29},{2,30},{3,31},{4,24},{5,25},{6,26},{7,27},{8,20},{9,... | collective-permute-start | bytes 245768 | tf_op jit(solution)/shard_map/ppermute | solution.py:510
  93.0 10.5 %all-to-all-start.2 = ((f32[32,1,128]{2,1,0:T(1,128)}), f32[32,1,128]{2,1,0:T(1,128)S(1)}, u32[]{:S(2)}, u32[]{:S(2)}) async-start(f32[32,1,128]{2,1,0:T(1,128)} %get-tuple-element.64), calls=%async_computation.2 | async-start | bytes 32768 | tf_op jit(solution)/shard_map/all_to_all | solution.py:581

commit v18 on v17

--- a/solution.py
+++ b/solution.py
@@ -14,6 +14,7 @@
 LX = 16
 ROWS = F * NB * LX
 HALF = SEG // 2
+QUARTER = SEG // 4
 SPLIT = 16
 X_TILES = 2
 Y_LINES = 16
@@ -223,6 +224,27 @@
     to[per] = ends_tile(jnp.where(q > 0, before, 0.0), jnp.where(q < spans - 1, after, 0.0))
 
 
+def cut_far_part(rows_ref, to, q, spans):
+    per = (to.shape[0] - 1) // F
+
+    def tile(f, b):
+        start = pl.multiple_of((f * NB + b) * LX, LX)
+        return rows_ref[pl.ds(start, LX), :]
+
+    beside = []
+    for f in range(F):
+        for j in range(per):
+            to[f * per + j] = tile(f, q * per + j)
+        before = tile(f, jnp.maximum(q * per - 1, 0))
+        after = tile(f, jnp.minimum(q * per + per, NB - 1))
+        beside.append(ends_tile(jnp.where(q > 0, before, 0.0),
+                                jnp.where(q < spans - 1, after, 0.0)))
+    lane = iota((LX, SEG), 1)
+    inner = jnp.where(lane < HALF, pltpu.roll(beside[1], QUARTER, 1),
+                      pltpu.roll(beside[1], SEG - QUARTER, 1))
+    to[F * per] = jnp.where((lane >= QUARTER) & (lane < SEG - QUARTER), inner, beside[0])
+
+
 def weights_kernel(half, cap, blk, across, *rest):
     w_refs, (_, meta_out, diagonal_out, side_out, acc_ref) = rest[:half], rest[half:]
     nb = cap // blk
@@ -261,8 +283,7 @@
     sum_products(half, cap, blk, 1, meta_ref, v_refs, acc_ref, far_ref)
     me = lax.axis_index("px")
     for k, far_out in enumerate(far_outs):
-        for f in range(F):
-            cut_part(far_ref, far_out.at[f], f, me ^ k, spans)
+        cut_far_part(far_ref, far_out, me ^ k, spans)
     sum_products(half, cap, blk, 0, meta_ref, v_refs, acc_ref, sums_ref)
     side[0] = d_ref[...] + far_d_ref[...]
     side[1] = e_ref[...] + far_e_ref[...]
@@ -379,12 +400,18 @@
 
 def join_kernel(spans, *rest):
     parts, out = rest[:spans], rest[spans]
+    per = out.shape[1] - 1
+    lane = iota((LX, SEG), 1)
     me = lax.axis_index("px")
     for k, part in enumerate(parts):
         rows = pl.ds(pl.multiple_of((me ^ k) * LX, LX), LX)
         for f in range(F):
-            for t in range(out.shape[1]):
-                out[f, t, rows, :] = part[f, t]
+            for t in range(per):
+                out[f, t, rows, :] = part[f * per + t]
+        beside = part[F * per]
+        out[0, per, rows, :] = beside
+        out[1, per, rows, :] = jnp.where(lane < HALF, pltpu.roll(beside, SEG - QUARTER, 1),
+                                         pltpu.roll(beside, QUARTER, 1))
 
 
 def solve_kernel(c0_ref, cx_ref, cy_ref, u_ref, obs_ref, far_ref, r_out, q_out, h_out, dots_out,
@@ -565,7 +592,8 @@
     meta, *side = sum_weights(0, token, 1)
     parts, *sums_across = call(
         functools.partial(products_kernel, half, cap, blk),
-        (f32(spans, 3 * F, tiles, LX, SEG),) + (f32(F, tiles, LX, SEG),) * spans,
+        (f32(spans, 3 * F, tiles, LX, SEG),)
+        + (f32(F * (tiles - 1) + 1, LX, SEG),) * spans,
         [vmem(ROWS, 2 * SEG), vmem(ROWS, SEG), vmem(ROWS, SEG), vmem(2, ROWS, SEG)],
     )(meta, *side, *side_across, *v_blocks)
     far_sums = call(

time: 105 us -> 104 us (level)
  waiting for transfers between devices: 38 us -> 36.8 us
    ppermute x4, waiting for transfers between devices: 12.8 us -> 11.6 us  [across(): lax.ppermute(parts[k], ('px', 'py'), [(i * groups + j, (i ^ k) * groups +...]
where the time goes in v18:
time: 104 us
  Pallas kernels  37 us (36%)
  waiting for transfers between devices  36.8 us (35%)
  starting transfers between devices  28.3 us (27%)
    ppermute x8, waiting for transfers between devices, to_half(): return lax.ppermute(block, 'py', [(i, i ^ k) for i in range(groups)])  19.7 us
    ppermute x4, waiting for transfers between devices, across(): lax.ppermute(parts[k], ('px', 'py'), [(i * groups + j, (i ^ k) * groups +...  11.6 us
    ppermute x8, starting transfers between devices, to_half(): return lax.ppermute(block, 'py', [(i, i ^ k) for i in range(groups)])  11.1 us
    pallas_call x1, Pallas kernels, shards(): call(solve_kernel, (f32(F, nx, width),) * 2 + (f32(F, tiles, nx, SEG), f3...  7.48 us
    pallas_call x1, Pallas kernels, shards(): call(functools.partial(pack_weights_kernel, groups, cap, blk, block_rows)...  6.91 us
    pallas_call x1, Pallas kernels, shards(): call(functools.partial(pack_products_kernel, groups, cap), (f32(2 * cap,...  6.76 us
    ppermute x4, starting transfers between devices, across(): lax.ppermute(parts[k], ('px', 'py'), [(i * groups + j, (i ^ k) * groups +...  6.44 us
    all_to_all x1, waiting for transfers between devices, shards(): lax.all_to_all(dots, ('px', 'py'), split_axis=0, concat_axis=0, tiled=True)  5.46 us
  transfers between devices with their start and end apart: 15, of which 8 were waited for; matrix products, arithmetic and copies ran while one was open for 0% of the time, Pallas kernels for 16%

profile of v18, /device:TPU:0, one launch (start us, length us, event | category | flops | bytes accessed | tf_op | source)
XLA Modules:
  0.0 103.6 jit_solution(16081295177224867736)
XLA Ops:
  0.6 6.9 %shard_map.104 = (f32[784,128]{1,0:T(8,128)}, f32[784,128]{1,0:T(8,128)}, f32[784,128]{1,0:T(8,128)}, f32[784,128]{1,0:T(8,128)}, s32[8,128]{1,0:T(8,128)}) custom-call(s32[8,128]{1,0:T(8,128)} %bitcast.19, s32[8,128]{1,0:T(8,128)} %bitcast.20, s32[8,128]{1,0:T(8,128)} %bitcast.21, f32[8,128]{1,0:T(8,128)} %bitcast.22, f32[1024,128]{1,0:T(8,128)} %w_hbm.3), custom_call_target="tpu_custom_call" | custom-call | flops 1 | bytes 1 | tf_op jit(solution)/shard_map/pallas_call | solution.py:542
  7.5 3.1 %collective-permute-start.1 = (f32[784,128]{1,0:T(8,128)}, f32[784,128]{1,0:T(8,128)S(1)}, u32[]{:S(2)}, u32[]{:S(2)}) collective-permute-start(f32[784,128]{1,0:T(8,128)} %get-tuple-element.43), channel_id=1, source_target_pairs={{0,2},{1,3},{2,0},{3,1},{4,6},{5,7},{6,4},{7,5},{8,10},{9,11},{10,... | collective-permute-start | bytes 1204232 | tf_op jit(solution)/shard_map/ppermute | solution.py:533
  12.2 2.5 %shard_map.105 = f32[4,272,128]{2,1,0:T(8,128)} custom-call(s32[8,128]{1,0:T(8,128)} %get-tuple-element.36._.slot_ref, f32[16,2048]{1,0:T(8,128)} %bitcast.18, f32[2,64,512]{2,1,0:T(8,128)} %bitcast.13, f32[64,512]{1,0:T(8,128)} %bitcast.16), custom_call_target="tpu_custom_call" | custom-call | flops 1 | bytes 1 | tf_op jit(solution)/shard_map/pallas_call | solution.py:567
  14.7 3.5 %all-to-all-start = ((f32[4,272,128]{2,1,0:T(8,128)}), f32[4,272,128]{2,1,0:T(8,128)S(1)}, u32[]{:S(2)}, u32[]{:S(2)}) async-start(f32[4,272,128]{2,1,0:T(8,128)} %shard_map.105), calls=%async_computation | async-start | bytes 1114112 | tf_op jit(solution)/shard_map/all_to_all | solution.py:574
  18.2 6.8 %shard_map.107 = (f32[768,128]{1,0:T(8,128)}, f32[768,128]{1,0:T(8,128)}, f32[768,128]{1,0:T(8,128)}, f32[768,128]{1,0:T(8,128)}) custom-call(s32[8,128]{1,0:T(8,128)} %get-tuple-element.36._.slot_ref, f32[1024,128]{1,0:T(8,128)} %w_hbm.3, f32[1024,128]{1,0:T(8,128)} %d_hbm.1), custom_call_target="tpu_custom_call" | custom-call | flops 1 | bytes 1 | tf_op jit(solution)/shard_map/pallas_call | solution.py:554
  25.0 1.9 %collective-permute-start.5 = (f32[768,128]{1,0:T(8,128)}, f32[768,128]{1,0:T(8,128)S(1)}, u32[]{:S(2)}, u32[]{:S(2)}) collective-permute-start(f32[768,128]{1,0:T(8,128)} %get-tuple-element.56), channel_id=1, source_target_pairs={{0,1},{1,0},{2,3},{3,2},{4,5},{5,4},{6,7},{7,6},{8,9},{9,8},{10,11... | collective-permute-start | bytes 1179656 | tf_op jit(solution)/shard_map/ppermute | solution.py:533
  26.9 1.6 %collective-permute-start.6 = (f32[768,128]{1,0:T(8,128)}, f32[768,128]{1,0:T(8,128)}, u32[]{:S(2)}, u32[]{:S(2)}) collective-permute-start(f32[768,128]{1,0:T(8,128)} %get-tuple-element.57), channel_id=1, source_target_pairs={{0,2},{1,3},{2,0},{3,1},{4,6},{5,7},{6,4},{7,5},{8,10},{9,11},{10,... | collective-permute-start | bytes 1179656 | tf_op jit(solution)/shard_map/ppermute | solution.py:533
  28.6 2.1 %collective-permute-done.rest_1_ = f32[784,128]{1,0:T(8,128)S(1)} collective-permute-done((f32[784,128]{1,0:T(8,128)}, f32[784,128]{1,0:T(8,128)S(1)}, u32[]{:S(2)}, u32[]{:S(2)}) %collective-permute-start) | collective-permute-done | bytes 401440 | tf_op jit(solution)/shard_map/ppermute | solution.py:533
  30.7 2.7 %shard_map.109 = (f32[4,16,128]{2,1,0:T(8,128)}, f32[512,128]{1,0:T(8,128)}, f32[512,128]{1,0:T(8,128)}) custom-call(f32[784,128]{1,0:T(8,128)S(1)} %copy-done, f32[784,128]{1,0:T(8,128)S(1)} %collective-permute-done.rest_1_, f32[784,128]{1,0:T(8,128)S(1)} %collective-permute-done.1.rest_2_, f32[784,128]{1,0:T(8,128)S(1)} %collective-permute-done.2.rest_3_, ...), custom_call_target="tpu_custom_call" | custom-call | flops 100000000 | bytes 100000000 | tf_op jit(solution)/shard_map/pallas_call | solution.py:583
  33.3 2.4 %collective-permute-start.3 = (f32[512,128]{1,0:T(8,128)}, f32[512,128]{1,0:T(8,128)}, u32[]{:S(2)}, u32[]{:S(2)}) collective-permute-start(f32[512,128]{1,0:T(8,128)} %get-tuple-element.53), channel_id=1, source_target_pairs={{0,4},{1,5},{2,6},{3,7},{4,0},{5,1},{6,2},{7,3},{8,12},{9,13},{10,... | collective-permute-start | bytes 786440 | tf_op jit(solution)/shard_map/ppermute | solution.py:533
  38.5 1.9 %shard_map.108 = (f32[4,16,128]{2,1,0:T(8,128)S(1)}, f32[512,128]{1,0:T(8,128)S(1)}, f32[512,128]{1,0:T(8,128)S(1)}) custom-call(f32[784,128]{1,0:T(8,128)S(1)} %copy-done, f32[784,128]{1,0:T(8,128)S(1)} %collective-permute-done.rest_1_, f32[784,128]{1,0:T(8,128)S(1)} %collective-permute-done.1.rest_2_, f32[784,128]{1,0:T(8,128)S(1)} %collective-permute-done.2.rest_3_, ...), custom_call_target="tpu_custom_call" | custom-call | flops 1 | bytes 1 | tf_op jit(solution)/shard_map/pallas_call | solution.py:583
  40.5 11.9 %collective-permute-done.3.far_d_ref = f32[512,128]{1,0:T(8,128)} collective-permute-done((f32[512,128]{1,0:T(8,128)}, f32[512,128]{1,0:T(8,128)}, u32[]{:S(2)}, u32[]{:S(2)}) %collective-permute-start.3) | collective-permute-done | bytes 262176 | tf_op jit(solution)/shard_map/ppermute | solution.py:533
  52.3 4.9 %collective-permute-done.4.far_e_ref = f32[512,128]{1,0:T(8,128)} collective-permute-done((f32[512,128]{1,0:T(8,128)}, f32[512,128]{1,0:T(8,128)}, u32[]{:S(2)}, u32[]{:S(2)}) %collective-permute-start.4) | collective-permute-done | bytes 262176 | tf_op jit(solution)/shard_map/ppermute | solution.py:533
  58.1 4.3 %shard_map.110 = (f32[4,6,5,16,128]{4,3,2,1,0:T(8,128)}, f32[9,16,128]{2,1,0:T(8,128)S(1)}, f32[9,16,128]{2,1,0:T(8,128)S(1)}, f32[9,16,128]{2,1,0:T(8,128)S(1)}, f32[9,16,128]{2,1,0:T(8,128)S(1)}) custom-call(f32[4,16,128]{2,1,0:T(8,128)S(1)} %get-tuple-element.50.meta_ref, f32[512,128]{1,0:T(8,128)S(1)} %get-tuple-element.51.d_ref, ...), custom_call_target="tpu_custom_call" | custom-call | flops 1 | bytes 1 | tf_op jit(solution)/shard_map/pallas_call | solution.py:593
  62.4 3.8 %all-to-all-start.1 = ((f32[4,6,5,16,128]{4,3,2,1,0:T(8,128)}), f32[4,6,5,16,128]{4,3,2,1,0:T(8,128)S(1)}, u32[]{:S(2)}, u32[]{:S(2)}) async-start(f32[4,6,5,16,128]{4,3,2,1,0:T(8,128)} %get-tuple-element.59), calls=%async_computation.1 | async-start | bytes 1966080 | tf_op jit(solution)/shard_map/all_to_all | solution.py:602
  66.3 2.6 %collective-permute-start.8 = (f32[9,16,128]{2,1,0:T(8,128)S(1)}, f32[9,16,128]{2,1,0:T(8,128)S(1)}, u32[]{:S(2)}, u32[]{:S(2)}) collective-permute-start(f32[9,16,128]{2,1,0:T(8,128)S(1)} %get-tuple-element.60), channel_id=1, source_target_pairs={{0,4},{1,5},{2,6},{3,7},{4,0},{5,1},{6,2},{7,3},{8,12},{9,13},{10,... | collective-permute-start | bytes 221192 | tf_op jit(solution)/shard_map/ppermute | solution.py:537
  68.9 3.6 %collective-permute-start.10 = (f32[9,16,128]{2,1,0:T(8,128)S(1)}, f32[9,16,128]{2,1,0:T(8,128)S(1)}, u32[]{:S(2)}, u32[]{:S(2)}) collective-permute-start(f32[9,16,128]{2,1,0:T(8,128)S(1)} %get-tuple-element.62), channel_id=1, source_target_pairs={{0,20},{1,21},{2,22},{3,23},{4,16},{5,17},{6,18},{7,19},{8,28},{9,... | collective-permute-start | bytes 221192 | tf_op jit(solution)/shard_map/ppermute | solution.py:537
  72.7 7.3 %collective-permute-done.9.rest_1_ = f32[9,16,128]{2,1,0:T(8,128)S(1)} collective-permute-done((f32[9,16,128]{2,1,0:T(8,128)S(1)}, f32[9,16,128]{2,1,0:T(8,128)S(1)}, u32[]{:S(2)}, u32[]{:S(2)}) %collective-permute-start.9) | collective-permute-done | bytes 73760 | tf_op jit(solution)/shard_map/ppermute | solution.py:537
  80.0 2.7 %collective-permute-done.10.rest_2_ = f32[9,16,128]{2,1,0:T(8,128)S(1)} collective-permute-done((f32[9,16,128]{2,1,0:T(8,128)S(1)}, f32[9,16,128]{2,1,0:T(8,128)S(1)}, u32[]{:S(2)}, u32[]{:S(2)}) %collective-permute-start.10) | collective-permute-done | bytes 73760 | tf_op jit(solution)/shard_map/ppermute | solution.py:537
  82.7 1.6 %collective-permute-done.11.rest_3_ = f32[9,16,128]{2,1,0:T(8,128)S(1)} collective-permute-done((f32[9,16,128]{2,1,0:T(8,128)S(1)}, f32[9,16,128]{2,1,0:T(8,128)S(1)}, u32[]{:S(2)}, u32[]{:S(2)}) %collective-permute-start.11) | collective-permute-done | bytes 73760 | tf_op jit(solution)/shard_map/ppermute | solution.py:537
  84.4 7.5 %shard_map.112 = (f32[2,64,512]{2,1,0:T(8,128)S(1)}, f32[2,64,512]{2,1,0:T(8,128)S(1)}, f32[2,5,64,128]{3,2,1,0:T(8,128)S(1)}, f32[32,1,128]{2,1,0:T(1,128)}) custom-call(f32[2,5,64,128]{3,2,1,0:T(8,128)S(1)} %copy-done.5, f32[5,64,128]{2,1,0:T(8,128)S(1)} %get-tuple-element.38.cx_ref, f32[5,64,128]{2,1,0:T(8,128)S(1)} %get-tuple-element.39.cy_ref, ...), custom_call_target="tpu_custom_call" | custom-call | flops 1 | bytes 1 | tf_op jit(solution)/shard_map/pallas_call | solution.py:604
  91.9 3.4 %all-to-all-start.2 = ((f32[32,1,128]{2,1,0:T(1,128)}), f32[32,1,128]{2,1,0:T(1,128)S(1)}, u32[]{:S(2)}, u32[]{:S(2)}) async-start(f32[32,1,128]{2,1,0:T(1,128)} %get-tuple-element.64), calls=%async_computation.2 | async-start | bytes 32768 | tf_op jit(solution)/shard_map/all_to_all | solution.py:609
  95.3 1.6 %shard_map.113.qq_ref = f32[2,64,512]{2,1,0:T(8,128)S(1)} custom-call(f32[2,5,64,128]{3,2,1,0:T(8,128)S(1)} %get-tuple-element.67.h_ref, f32[2,64,512]{2,1,0:T(8,128)S(1)} %get-tuple-element.66.q_ref, f32[5,64,128]{2,1,0:T(8,128)S(1)} %get-tuple-element.38.cx_ref, f32[5,64,128]{2,1,0:T(8,128)S(1)} %get-tuple-element.39.cy_ref), custom_call_target="tpu_custom_call" | custom-call | flops 1 | bytes 1 | tf_op jit(solution)/shard_map/pallas_call | solution.py:610
  96.9 5.5 %all-to-all-done.2.dots_ref = f32[32,1,128]{2,1,0:T(1,128)S(1)} async-done(((f32[32,1,128]{2,1,0:T(1,128)}), f32[32,1,128]{2,1,0:T(1,128)S(1)}, u32[]{:S(2)}, u32[]{:S(2)}) %all-to-all-start.2) | async-done | bytes 16416 | tf_op jit(solution)/shard_map/all_to_all | solution.py:609
  (33 shorter events, 6.9 us)
Async XLA Ops:
  7.5 17.4 %collective-permute-start.1 = (f32[784,128]{1,0:T(8,128)}, f32[784,128]{1,0:T(8,128)S(1)}, u32[]{:S(2)}, u32[]{:S(2)}) collective-permute-start(f32[784,128]{1,0:T(8,128)} %get-tuple-element.43), channel_id=1, source_target_pairs={{0,2},{1,3},{2,0},{3,1},{4,6},{5,7},{6,4},{7,5},{8,10},{9,11},{10,... | collective-permute-start | bytes 1204232 | tf_op jit(solution)/shard_map/ppermute | solution.py:533
  10.6 20.0 %collective-permute-start = (f32[784,128]{1,0:T(8,128)}, f32[784,128]{1,0:T(8,128)S(1)}, u32[]{:S(2)}, u32[]{:S(2)}) collective-permute-start(f32[784,128]{1,0:T(8,128)} %get-tuple-element.42), channel_id=1, source_target_pairs={{0,1},{1,0},{2,3},{3,2},{4,5},{5,4},{6,7},{7,6},{8,9},{9,8},{10,11... | collective-permute-start | bytes 1204232 | tf_op jit(solution)/shard_map/ppermute | solution.py:533
  12.1 18.5 %collective-permute-start.2 = (f32[784,128]{1,0:T(8,128)}, f32[784,128]{1,0:T(8,128)S(1)}, u32[]{:S(2)}, u32[]{:S(2)}) collective-permute-start(f32[784,128]{1,0:T(8,128)} %get-tuple-element.48), channel_id=1, source_target_pairs={{0,3},{1,2},{2,1},{3,0},{4,7},{5,6},{6,5},{7,4},{8,11},{9,10},{10,... | collective-permute-start | bytes 1204232 | tf_op jit(solution)/shard_map/ppermute | solution.py:533
  14.7 21.6 %all-to-all-start = ((f32[4,272,128]{2,1,0:T(8,128)}), f32[4,272,128]{2,1,0:T(8,128)S(1)}, u32[]{:S(2)}, u32[]{:S(2)}) async-start(f32[4,272,128]{2,1,0:T(8,128)} %shard_map.105), calls=%async_computation | async-start | bytes 1114112 | tf_op jit(solution)/shard_map/all_to_all | solution.py:574
  18.2 12.4 %copy-start = (f32[784,128]{1,0:T(8,128)S(1)}, f32[784,128]{1,0:T(8,128)}, u32[]{:S(2)}) copy-start(f32[784,128]{1,0:T(8,128)} %get-tuple-element.41.rest_0_.rest_4_) | copy-start | bytes 1204228
  25.0 32.2 %collective-permute-start.5 = (f32[768,128]{1,0:T(8,128)}, f32[768,128]{1,0:T(8,128)S(1)}, u32[]{:S(2)}, u32[]{:S(2)}) collective-permute-start(f32[768,128]{1,0:T(8,128)} %get-tuple-element.56), channel_id=1, source_target_pairs={{0,1},{1,0},{2,3},{3,2},{4,5},{5,4},{6,7},{7,6},{8,9},{9,8},{10,11... | collective-permute-start | bytes 1179656 | tf_op jit(solution)/shard_map/ppermute | solution.py:533
  26.9 30.3 %collective-permute-start.6 = (f32[768,128]{1,0:T(8,128)}, f32[768,128]{1,0:T(8,128)}, u32[]{:S(2)}, u32[]{:S(2)}) collective-permute-start(f32[768,128]{1,0:T(8,128)} %get-tuple-element.57), channel_id=1, source_target_pairs={{0,2},{1,3},{2,0},{3,1},{4,6},{5,7},{6,4},{7,5},{8,10},{9,11},{10,... | collective-permute-start | bytes 1179656 | tf_op jit(solution)/shard_map/ppermute | solution.py:533
  28.5 29.6 %collective-permute-start.7 = (f32[768,128]{1,0:T(8,128)}, f32[768,128]{1,0:T(8,128)}, u32[]{:S(2)}, u32[]{:S(2)}) collective-permute-start(f32[768,128]{1,0:T(8,128)} %get-tuple-element.58), channel_id=1, source_target_pairs={{0,3},{1,2},{2,1},{3,0},{4,7},{5,6},{6,5},{7,4},{8,11},{9,10},{10,... | collective-permute-start | bytes 1179656 | tf_op jit(solution)/shard_map/ppermute | solution.py:533
  30.6 5.6 %copy-start.1 = (f32[2,1,64,512]{3,2,1,0:T(8,128)S(1)}, f32[2,1,64,512]{3,2,1,0:T(8,128)}, u32[]{:S(2)}) copy-start(f32[2,1,64,512]{3,2,1,0:T(8,128)} %param.9) | copy-start | bytes 786436
  30.6 5.6 %copy-start.2 = (f32[1,64,512]{2,1,0:T(8,128)S(1)}, f32[1,64,512]{2,1,0:T(8,128)}, u32[]{:S(2)}) copy-start(f32[1,64,512]{2,1,0:T(8,128)} %param.10) | copy-start | bytes 393220
  33.3 19.0 %collective-permute-start.3 = (f32[512,128]{1,0:T(8,128)}, f32[512,128]{1,0:T(8,128)}, u32[]{:S(2)}, u32[]{:S(2)}) collective-permute-start(f32[512,128]{1,0:T(8,128)} %get-tuple-element.53), channel_id=1, source_target_pairs={{0,4},{1,5},{2,6},{3,7},{4,0},{5,1},{6,2},{7,3},{8,12},{9,13},{10,... | collective-permute-start | bytes 786440 | tf_op jit(solution)/shard_map/ppermute | solution.py:533
  35.8 21.4 %collective-permute-start.4 = (f32[512,128]{1,0:T(8,128)}, f32[512,128]{1,0:T(8,128)}, u32[]{:S(2)}, u32[]{:S(2)}) collective-permute-start(f32[512,128]{1,0:T(8,128)} %get-tuple-element.54), channel_id=1, source_target_pairs={{0,4},{1,5},{2,6},{3,7},{4,0},{5,1},{6,2},{7,3},{8,12},{9,13},{10,... | collective-permute-start | bytes 786440 | tf_op jit(solution)/shard_map/ppermute | solution.py:533
  37.8 0.7 copy-start.6
  38.5 1.9 %copy-start.4 = (f32[2,5,64,128]{3,2,1,0:T(8,128)}, f32[2,5,64,128]{3,2,1,0:T(8,128)S(1)}, u32[]{:S(2)}) copy-start(f32[2,5,64,128]{3,2,1,0:T(8,128)S(1)} %get-tuple-element.37.c0_ref) | copy-start | bytes 983044
  38.5 19.5 %copy-start.3 = (f32[768,128]{1,0:T(8,128)S(1)}, f32[768,128]{1,0:T(8,128)}, u32[]{:S(2)}) copy-start(f32[768,128]{1,0:T(8,128)} %get-tuple-element.55.rest_0_) | copy-start | bytes 1179652
  62.4 22.0 %copy-start.7 = (f32[2,5,64,128]{3,2,1,0:T(8,128)S(1)}, f32[2,5,64,128]{3,2,1,0:T(8,128)}, u32[]{:S(2)}) copy-start(f32[2,5,64,128]{3,2,1,0:T(8,128)} %copy-done.6) | copy-start | bytes 983044
  62.4 22.0 %all-to-all-start.1 = ((f32[4,6,5,16,128]{4,3,2,1,0:T(8,128)}), f32[4,6,5,16,128]{4,3,2,1,0:T(8,128)S(1)}, u32[]{:S(2)}, u32[]{:S(2)}) async-start(f32[4,6,5,16,128]{4,3,2,1,0:T(8,128)} %get-tuple-element.59), calls=%async_computation.1 | async-start | bytes 1966080 | tf_op jit(solution)/shard_map/all_to_all | solution.py:602
  66.3 18.2 %copy-start.5 = (f32[2,5,64,128]{3,2,1,0:T(8,128)S(1)}, f32[2,5,64,128]{3,2,1,0:T(8,128)}, u32[]{:S(2)}) copy-start(f32[2,5,64,128]{3,2,1,0:T(8,128)} %copy-done.4) | copy-start | bytes 983044
  66.3 6.4 %collective-permute-start.8 = (f32[9,16,128]{2,1,0:T(8,128)S(1)}, f32[9,16,128]{2,1,0:T(8,128)S(1)}, u32[]{:S(2)}, u32[]{:S(2)}) collective-permute-start(f32[9,16,128]{2,1,0:T(8,128)S(1)} %get-tuple-element.60), channel_id=1, source_target_pairs={{0,4},{1,5},{2,6},{3,7},{4,0},{5,1},{6,2},{7,3},{8,12},{9,13},{10,... | collective-permute-start | bytes 221192 | tf_op jit(solution)/shard_map/ppermute | solution.py:537
  68.8 11.2 %collective-permute-start.9 = (f32[9,16,128]{2,1,0:T(8,128)S(1)}, f32[9,16,128]{2,1,0:T(8,128)S(1)}, u32[]{:S(2)}, u32[]{:S(2)}) collective-permute-start(f32[9,16,128]{2,1,0:T(8,128)S(1)} %get-tuple-element.61), channel_id=1, source_target_pairs={{0,12},{1,13},{2,14},{3,15},{4,8},{5,9},{6,10},{7,11},{8,4},{9,5},... | collective-permute-start | bytes 221192 | tf_op jit(solution)/shard_map/ppermute | solution.py:537
  68.9 13.9 %collective-permute-start.10 = (f32[9,16,128]{2,1,0:T(8,128)S(1)}, f32[9,16,128]{2,1,0:T(8,128)S(1)}, u32[]{:S(2)}, u32[]{:S(2)}) collective-permute-start(f32[9,16,128]{2,1,0:T(8,128)S(1)} %get-tuple-element.62), channel_id=1, source_target_pairs={{0,20},{1,21},{2,22},{3,23},{4,16},{5,17},{6,18},{7,19},{8,28},{9,... | collective-permute-start | bytes 221192 | tf_op jit(solution)/shard_map/ppermute | solution.py:537
  72.4 11.9 %collective-permute-start.11 = (f32[9,16,128]{2,1,0:T(8,128)S(1)}, f32[9,16,128]{2,1,0:T(8,128)S(1)}, u32[]{:S(2)}, u32[]{:S(2)}) collective-permute-start(f32[9,16,128]{2,1,0:T(8,128)S(1)} %get-tuple-element.63), channel_id=1, source_target_pairs={{0,28},{1,29},{2,30},{3,31},{4,24},{5,25},{6,26},{7,27},{8,20},{9,... | collective-permute-start | bytes 221192 | tf_op jit(solution)/shard_map/ppermute | solution.py:537
  91.9 10.5 %all-to-all-start.2 = ((f32[32,1,128]{2,1,0:T(1,128)}), f32[32,1,128]{2,1,0:T(1,128)S(1)}, u32[]{:S(2)}, u32[]{:S(2)}) async-start(f32[32,1,128]{2,1,0:T(1,128)} %get-tuple-element.64), calls=%async_computation.2 | async-start | bytes 32768 | tf_op jit(solution)/shard_map/all_to_all | solution.py:609

commit v19 on v18

--- a/solution.py
+++ b/solution.py
@@ -16,8 +16,8 @@
 HALF = SEG // 2
 QUARTER = SEG // 4
 SPLIT = 16
-X_TILES = 2
-Y_LINES = 16
+X_TILES = 1
+Y_LINES = 8
 VMEM_BYTES = 32 * 1024 * 1024
 PACK_BYTES = 60 * 1024 * 1024
 FIRST = 100_000_000

time: 104 us -> 107 us (1.029)
  Pallas kernels: 37 us -> 40.4 us
    pallas_call x1, Pallas kernels: 7.48 us -> 10.2 us  [shards(): call(solve_kernel, (f32(F, nx, width),) * 2 + (f32(F, tiles, nx, SEG), f3...]
  transfers between devices with their start and end apart: 15 -> 15, of which waited for: 8 -> 8; matrix products, arithmetic and copies ran while one was open for 0% -> 0% of each run, Pallas kernels for 16% -> 17%
where the time goes in v19:
time: 107 us; the launch traced here: 106 us
  Pallas kernels  40.4 us (38%)
  waiting for transfers between devices  36.1 us (34%)
  starting transfers between devices  28.3 us (26%)
    ppermute x8, waiting for transfers between devices, to_half(): return lax.ppermute(block, 'py', [(i, i ^ k) for i in range(groups)])  19.4 us
    ppermute x4, waiting for transfers between devices, across(): lax.ppermute(parts[k], ('px', 'py'), [(i * groups + j, (i ^ k) * groups +...  11.6 us
    ppermute x8, starting transfers between devices, to_half(): return lax.ppermute(block, 'py', [(i, i ^ k) for i in range(groups)])  11.1 us
    pallas_call x1, Pallas kernels, shards(): call(solve_kernel, (f32(F, nx, width),) * 2 + (f32(F, tiles, nx, SEG), f3...  10.2 us
    pallas_call x1, Pallas kernels, shards(): call(functools.partial(pack_weights_kernel, groups, cap, blk, block_rows)...  6.91 us
    pallas_call x1, Pallas kernels, shards(): call(functools.partial(pack_products_kernel, groups, cap), (f32(2 * cap,...  6.76 us
    ppermute x4, starting transfers between devices, across(): lax.ppermute(parts[k], ('px', 'py'), [(i * groups + j, (i ^ k) * groups +...  6.44 us
    all_to_all x1, waiting for transfers between devices, shards(): lax.all_to_all(dots, ('px', 'py'), split_axis=0, concat_axis=0, tiled=True)  5.1 us
  transfers between devices with their start and end apart: 15, of which 8 were waited for; matrix products, arithmetic and copies ran while one was open for 0% of the time, Pallas kernels for 17%

profile of v19, /device:TPU:0, one launch (start us, length us, event | category | flops | bytes accessed | tf_op | source)
XLA Modules:
  0.0 106.3 jit_solution(13680726807137030913)
XLA Ops:
  0.6 6.9 %shard_map.104 = (f32[784,128]{1,0:T(8,128)}, f32[784,128]{1,0:T(8,128)}, f32[784,128]{1,0:T(8,128)}, f32[784,128]{1,0:T(8,128)}, s32[8,128]{1,0:T(8,128)}) custom-call(s32[8,128]{1,0:T(8,128)} %bitcast.19, s32[8,128]{1,0:T(8,128)} %bitcast.20, s32[8,128]{1,0:T(8,128)} %bitcast.21, f32[8,128]{1,0:T(8,128)} %bitcast.22, f32[1024,128]{1,0:T(8,128)} %w_hbm.3), custom_call_target="tpu_custom_call" | custom-call | flops 1 | bytes 1 | tf_op jit(solution)/shard_map/pallas_call | solution.py:542
  7.5 3.1 %collective-permute-start.1 = (f32[784,128]{1,0:T(8,128)}, f32[784,128]{1,0:T(8,128)S(1)}, u32[]{:S(2)}, u32[]{:S(2)}) collective-permute-start(f32[784,128]{1,0:T(8,128)} %get-tuple-element.43), channel_id=1, source_target_pairs={{0,2},{1,3},{2,0},{3,1},{4,6},{5,7},{6,4},{7,5},{8,10},{9,11},{10,... | collective-permute-start | bytes 1204232 | tf_op jit(solution)/shard_map/ppermute | solution.py:533
  12.2 2.5 %shard_map.105 = f32[4,272,128]{2,1,0:T(8,128)} custom-call(s32[8,128]{1,0:T(8,128)} %get-tuple-element.36._.slot_ref, f32[16,2048]{1,0:T(8,128)} %bitcast.18, f32[2,64,512]{2,1,0:T(8,128)} %bitcast.13, f32[64,512]{1,0:T(8,128)} %bitcast.16), custom_call_target="tpu_custom_call" | custom-call | flops 1 | bytes 1 | tf_op jit(solution)/shard_map/pallas_call | solution.py:567
  14.7 3.5 %all-to-all-start = ((f32[4,272,128]{2,1,0:T(8,128)}), f32[4,272,128]{2,1,0:T(8,128)S(1)}, u32[]{:S(2)}, u32[]{:S(2)}) async-start(f32[4,272,128]{2,1,0:T(8,128)} %shard_map.105), calls=%async_computation | async-start | bytes 1114112 | tf_op jit(solution)/shard_map/all_to_all | solution.py:574
  18.2 6.8 %shard_map.107 = (f32[768,128]{1,0:T(8,128)}, f32[768,128]{1,0:T(8,128)}, f32[768,128]{1,0:T(8,128)}, f32[768,128]{1,0:T(8,128)}) custom-call(s32[8,128]{1,0:T(8,128)} %get-tuple-element.36._.slot_ref, f32[1024,128]{1,0:T(8,128)} %w_hbm.3, f32[1024,128]{1,0:T(8,128)} %d_hbm.1), custom_call_target="tpu_custom_call" | custom-call | flops 1 | bytes 1 | tf_op jit(solution)/shard_map/pallas_call | solution.py:554
  25.0 1.9 %collective-permute-start.5 = (f32[768,128]{1,0:T(8,128)}, f32[768,128]{1,0:T(8,128)S(1)}, u32[]{:S(2)}, u32[]{:S(2)}) collective-permute-start(f32[768,128]{1,0:T(8,128)} %get-tuple-element.56), channel_id=1, source_target_pairs={{0,1},{1,0},{2,3},{3,2},{4,5},{5,4},{6,7},{7,6},{8,9},{9,8},{10,11... | collective-permute-start | bytes 1179656 | tf_op jit(solution)/shard_map/ppermute | solution.py:533
  28.6 2.1 %collective-permute-done.rest_1_ = f32[784,128]{1,0:T(8,128)S(1)} collective-permute-done((f32[784,128]{1,0:T(8,128)}, f32[784,128]{1,0:T(8,128)S(1)}, u32[]{:S(2)}, u32[]{:S(2)}) %collective-permute-start) | collective-permute-done | bytes 401440 | tf_op jit(solution)/shard_map/ppermute | solution.py:533
  30.7 2.7 %shard_map.109 = (f32[4,16,128]{2,1,0:T(8,128)}, f32[512,128]{1,0:T(8,128)}, f32[512,128]{1,0:T(8,128)}) custom-call(f32[784,128]{1,0:T(8,128)S(1)} %copy-done, f32[784,128]{1,0:T(8,128)S(1)} %collective-permute-done.rest_1_, f32[784,128]{1,0:T(8,128)S(1)} %collective-permute-done.1.rest_2_, f32[784,128]{1,0:T(8,128)S(1)} %collective-permute-done.2.rest_3_, ...), custom_call_target="tpu_custom_call" | custom-call | flops 100000000 | bytes 100000000 | tf_op jit(solution)/shard_map/pallas_call | solution.py:583
  33.3 2.4 %collective-permute-start.3 = (f32[512,128]{1,0:T(8,128)}, f32[512,128]{1,0:T(8,128)}, u32[]{:S(2)}, u32[]{:S(2)}) collective-permute-start(f32[512,128]{1,0:T(8,128)} %get-tuple-element.53), channel_id=1, source_target_pairs={{0,4},{1,5},{2,6},{3,7},{4,0},{5,1},{6,2},{7,3},{8,12},{9,13},{10,... | collective-permute-start | bytes 786440 | tf_op jit(solution)/shard_map/ppermute | solution.py:533
  36.3 1.9 %shard_map.106 = (f32[2,5,64,128]{3,2,1,0:T(8,128)S(1)}, f32[5,64,128]{2,1,0:T(8,128)S(1)}, f32[5,64,128]{2,1,0:T(8,128)S(1)}, f32[2,5,64,128]{3,2,1,0:T(8,128)S(1)}, f32[8,128]{1,0:T(8,128)S(1)}) custom-call(f32[2,64,512]{2,1,0:T(8,128)S(1)} %bitcast.14, f32[64,512]{1,0:T(8,128)S(1)} %bitcast.17, f32[4,272,128]{2,1,0:T(8,128)S(1)} %all-to-all-done.swap_ref), custom_call_target="tpu_custom_call" | custom-call | flops 1 | bytes 1 | tf_op jit(solution)/shard_map/pallas_call | solution.py:575
  38.9 1.9 %shard_map.108 = (f32[4,16,128]{2,1,0:T(8,128)S(1)}, f32[512,128]{1,0:T(8,128)S(1)}, f32[512,128]{1,0:T(8,128)S(1)}) custom-call(f32[784,128]{1,0:T(8,128)S(1)} %copy-done, f32[784,128]{1,0:T(8,128)S(1)} %collective-permute-done.rest_1_, f32[784,128]{1,0:T(8,128)S(1)} %collective-permute-done.1.rest_2_, f32[784,128]{1,0:T(8,128)S(1)} %collective-permute-done.2.rest_3_, ...), custom_call_target="tpu_custom_call" | custom-call | flops 1 | bytes 1 | tf_op jit(solution)/shard_map/pallas_call | solution.py:583
  40.8 11.5 %collective-permute-done.3.far_d_ref = f32[512,128]{1,0:T(8,128)} collective-permute-done((f32[512,128]{1,0:T(8,128)}, f32[512,128]{1,0:T(8,128)}, u32[]{:S(2)}, u32[]{:S(2)}) %collective-permute-start.3) | collective-permute-done | bytes 262176 | tf_op jit(solution)/shard_map/ppermute | solution.py:533
  52.3 4.9 %collective-permute-done.4.far_e_ref = f32[512,128]{1,0:T(8,128)} collective-permute-done((f32[512,128]{1,0:T(8,128)}, f32[512,128]{1,0:T(8,128)}, u32[]{:S(2)}, u32[]{:S(2)}) %collective-permute-start.4) | collective-permute-done | bytes 262176 | tf_op jit(solution)/shard_map/ppermute | solution.py:533
  58.1 4.3 %shard_map.110 = (f32[4,6,5,16,128]{4,3,2,1,0:T(8,128)}, f32[9,16,128]{2,1,0:T(8,128)S(1)}, f32[9,16,128]{2,1,0:T(8,128)S(1)}, f32[9,16,128]{2,1,0:T(8,128)S(1)}, f32[9,16,128]{2,1,0:T(8,128)S(1)}) custom-call(f32[4,16,128]{2,1,0:T(8,128)S(1)} %get-tuple-element.50.meta_ref, f32[512,128]{1,0:T(8,128)S(1)} %get-tuple-element.51.d_ref, ...), custom_call_target="tpu_custom_call" | custom-call | flops 1 | bytes 1 | tf_op jit(solution)/shard_map/pallas_call | solution.py:593
  62.4 3.8 %all-to-all-start.1 = ((f32[4,6,5,16,128]{4,3,2,1,0:T(8,128)}), f32[4,6,5,16,128]{4,3,2,1,0:T(8,128)S(1)}, u32[]{:S(2)}, u32[]{:S(2)}) async-start(f32[4,6,5,16,128]{4,3,2,1,0:T(8,128)} %get-tuple-element.59), calls=%async_computation.1 | async-start | bytes 1966080 | tf_op jit(solution)/shard_map/all_to_all | solution.py:602
  66.3 2.6 %collective-permute-start.8 = (f32[9,16,128]{2,1,0:T(8,128)S(1)}, f32[9,16,128]{2,1,0:T(8,128)S(1)}, u32[]{:S(2)}, u32[]{:S(2)}) collective-permute-start(f32[9,16,128]{2,1,0:T(8,128)S(1)} %get-tuple-element.60), channel_id=1, source_target_pairs={{0,4},{1,5},{2,6},{3,7},{4,0},{5,1},{6,2},{7,3},{8,12},{9,13},{10,... | collective-permute-start | bytes 221192 | tf_op jit(solution)/shard_map/ppermute | solution.py:537
  68.9 3.6 %collective-permute-start.10 = (f32[9,16,128]{2,1,0:T(8,128)S(1)}, f32[9,16,128]{2,1,0:T(8,128)S(1)}, u32[]{:S(2)}, u32[]{:S(2)}) collective-permute-start(f32[9,16,128]{2,1,0:T(8,128)S(1)} %get-tuple-element.62), channel_id=1, source_target_pairs={{0,20},{1,21},{2,22},{3,23},{4,16},{5,17},{6,18},{7,19},{8,28},{9,... | collective-permute-start | bytes 221192 | tf_op jit(solution)/shard_map/ppermute | solution.py:537
  72.7 7.3 %collective-permute-done.9.rest_1_ = f32[9,16,128]{2,1,0:T(8,128)S(1)} collective-permute-done((f32[9,16,128]{2,1,0:T(8,128)S(1)}, f32[9,16,128]{2,1,0:T(8,128)S(1)}, u32[]{:S(2)}, u32[]{:S(2)}) %collective-permute-start.9) | collective-permute-done | bytes 73760 | tf_op jit(solution)/shard_map/ppermute | solution.py:537
  80.0 2.7 %collective-permute-done.10.rest_2_ = f32[9,16,128]{2,1,0:T(8,128)S(1)} collective-permute-done((f32[9,16,128]{2,1,0:T(8,128)S(1)}, f32[9,16,128]{2,1,0:T(8,128)S(1)}, u32[]{:S(2)}, u32[]{:S(2)}) %collective-permute-start.10) | collective-permute-done | bytes 73760 | tf_op jit(solution)/shard_map/ppermute | solution.py:537
  82.7 1.6 %collective-permute-done.11.rest_3_ = f32[9,16,128]{2,1,0:T(8,128)S(1)} collective-permute-done((f32[9,16,128]{2,1,0:T(8,128)S(1)}, f32[9,16,128]{2,1,0:T(8,128)S(1)}, u32[]{:S(2)}, u32[]{:S(2)}) %collective-permute-start.11) | collective-permute-done | bytes 73760 | tf_op jit(solution)/shard_map/ppermute | solution.py:537
  84.4 10.2 %shard_map.112 = (f32[2,64,512]{2,1,0:T(8,128)S(1)}, f32[2,64,512]{2,1,0:T(8,128)S(1)}, f32[2,5,64,128]{3,2,1,0:T(8,128)S(1)}, f32[32,1,128]{2,1,0:T(1,128)}) custom-call(f32[2,5,64,128]{3,2,1,0:T(8,128)S(1)} %copy-done.5, f32[5,64,128]{2,1,0:T(8,128)S(1)} %get-tuple-element.38.cx_ref, f32[5,64,128]{2,1,0:T(8,128)S(1)} %get-tuple-element.39.cy_ref, ...), custom_call_target="tpu_custom_call" | custom-call | flops 1 | bytes 1 | tf_op jit(solution)/shard_map/pallas_call | solution.py:604
  94.6 3.4 %all-to-all-start.2 = ((f32[32,1,128]{2,1,0:T(1,128)}), f32[32,1,128]{2,1,0:T(1,128)S(1)}, u32[]{:S(2)}, u32[]{:S(2)}) async-start(f32[32,1,128]{2,1,0:T(1,128)} %get-tuple-element.64), calls=%async_computation.2 | async-start | bytes 32768 | tf_op jit(solution)/shard_map/all_to_all | solution.py:609
  98.0 1.9 %shard_map.113.qq_ref = f32[2,64,512]{2,1,0:T(8,128)S(1)} custom-call(f32[2,5,64,128]{3,2,1,0:T(8,128)S(1)} %get-tuple-element.67.h_ref, f32[2,64,512]{2,1,0:T(8,128)S(1)} %get-tuple-element.66.q_ref, f32[5,64,128]{2,1,0:T(8,128)S(1)} %get-tuple-element.38.cx_ref, f32[5,64,128]{2,1,0:T(8,128)S(1)} %get-tuple-element.39.cy_ref), custom_call_target="tpu_custom_call" | custom-call | flops 1 | bytes 1 | tf_op jit(solution)/shard_map/pallas_call | solution.py:610
  100.0 5.1 %all-to-all-done.2.dots_ref = f32[32,1,128]{2,1,0:T(1,128)S(1)} async-done(((f32[32,1,128]{2,1,0:T(1,128)}), f32[32,1,128]{2,1,0:T(1,128)S(1)}, u32[]{:S(2)}, u32[]{:S(2)}) %all-to-all-start.2) | async-done | bytes 16416 | tf_op jit(solution)/shard_map/all_to_all | solution.py:609
  (33 shorter events, 6.9 us)
Async XLA Ops:
  7.5 17.4 %collective-permute-start.1 = (f32[784,128]{1,0:T(8,128)}, f32[784,128]{1,0:T(8,128)S(1)}, u32[]{:S(2)}, u32[]{:S(2)}) collective-permute-start(f32[784,128]{1,0:T(8,128)} %get-tuple-element.43), channel_id=1, source_target_pairs={{0,2},{1,3},{2,0},{3,1},{4,6},{5,7},{6,4},{7,5},{8,10},{9,11},{10,... | collective-permute-start | bytes 1204232 | tf_op jit(solution)/shard_map/ppermute | solution.py:533
  10.6 20.0 %collective-permute-start = (f32[784,128]{1,0:T(8,128)}, f32[784,128]{1,0:T(8,128)S(1)}, u32[]{:S(2)}, u32[]{:S(2)}) collective-permute-start(f32[784,128]{1,0:T(8,128)} %get-tuple-element.42), channel_id=1, source_target_pairs={{0,1},{1,0},{2,3},{3,2},{4,5},{5,4},{6,7},{7,6},{8,9},{9,8},{10,11... | collective-permute-start | bytes 1204232 | tf_op jit(solution)/shard_map/ppermute | solution.py:533
  12.1 18.5 %collective-permute-start.2 = (f32[784,128]{1,0:T(8,128)}, f32[784,128]{1,0:T(8,128)S(1)}, u32[]{:S(2)}, u32[]{:S(2)}) collective-permute-start(f32[784,128]{1,0:T(8,128)} %get-tuple-element.48), channel_id=1, source_target_pairs={{0,3},{1,2},{2,1},{3,0},{4,7},{5,6},{6,5},{7,4},{8,11},{9,10},{10,... | collective-permute-start | bytes 1204232 | tf_op jit(solution)/shard_map/ppermute | solution.py:533
  14.7 21.6 %all-to-all-start = ((f32[4,272,128]{2,1,0:T(8,128)}), f32[4,272,128]{2,1,0:T(8,128)S(1)}, u32[]{:S(2)}, u32[]{:S(2)}) async-start(f32[4,272,128]{2,1,0:T(8,128)} %shard_map.105), calls=%async_computation | async-start | bytes 1114112 | tf_op jit(solution)/shard_map/all_to_all | solution.py:574
  18.2 12.4 %copy-start = (f32[784,128]{1,0:T(8,128)S(1)}, f32[784,128]{1,0:T(8,128)}, u32[]{:S(2)}) copy-start(f32[784,128]{1,0:T(8,128)} %get-tuple-element.41.rest_0_.rest_4_) | copy-start | bytes 1204228
  25.0 32.2 %collective-permute-start.5 = (f32[768,128]{1,0:T(8,128)}, f32[768,128]{1,0:T(8,128)S(1)}, u32[]{:S(2)}, u32[]{:S(2)}) collective-permute-start(f32[768,128]{1,0:T(8,128)} %get-tuple-element.56), channel_id=1, source_target_pairs={{0,1},{1,0},{2,3},{3,2},{4,5},{5,4},{6,7},{7,6},{8,9},{9,8},{10,11... | collective-permute-start | bytes 1179656 | tf_op jit(solution)/shard_map/ppermute | solution.py:533
  26.9 30.3 %collective-permute-start.6 = (f32[768,128]{1,0:T(8,128)}, f32[768,128]{1,0:T(8,128)}, u32[]{:S(2)}, u32[]{:S(2)}) collective-permute-start(f32[768,128]{1,0:T(8,128)} %get-tuple-element.57), channel_id=1, source_target_pairs={{0,2},{1,3},{2,0},{3,1},{4,6},{5,7},{6,4},{7,5},{8,10},{9,11},{10,... | collective-permute-start | bytes 1179656 | tf_op jit(solution)/shard_map/ppermute | solution.py:533
  28.5 29.6 %collective-permute-start.7 = (f32[768,128]{1,0:T(8,128)}, f32[768,128]{1,0:T(8,128)}, u32[]{:S(2)}, u32[]{:S(2)}) collective-permute-start(f32[768,128]{1,0:T(8,128)} %get-tuple-element.58), channel_id=1, source_target_pairs={{0,3},{1,2},{2,1},{3,0},{4,7},{5,6},{6,5},{7,4},{8,11},{9,10},{10,... | collective-permute-start | bytes 1179656 | tf_op jit(solution)/shard_map/ppermute | solution.py:533
  30.6 5.6 %copy-start.1 = (f32[2,1,64,512]{3,2,1,0:T(8,128)S(1)}, f32[2,1,64,512]{3,2,1,0:T(8,128)}, u32[]{:S(2)}) copy-start(f32[2,1,64,512]{3,2,1,0:T(8,128)} %param.9) | copy-start | bytes 786436
  30.6 5.6 %copy-start.2 = (f32[1,64,512]{2,1,0:T(8,128)S(1)}, f32[1,64,512]{2,1,0:T(8,128)}, u32[]{:S(2)}) copy-start(f32[1,64,512]{2,1,0:T(8,128)} %param.10) | copy-start | bytes 393220
  33.3 19.0 %collective-permute-start.3 = (f32[512,128]{1,0:T(8,128)}, f32[512,128]{1,0:T(8,128)}, u32[]{:S(2)}, u32[]{:S(2)}) collective-permute-start(f32[512,128]{1,0:T(8,128)} %get-tuple-element.53), channel_id=1, source_target_pairs={{0,4},{1,5},{2,6},{3,7},{4,0},{5,1},{6,2},{7,3},{8,12},{9,13},{10,... | collective-permute-start | bytes 786440 | tf_op jit(solution)/shard_map/ppermute | solution.py:533
  35.8 21.4 %collective-permute-start.4 = (f32[512,128]{1,0:T(8,128)}, f32[512,128]{1,0:T(8,128)}, u32[]{:S(2)}, u32[]{:S(2)}) collective-permute-start(f32[512,128]{1,0:T(8,128)} %get-tuple-element.54), channel_id=1, source_target_pairs={{0,4},{1,5},{2,6},{3,7},{4,0},{5,1},{6,2},{7,3},{8,12},{9,13},{10,... | collective-permute-start | bytes 786440 | tf_op jit(solution)/shard_map/ppermute | solution.py:533
  38.2 0.7 copy-start.6
  38.9 1.9 %copy-start.4 = (f32[2,5,64,128]{3,2,1,0:T(8,128)}, f32[2,5,64,128]{3,2,1,0:T(8,128)S(1)}, u32[]{:S(2)}) copy-start(f32[2,5,64,128]{3,2,1,0:T(8,128)S(1)} %get-tuple-element.37.c0_ref) | copy-start | bytes 983044
  38.9 19.2 %copy-start.3 = (f32[768,128]{1,0:T(8,128)S(1)}, f32[768,128]{1,0:T(8,128)}, u32[]{:S(2)}) copy-start(f32[768,128]{1,0:T(8,128)} %get-tuple-element.55.rest_0_) | copy-start | bytes 1179652
  62.4 22.0 %copy-start.7 = (f32[2,5,64,128]{3,2,1,0:T(8,128)S(1)}, f32[2,5,64,128]{3,2,1,0:T(8,128)}, u32[]{:S(2)}) copy-start(f32[2,5,64,128]{3,2,1,0:T(8,128)} %copy-done.6) | copy-start | bytes 983044
  62.4 22.0 %all-to-all-start.1 = ((f32[4,6,5,16,128]{4,3,2,1,0:T(8,128)}), f32[4,6,5,16,128]{4,3,2,1,0:T(8,128)S(1)}, u32[]{:S(2)}, u32[]{:S(2)}) async-start(f32[4,6,5,16,128]{4,3,2,1,0:T(8,128)} %get-tuple-element.59), calls=%async_computation.1 | async-start | bytes 1966080 | tf_op jit(solution)/shard_map/all_to_all | solution.py:602
  66.3 18.2 %copy-start.5 = (f32[2,5,64,128]{3,2,1,0:T(8,128)S(1)}, f32[2,5,64,128]{3,2,1,0:T(8,128)}, u32[]{:S(2)}) copy-start(f32[2,5,64,128]{3,2,1,0:T(8,128)} %copy-done.4) | copy-start | bytes 983044
  66.3 6.4 %collective-permute-start.8 = (f32[9,16,128]{2,1,0:T(8,128)S(1)}, f32[9,16,128]{2,1,0:T(8,128)S(1)}, u32[]{:S(2)}, u32[]{:S(2)}) collective-permute-start(f32[9,16,128]{2,1,0:T(8,128)S(1)} %get-tuple-element.60), channel_id=1, source_target_pairs={{0,4},{1,5},{2,6},{3,7},{4,0},{5,1},{6,2},{7,3},{8,12},{9,13},{10,... | collective-permute-start | bytes 221192 | tf_op jit(solution)/shard_map/ppermute | solution.py:537
  68.8 11.2 %collective-permute-start.9 = (f32[9,16,128]{2,1,0:T(8,128)S(1)}, f32[9,16,128]{2,1,0:T(8,128)S(1)}, u32[]{:S(2)}, u32[]{:S(2)}) collective-permute-start(f32[9,16,128]{2,1,0:T(8,128)S(1)} %get-tuple-element.61), channel_id=1, source_target_pairs={{0,12},{1,13},{2,14},{3,15},{4,8},{5,9},{6,10},{7,11},{8,4},{9,5},... | collective-permute-start | bytes 221192 | tf_op jit(solution)/shard_map/ppermute | solution.py:537
  68.9 13.9 %collective-permute-start.10 = (f32[9,16,128]{2,1,0:T(8,128)S(1)}, f32[9,16,128]{2,1,0:T(8,128)S(1)}, u32[]{:S(2)}, u32[]{:S(2)}) collective-permute-start(f32[9,16,128]{2,1,0:T(8,128)S(1)} %get-tuple-element.62), channel_id=1, source_target_pairs={{0,20},{1,21},{2,22},{3,23},{4,16},{5,17},{6,18},{7,19},{8,28},{9,... | collective-permute-start | bytes 221192 | tf_op jit(solution)/shard_map/ppermute | solution.py:537
  72.4 11.9 %collective-permute-start.11 = (f32[9,16,128]{2,1,0:T(8,128)S(1)}, f32[9,16,128]{2,1,0:T(8,128)S(1)}, u32[]{:S(2)}, u32[]{:S(2)}) collective-permute-start(f32[9,16,128]{2,1,0:T(8,128)S(1)} %get-tuple-element.63), channel_id=1, source_target_pairs={{0,28},{1,29},{2,30},{3,31},{4,24},{5,25},{6,26},{7,27},{8,20},{9,... | collective-permute-start | bytes 221192 | tf_op jit(solution)/shard_map/ppermute | solution.py:537
  94.6 10.5 %all-to-all-start.2 = ((f32[32,1,128]{2,1,0:T(1,128)}), f32[32,1,128]{2,1,0:T(1,128)S(1)}, u32[]{:S(2)}, u32[]{:S(2)}) async-start(f32[32,1,128]{2,1,0:T(1,128)} %get-tuple-element.64), calls=%async_computation.2 | async-start | bytes 32768 | tf_op jit(solution)/shard_map/all_to_all | solution.py:609
